TPU v7x, 512 devices: a whole 4x8x8 slice. The times are simulated.
512 devices in a mesh: dp: 64 (over z, x, y_hi), mp: 8 (over y_lo, core).
Axes of the slice: x: 4, y: 8 (y_hi: 2, y_lo: 4; y = y_hi * 4 + y_lo), z: 8, core: 2. Of those that a mesh axis runs over, the one named last changes fastest.
Arguments:
- query_emb: bfloat16 [512, 4096], P('dp', 'mp'), as said below
- item_emb: bfloat16 [512, 4096], P('dp', 'mp'), as said below
- pair_index: int32 [512], P('dp'), may hold values from 0 to 511, each once
- hard_index: int32 [512, 4], P('dp'), may hold values from 0 to 511
- hidden_in: bfloat16 [2, 64, 152, 4096], P(None, 'dp', None, 'mp'), may hold values from -24 to 24
- lengths: int32 [2, 64], P(None, 'dp'), may hold values from 76 to 152
- w_query: bfloat16 [4096, 4096], P('dp', 'mp'), as said below
- key_weight_matrix: bfloat16 [4096, 1024], P(None, 'mp'), as said below
- value_weight_matrix: bfloat16 [4096, 1024], P(None, 'mp'), may hold values from -0.09375 to 0.09375
- w_out: bfloat16 [4096, 4096], P('mp', 'dp'), may hold values from -0.09375 to 0.09375
- key_down_matrix: bfloat16 [4096, 16], replicated, may hold values from -0.09375 to 0.09375
- key_up_matrix: bfloat16 [16, 1024], P(None, 'mp'), may hold values from -0.29882812 to 0.29882812
- value_down: bfloat16 [4096, 16], replicated, may hold values from -0.09375 to 0.09375
- value_up_matrix: bfloat16 [16, 1024], P(None, 'mp'), may hold values from -0.29882812 to 0.29882812
Outputs:
- mean_loss: float32 [], replicated
- query_grad: bfloat16 [512, 4096], P('dp', 'mp')
- item_grad: bfloat16 [512, 4096], P('dp', 'mp')
- input_grad: bfloat16 [2, 64, 152, 4096], P(None, 'dp', None, 'mp')
- key_down_grad: float32 [4096, 16], replicated
- value_down_grad: float32 [4096, 16], replicated
- key_up_grad: float32 [16, 1024], P(None, 'mp')
- value_up_grad: float32 [16, 1024], P(None, 'mp')
Inputs may be any that keep to these rules, and one draw needn't show every extreme that they name: `query_emb`: entries within 10 / sqrt(4096) in magnitude. `item_emb`: entries within 10 / sqrt(4096) in magnitude. `w_query`: entries within 16 / sqrt(4096) in magnitude. `key_weight_matrix`: entries within 6 / sqrt(4096) in magnitude.
All inputs are finite; a program needn't handle non-finite values.
Results may differ from a plain program's by a relative error of at most 0.025.
The roundings to bfloat16 on the way count: a program that leaves them out, or rounds other values in their place, can miss the bound.
Values may be sent and summed in bfloat16 or wider, within the bound.
No kernel may reach another device: no remote copies, remote signals or barrier semaphores. Data moves between devices by JAX's collectives and lax.ppermute only.
A program may use at most 64 MiB of HBM per device.

v0:
```python
import math

import jax
import jax.numpy as jnp
from jax import lax
from jax.sharding import PartitionSpec as P

HEADS = 32
KV_HEADS = 8
HEAD_DIM = 128


INV_TEMP = 50.0
HARD_NEGATIVE_ADD = 4.0
ADAPTER_SCALE = 2.0


def final_product(left_side, right_side):
    return lax.dot_general(
        left_side, right_side, (((1,), (1,)), ((), ())), preferred_element_type=jnp.float32
    )


def first_product(left_side, right_side):
    return lax.dot_general(
        left_side, right_side, (((0,), (0,)), ((), ())), preferred_element_type=jnp.float32
    )


def local(
    query_emb,
    item_emb,
    pair_index,
    hard_index,
    hidden_in,
    lengths,
    w_query,
    key_weight_matrix,
    value_weight_matrix,
    w_out,
    key_down_matrix,
    key_up_matrix,
    value_down,
    value_up_matrix,
):
    dp_count = lax.axis_size("dp")
    local_rows = query_emb.shape[0]
    batch_size = local_rows * dp_count
    items_all = lax.all_gather(item_emb, "dp", axis=0, tiled=True)
    partial_scores = final_product(query_emb, items_all)
    pair_scores = lax.psum(partial_scores, "mp") * INV_TEMP
    columns = jnp.arange(batch_size, dtype=jnp.int32)
    hard_negative_count = jnp.sum(
        (hard_index[:, :, None] == columns[None, None, :]).astype(jnp.float32), axis=1
    )
    score_logits = pair_scores + HARD_NEGATIVE_ADD * hard_negative_count
    row_top = jnp.max(score_logits, axis=1, keepdims=True)
    log_total = row_top[:, 0] + jnp.log(jnp.sum(jnp.exp(score_logits - row_top), axis=1))
    target = (pair_index[:, None] == columns[None, :]).astype(jnp.float32)
    picked = jnp.sum(target * score_logits, axis=1)
    loss_part = jnp.sum(log_total - picked)
    residual = (jnp.exp(score_logits - log_total[:, None]) - target).astype(jnp.bfloat16)
    query_grad = (
        jnp.dot(residual, items_all, preferred_element_type=jnp.float32) * INV_TEMP
    ).astype(jnp.bfloat16)
    item_grad = lax.psum_scatter(
        first_product(residual, query_emb) * INV_TEMP, "dp", scatter_dimension=0, tiled=True
    ).astype(jnp.bfloat16)
    sub_count = hidden_in.shape[0]
    seq_len = hidden_in.shape[2]
    full_rows = lax.all_gather(hidden_in, "mp", axis=3, tiled=True)
    model_width = full_rows.shape[3]
    token_inputs = full_rows.reshape(sub_count * seq_len, model_width)
    seq_lengths = lengths[:, 0]
    last_rows = jnp.arange(sub_count, dtype=jnp.int32) * seq_len + seq_lengths - 1
    last_tokens = jnp.take(token_inputs, last_rows, axis=0)
    cot_local = item_grad[:sub_count]
    cot_full = lax.all_gather(cot_local, "mp", axis=1, tiled=True)
    adapter_rank = key_down_matrix.shape[1]
    down_both = jnp.concatenate([key_down_matrix, value_down], axis=1)
    reduced_pair = jnp.dot(token_inputs, down_both, preferred_element_type=jnp.float32).astype(
        jnp.bfloat16
    )
    reduced_key = reduced_pair[:, :adapter_rank]
    reduced_value = reduced_pair[:, adapter_rank:]
    key_rows = (
        jnp.dot(token_inputs, key_weight_matrix, preferred_element_type=jnp.float32)
        + ADAPTER_SCALE * jnp.dot(reduced_key, key_up_matrix, preferred_element_type=jnp.float32)
    ).astype(jnp.bfloat16)
    value_rows = (
        jnp.dot(token_inputs, value_weight_matrix, preferred_element_type=jnp.float32)
        + ADAPTER_SCALE
        * jnp.dot(reduced_value, value_up_matrix, preferred_element_type=jnp.float32)
    ).astype(jnp.bfloat16)
    query_width = w_query.shape[1]
    wq_full, wo_full = (
        lax.all_gather(w_query, "dp", axis=0, tiled=True),
        lax.all_gather(w_out, "dp", axis=1, tiled=True),
    )
    query = jnp.dot(last_tokens, wq_full, preferred_element_type=jnp.float32).astype(jnp.bfloat16)
    attn_grad = final_product(cot_full, wo_full).astype(jnp.bfloat16)
    group_size = HEADS // KV_HEADS
    kv_local = key_rows.shape[1] // HEAD_DIM
    score_scale = 1.0 / math.sqrt(HEAD_DIM)
    q_heads = query.reshape(sub_count, kv_local, group_size, HEAD_DIM)
    k_heads = key_rows.reshape(sub_count, seq_len, kv_local, HEAD_DIM)
    v_heads = value_rows.reshape(sub_count, seq_len, kv_local, HEAD_DIM)
    raw_scores = (
        jnp.einsum("bkgd,bjkd->bkgj", q_heads, k_heads, preferred_element_type=jnp.float32)
        * score_scale
    )
    live_mask = jnp.arange(seq_len, dtype=jnp.int32)[None, :] < seq_lengths[:, None]
    raw_scores = jnp.where(live_mask[:, None, None, :], raw_scores, -jnp.inf)
    row_peak = jnp.max(raw_scores, axis=-1, keepdims=True)
    weights = jnp.exp(raw_scores - row_peak)
    softmax_probs = weights / jnp.sum(weights, axis=-1, keepdims=True)
    prob_half = softmax_probs.astype(jnp.bfloat16)
    grad_heads = attn_grad.reshape(sub_count, kv_local, group_size, HEAD_DIM)
    prob_grad = jnp.einsum(
        "bkgd,bjkd->bkgj", grad_heads, v_heads, preferred_element_type=jnp.float32
    )
    score_grad = (
        softmax_probs
        * (prob_grad - jnp.sum(softmax_probs * prob_grad, axis=-1, keepdims=True))
        * score_scale
    ).astype(jnp.bfloat16)
    query_delta = (
        jnp.einsum("bkgj,bjkd->bkgd", score_grad, k_heads, preferred_element_type=jnp.float32)
        .astype(jnp.bfloat16)
        .reshape(sub_count, query_width)
    )
    key_adapter_change = (
        jnp.einsum("bkgj,bkgd->bjkd", score_grad, q_heads, preferred_element_type=jnp.float32)
        .astype(jnp.bfloat16)
        .reshape(sub_count * seq_len, kv_local * HEAD_DIM)
    )
    value_adapter_change = (
        jnp.einsum("bkgj,bkgd->bjkd", prob_half, grad_heads, preferred_element_type=jnp.float32)
        .astype(jnp.bfloat16)
        .reshape(sub_count * seq_len, kv_local * HEAD_DIM)
    )
    last_part = final_product(query_delta, wq_full)
    key_coefficient = final_product(key_adapter_change, key_up_matrix).astype(jnp.bfloat16)
    value_coefficient = final_product(value_adapter_change, value_up_matrix).astype(jnp.bfloat16)
    input_portion = final_product(key_adapter_change, key_weight_matrix) + final_product(
        value_adapter_change, value_weight_matrix
    )
    input_portion = input_portion + ADAPTER_SCALE * (
        final_product(key_coefficient, key_down_matrix)
        + final_product(value_coefficient, value_down)
    )
    input_portion = input_portion.at[last_rows].add(last_part)
    input_sum = lax.psum_scatter(
        input_portion.astype(jnp.bfloat16), "mp", scatter_dimension=1, tiled=True
    ).astype(jnp.float32)
    input_sum = input_sum.at[last_rows].add(cot_local.astype(jnp.float32))
    input_grad = input_sum.astype(jnp.bfloat16).reshape(hidden_in.shape)
    key_down_grad, value_down_grad = lax.psum(
        (
            ADAPTER_SCALE * first_product(token_inputs, key_coefficient),
            ADAPTER_SCALE * first_product(token_inputs, value_coefficient),
        ),
        ("dp", "mp"),
    )
    total_loss, key_up_grad, value_up_grad = lax.psum(
        (
            loss_part,
            ADAPTER_SCALE * first_product(reduced_key, key_adapter_change),
            ADAPTER_SCALE * first_product(reduced_value, value_adapter_change),
        ),
        "dp",
    )
    mean_loss = total_loss / batch_size
    return (
        mean_loss,
        query_grad,
        item_grad,
        input_grad,
        key_down_grad,
        value_down_grad,
        key_up_grad,
        value_up_grad,
    )


def solution(mesh):
    in_specs = (
        P("dp", "mp"),
        P("dp", "mp"),
        P("dp"),
        P("dp", None),
        P(None, "dp", None, "mp"),
        P(None, "dp"),
        P("dp", "mp"),
        P(None, "mp"),
        P(None, "mp"),
        P("mp", "dp"),
        P(),
        P(None, "mp"),
        P(),
        P(None, "mp"),
    )
    out_specs = (
        P(),
        P("dp", "mp"),
        P("dp", "mp"),
        P(None, "dp", None, "mp"),
        P(),
        P(),
        P(None, "mp"),
        P(None, "mp"),
    )
    return jax.shard_map(local, mesh=mesh, in_specs=in_specs, out_specs=out_specs, check_vma=False)
```

profile of v0, /device:TPU:16, one launch (start us, length us, event | category | flops | bytes accessed | tf_op | source)
XLA Modules:
  0.0 1289.2 jit_solution(13765281510140379028)
XLA Ops:
  8.1 0.8 convert_reduce_fusion
  8.9 231.5 %all_gather.15 = bf16[512,512]{1,0:T(8,128)(2,1)S(1)} all-gather(bf16[8,512]{1,0:T(8,128)(2,1)} %param.15), channel_id=1, replica_groups=mesh['dp'=64,'mp'=8] {'dp'}, dimensions={0}, use_global_device_ids=true | all-gather | bytes 532480 | tf_op jit(solution)/shard_map/all_gather | solution.py:49
  240.4 0.8 copy-done.4
  241.2 0.9 fusion.47
  242.1 20.6 %psum.42 = f32[8,512]{1,0:T(8,128)S(1)} all-reduce(f32[8,512]{1,0:T(8,128)S(1)} %fusion.47), channel_id=1, replica_groups=mesh['dp'=64,'mp'=8] {'mp'}, use_global_device_ids=true, to_apply=%region_0.0 | all-reduce | flops 4096 | bytes 32768 | tf_op jit(solution)/shard_map/psum | solution.py:51
  262.9 0.9 select_reduce_fusion
  264.4 2.1 convolution_multiply_fusion.2
  268.3 1.2 and_bitcast_fusion
  270.1 1.3 iota_compare_fusion.2
  271.3 497.6 %reduce-scatter.3.cloned.1.call-done = f32[8,512]{1,0:T(8,128)} async-done(((f32[512,512]{1,0:T(8,128)}), f32[8,512]{1,0:T(8,128)}) %reduce-scatter.3.cloned.1.call-update) | async-done | bytes 16400 | tf_op jit(solution)/shard_map/reduce_scatter | solution.py:66
  769.0 0.7 convert_element_type.85
  770.3 12.3 all_gather.18
  782.7 3.5 gather_fusion
  786.1 2.7 fusion.8
  788.8 0.9 convolution_multiply_fusion.3
  789.8 0.9 convolution_multiply_fusion.4
  790.7 3.4 fusion.7
  794.1 1.5 fusion.6
  795.6 3.5 convolution_convert_fusion.7
  799.1 1.2 reshape.140
  800.3 1.0 fusion.15
  801.3 0.6 copy-done.11
  801.9 1.2 fusion.46
  803.2 3.4 convolution_convert_fusion.6
  806.6 1.3 reshape.142
  807.9 1.6 fusion.48
  809.5 1.8 fusion.17
  811.3 1.8 convolution_convert_fusion.1
  813.2 1.7 convolution_convert_fusion
  814.9 1.0 convolution_convert_fusion.4
  816.0 1.7 fusion.49
  817.9 0.8 fusion.50
  818.8 0.8 fusion.2
  820.0 3.1 fusion.3
  823.3 1.8 fusion.35
  825.1 5.5 scatter_fusion
  830.6 4.2 convert_element_type.103
  834.9 1.9 fusion.10
  836.8 1.9 fusion.4
  838.7 1.9 fusion.5
  840.7 1.0 convolution_multiply_fusion.7
  841.7 1.0 convolution_multiply_fusion.6
  842.7 430.8 %all-reduce.1 = (f32[]{:T(128)}, f32[16,128]{1,0:T(8,128)}, f32[16,128]{1,0:T(8,128)}) all-reduce(f32[]{:T(128)} %get-tuple-element.33, f32[16,128]{1,0:T(8,128)S(1)} %convolution_multiply_fusion.7, f32[16,128]{1,0:T(8,128)S(1)} %convolution_multiply_fusion.6), channel_id=1, replica_groups=mesh['dp'=64,'mp'=8] {'dp'}, use_global_device_ids=true, to_apply=%region_6.0 | all-reduce | flops 4097 | bytes 32776 | tf_op jit(solution)/shard_map/psum | solution.py:165
  1274.3 1.0 convert_element_type.104
  1275.3 1.0 scatter_custom_fusion.1
  1276.3 0.8 convert_element_type.106
  1277.1 1.7 copy.34
  1278.8 1.7 copy.35
  (54 shorter events, 4.7 us)
Async XLA Ops:
  8.0 786.1 %copy-start = (bf16[4096,128]{1,0:T(8,128)(2,1)S(1)}, bf16[4096,128]{1,0:T(8,128)(2,1)}, u32[]{:S(2)}) copy-start(bf16[4096,128]{1,0:T(8,128)(2,1)} %param.21) | copy-start | bytes 3145732
  8.0 761.0 %reduce-scatter.3.cloned.1.call-start = ((), (), s32[]{:S(2)}) async-start(), calls=%async_computation.2 | async-start | bytes 1064960 | tf_op jit(solution)/shard_map/reduce_scatter | solution.py:66
  240.4 0.8 copy-start.4
  264.4 518.3 %copy-start.14 = (f32[8]{0:T(128)}, f32[8]{0:T(128)S(1)}, u32[]{:S(2)}) copy-start(f32[8]{0:T(128)S(1)} %get-tuple-element.34) | copy-start | bytes 100
  266.5 516.2 %all-gather.4.cloned.1.call-start = ((), (), s32[]{:S(2)}) async-start(), calls=%async_computation.3 | async-start | bytes 2801664 | tf_op jit(solution)/shard_map/all_gather | solution.py:71
  267.1 528.5 %all-gather.6.cloned.1.call-start = ((), (), s32[]{:S(2)}) async-start(), calls=%async_computation.4 | async-start | bytes 4259840 | tf_op jit(solution)/shard_map/all_gather | solution.py:97
  267.7 535.5 %all-gather.8.cloned.1.call-start = ((), (), s32[]{:S(2)}) async-start(), calls=%async_computation.5 | async-start | bytes 4259840 | tf_op jit(solution)/shard_map/all_gather | solution.py:98
  268.2 1006.0 %reduce-scatter.5.cloned.1.call-start = ((), (), s32[]{:S(2)}) async-start(), calls=%async_computation.6 | async-start | bytes 2801664 | tf_op jit(solution)/shard_map/reduce_scatter | solution.py:153
  269.5 513.2 %copy-start.16 = (s32[2,1]{0,1:T(1,128)}, s32[2,1]{0,1:T(1,128)S(1)}, u32[]{:S(2)}) copy-start(s32[2,1]{0,1:T(1,128)S(1)} %get-tuple-element.32) | copy-start | bytes 28
  769.7 0.6 copy-start.12
  782.7 11.5 copy-start.1
  788.8 5.3 copy-start.8
  801.3 0.6 copy-start.11
  815.9 1.9 copy-start.9
  815.9 1.8 copy-start.5
  815.9 1.8 copy-start.13
  816.0 1.9 copy-start.6
  817.9 0.9 copy-start.10
  817.9 0.9 copy-start.7
  818.8 1.2 copy-start.3
  820.0 3.3 copy-start.2
  820.0 3.3 copy-start.15
  834.9 442.2 %all-reduce.4.cloned.1.call-start = ((), (), s32[]{:S(2)}) async-start(), calls=%async_computation.7 | async-start | bytes 1048576 | tf_op jit(solution)/shard_map/psum | solution.py:158
Sparse Core Ops, SparseCore 0:
  266.6 502.3 reduce-scatter.2
  841.5 265.8 all-reduce.3
Sparse Core Ops, SparseCore 1:
  269.0 35.5 all-gather.3
  308.8 158.1 all-gather.5
  472.0 149.3 all-gather.7
  835.0 31.0 reduce-scatter.4
where the time goes:
time: 1290 us
  blocking collectives  695 us (54%)
  waiting for transfers between devices  499 us (39%)
  matrix products  44.6 us (3%)
  other arithmetic  20 us (2%)
  between operations  17.7 us (1%)
    reduce_scatter x1, waiting for transfers between devices, local(): lax.psum_scatter(first_product(residual, query_emb) * INV_TEMP, 'dp', sca...  498 us
    psum x1, blocking collectives, local(): lax.psum((loss_part, ADAPTER_SCALE * first_product(reduced_key, key_adapt...  431 us
    all_gather x1, blocking collectives, local(): items_all = lax.all_gather(item_emb, 'dp', axis=0, tiled=True)  231 us
  transfers between devices with their start and end apart: 6, of which 1 were waited for; matrix products, arithmetic and copies ran while one was open for 3% of the time, Pallas kernels for 0%

commit v1 on v0

--- a/solution.py
+++ b/solution.py
@@ -3,17 +3,19 @@
 import jax
 import jax.numpy as jnp
 from jax import lax
+from jax.sharding import Mesh
 from jax.sharding import PartitionSpec as P
 
 HEADS = 32
 KV_HEADS = 8
 HEAD_DIM = 128
 
-
 INV_TEMP = 50.0
 HARD_NEGATIVE_ADD = 4.0
 ADAPTER_SCALE = 2.0
 
+DP = ("z", "x", "h")
+
 
 def final_product(left_side, right_side):
     return lax.dot_general(
@@ -25,6 +27,16 @@
     return lax.dot_general(
         left_side, right_side, (((0,), (0,)), ((), ())), preferred_element_type=jnp.float32
     )
+
+
+def spread(block, axes):
+    count = lax.axis_size(axes)
+    copies = jnp.broadcast_to(block[None], (count,) + block.shape)
+    return lax.all_to_all(copies, axes, split_axis=0, concat_axis=0, tiled=True)
+
+
+def swap(blocks, axes):
+    return lax.all_to_all(blocks, axes, split_axis=0, concat_axis=0, tiled=True)
 
 
 def local(
@@ -43,29 +55,12 @@
     value_down,
     value_up_matrix,
 ):
-    dp_count = lax.axis_size("dp")
+    dp_count = lax.axis_size(DP)
+    mp_count = lax.axis_size("mp")
     local_rows = query_emb.shape[0]
     batch_size = local_rows * dp_count
-    items_all = lax.all_gather(item_emb, "dp", axis=0, tiled=True)
-    partial_scores = final_product(query_emb, items_all)
-    pair_scores = lax.psum(partial_scores, "mp") * INV_TEMP
-    columns = jnp.arange(batch_size, dtype=jnp.int32)
-    hard_negative_count = jnp.sum(
-        (hard_index[:, :, None] == columns[None, None, :]).astype(jnp.float32), axis=1
-    )
-    score_logits = pair_scores + HARD_NEGATIVE_ADD * hard_negative_count
-    row_top = jnp.max(score_logits, axis=1, keepdims=True)
-    log_total = row_top[:, 0] + jnp.log(jnp.sum(jnp.exp(score_logits - row_top), axis=1))
-    target = (pair_index[:, None] == columns[None, :]).astype(jnp.float32)
-    picked = jnp.sum(target * score_logits, axis=1)
-    loss_part = jnp.sum(log_total - picked)
-    residual = (jnp.exp(score_logits - log_total[:, None]) - target).astype(jnp.bfloat16)
-    query_grad = (
-        jnp.dot(residual, items_all, preferred_element_type=jnp.float32) * INV_TEMP
-    ).astype(jnp.bfloat16)
-    item_grad = lax.psum_scatter(
-        first_product(residual, query_emb) * INV_TEMP, "dp", scatter_dimension=0, tiled=True
-    ).astype(jnp.bfloat16)
+    feature_width = query_emb.shape[1]
+
     sub_count = hidden_in.shape[0]
     seq_len = hidden_in.shape[2]
     full_rows = lax.all_gather(hidden_in, "mp", axis=3, tiled=True)
@@ -74,8 +69,43 @@
     seq_lengths = lengths[:, 0]
     last_rows = jnp.arange(sub_count, dtype=jnp.int32) * seq_len + seq_lengths - 1
     last_tokens = jnp.take(token_inputs, last_rows, axis=0)
+
+    rows_here, query_width = w_query.shape
+    both = jnp.stack([w_query, w_out.T])
+    both = lax.all_gather(both, "h", axis=0, tiled=False)
+    both = spread(both, "x")
+    plane_rows = both.shape[0] * both.shape[1] * rows_here
+    wq_plane = both[:, :, 0].reshape(plane_rows, query_width)
+    wo_plane = both[:, :, 1].reshape(plane_rows, query_width)
+    wq_full = lax.all_gather(wq_plane, "z", axis=0, tiled=True)
+    wo_full = lax.all_gather(wo_plane, "z", axis=0, tiled=True)
+
+    emb_all = spread(jnp.concatenate([item_emb, query_emb], axis=0), DP)
+    items_all = emb_all[:, :local_rows].reshape(batch_size, feature_width)
+    queries_all = emb_all[:, local_rows:].reshape(batch_size, feature_width)
+    partial_scores = final_product(query_emb, items_all)
+    pair_scores = jnp.sum(spread(partial_scores, "mp"), axis=0) * INV_TEMP
+    columns = jnp.arange(batch_size, dtype=jnp.int32)
+    hard_negative_count = jnp.sum(
+        (hard_index[:, :, None] == columns[None, None, :]).astype(jnp.float32), axis=1
+    )
+    score_logits = pair_scores + HARD_NEGATIVE_ADD * hard_negative_count
+    row_top = jnp.max(score_logits, axis=1, keepdims=True)
+    log_total = row_top[:, 0] + jnp.log(jnp.sum(jnp.exp(score_logits - row_top), axis=1))
+    target = (pair_index[:, None] == columns[None, :]).astype(jnp.float32)
+    picked = jnp.sum(target * score_logits, axis=1)
+    loss_part = jnp.sum(log_total - picked)
+    residual = (jnp.exp(score_logits - log_total[:, None]) - target).astype(jnp.bfloat16)
+    residual_columns = swap(
+        residual.reshape(local_rows, dp_count, local_rows).transpose(1, 0, 2), DP
+    ).reshape(batch_size, local_rows)
+    item_grad = (first_product(residual_columns, queries_all) * INV_TEMP).astype(jnp.bfloat16)
+    query_grad = (
+        jnp.dot(residual, items_all, preferred_element_type=jnp.float32) * INV_TEMP
+    ).astype(jnp.bfloat16)
     cot_local = item_grad[:sub_count]
-    cot_full = lax.all_gather(cot_local, "mp", axis=1, tiled=True)
+    cot_full = spread(cot_local, "mp").transpose(1, 0, 2).reshape(sub_count, model_width)
+
     adapter_rank = key_down_matrix.shape[1]
     down_both = jnp.concatenate([key_down_matrix, value_down], axis=1)
     reduced_pair = jnp.dot(token_inputs, down_both, preferred_element_type=jnp.float32).astype(
@@ -92,13 +122,8 @@
         + ADAPTER_SCALE
         * jnp.dot(reduced_value, value_up_matrix, preferred_element_type=jnp.float32)
     ).astype(jnp.bfloat16)
-    query_width = w_query.shape[1]
-    wq_full, wo_full = (
-        lax.all_gather(w_query, "dp", axis=0, tiled=True),
-        lax.all_gather(w_out, "dp", axis=1, tiled=True),
-    )
     query = jnp.dot(last_tokens, wq_full, preferred_element_type=jnp.float32).astype(jnp.bfloat16)
-    attn_grad = final_product(cot_full, wo_full).astype(jnp.bfloat16)
+    attn_grad = jnp.dot(cot_full, wo_full, preferred_element_type=jnp.float32).astype(jnp.bfloat16)
     group_size = HEADS // KV_HEADS
     kv_local = key_rows.shape[1] // HEAD_DIM
     score_scale = 1.0 / math.sqrt(HEAD_DIM)
@@ -155,46 +180,67 @@
     ).astype(jnp.float32)
     input_sum = input_sum.at[last_rows].add(cot_local.astype(jnp.float32))
     input_grad = input_sum.astype(jnp.bfloat16).reshape(hidden_in.shape)
-    key_down_grad, value_down_grad = lax.psum(
-        (
-            ADAPTER_SCALE * first_product(token_inputs, key_coefficient),
-            ADAPTER_SCALE * first_product(token_inputs, value_coefficient),
-        ),
-        ("dp", "mp"),
-    )
-    total_loss, key_up_grad, value_up_grad = lax.psum(
-        (
-            loss_part,
-            ADAPTER_SCALE * first_product(reduced_key, key_adapter_change),
-            ADAPTER_SCALE * first_product(reduced_value, value_adapter_change),
-        ),
-        "dp",
-    )
-    mean_loss = total_loss / batch_size
+
+    own_rows = hidden_in.reshape(sub_count * seq_len, feature_width)
+    coefficients = spread(jnp.concatenate([key_coefficient, value_coefficient], axis=1), "mp")
+    coefficient_sum = jnp.sum(coefficients.astype(jnp.float32), axis=0)
+    down_part = ADAPTER_SCALE * lax.dot_general(
+        coefficient_sum,
+        own_rows.astype(jnp.float32),
+        (((0,), (0,)), ((), ())),
+        precision=lax.Precision.HIGHEST,
+        preferred_element_type=jnp.float32,
+    )
+    up_part = ADAPTER_SCALE * jnp.concatenate(
+        [
+            first_product(reduced_key, key_adapter_change),
+            first_product(reduced_value, value_adapter_change),
+        ],
+        axis=0,
+    )
+    down_cut = down_part.size // dp_count
+    up_cut = up_part.size // dp_count
+    shares = jnp.concatenate(
+        [
+            down_part.reshape(dp_count, down_cut),
+            up_part.reshape(dp_count, up_cut),
+            jnp.broadcast_to(loss_part, (dp_count, HEAD_DIM - up_cut)),
+        ],
+        axis=1,
+    )
+    share_sum = jnp.sum(swap(shares, DP), axis=0)
+    mean_loss = share_sum[down_cut + up_cut] / batch_size
+    summed = spread(share_sum, DP)
+    up_grad = summed[:, down_cut : down_cut + up_cut].reshape(up_part.shape)
+    down_slice = summed[:, :down_cut].reshape(down_part.shape)
+    down_grad = spread(down_slice, "mp").transpose(1, 0, 2).reshape(-1, model_width).T
     return (
         mean_loss,
         query_grad,
         item_grad,
         input_grad,
-        key_down_grad,
-        value_down_grad,
-        key_up_grad,
-        value_up_grad,
+        down_grad[:, :adapter_rank],
+        down_grad[:, adapter_rank:],
+        up_grad[:adapter_rank],
+        up_grad[adapter_rank:],
     )
 
 
 def solution(mesh):
+    fine = Mesh(
+        mesh.devices.reshape(8, 4, 2, mesh.devices.shape[1]), ("z", "x", "h", "mp")
+    )
     in_specs = (
-        P("dp", "mp"),
-        P("dp", "mp"),
-        P("dp"),
-        P("dp", None),
-        P(None, "dp", None, "mp"),
-        P(None, "dp"),
-        P("dp", "mp"),
-        P(None, "mp"),
-        P(None, "mp"),
-        P("mp", "dp"),
+        P(DP, "mp"),
+        P(DP, "mp"),
+        P(DP),
+        P(DP, None),
+        P(None, DP, None, "mp"),
+        P(None, DP),
+        P(DP, "mp"),
+        P(None, "mp"),
+        P(None, "mp"),
+        P("mp", DP),
         P(),
         P(None, "mp"),
         P(),
@@ -202,12 +248,12 @@
     )
     out_specs = (
         P(),
-        P("dp", "mp"),
-        P("dp", "mp"),
-        P(None, "dp", None, "mp"),
-        P(),
-        P(),
-        P(None, "mp"),
-        P(None, "mp"),
-    )
-    return jax.shard_map(local, mesh=mesh, in_specs=in_specs, out_specs=out_specs, check_vma=False)
+        P(DP, "mp"),
+        P(DP, "mp"),
+        P(None, DP, None, "mp"),
+        P(),
+        P(),
+        P(None, "mp"),
+        P(None, "mp"),
+    )
+    return jax.shard_map(local, mesh=fine, in_specs=in_specs, out_specs=out_specs, check_vma=False)

time: 1290 us -> 298 us (0.23)
  the two profiles are of different devices: /device:TPU:16 before, /device:TPU:1 now
where the time goes in v1:
time: 298 us; the launch traced here: 297 us
  waiting for transfers between devices  92.6 us (31%)
  blocking collectives  66.7 us (22%)
  starting transfers between devices  64.9 us (22%)
  matrix products  25.6 us (9%)
  other arithmetic  16.5 us (6%)
  between operations  16 us (5%)
  local copies, waits for them, and re-layouts  14.3 us (5%)
    all_to_all x5, starting transfers between devices, spread(): return lax.all_to_all(copies, axes, split_axis=0, concat_axis=0, tiled=True)  57.4 us
    all_to_all x5, waiting for transfers between devices, spread(): return lax.all_to_all(copies, axes, split_axis=0, concat_axis=0, tiled=True)  41.4 us
    all_gather x1, waiting for transfers between devices, local(): wo_full = lax.all_gather(wo_plane, 'z', axis=0, tiled=True)  36.8 us
    all_to_all x2, blocking collectives, spread(): return lax.all_to_all(copies, axes, split_axis=0, concat_axis=0, tiled=True)  29.7 us
    all_to_all x1, blocking collectives, swap(): return lax.all_to_all(blocks, axes, split_axis=0, concat_axis=0, tiled=True)  25 us
    all_to_all x1, waiting for transfers between devices, swap(): return lax.all_to_all(blocks, axes, split_axis=0, concat_axis=0, tiled=True)  13 us
    all_gather x1, blocking collectives, local(): both = lax.all_gather(both, 'h', axis=0, tiled=False)  11.9 us
    all_to_all x1, starting transfers between devices, swap(): return lax.all_to_all(blocks, axes, split_axis=0, concat_axis=0, tiled=True)  7.33 us
  transfers between devices with their start and end apart: 10, of which 6 were waited for; matrix products, arithmetic and copies ran while one was open for 11% of the time, Pallas kernels for 0%

profile of v1, /device:TPU:1, one launch (start us, length us, event | category | flops | bytes accessed | tf_op | source)
XLA Modules:
  0.0 296.6 jit_solution(15741318507691150498)
XLA Ops:
  7.2 0.7 all-gather.5.cloned.1.call-update
  8.0 0.9 pad_maximum_fusion
  8.9 11.9 %all-gather = bf16[4,64,512]{2,1,0:T(8,128)(2,1)S(1)} all-gather(bf16[2,64,512]{2,1,0:T(8,128)(2,1)S(1)} %pad_maximum_fusion), channel_id=2, replica_groups=mesh['z'=8,'x'=4,'h'=2,'mp'=8] {'h'}, dimensions={0}, use_global_device_ids=true | all-gather | bytes 393216 | tf_op jit(solution)/shard_map/all_gather | solution.py:75
  20.9 12.2 %all_to_all.53 = bf16[4,2,2,64,512]{4,3,2,1,0:T(8,128)(2,1)S(1)} all-to-all(bf16[4,2,2,64,512]{4,3,2,1,0:T(8,128)(2,1)S(1)} %broadcast_in_dim.42), channel_id=1, replica_groups=mesh['z'=8,'x'=4,'h'=2,'mp'=8] {'x'}, dimensions={0} | all-to-all | bytes 2097152 | tf_op jit(solution)/shard_map/all_to_all | solution.py:35
  33.1 1.2 fusion.53
  34.3 0.7 all-gather.9.cloned.1.call-update
  35.1 1.1 broadcast_in_dim.45
  36.2 17.2 %all-to-all-start.1 = ((bf16[64,16,512]{2,1,0:T(8,128)(2,1)}), bf16[64,16,512]{2,1,0:T(8,128)(2,1)S(1)}, u32[]{:S(2)}, u32[]{:S(2)}) async-start(bf16[64,16,512]{2,1,0:T(8,128)(2,1)} %broadcast_in_dim.45), calls=%async_computation.1 | async-start | bytes 2097152 | tf_op jit(solution)/shard_map/all_to_all | solution.py:35
  54.0 19.0 %all-to-all-done.1 = bf16[64,16,512]{2,1,0:T(8,128)(2,1)S(1)} async-done(((bf16[64,16,512]{2,1,0:T(8,128)(2,1)}), bf16[64,16,512]{2,1,0:T(8,128)(2,1)S(1)}, u32[]{:S(2)}, u32[]{:S(2)}) %all-to-all-start.1) | async-done | bytes 1048608 | tf_op jit(solution)/shard_map/all_to_all | solution.py:35
  73.2 0.8 broadcast_in_dim.46
  74.0 21.1 %all-to-all-start.2 = ((f32[8,8,512]{2,1,0:T(8,128)}), f32[8,8,512]{2,1,0:T(8,128)S(1)}, u32[]{:S(2)}, u32[]{:S(2)}) async-start(f32[8,8,512]{2,1,0:T(8,128)} %broadcast_in_dim.46), calls=%async_computation.2 | async-start | bytes 262144 | tf_op jit(solution)/shard_map/all_to_all | solution.py:35
  95.8 5.2 %all-to-all-done.2 = f32[8,8,512]{2,1,0:T(8,128)S(1)} async-done(((f32[8,8,512]{2,1,0:T(8,128)}), f32[8,8,512]{2,1,0:T(8,128)S(1)}, u32[]{:S(2)}, u32[]{:S(2)}) %all-to-all-start.2) | async-done | bytes 131104 | tf_op jit(solution)/shard_map/all_to_all | solution.py:35
  102.3 0.8 copy.53
  103.1 7.3 %all-to-all-start.3 = ((bf16[64,8,8]{2,1,0:T(8,128)(2,1)}), bf16[64,8,8]{2,1,0:T(8,128)(2,1)S(1)}, u32[]{:S(2)}, u32[]{:S(2)}) async-start(bf16[64,8,8]{2,1,0:T(8,128)(2,1)} %copy.53), calls=%async_computation.3 | async-start | bytes 262144 | tf_op jit(solution)/shard_map/all_to_all | solution.py:39
  111.1 13.0 %all-to-all-done.3 = bf16[64,8,8]{2,1,0:T(8,128)(2,1)S(1)} async-done(((bf16[64,8,8]{2,1,0:T(8,128)(2,1)}), bf16[64,8,8]{2,1,0:T(8,128)(2,1)S(1)}, u32[]{:S(2)}, u32[]{:S(2)}) %all-to-all-start.3) | async-done | bytes 8224 | tf_op jit(solution)/shard_map/all_to_all | solution.py:39
  125.0 6.2 %all-to-all-start.4 = ((bf16[8,2,512]{2,1,0:T(2,128)(2,1)}), bf16[8,2,512]{2,1,0:T(2,128)(2,1)}, u32[]{:S(2)}, u32[]{:S(2)}) async-start(bf16[8,2,512]{2,1,0:T(2,128)(2,1)} %broadcast_in_dim.47), calls=%async_computation.4 | async-start | bytes 32768 | tf_op jit(solution)/shard_map/all_to_all | solution.py:35
  131.2 3.5 %gather_fusion = bf16[2,4096]{1,0:T(2,128)(2,1)} fusion(bf16[304,4096]{1,0:T(8,128)(2,1)} %bitcast.98, s32[1024]{0:T(1024)} %pad_clamp_fusion), kind=kCustom, calls=%fused_computation | custom fusion | bytes 32776 | tf_op jit(solution)/shard_map/jit(_take)/gather | solution.py:71
  134.6 2.7 fusion.6
  137.4 0.9 convolution_multiply_fusion
  138.3 0.9 convolution_multiply_fusion.1
  139.2 3.6 %fusion.5 = bf16[304,128]{1,0:T(8,128)(2,1)} fusion(f32[304,128]{1,0:T(8,128)S(1)} %convolution_multiply_fusion, bf16[304,4096]{1,0:T(8,128)(2,1)} %bitcast.100, bf16[4096,128]{1,0:T(8,128)(2,1)} %param.22), kind=kOutput, calls=%fused_computation.14 | convolution fusion | flops 318844928 | bytes 3772416 | tf_op jit(solution)/shard_map/dot_general | solution.py:121
  142.8 1.5 fusion.4
  144.3 3.0 convolution_convert_fusion.7
  147.6 36.8 %all-gather.9.cloned.1.call-done = bf16[4096,512]{1,0:T(8,128)(2,1)} async-done(((bf16[512,512]{1,0:T(8,128)(2,1)}), bf16[4096,512]{1,0:T(8,128)(2,1)}) %all-gather.9.cloned.1.call-update) | async-done | bytes 4194320 | tf_op jit(solution)/shard_map/all_gather | solution.py:81
  184.5 2.8 convolution_convert_fusion.6
  188.6 0.8 fusion.58
  189.6 0.8 fusion.59
  190.5 0.8 fusion.2
  191.8 3.1 %fusion.3 = f32[304,4096]{1,0:T(8,128)} fusion(f32[304,4096]{1,0:T(8,128)S(1)} %fusion.2, f32[304,4096]{1,0:T(8,128)S(1)} %fusion.58, bf16[304,128]{1,0:T(8,128)(2,1)S(1)} %bitcast.112, bf16[4096,128]{1,0:T(8,128)(2,1)S(1)} %copy-done.3), kind=kOutput, calls=%fused_computation.8 | convolution fusion | flops 321257472 | bytes 16068608 | tf_op jit(solution)/shard_map/dot_general | solution.py:21
  194.9 1.2 fusion.42
  196.1 5.3 %scatter_fusion = f32[304,4096]{1,0:T(8,128)} fusion(f32[304,4096]{1,0:T(8,128)} %fusion.3, s32[2]{0:T(128)S(1)} %bitcast.123, f32[2,4096]{1,0:T(2,128)S(1)} %fusion.42), kind=kCustom, calls=%fused_computation.1 | custom fusion | flops 8192 | bytes 98312 | tf_op jit(solution)/shard_map/scatter-add | solution.py:177
  201.4 4.2 %convert_element_type.116 = bf16[304,4096]{1,0:T(8,128)(2,1)} convert(f32[304,4096]{1,0:T(8,128)} %scatter_fusion) | non-fusion elementwise | flops 1245184 | bytes 7471104 | tf_op jit(solution)/shard_map/convert_element_type | solution.py:179
  205.7 0.7 broadcast_in_dim.49
  206.5 0.7 broadcast_in_dim.48
  207.2 5.3 %all-to-all-start.5 = ((bf16[8,304,32]{1,2,0:T(8,128)(2,1)}), bf16[8,304,32]{1,2,0:T(8,128)(2,1)S(1)}, u32[]{:S(2)}, u32[]{:S(2)}) async-start(bf16[8,304,32]{1,2,0:T(8,128)(2,1)} %broadcast_in_dim.48), calls=%async_computation.5 | async-start | bytes 393216 | tf_op jit(solution)/shard_map/all_to_all | solution.py:35
  212.8 6.1 %all-to-all-done.5 = bf16[8,304,32]{1,2,0:T(8,128)(2,1)S(1)} async-done(((bf16[8,304,32]{1,2,0:T(8,128)(2,1)}), bf16[8,304,32]{1,2,0:T(8,128)(2,1)S(1)}, u32[]{:S(2)}, u32[]{:S(2)}) %all-to-all-start.5) | async-done | bytes 155680 | tf_op jit(solution)/shard_map/all_to_all | solution.py:35
  219.4 25.0 %all_to_all.54 = f32[64,1,384]{2,1,0:T(1,128)S(1)} all-to-all(f32[64,1,384]{2,1,0:T(1,128)S(1)} %all_to_all.39), channel_id=1, replica_groups=mesh['z'=8,'x'=4,'h'=2,'mp'=8] {'z','x','h'}, dimensions={0} | all-to-all | bytes 196608 | tf_op jit(solution)/shard_map/all_to_all | solution.py:39
  244.6 17.5 %all_to_all.55 = f32[64,1,384]{2,1,0:T(1,128)S(1)} all-to-all(f32[64,1,384]{2,1,0:T(1,128)S(1)} %broadcast_in_dim.50), channel_id=1, replica_groups=mesh['z'=8,'x'=4,'h'=2,'mp'=8] {'z','x','h'}, dimensions={0} | all-to-all | bytes 196608 | tf_op jit(solution)/shard_map/all_to_all | solution.py:35
  262.1 0.9 broadcast_in_dim.52
  263.0 7.7 %all-to-all-start.8 = ((f32[8,32,512]{2,1,0:T(8,128)}), f32[8,32,512]{2,1,0:T(8,128)S(1)}, u32[]{:S(2)}, u32[]{:S(2)}) async-start(f32[8,32,512]{2,1,0:T(8,128)} %broadcast_in_dim.52), calls=%async_computation.9 | async-start | bytes 1048576 | tf_op jit(solution)/shard_map/all_to_all | solution.py:35
  270.7 0.8 fusion.10
  272.8 0.7 slice.62
  273.4 0.7 slice.60
  274.1 11.1 %all-to-all-done.8 = f32[8,32,512]{2,1,0:T(8,128)S(1)} async-done(((f32[8,32,512]{2,1,0:T(8,128)}), f32[8,32,512]{2,1,0:T(8,128)S(1)}, u32[]{:S(2)}, u32[]{:S(2)}) %all-to-all-start.8) | async-done | bytes 524320 | tf_op jit(solution)/shard_map/all_to_all | solution.py:35
  285.2 0.8 fusion.54
  286.1 1.0 convert_element_type.117
  287.1 1.0 scatter_custom_fusion.1
  288.1 0.8 convert_element_type.119
  (112 shorter events, 8.6 us)
Async XLA Ops:
  7.2 135.6 %copy-start = (bf16[4096,128]{1,0:T(8,128)(2,1)S(1)}, bf16[4096,128]{1,0:T(8,128)(2,1)}, u32[]{:S(2)}) copy-start(bf16[4096,128]{1,0:T(8,128)(2,1)} %param.21) | copy-start | bytes 3145732
  7.2 27.8 %copy-start.17 = (bf16[8,512]{1,0:T(8,128)(2,1)S(1)}, bf16[8,512]{1,0:T(8,128)(2,1)}, u32[]{:S(2)}) copy-start(bf16[8,512]{1,0:T(8,128)(2,1)} %param.14) | copy-start | bytes 24580
  7.2 27.8 %copy-start.16 = (bf16[8,512]{1,0:T(8,128)(2,1)S(1)}, bf16[8,512]{1,0:T(8,128)(2,1)}, u32[]{:S(2)}) copy-start(bf16[8,512]{1,0:T(8,128)(2,1)} %param.15) | copy-start | bytes 24580
  7.2 123.9 %all-gather.5.cloned.1.call-start = ((), (), s32[]{:S(2)}) async-start(), calls=%async_computation.10 | async-start | bytes 2801664 | tf_op jit(solution)/shard_map/all_gather | solution.py:66
  7.9 136.3 %all-gather.7.cloned.1.call-start = ((), (), s32[]{:S(2)}) async-start(), calls=%async_computation.11 | async-start | bytes 4718592 | tf_op jit(solution)/shard_map/all_gather | solution.py:80
  20.9 32.5 %copy-start.24 = (s32[8,4]{0,1:T(4,128)S(1)}, s32[8,4]{0,1:T(4,128)}, u32[]{:S(2)}) copy-start(s32[8,4]{0,1:T(4,128)} %param.17) | copy-start | bytes 388
  20.9 32.5 %copy-start.26 = (s32[2,1]{0,1:T(1,128)S(1)}, s32[2,1]{0,1:T(1,128)}, u32[]{:S(2)}) copy-start(s32[2,1]{0,1:T(1,128)} %param.19) | copy-start | bytes 28
  33.1 68.2 %copy-start.18 = (s32[8]{0:T(128)S(1)}, s32[8]{0:T(128)}, u32[]{:S(2)}) copy-start(s32[8]{0:T(128)} %param.16) | copy-start | bytes 100
  34.3 150.2 %all-gather.9.cloned.1.call-start = ((), (), s32[]{:S(2)}) async-start(), calls=%async_computation.12 | async-start | bytes 4718592 | tf_op jit(solution)/shard_map/all_gather | solution.py:81
  36.2 36.9 %all-to-all-start.1 = ((bf16[64,16,512]{2,1,0:T(8,128)(2,1)}), bf16[64,16,512]{2,1,0:T(8,128)(2,1)S(1)}, u32[]{:S(2)}, u32[]{:S(2)}) async-start(bf16[64,16,512]{2,1,0:T(8,128)(2,1)} %broadcast_in_dim.45), calls=%async_computation.1 | async-start | bytes 2097152 | tf_op jit(solution)/shard_map/all_to_all | solution.py:35
  54.0 56.4 %copy-start.20 = (s32[2,1]{0,1:T(1,128)}, s32[2,1]{0,1:T(1,128)S(1)}, u32[]{:S(2)}) copy-start(s32[2,1]{0,1:T(1,128)S(1)} %get-tuple-element.69) | copy-start | bytes 28
  73.0 58.1 %copy-start.4 = (bf16[64,16,512]{2,1,0:T(8,128)(2,1)}, bf16[64,16,512]{2,1,0:T(8,128)(2,1)S(1)}, u32[]{:S(2)}) copy-start(bf16[64,16,512]{2,1,0:T(8,128)(2,1)S(1)} %all-to-all-done.1) | copy-start | bytes 3145732
  74.0 26.9 %all-to-all-start.2 = ((f32[8,8,512]{2,1,0:T(8,128)}), f32[8,8,512]{2,1,0:T(8,128)S(1)}, u32[]{:S(2)}, u32[]{:S(2)}) async-start(f32[8,8,512]{2,1,0:T(8,128)} %broadcast_in_dim.46), calls=%async_computation.2 | async-start | bytes 262144 | tf_op jit(solution)/shard_map/all_to_all | solution.py:35
  102.2 8.2 %copy-start.22 = (f32[8]{0:T(128)}, f32[8]{0:T(128)S(1)}, u32[]{:S(2)}) copy-start(f32[8]{0:T(128)S(1)} %get-tuple-element.67) | copy-start | bytes 100
  103.1 21.0 %all-to-all-start.3 = ((bf16[64,8,8]{2,1,0:T(8,128)(2,1)}), bf16[64,8,8]{2,1,0:T(8,128)(2,1)S(1)}, u32[]{:S(2)}, u32[]{:S(2)}) async-start(bf16[64,8,8]{2,1,0:T(8,128)(2,1)} %copy.53), calls=%async_computation.3 | async-start | bytes 262144 | tf_op jit(solution)/shard_map/all_to_all | solution.py:39
  124.3 6.8 %copy-start.13 = (bf16[8,512]{1,0:T(8,128)(2,1)}, bf16[8,512]{1,0:T(8,128)(2,1)S(1)}, u32[]{:S(2)}) copy-start(bf16[8,512]{1,0:T(8,128)(2,1)S(1)} %fusion.8) | copy-start | bytes 24580
  125.0 22.7 %all-to-all-start.4 = ((bf16[8,2,512]{2,1,0:T(2,128)(2,1)}), bf16[8,2,512]{2,1,0:T(2,128)(2,1)}, u32[]{:S(2)}, u32[]{:S(2)}) async-start(bf16[8,2,512]{2,1,0:T(2,128)(2,1)} %broadcast_in_dim.47), calls=%async_computation.4 | async-start | bytes 32768 | tf_op jit(solution)/shard_map/all_to_all | solution.py:35
  131.1 154.9 %reduce-scatter.2.cloned.1.call-start = ((), (), s32[]{:S(2)}) async-start(), calls=%async_computation.13 | async-start | bytes 2801664 | tf_op jit(solution)/shard_map/reduce_scatter | solution.py:178
  131.2 11.7 %copy-start.1 = (bf16[2,1,152,4096]{3,2,1,0:T(8,128)(2,1)S(1)}, bf16[2,1,152,4096]{3,2,1,0:T(8,128)(2,1)}, u32[]{:S(2)}) copy-start(bf16[2,1,152,4096]{3,2,1,0:T(8,128)(2,1)} %all-gather.5.cloned.1.call-done) | copy-start | bytes 7471108
  137.3 5.5 %copy-start.11 = (bf16[304,32]{0,1:T(8,128)(2,1)}, bf16[304,32]{0,1:T(8,128)(2,1)S(1)}, u32[]{:S(2)}) copy-start(bf16[304,32]{0,1:T(8,128)(2,1)S(1)} %fusion.6) | copy-start | bytes 58372
  144.3 3.0 %copy-start.9 = (bf16[304,128]{1,0:T(8,128)(2,1)S(1)}, bf16[304,128]{1,0:T(8,128)(2,1)}, u32[]{:S(2)}) copy-start(bf16[304,128]{1,0:T(8,128)(2,1)} %fusion.4) | copy-start | bytes 233476
  144.3 3.0 %copy-start.25 = (pred[2,152]{1,0:T(4,128)(4,1)S(1)}, pred[2,152]{1,0:T(4,128)(4,1)}, u32[]{:S(2)}) copy-start(pred[2,152]{1,0:T(4,128)(4,1)} %iota_compare_fusion.2) | copy-start | bytes 916
  144.3 43.0 %copy-start.10 = (bf16[304,128]{1,0:T(8,128)(2,1)S(1)}, bf16[304,128]{1,0:T(8,128)(2,1)}, u32[]{:S(2)}) copy-start(bf16[304,128]{1,0:T(8,128)(2,1)} %fusion.5) | copy-start | bytes 233476
  144.3 44.2 %copy-start.14 = (bf16[16,128]{1,0:T(8,128)(2,1)S(1)}, bf16[16,128]{1,0:T(8,128)(2,1)}, u32[]{:S(2)}) copy-start(bf16[16,128]{1,0:T(8,128)(2,1)} %param.25) | copy-start | bytes 12292
  188.6 0.8 copy-start.15
  188.6 1.0 copy-start.7
  189.6 0.9 copy-start.8
  190.5 1.2 copy-start.3
  191.8 3.2 %copy-start.2 = (bf16[4096,512]{1,0:T(8,128)(2,1)S(1)}, bf16[4096,512]{1,0:T(8,128)(2,1)}, u32[]{:S(2)}) copy-start(bf16[4096,512]{1,0:T(8,128)(2,1)} %all-gather.7.cloned.1.call-done) | copy-start | bytes 12582916
  194.9 1.2 copy-start.21
  201.4 11.1 %copy-start.12 = (bf16[304,32]{0,1:T(8,128)(2,1)S(1)}, bf16[304,32]{0,1:T(8,128)(2,1)}, u32[]{:S(2)}) copy-start(bf16[304,32]{0,1:T(8,128)(2,1)} %copy-done.11) | copy-start | bytes 58372
  201.4 17.6 %copy-start.6 = (bf16[2,1,152,512]{3,2,1,0:T(8,128)(2,1)S(1)}, bf16[2,1,152,512]{3,2,1,0:T(8,128)(2,1)}, u32[]{:S(2)}) copy-start(bf16[2,1,152,512]{3,2,1,0:T(8,128)(2,1)} %param.18) | copy-start | bytes 933892
  205.6 65.1 %copy-start.5 = (bf16[64,16,512]{2,1,0:T(8,128)(2,1)S(1)}, bf16[64,16,512]{2,1,0:T(8,128)(2,1)}, u32[]{:S(2)}) copy-start(bf16[64,16,512]{2,1,0:T(8,128)(2,1)} %copy-done.4) | copy-start | bytes 3145732
  205.6 65.1 %copy-start.19 = (s32[8]{0:T(128)S(1)}, s32[8]{0:T(128)}, u32[]{:S(2)}) copy-start(s32[8]{0:T(128)} %param.16) | copy-start | bytes 100
  205.6 65.1 %copy-start.23 = (f32[8]{0:T(128)S(1)}, f32[8]{0:T(128)}, u32[]{:S(2)}) copy-start(f32[8]{0:T(128)} %copy-done.22) | copy-start | bytes 100
  207.2 11.7 %all-to-all-start.5 = ((bf16[8,304,32]{1,2,0:T(8,128)(2,1)}), bf16[8,304,32]{1,2,0:T(8,128)(2,1)S(1)}, u32[]{:S(2)}, u32[]{:S(2)}) async-start(bf16[8,304,32]{1,2,0:T(8,128)(2,1)} %broadcast_in_dim.48), calls=%async_computation.5 | async-start | bytes 393216 | tf_op jit(solution)/shard_map/all_to_all | solution.py:35
  263.0 22.2 %all-to-all-start.8 = ((f32[8,32,512]{2,1,0:T(8,128)}), f32[8,32,512]{2,1,0:T(8,128)S(1)}, u32[]{:S(2)}, u32[]{:S(2)}) async-start(f32[8,32,512]{2,1,0:T(8,128)} %broadcast_in_dim.52), calls=%async_computation.9 | async-start | bytes 1048576 | tf_op jit(solution)/shard_map/all_to_all | solution.py:35
Sparse Core Ops, SparseCore 0:
  10.1 46.8 all-gather.4
  59.1 63.1 all-gather.6
  124.3 60.0 all-gather.8
  205.8 42.2 reduce-scatter.1

commit v2 on v1

--- a/solution.py
+++ b/solution.py
@@ -14,6 +14,7 @@
 HARD_NEGATIVE_ADD = 4.0
 ADAPTER_SCALE = 2.0
 
+PLANE = ("x", "h")
 DP = ("z", "x", "h")
 
 
@@ -55,7 +56,9 @@
     value_down,
     value_up_matrix,
 ):
-    dp_count = lax.axis_size(DP)
+    z_count = lax.axis_size("z")
+    plane_count = lax.axis_size(PLANE)
+    dp_count = z_count * plane_count
     mp_count = lax.axis_size("mp")
     local_rows = query_emb.shape[0]
     batch_size = local_rows * dp_count
@@ -63,48 +66,47 @@
 
     sub_count = hidden_in.shape[0]
     seq_len = hidden_in.shape[2]
+    token_count = sub_count * seq_len
     full_rows = lax.all_gather(hidden_in, "mp", axis=3, tiled=True)
     model_width = full_rows.shape[3]
-    token_inputs = full_rows.reshape(sub_count * seq_len, model_width)
+    token_inputs = full_rows.reshape(token_count, model_width)
     seq_lengths = lengths[:, 0]
     last_rows = jnp.arange(sub_count, dtype=jnp.int32) * seq_len + seq_lengths - 1
-    last_tokens = jnp.take(token_inputs, last_rows, axis=0)
+    last_tokens = jnp.concatenate(
+        [
+            lax.dynamic_slice_in_dim(token_inputs, last_rows[sub], 1, 0)
+            for sub in range(sub_count)
+        ],
+        axis=0,
+    )
 
     rows_here, query_width = w_query.shape
     both = jnp.stack([w_query, w_out.T])
-    both = lax.all_gather(both, "h", axis=0, tiled=False)
+    other = lax.ppermute(both, "h", [(0, 1), (1, 0)])
+    lower = lax.axis_index("h") == 0
+    both = jnp.stack([jnp.where(lower, both, other), jnp.where(lower, other, both)])
     both = spread(both, "x")
-    plane_rows = both.shape[0] * both.shape[1] * rows_here
+    plane_rows = plane_count * rows_here
     wq_plane = both[:, :, 0].reshape(plane_rows, query_width)
     wo_plane = both[:, :, 1].reshape(plane_rows, query_width)
     wq_full = lax.all_gather(wq_plane, "z", axis=0, tiled=True)
-    wo_full = lax.all_gather(wo_plane, "z", axis=0, tiled=True)
-
-    emb_all = spread(jnp.concatenate([item_emb, query_emb], axis=0), DP)
+
+    query_slices = spread(query_emb, "mp")
+    chunks = jnp.concatenate(
+        [
+            jnp.broadcast_to(item_emb[None], query_slices.shape),
+            query_slices,
+        ],
+        axis=1,
+    )
+    chunks = jnp.broadcast_to(
+        chunks[:, None], (z_count, plane_count) + chunks.shape[1:]
+    ).reshape((dp_count,) + chunks.shape[1:])
+    emb_all = swap(chunks, DP)
     items_all = emb_all[:, :local_rows].reshape(batch_size, feature_width)
     queries_all = emb_all[:, local_rows:].reshape(batch_size, feature_width)
     partial_scores = final_product(query_emb, items_all)
-    pair_scores = jnp.sum(spread(partial_scores, "mp"), axis=0) * INV_TEMP
-    columns = jnp.arange(batch_size, dtype=jnp.int32)
-    hard_negative_count = jnp.sum(
-        (hard_index[:, :, None] == columns[None, None, :]).astype(jnp.float32), axis=1
-    )
-    score_logits = pair_scores + HARD_NEGATIVE_ADD * hard_negative_count
-    row_top = jnp.max(score_logits, axis=1, keepdims=True)
-    log_total = row_top[:, 0] + jnp.log(jnp.sum(jnp.exp(score_logits - row_top), axis=1))
-    target = (pair_index[:, None] == columns[None, :]).astype(jnp.float32)
-    picked = jnp.sum(target * score_logits, axis=1)
-    loss_part = jnp.sum(log_total - picked)
-    residual = (jnp.exp(score_logits - log_total[:, None]) - target).astype(jnp.bfloat16)
-    residual_columns = swap(
-        residual.reshape(local_rows, dp_count, local_rows).transpose(1, 0, 2), DP
-    ).reshape(batch_size, local_rows)
-    item_grad = (first_product(residual_columns, queries_all) * INV_TEMP).astype(jnp.bfloat16)
-    query_grad = (
-        jnp.dot(residual, items_all, preferred_element_type=jnp.float32) * INV_TEMP
-    ).astype(jnp.bfloat16)
-    cot_local = item_grad[:sub_count]
-    cot_full = spread(cot_local, "mp").transpose(1, 0, 2).reshape(sub_count, model_width)
+    score_parts = spread(partial_scores, "mp")
 
     adapter_rank = key_down_matrix.shape[1]
     down_both = jnp.concatenate([key_down_matrix, value_down], axis=1)
@@ -122,8 +124,50 @@
         + ADAPTER_SCALE
         * jnp.dot(reduced_value, value_up_matrix, preferred_element_type=jnp.float32)
     ).astype(jnp.bfloat16)
+    score_parts, key_rows, value_rows = lax.optimization_barrier(
+        (score_parts, key_rows, value_rows)
+    )
+
+    pair_scores = jnp.sum(score_parts, axis=0) * INV_TEMP
+    columns = jnp.arange(batch_size, dtype=jnp.int32)
+    hard_negative_count = jnp.sum(
+        (hard_index[:, :, None] == columns[None, None, :]).astype(jnp.float32), axis=1
+    )
+    score_logits = pair_scores + HARD_NEGATIVE_ADD * hard_negative_count
+    row_top = jnp.max(score_logits, axis=1, keepdims=True)
+    log_total = row_top[:, 0] + jnp.log(jnp.sum(jnp.exp(score_logits - row_top), axis=1))
+    target = (pair_index[:, None] == columns[None, :]).astype(jnp.float32)
+    residual = (jnp.exp(score_logits - log_total[:, None]) - target).astype(jnp.bfloat16)
+    plane_columns = (
+        residual.reshape(local_rows, z_count, plane_count, local_rows)
+        .transpose(2, 0, 1, 3)
+        .reshape(1, plane_count, local_rows, z_count * local_rows)
+    )
+    plane_columns = jnp.broadcast_to(plane_columns, (z_count,) + plane_columns.shape[1:])
+    column_rows = swap(
+        plane_columns.reshape((dp_count,) + plane_columns.shape[2:]), DP
+    ).reshape(batch_size, z_count * local_rows)
+    column_grads = (
+        (first_product(column_rows, queries_all) * INV_TEMP)
+        .astype(jnp.bfloat16)
+        .reshape(z_count, local_rows, feature_width)
+    )
+    cotangents = column_grads[:, :sub_count].reshape(z_count * sub_count, feature_width)
+    attn_parts = jnp.dot(cotangents, wo_plane, preferred_element_type=jnp.float32)
+    attn_parts = swap(attn_parts.reshape(z_count, sub_count, query_width), "z")
+    attn_grad = jnp.sum(attn_parts, axis=0).astype(jnp.bfloat16)
+    item_grad = lax.ppermute(
+        lax.dynamic_index_in_dim(column_grads, lax.axis_index("mp"), 0, keepdims=False),
+        ("z", "mp"),
+        [(a * mp_count + b, b * mp_count + a) for a in range(z_count) for b in range(mp_count)],
+    )
+    picked = jnp.sum(target * score_logits, axis=1)
+    loss_part = jnp.sum(log_total - picked)
+    query_grad = (
+        jnp.dot(residual, items_all, preferred_element_type=jnp.float32) * INV_TEMP
+    ).astype(jnp.bfloat16)
+
     query = jnp.dot(last_tokens, wq_full, preferred_element_type=jnp.float32).astype(jnp.bfloat16)
-    attn_grad = jnp.dot(cot_full, wo_full, preferred_element_type=jnp.float32).astype(jnp.bfloat16)
     group_size = HEADS // KV_HEADS
     kv_local = key_rows.shape[1] // HEAD_DIM
     score_scale = 1.0 / math.sqrt(HEAD_DIM)
@@ -157,31 +201,17 @@
     key_adapter_change = (
         jnp.einsum("bkgj,bkgd->bjkd", score_grad, q_heads, preferred_element_type=jnp.float32)
         .astype(jnp.bfloat16)
-        .reshape(sub_count * seq_len, kv_local * HEAD_DIM)
+        .reshape(token_count, kv_local * HEAD_DIM)
     )
     value_adapter_change = (
         jnp.einsum("bkgj,bkgd->bjkd", prob_half, grad_heads, preferred_element_type=jnp.float32)
         .astype(jnp.bfloat16)
-        .reshape(sub_count * seq_len, kv_local * HEAD_DIM)
-    )
-    last_part = final_product(query_delta, wq_full)
+        .reshape(token_count, kv_local * HEAD_DIM)
+    )
     key_coefficient = final_product(key_adapter_change, key_up_matrix).astype(jnp.bfloat16)
     value_coefficient = final_product(value_adapter_change, value_up_matrix).astype(jnp.bfloat16)
-    input_portion = final_product(key_adapter_change, key_weight_matrix) + final_product(
-        value_adapter_change, value_weight_matrix
-    )
-    input_portion = input_portion + ADAPTER_SCALE * (
-        final_product(key_coefficient, key_down_matrix)
-        + final_product(value_coefficient, value_down)
-    )
-    input_portion = input_portion.at[last_rows].add(last_part)
-    input_sum = lax.psum_scatter(
-        input_portion.astype(jnp.bfloat16), "mp", scatter_dimension=1, tiled=True
-    ).astype(jnp.float32)
-    input_sum = input_sum.at[last_rows].add(cot_local.astype(jnp.float32))
-    input_grad = input_sum.astype(jnp.bfloat16).reshape(hidden_in.shape)
-
-    own_rows = hidden_in.reshape(sub_count * seq_len, feature_width)
+
+    own_rows = hidden_in.reshape(token_count, feature_width)
     coefficients = spread(jnp.concatenate([key_coefficient, value_coefficient], axis=1), "mp")
     coefficient_sum = jnp.sum(coefficients.astype(jnp.float32), axis=0)
     down_part = ADAPTER_SCALE * lax.dot_general(
@@ -198,22 +228,47 @@
         ],
         axis=0,
     )
-    down_cut = down_part.size // dp_count
-    up_cut = up_part.size // dp_count
+    up_width = up_part.shape[1]
     shares = jnp.concatenate(
-        [
-            down_part.reshape(dp_count, down_cut),
-            up_part.reshape(dp_count, up_cut),
-            jnp.broadcast_to(loss_part, (dp_count, HEAD_DIM - up_cut)),
-        ],
-        axis=1,
-    )
-    share_sum = jnp.sum(swap(shares, DP), axis=0)
-    mean_loss = share_sum[down_cut + up_cut] / batch_size
-    summed = spread(share_sum, DP)
-    up_grad = summed[:, down_cut : down_cut + up_cut].reshape(up_part.shape)
-    down_slice = summed[:, :down_cut].reshape(down_part.shape)
-    down_grad = spread(down_slice, "mp").transpose(1, 0, 2).reshape(-1, model_width).T
+        [down_part, up_part, jnp.broadcast_to(loss_part, up_part.shape)], axis=1
+    )
+    shares = shares.reshape(z_count, -1, shares.shape[1])
+
+    shares, key_adapter_change, value_adapter_change, query_delta = lax.optimization_barrier(
+        (shares, key_adapter_change, value_adapter_change, query_delta)
+    )
+    last_part = final_product(query_delta, wq_full)
+    input_portion = final_product(key_adapter_change, key_weight_matrix) + final_product(
+        value_adapter_change, value_weight_matrix
+    )
+    input_portion = input_portion + ADAPTER_SCALE * (
+        final_product(key_coefficient, key_down_matrix)
+        + final_product(value_coefficient, value_down)
+    )
+    row_ids = jnp.arange(token_count, dtype=jnp.int32)[:, None]
+    for sub in range(sub_count):
+        input_portion = input_portion + jnp.where(
+            row_ids == last_rows[sub], last_part[sub][None, :], 0.0
+        )
+    input_sum = lax.psum_scatter(
+        input_portion.astype(jnp.bfloat16), "mp", scatter_dimension=1, tiled=True
+    ).astype(jnp.float32)
+    for sub in range(sub_count):
+        input_sum = input_sum + jnp.where(
+            row_ids == last_rows[sub], item_grad[sub][None, :].astype(jnp.float32), 0.0
+        )
+    input_grad = input_sum.astype(jnp.bfloat16).reshape(hidden_in.shape)
+
+    share_sum = jnp.sum(swap(shares, "z"), axis=0)
+    share_sum = jnp.sum(spread(share_sum, PLANE), axis=0)
+    mean_loss = share_sum[0, feature_width + up_width] / batch_size
+    summed = spread(share_sum[:, : feature_width + up_width], "z")
+    summed = summed.reshape(2 * adapter_rank, feature_width + up_width)
+    up_grad = summed[:, feature_width:]
+    down_slice = summed[:, :feature_width].astype(jnp.bfloat16)
+    down_grad = (
+        spread(down_slice, "mp").transpose(1, 0, 2).reshape(-1, model_width).astype(jnp.float32).T
+    )
     return (
         mean_loss,
         query_grad,

time: 298 us -> 278 us (0.933)
  waiting for transfers between devices: 92.6 us -> 45.9 us
  matrix products: 25.6 us -> 36.8 us
  starting transfers between devices: 64.9 us -> 75.6 us
  local copies, waits for them, and re-layouts: 14.3 us -> 24.2 us
  blocking collectives: 66.7 us -> 57.5 us
  between operations: 16 us -> 19.8 us
    all_gather x1 -> x0, waiting for transfers between devices: 36.8 us -> none  [local(): wo_full = lax.all_gather(wo_plane, 'z', axis=0, tiled=True)]
    all_to_all x5 -> x4, waiting for transfers between devices: 41.4 us -> 6.71 us  [spread(): return lax.all_to_all(copies, axes, split_axis=0, concat_axis=0, tiled=True)]
    all_to_all x5 -> x4, starting transfers between devices: 57.4 us -> 30.8 us  [spread(): return lax.all_to_all(copies, axes, split_axis=0, concat_axis=0, tiled=True)]
    all_to_all x1 -> x3, starting transfers between devices: 7.33 us -> 28.3 us  [swap(): return lax.all_to_all(blocks, axes, split_axis=0, concat_axis=0, tiled=True)]
    all_to_all x1 -> x3, waiting for transfers between devices: 13 us -> 33.6 us  [swap(): return lax.all_to_all(blocks, axes, split_axis=0, concat_axis=0, tiled=True)]
    all_to_all x2 -> x3, blocking collectives: 29.7 us -> 47.5 us  [spread(): return lax.all_to_all(copies, axes, split_axis=0, concat_axis=0, tiled=True)]
    ppermute x0 -> x2, starting transfers between devices: none -> 16.2 us  [the longest x1 8.28 us: local(): other = lax.ppermute(both, 'h', [(0, 1), (1, 0)])]
    all_to_all x1, blocking collectives: 25 us -> 10.1 us  [swap(): return lax.all_to_all(blocks, axes, split_axis=0, concat_axis=0, tiled=True)]
  transfers between devices with their start and end apart: 10 -> 12, of which waited for: 6 -> 6; matrix products, arithmetic and copies ran while one was open for 11% -> 19% of each run, Pallas kernels for 0% -> 0%
where the time goes in v2:
time: 278 us; the launch traced here: 276 us
  starting transfers between devices  75.6 us (27%)
  blocking collectives  57.5 us (21%)
  waiting for transfers between devices  45.9 us (17%)
  matrix products  36.8 us (13%)
  local copies, waits for them, and re-layouts  24.2 us (9%)
  between operations  19.8 us (7%)
  other arithmetic  15.9 us (6%)
    all_to_all x3, blocking collectives, spread(): return lax.all_to_all(copies, axes, split_axis=0, concat_axis=0, tiled=True)  47.5 us
    all_to_all x3, waiting for transfers between devices, swap(): return lax.all_to_all(blocks, axes, split_axis=0, concat_axis=0, tiled=True)  33.6 us
    all_to_all x4, starting transfers between devices, spread(): return lax.all_to_all(copies, axes, split_axis=0, concat_axis=0, tiled=True)  30.8 us
    all_to_all x3, starting transfers between devices, swap(): return lax.all_to_all(blocks, axes, split_axis=0, concat_axis=0, tiled=True)  28.3 us
    dot_general x8, matrix products, final_product(): lax.dot_general(left_side, right_side, (((1,), (1,)), ((), ())), preferre...  17 us
    all_to_all x1, blocking collectives, swap(): return lax.all_to_all(blocks, axes, split_axis=0, concat_axis=0, tiled=True)  10.1 us
    ppermute x1, starting transfers between devices, local(): other = lax.ppermute(both, 'h', [(0, 1), (1, 0)])  8.28 us
    ppermute x1, starting transfers between devices, local(): lax.ppermute(lax.dynamic_index_in_dim(column_grads, lax.axis_index('mp'),...  7.91 us
  transfers between devices with their start and end apart: 12, of which 6 were waited for; matrix products, arithmetic and copies ran while one was open for 19% of the time, Pallas kernels for 0%

profile of v2, /device:TPU:1, one launch (start us, length us, event | category | flops | bytes accessed | tf_op | source)
XLA Modules:
  0.0 275.7 jit_solution(17113284200051714657)
XLA Ops:
  8.9 8.3 %collective-permute-start = (bf16[2,64,512]{2,1,0:T(8,128)(2,1)S(1)}, bf16[2,64,512]{2,1,0:T(8,128)(2,1)S(1)}, u32[]{:S(2)}, u32[]{:S(2)}) collective-permute-start(bf16[2,64,512]{2,1,0:T(8,128)(2,1)S(1)} %pad_maximum_fusion.1), channel_id=1, source_target_pairs={{0,8},{8,0},{1,9},{9,1},{2,10},{10,2},{3,11},{11,3},{4,12},{12,4},... | collective-permute-start | bytes 393224 | tf_op jit(solution)/shard_map/ppermute | solution.py:85
  17.2 4.9 %collective-permute-done = bf16[2,64,512]{2,1,0:T(8,128)(2,1)S(1)} collective-permute-done((bf16[2,64,512]{2,1,0:T(8,128)(2,1)S(1)}, bf16[2,64,512]{2,1,0:T(8,128)(2,1)S(1)}, u32[]{:S(2)}, u32[]{:S(2)}) %collective-permute-start) | collective-permute-done | bytes 131104 | tf_op jit(solution)/shard_map/ppermute | solution.py:85
  22.0 0.9 select_bitcast_fusion.1
  23.1 12.4 %all_to_all.55 = bf16[4,2,2,64,512]{4,3,1,2,0:T(8,128)(2,1)S(1)} all-to-all(bf16[4,2,2,64,512]{4,3,1,2,0:T(8,128)(2,1)S(1)} %broadcast_in_dim.164), channel_id=1, replica_groups=mesh['z'=8,'x'=4,'h'=2,'mp'=8] {'x'}, dimensions={0} | all-to-all | bytes 2097152 | tf_op jit(solution)/shard_map/all_to_all | solution.py:36
  35.5 1.1 fusion.58
  36.7 18.6 %all_to_all.56 = bf16[8,8,512]{2,1,0:T(8,128)(2,1)S(1)} all-to-all(bf16[8,8,512]{2,1,0:T(8,128)(2,1)S(1)} %broadcast_in_dim.167), channel_id=1, replica_groups=mesh['z'=8,'x'=4,'h'=2,'mp'=8] {'mp'}, dimensions={0} | all-to-all | bytes 131072 | tf_op jit(solution)/shard_map/all_to_all | solution.py:36
  55.3 1.1 broadcast_in_dim.168
  56.4 14.2 %all-to-all-start.2 = ((bf16[64,16,512]{2,1,0:T(8,128)(2,1)}), bf16[64,16,512]{2,1,0:T(8,128)(2,1)S(1)}, u32[]{:S(2)}, u32[]{:S(2)}) async-start(bf16[64,16,512]{2,1,0:T(8,128)(2,1)} %bitcast.10), calls=%async_computation.2 | async-start | bytes 2097152 | tf_op jit(solution)/shard_map/all_to_all | solution.py:40
  73.1 23.6 %all-to-all-done.2 = bf16[64,16,512]{2,1,0:T(8,128)(2,1)S(1)} async-done(((bf16[64,16,512]{2,1,0:T(8,128)(2,1)}), bf16[64,16,512]{2,1,0:T(8,128)(2,1)S(1)}, u32[]{:S(2)}, u32[]{:S(2)}) %all-to-all-start.2) | async-done | bytes 1048608 | tf_op jit(solution)/shard_map/all_to_all | solution.py:40
  97.7 11.9 %all-to-all-start.3 = ((f32[8,8,512]{2,1,0:T(8,128)}), f32[8,8,512]{2,1,0:T(8,128)}, u32[]{:S(2)}, u32[]{:S(2)}) async-start(f32[8,8,512]{2,1,0:T(8,128)} %broadcast_in_dim.169), calls=%async_computation.3 | async-start | bytes 262144 | tf_op jit(solution)/shard_map/all_to_all | solution.py:36
  109.7 2.8 %fusion.12 = bf16[304,32]{0,1:T(8,128)(2,1)S(1)} fusion(bf16[304,4096]{1,0:T(8,128)(2,1)} %bitcast.112, bf16[4096,16]{0,1:T(8,128)(2,1)} %param.26, bf16[4096,16]{0,1:T(8,128)(2,1)} %param.24), kind=kOutput, calls=%fused_computation.23 | convolution fusion | flops 80225792 | bytes 2771968 | tf_op jit(solution)/shard_map/dot_general | solution.py:113
  113.0 3.5 %fusion.9 = bf16[304,128]{1,0:T(8,128)(2,1)} fusion(f32[304,128]{1,0:T(8,128)S(1)} %convolution_multiply_fusion, bf16[304,4096]{1,0:T(8,128)(2,1)} %bitcast.113, bf16[4096,128]{1,0:T(8,128)(2,1)} %param.22), kind=kOutput, calls=%fused_computation.16 | convolution fusion | flops 318844928 | bytes 3772416 | tf_op jit(solution)/shard_map/dot_general | solution.py:123
  116.5 1.5 fusion.8
  118.0 1.5 reduce_sum.100
  119.5 1.4 fusion.57
  121.7 0.9 select_reduce_fusion
  122.6 1.3 subtract_reduce_fusion
  124.4 1.8 fusion.29
  126.2 1.7 broadcast_in_dim.171
  127.9 1.4 broadcast_in_dim.172
  129.2 1.7 reshape.232
  130.9 10.1 %all-to-all-start.4 = ((bf16[64,2,256]{2,1,0:T(2,128)(2,1)}), bf16[64,2,256]{2,1,0:T(2,128)(2,1)}, u32[]{:S(2)}, u32[]{:S(2)}) async-start(bf16[64,2,256]{2,1,0:T(2,128)(2,1)} %reshape.232), calls=%async_computation.4 | async-start | bytes 131072 | tf_op jit(solution)/shard_map/all_to_all | solution.py:40
  141.0 1.3 fusion.62
  146.2 1.8 iota_compare_fusion.2
  148.0 1.9 slice.92
  149.9 4.3 %all-to-all-done.4 = bf16[64,2,256]{2,1,0:T(2,128)(2,1)} async-done(((bf16[64,2,256]{2,1,0:T(2,128)(2,1)}), bf16[64,2,256]{2,1,0:T(2,128)(2,1)}, u32[]{:S(2)}, u32[]{:S(2)}) %all-to-all-start.4) | async-done | bytes 65568 | tf_op jit(solution)/shard_map/all_to_all | solution.py:40
  154.2 1.7 reshape.233
  155.9 1.4 fusion.11
  157.9 1.2 fusion.34
  159.8 4.0 %all-to-all-start.5 = ((f32[8,2,512]{2,1,0:T(2,128)}), f32[8,2,512]{2,1,0:T(2,128)}, u32[]{:S(2)}, u32[]{:S(2)}) async-start(f32[8,2,512]{2,1,0:T(2,128)} %copy.74), calls=%async_computation.5 | async-start | bytes 65536 | tf_op jit(solution)/shard_map/all_to_all | solution.py:40
  165.1 5.6 %all-to-all-done.5 = f32[8,2,512]{2,1,0:T(2,128)} async-done(((f32[8,2,512]{2,1,0:T(2,128)}), f32[8,2,512]{2,1,0:T(2,128)}, u32[]{:S(2)}, u32[]{:S(2)}) %all-to-all-start.5) | async-done | bytes 32800 | tf_op jit(solution)/shard_map/all_to_all | solution.py:40
  171.6 1.0 fusion.64
  172.6 2.9 %convolution_convert_fusion.6 = bf16[2,512]{1,0:T(2,128)(2,1)S(1)} fusion(bf16[4096,512]{1,0:T(8,128)(2,1)} %all-gather.5.cloned.1.call-done, bf16[1,4096]{1,0:T(2,128)(2,1)} %get-tuple-element.85, bf16[1,4096]{1,0:T(2,128)(2,1)} %get-tuple-element.84), kind=kOutput, calls=%fused_computation.38 | convolution fusion | flops 8422400 | bytes 4212736 | tf_op jit(solution)/shard_map/dot_general | solution.py:170
  175.5 1.0 fusion.19
  176.7 1.2 fusion.21
  180.5 3.1 %fusion.66 = f32[304,4096]{1,0:T(8,128)} fusion(bf16[304,16]{0,1:T(8,128)(2,1)S(1)} %convolution_convert_fusion.4, bf16[4096,16]{0,1:T(8,128)(2,1)S(1)} %copy-done.6), kind=kOutput, calls=%fused_computation.118 | convolution fusion | flops 39845888 | bytes 5121536 | tf_op jit(solution)/shard_map/dot_general | solution.py:22
  184.2 7.6 %all-to-all-start.6 = ((bf16[8,304,32]{1,2,0:T(8,128)(2,1)}), bf16[8,304,32]{1,2,0:T(8,128)(2,1)S(1)}, u32[]{:S(2)}, u32[]{:S(2)}) async-start(bf16[8,304,32]{1,2,0:T(8,128)(2,1)} %broadcast_in_dim.173), calls=%async_computation.6 | async-start | bytes 393216 | tf_op jit(solution)/shard_map/all_to_all | solution.py:36
  192.0 5.5 %fusion.2 = f32[304,4096]{1,0:T(8,128)} fusion(f32[304,4096]{1,0:T(8,128)} %fusion.66, bf16[304,16]{0,1:T(8,128)(2,1)S(1)} %convolution_convert_fusion.3, bf16[4096,16]{0,1:T(8,128)(2,1)S(1)} %copy-done.7), kind=kOutput, calls=%fused_computation.3 | convolution fusion | flops 42336256 | bytes 10102272 | tf_op jit(solution)/shard_map/dot_general | solution.py:22
  198.7 3.4 %fusion.67 = f32[2,4096]{1,0:T(2,128)S(1)} fusion(bf16[2,512]{1,0:T(2,128)(2,1)S(1)} %bitcast.139, bf16[4096,512]{1,0:T(8,128)(2,1)} %all-gather.5.cloned.1.call-done), kind=kOutput, calls=%fused_computation.119 | convolution fusion | flops 8388608 | bytes 4229120 | tf_op jit(solution)/shard_map/dot_general | solution.py:22
  202.9 1.3 slice-done
  204.8 3.1 %fusion.6 = bf16[304,4096]{1,0:T(8,128)(2,1)} fusion(f32[304,4096]{1,0:T(8,128)S(1)} %bitcast.117, f32[304,4096]{1,0:T(8,128)S(1)} %fusion.65, bf16[304,128]{1,0:T(8,128)(2,1)S(1)} %bitcast.127, bf16[4096,128]{1,0:T(8,128)(2,1)S(1)} %copy-done.2, f32[4096]{0:T(1024)S(1)} %bitcast.138, f32[4096]{0:T(1024)S(1)} %bitcast.137, pred[304]{0:T(512)(128)(4,1)S(1)} %copy-done.16, ...), kind=kOutput, calls=%fused_computation.8 | convolution fusion | flops 327483392 | bytes 13611616 | tf_op jit(solution)/shard_map/dot_general | solution.py:22
  207.9 10.1 %all_to_all.57 = f32[8,4,768]{2,1,0:T(4,128)S(1)} all-to-all(f32[8,4,768]{2,1,0:T(4,128)S(1)} %reshape.223), channel_id=1, replica_groups=mesh['z'=8,'x'=4,'h'=2,'mp'=8] {'z'}, dimensions={0} | all-to-all | bytes 196608 | tf_op jit(solution)/shard_map/all_to_all | solution.py:40
  218.0 16.5 %all_to_all.58 = f32[8,4,768]{2,1,0:T(4,128)S(1)} all-to-all(f32[8,4,768]{2,1,0:T(4,128)S(1)} %broadcast_in_dim.175), channel_id=1, replica_groups=mesh['z'=8,'x'=4,'h'=2,'mp'=8] {'x','h'}, dimensions={0} | all-to-all | bytes 196608 | tf_op jit(solution)/shard_map/all_to_all | solution.py:36
  235.2 3.4 %all-to-all-start.9 = ((f32[8,4,640]{2,1,0:T(4,128)}), f32[8,4,640]{2,1,0:T(4,128)S(1)}, u32[]{:S(2)}, u32[]{:S(2)}) async-start(f32[8,4,640]{2,1,0:T(4,128)} %broadcast_in_dim.192), calls=%async_computation.10 | async-start | bytes 163840 | tf_op jit(solution)/shard_map/all_to_all | solution.py:36
  239.2 7.9 %collective-permute-start.1 = (bf16[8,512]{1,0:T(8,128)(2,1)S(1)}, bf16[8,512]{1,0:T(8,128)(2,1)S(1)}, u32[]{:S(2)}, u32[]{:S(2)}) collective-permute-start(bf16[8,512]{1,0:T(8,128)(2,1)S(1)} %dynamic-slice_bitcast_fusion), channel_id=1, source_target_pairs={{0,0},{1,64},{2,128},{3,192},{4,256},{5,320},{6,384},{7,448},{64,1... | collective-permute-start | bytes 24584 | tf_op jit(solution)/shard_map/ppermute | solution.py:159
  247.9 8.0 %all-to-all-start.10 = ((bf16[8,32,512]{2,1,0:T(8,128)(2,1)}), bf16[8,32,512]{2,1,0:T(8,128)(2,1)S(1)}, u32[]{:S(2)}, u32[]{:S(2)}) async-start(bf16[8,32,512]{2,1,0:T(8,128)(2,1)} %broadcast_in_dim.193), calls=%async_computation.11 | async-start | bytes 524288 | tf_op jit(solution)/shard_map/all_to_all | solution.py:36
  258.5 6.1 %all-to-all-done.10 = bf16[8,32,512]{2,1,0:T(8,128)(2,1)S(1)} async-done(((bf16[8,32,512]{2,1,0:T(8,128)(2,1)}), bf16[8,32,512]{2,1,0:T(8,128)(2,1)S(1)}, u32[]{:S(2)}, u32[]{:S(2)}) %all-to-all-start.10) | async-done | bytes 262176 | tf_op jit(solution)/shard_map/all_to_all | solution.py:36
  265.5 1.9 add_convert_fusion
  (121 shorter events, 22.5 us)
Async XLA Ops:
  7.2 109.3 %copy-start = (bf16[4096,128]{1,0:T(8,128)(2,1)S(1)}, bf16[4096,128]{1,0:T(8,128)(2,1)}, u32[]{:S(2)}) copy-start(bf16[4096,128]{1,0:T(8,128)(2,1)} %param.21) | copy-start | bytes 3145732
  7.2 29.5 %copy-start.15 = (bf16[8,512]{1,0:T(8,128)(2,1)S(1)}, bf16[8,512]{1,0:T(8,128)(2,1)}, u32[]{:S(2)}) copy-start(bf16[8,512]{1,0:T(8,128)(2,1)} %param.14) | copy-start | bytes 24580
  7.2 48.1 %copy-start.14 = (bf16[8,512]{1,0:T(8,128)(2,1)S(1)}, bf16[8,512]{1,0:T(8,128)(2,1)}, u32[]{:S(2)}) copy-start(bf16[8,512]{1,0:T(8,128)(2,1)} %param.15) | copy-start | bytes 24580
  7.2 102.5 %all-gather.3.cloned.1.call-start = ((), (), s32[]{:S(2)}) async-start(), calls=%async_computation.12 | async-start | bytes 2801664 | tf_op jit(solution)/shard_map/all_gather | solution.py:70
  7.9 164.6 %all-gather.5.cloned.1.call-start = ((), (), s32[]{:S(2)}) async-start(), calls=%async_computation.13 | async-start | bytes 4718592 | tf_op jit(solution)/shard_map/all_gather | solution.py:92
  8.9 13.2 %collective-permute-start = (bf16[2,64,512]{2,1,0:T(8,128)(2,1)S(1)}, bf16[2,64,512]{2,1,0:T(8,128)(2,1)S(1)}, u32[]{:S(2)}, u32[]{:S(2)}) collective-permute-start(bf16[2,64,512]{2,1,0:T(8,128)(2,1)S(1)} %pad_maximum_fusion.1), channel_id=1, source_target_pairs={{0,8},{8,0},{1,9},{9,1},{2,10},{10,2},{3,11},{11,3},{4,12},{12,4},... | collective-permute-start | bytes 393224 | tf_op jit(solution)/shard_map/ppermute | solution.py:85
  23.0 48.3 %copy-start.21 = (s32[8,4]{0,1:T(4,128)S(1)}, s32[8,4]{0,1:T(4,128)}, u32[]{:S(2)}) copy-start(s32[8,4]{0,1:T(4,128)} %param.17) | copy-start | bytes 388
  23.0 48.9 %copy-start.22 = (s32[2,1]{0,1:T(1,128)S(1)}, s32[2,1]{0,1:T(1,128)}, u32[]{:S(2)}) copy-start(s32[2,1]{0,1:T(1,128)} %param.19) | copy-start | bytes 28
  35.5 77.0 %copy-start.12 = (bf16[16,128]{1,0:T(8,128)(2,1)S(1)}, bf16[16,128]{1,0:T(8,128)(2,1)}, u32[]{:S(2)}) copy-start(bf16[16,128]{1,0:T(8,128)(2,1)} %param.27) | copy-start | bytes 12292
  35.5 77.3 %copy-start.11 = (bf16[16,128]{1,0:T(8,128)(2,1)S(1)}, bf16[16,128]{1,0:T(8,128)(2,1)}, u32[]{:S(2)}) copy-start(bf16[16,128]{1,0:T(8,128)(2,1)} %param.25) | copy-start | bytes 12292
  56.4 40.3 %all-to-all-start.2 = ((bf16[64,16,512]{2,1,0:T(8,128)(2,1)}), bf16[64,16,512]{2,1,0:T(8,128)(2,1)S(1)}, u32[]{:S(2)}, u32[]{:S(2)}) async-start(bf16[64,16,512]{2,1,0:T(8,128)(2,1)} %bitcast.10), calls=%async_computation.2 | async-start | bytes 2097152 | tf_op jit(solution)/shard_map/all_to_all | solution.py:40
  96.7 12.9 %copy-start.3 = (bf16[64,16,512]{2,1,0:T(8,128)(2,1)}, bf16[64,16,512]{2,1,0:T(8,128)(2,1)S(1)}, u32[]{:S(2)}) copy-start(bf16[64,16,512]{2,1,0:T(8,128)(2,1)S(1)} %all-to-all-done.2) | copy-start | bytes 3145732
  97.7 20.2 %all-to-all-start.3 = ((f32[8,8,512]{2,1,0:T(8,128)}), f32[8,8,512]{2,1,0:T(8,128)}, u32[]{:S(2)}, u32[]{:S(2)}) async-start(f32[8,8,512]{2,1,0:T(8,128)} %broadcast_in_dim.169), calls=%async_computation.3 | async-start | bytes 262144 | tf_op jit(solution)/shard_map/all_to_all | solution.py:36
  109.7 6.8 %copy-start.1 = (bf16[2,1,152,4096]{3,2,1,0:T(8,128)(2,1)S(1)}, bf16[2,1,152,4096]{3,2,1,0:T(8,128)(2,1)}, u32[]{:S(2)}) copy-start(bf16[2,1,152,4096]{3,2,1,0:T(8,128)(2,1)} %all-gather.3.cloned.1.call-done) | copy-start | bytes 7471108
  112.6 3.9 %copy-start.8 = (bf16[304,32]{0,1:T(8,128)(2,1)}, bf16[304,32]{0,1:T(8,128)(2,1)S(1)}, u32[]{:S(2)}) copy-start(bf16[304,32]{0,1:T(8,128)(2,1)S(1)} %fusion.12) | copy-start | bytes 58372
  123.9 0.5 copy-start.19
  130.9 23.3 %all-to-all-start.4 = ((bf16[64,2,256]{2,1,0:T(2,128)(2,1)}), bf16[64,2,256]{2,1,0:T(2,128)(2,1)}, u32[]{:S(2)}, u32[]{:S(2)}) async-start(bf16[64,2,256]{2,1,0:T(2,128)(2,1)} %reshape.232), calls=%async_computation.4 | async-start | bytes 131072 | tf_op jit(solution)/shard_map/all_to_all | solution.py:40
  157.3 0.6 copy-start.10
  159.8 10.9 %all-to-all-start.5 = ((f32[8,2,512]{2,1,0:T(2,128)}), f32[8,2,512]{2,1,0:T(2,128)}, u32[]{:S(2)}, u32[]{:S(2)}) async-start(f32[8,2,512]{2,1,0:T(2,128)} %copy.74), calls=%async_computation.5 | async-start | bytes 65536 | tf_op jit(solution)/shard_map/all_to_all | solution.py:40
  164.4 15.9 %copy-start.13 = (bf16[16,128]{1,0:T(8,128)(2,1)S(1)}, bf16[16,128]{1,0:T(8,128)(2,1)}, u32[]{:S(2)}) copy-start(bf16[16,128]{1,0:T(8,128)(2,1)} %param.27) | copy-start | bytes 12292
  164.4 16.0 %copy-start.6 = (bf16[4096,16]{0,1:T(8,128)(2,1)S(1)}, bf16[4096,16]{0,1:T(8,128)(2,1)}, u32[]{:S(2)}) copy-start(bf16[4096,16]{0,1:T(8,128)(2,1)} %param.24) | copy-start | bytes 393220
  176.7 15.3 %copy-start.7 = (bf16[4096,16]{0,1:T(8,128)(2,1)S(1)}, bf16[4096,16]{0,1:T(8,128)(2,1)}, u32[]{:S(2)}) copy-start(bf16[4096,16]{0,1:T(8,128)(2,1)} %param.26) | copy-start | bytes 393220
  184.2 14.0 %all-to-all-start.6 = ((bf16[8,304,32]{1,2,0:T(8,128)(2,1)}), bf16[8,304,32]{1,2,0:T(8,128)(2,1)S(1)}, u32[]{:S(2)}, u32[]{:S(2)}) async-start(bf16[8,304,32]{1,2,0:T(8,128)(2,1)} %broadcast_in_dim.173), calls=%async_computation.6 | async-start | bytes 393216 | tf_op jit(solution)/shard_map/all_to_all | solution.py:36
  191.8 5.7 %copy-start.9 = (bf16[304,32]{0,1:T(8,128)(2,1)S(1)}, bf16[304,32]{0,1:T(8,128)(2,1)}, u32[]{:S(2)}) copy-start(bf16[304,32]{0,1:T(8,128)(2,1)} %copy-done.8) | copy-start | bytes 58372
  191.8 6.5 %copy-start.5 = (bf16[2,1,152,512]{3,2,1,0:T(8,128)(2,1)S(1)}, bf16[2,1,152,512]{3,2,1,0:T(8,128)(2,1)}, u32[]{:S(2)}) copy-start(bf16[2,1,152,512]{3,2,1,0:T(8,128)(2,1)} %param.18) | copy-start | bytes 933892
  191.8 73.7 %reduce-scatter.2.cloned.1.call-start = ((), (), s32[]{:S(2)}) async-start(), calls=%async_computation.14 | async-start | bytes 2801664 | tf_op jit(solution)/shard_map/reduce_scatter | solution.py:253
  202.0 2.2 slice-start
  202.0 2.5 copy-start.2
  202.0 2.5 copy-start.16
  202.0 2.5 copy-start.17
  202.1 2.7 slice-start.1
  204.8 51.1 %copy-start.4 = (bf16[64,16,512]{2,1,0:T(8,128)(2,1)S(1)}, bf16[64,16,512]{2,1,0:T(8,128)(2,1)}, u32[]{:S(2)}) copy-start(bf16[64,16,512]{2,1,0:T(8,128)(2,1)} %copy-done.3) | copy-start | bytes 3145732
  204.8 51.1 %copy-start.18 = (s32[8]{0:T(128)S(1)}, s32[8]{0:T(128)}, u32[]{:S(2)}) copy-start(s32[8]{0:T(128)} %param.16) | copy-start | bytes 100
  204.8 51.1 %copy-start.20 = (f32[8]{0:T(128)S(1)}, f32[8]{0:T(128)}, u32[]{:S(2)}) copy-start(f32[8]{0:T(128)} %copy-done.19) | copy-start | bytes 100
  235.2 12.0 %all-to-all-start.9 = ((f32[8,4,640]{2,1,0:T(4,128)}), f32[8,4,640]{2,1,0:T(4,128)S(1)}, u32[]{:S(2)}, u32[]{:S(2)}) async-start(f32[8,4,640]{2,1,0:T(4,128)} %broadcast_in_dim.192), calls=%async_computation.10 | async-start | bytes 163840 | tf_op jit(solution)/shard_map/all_to_all | solution.py:36
  239.2 17.5 %collective-permute-start.1 = (bf16[8,512]{1,0:T(8,128)(2,1)S(1)}, bf16[8,512]{1,0:T(8,128)(2,1)S(1)}, u32[]{:S(2)}, u32[]{:S(2)}) collective-permute-start(bf16[8,512]{1,0:T(8,128)(2,1)S(1)} %dynamic-slice_bitcast_fusion), channel_id=1, source_target_pairs={{0,0},{1,64},{2,128},{3,192},{4,256},{5,320},{6,384},{7,448},{64,1... | collective-permute-start | bytes 24584 | tf_op jit(solution)/shard_map/ppermute | solution.py:159
  247.9 16.7 %all-to-all-start.10 = ((bf16[8,32,512]{2,1,0:T(8,128)(2,1)}), bf16[8,32,512]{2,1,0:T(8,128)(2,1)S(1)}, u32[]{:S(2)}, u32[]{:S(2)}) async-start(bf16[8,32,512]{2,1,0:T(8,128)(2,1)} %broadcast_in_dim.193), calls=%async_computation.11 | async-start | bytes 524288 | tf_op jit(solution)/shard_map/all_to_all | solution.py:36
Sparse Core Ops, SparseCore 0:
  10.1 47.6 all-gather.2
  59.9 76.6 all-gather.4
  208.0 38.2 reduce-scatter.1

commit v3 on v2

v3 whole, which is shorter than its diff:
```python
import functools
import math

import jax
import jax.numpy as jnp
from jax import lax
from jax.experimental import pallas as pl
from jax.experimental.pallas import tpu as pltpu
from jax.sharding import Mesh
from jax.sharding import PartitionSpec as P

HEADS = 32
KV_HEADS = 8
HEAD_DIM = 128
LANES = 128

INV_TEMP = 50.0
HARD_NEGATIVE_ADD = 4.0
ADAPTER_SCALE = 2.0

PLANE = ("x", "h")
DP = ("z", "x", "h")


def final_product(left_side, right_side):
    return lax.dot_general(
        left_side, right_side, (((1,), (1,)), ((), ())), preferred_element_type=jnp.float32
    )


def first_product(left_side, right_side):
    return lax.dot_general(
        left_side, right_side, (((0,), (0,)), ((), ())), preferred_element_type=jnp.float32
    )


def spread(block, axes):
    count = lax.axis_size(axes)
    copies = jnp.broadcast_to(block[None], (count,) + block.shape)
    return lax.all_to_all(copies, axes, split_axis=0, concat_axis=0, tiled=True)


def swap(blocks, axes):
    return lax.all_to_all(blocks, axes, split_axis=0, concat_axis=0, tiled=True)


def call(kernel, out_shape, flops):
    return pl.pallas_call(
        kernel,
        out_shape=out_shape,
        compiler_params=pltpu.CompilerParams(vmem_limit_bytes=32 * 1024 * 1024),
        cost_estimate=pl.CostEstimate(flops=flops, bytes_accessed=2**20, transcendentals=4096),
    )


def residual_kernel(z_count, plane_count, parts, hard, pair, chunks, residual_out, loss_out):
    rows = parts.shape[1]
    batch_size = parts.shape[2]
    pair_scores = parts[0]
    for part in range(1, parts.shape[0]):
        pair_scores = pair_scores + parts[part]
    column = lax.broadcasted_iota(jnp.int32, (rows, batch_size), 1)
    inner = column % rows
    outer = column // rows
    item = ((outer % z_count) * plane_count + outer // z_count) * rows + inner
    count = jnp.zeros((rows, batch_size), jnp.float32)
    for choice in range(hard.shape[1]):
        count = count + jnp.where(hard[:, choice : choice + 1] == item, 1.0, 0.0)
    logits = pair_scores * INV_TEMP + HARD_NEGATIVE_ADD * count
    top = jnp.max(logits, axis=1, keepdims=True)
    log_total = top + jnp.log(jnp.sum(jnp.exp(logits - top), axis=1, keepdims=True))
    target = jnp.where(pair[...] == item, 1.0, 0.0)
    picked = jnp.sum(target * logits, axis=1, keepdims=True)
    loss = jnp.sum(log_total - picked, axis=0, keepdims=True)
    loss_out[...] = jnp.broadcast_to(loss, loss_out.shape)
    residual = jnp.exp(logits - log_total) - target
    residual_out[...] = residual.astype(jnp.bfloat16)
    width = z_count * rows
    pad = jnp.zeros((rows, chunks.shape[2] - width), jnp.float32)
    for plane in range(plane_count):
        block = jnp.concatenate([residual[:, plane * width : (plane + 1) * width], pad], axis=1)
        block = block.astype(jnp.bfloat16)
        for z in range(z_count):
            chunks[z * plane_count + plane] = block


def gradient_kernel(
    z_count, subs, columns, queries, wo_plane, wq_plane, last_tokens, item_out, parts_out
):
    item_rows = item_out.shape[0]
    every = lax.dot_general(
        columns[...], queries[...], (((0,), (0,)), ((), ())), preferred_element_type=jnp.float32
    )
    grads = (every[:item_rows] * INV_TEMP).astype(jnp.bfloat16)
    item_out[...] = grads
    row = lax.broadcasted_iota(jnp.int32, (subs * z_count, item_rows), 0)
    column = lax.broadcasted_iota(jnp.int32, (subs * z_count, item_rows), 1)
    per_z = item_rows // z_count
    wanted = jnp.where((row // subs) * per_z + row % subs == column, 1.0, 0.0)
    cotangents = jnp.dot(
        wanted.astype(jnp.bfloat16), grads, preferred_element_type=jnp.float32
    ).astype(jnp.bfloat16)
    attn = jnp.dot(cotangents, wo_plane[...], preferred_element_type=jnp.float32)
    query = jnp.dot(last_tokens[...], wq_plane[...], preferred_element_type=jnp.float32)
    for z in range(z_count):
        parts_out[z, :subs] = attn[z * subs : (z + 1) * subs]
        parts_out[z, subs:] = query[z * subs : (z + 1) * subs]


def attention_kernel(
    lengths,
    parts,
    keys,
    values,
    key_up,
    value_up,
    reduced,
    query_delta_out,
    key_change_out,
    value_change_out,
    coef_out,
    up_out,
):
    subs = parts.shape[1] // 2
    width = parts.shape[2]
    token_count = keys.shape[0]
    seq_len = token_count // subs
    group = width // HEAD_DIM
    both = parts[0]
    for part in range(1, parts.shape[0]):
        both = both + parts[part]
    both = both.astype(jnp.bfloat16).astype(jnp.float32)

    def heads(first):
        return jnp.concatenate(
            [
                both[first + sub : first + sub + 1, head * HEAD_DIM : (head + 1) * HEAD_DIM]
                for sub in range(subs)
                for head in range(group)
            ],
            axis=0,
        )

    grad_heads = heads(0)
    q_heads = heads(subs)
    score_scale = 1.0 / math.sqrt(HEAD_DIM)
    raw = final_product(q_heads.astype(jnp.bfloat16), keys[...]) * score_scale
    row_sub = lax.broadcasted_iota(jnp.int32, raw.shape, 0) // group
    token = lax.broadcasted_iota(jnp.int32, raw.shape, 1)
    live = jnp.zeros(raw.shape, jnp.bool_)
    for sub in range(subs):
        first = sub * seq_len
        inside = (token >= first) & (token < first + lengths[sub, 0])
        live = live | (inside & (row_sub == sub))
    raw = jnp.where(live, raw, -jnp.inf)
    weights = jnp.exp(raw - jnp.max(raw, axis=1, keepdims=True))
    probs = weights / jnp.sum(weights, axis=1, keepdims=True)
    prob_half = probs.astype(jnp.bfloat16).astype(jnp.float32)
    prob_grad = final_product(grad_heads.astype(jnp.bfloat16), values[...])
    score_grad = (
        probs * (prob_grad - jnp.sum(probs * prob_grad, axis=1, keepdims=True)) * score_scale
    )
    score_grad = score_grad.astype(jnp.bfloat16)
    delta = jnp.dot(score_grad, keys[...], preferred_element_type=jnp.float32)
    for sub in range(subs):
        for head in range(group):
            row = sub * group + head
            query_delta_out[sub : sub + 1, head * HEAD_DIM : (head + 1) * HEAD_DIM] = delta[
                row : row + 1
            ]
    score_grad = score_grad.astype(jnp.float32)
    key_change = first_product(score_grad, q_heads).astype(jnp.bfloat16)
    value_change = first_product(prob_half, grad_heads).astype(jnp.bfloat16)
    key_change_out[...] = key_change
    value_change_out[...] = value_change
    key_coef = final_product(key_change, key_up[...])
    value_coef = final_product(value_change, value_up[...])
    coef = jnp.concatenate([key_coef, value_coef], axis=1).astype(jnp.bfloat16)
    for copy in range(coef_out.shape[0]):
        coef_out[copy] = coef
    rank = key_up.shape[0]
    up_out[:rank] = ADAPTER_SCALE * first_product(reduced[...], key_change)[:rank]
    up_out[rank:] = ADAPTER_SCALE * first_product(reduced[...], value_change)[rank:]


def share_kernel(coefs, tokens, ups, loss, deltas, wq_plane, out):
    total = coefs[0].astype(jnp.float32)
    for part in range(1, coefs.shape[0]):
        total = total + coefs[part].astype(jnp.float32)
    upper = total.astype(jnp.bfloat16)
    lower = (total - upper.astype(jnp.float32)).astype(jnp.bfloat16)
    down = ADAPTER_SCALE * (first_product(upper, tokens[...]) + first_product(lower, tokens[...]))
    last = final_product(deltas[...], wq_plane[...])
    z_count, rows, _ = out.shape
    subs = deltas.shape[0] // z_count
    feature_width = tokens.shape[1]
    up_end = feature_width + ups.shape[1]
    loss_end = up_end + loss.shape[1]
    for z in range(z_count):
        mine = slice(z * rows, (z + 1) * rows)
        out[z, :, :feature_width] = down[mine]
        out[z, :, feature_width:up_end] = ups[mine]
        out[z, :, up_end:loss_end] = loss[:rows]
        out[z, :subs, loss_end:] = last[z * subs : (z + 1) * subs]
        out[z, subs:, loss_end:] = jnp.zeros((rows - subs, feature_width), jnp.float32)


def local(
    query_emb,
    item_emb,
    pair_index,
    hard_index,
    hidden_in,
    lengths,
    w_query,
    key_weight_matrix,
    value_weight_matrix,
    w_out,
    key_down_matrix,
    key_up_matrix,
    value_down,
    value_up_matrix,
):
    z_count = lax.axis_size("z")
    plane_count = lax.axis_size(PLANE)
    dp_count = z_count * plane_count
    mp_count = lax.axis_size("mp")
    local_rows = query_emb.shape[0]
    batch_size = local_rows * dp_count
    feature_width = query_emb.shape[1]
    turn = [(a * mp_count + b, b * mp_count + a) for a in range(z_count) for b in range(mp_count)]

    sub_count = hidden_in.shape[0]
    seq_len = hidden_in.shape[2]
    token_count = sub_count * seq_len
    full_rows = lax.all_gather(hidden_in, "mp", axis=3, tiled=True)
    model_width = full_rows.shape[3]
    token_inputs = full_rows.reshape(token_count, model_width)
    seq_lengths = lengths[:, 0]
    last_rows = jnp.arange(sub_count, dtype=jnp.int32) * seq_len + seq_lengths - 1

    turned = lax.ppermute(query_emb, ("z", "mp"), turn)
    queries_all = spread(turned, PLANE + ("mp",))
    queries_all = (
        queries_all.reshape(plane_count, mp_count, local_rows, feature_width)
        .transpose(1, 0, 2, 3)
        .reshape(batch_size, feature_width)
    )
    items_all = (
        spread(item_emb, DP)
        .reshape(z_count, plane_count, local_rows, feature_width)
        .transpose(1, 0, 2, 3)
        .reshape(batch_size, feature_width)
    )
    partial_scores = final_product(query_emb, items_all)
    score_parts = spread(partial_scores, "mp")

    rows_here, query_width = w_query.shape
    both = jnp.stack([w_query, w_out.T])
    both, partial_scores = lax.optimization_barrier((both, partial_scores))
    other = lax.ppermute(both, "h", [(0, 1), (1, 0)])
    lower = lax.axis_index("h") == 0
    both = jnp.stack([jnp.where(lower, both, other), jnp.where(lower, other, both)])
    both = spread(both, "x")
    plane_rows = plane_count * rows_here
    wq_plane = both[:, :, 0].reshape(plane_rows, query_width)
    wo_plane = both[:, :, 1].reshape(plane_rows, query_width)

    last_tokens = jnp.concatenate(
        [
            lax.dynamic_slice_in_dim(token_inputs, last_rows[sub], 1, 0)
            for sub in range(sub_count)
        ],
        axis=0,
    )
    last_slices = swap(
        last_tokens.reshape(sub_count, z_count, feature_width).transpose(1, 0, 2), "z"
    ).reshape(z_count * sub_count, feature_width)

    adapter_rank = key_down_matrix.shape[1]
    down_both = jnp.concatenate([key_down_matrix, value_down], axis=1)
    reduced_pair = jnp.dot(token_inputs, down_both, preferred_element_type=jnp.float32).astype(
        jnp.bfloat16
    )
    reduced_key = reduced_pair[:, :adapter_rank]
    reduced_value = reduced_pair[:, adapter_rank:]
    key_rows = (
        jnp.dot(token_inputs, key_weight_matrix, preferred_element_type=jnp.float32)
        + ADAPTER_SCALE * jnp.dot(reduced_key, key_up_matrix, preferred_element_type=jnp.float32)
    ).astype(jnp.bfloat16)
    value_rows = (
        jnp.dot(token_inputs, value_weight_matrix, preferred_element_type=jnp.float32)
        + ADAPTER_SCALE
        * jnp.dot(reduced_value, value_up_matrix, preferred_element_type=jnp.float32)
    ).astype(jnp.bfloat16)

    bf16, f32 = jnp.bfloat16, jnp.float32
    chunks, residual, loss_part = call(
        functools.partial(residual_kernel, z_count, plane_count),
        (
            jax.ShapeDtypeStruct((dp_count, local_rows, LANES), bf16),
            jax.ShapeDtypeStruct((local_rows, batch_size), bf16),
            jax.ShapeDtypeStruct((local_rows, LANES), f32),
        ),
        2**24,
    )(score_parts, hard_index, pair_index[:, None])
    column_rows = swap(chunks, DP).reshape(batch_size, LANES)
    column_rows, key_rows, value_rows = lax.optimization_barrier(
        (column_rows, key_rows, value_rows)
    )
    column_grads, parts = call(
        functools.partial(gradient_kernel, z_count, sub_count),
        (
            jax.ShapeDtypeStruct((z_count * local_rows, feature_width), bf16),
            jax.ShapeDtypeStruct((z_count, 2 * sub_count, query_width), f32),
        ),
        2**26,
    )(column_rows, queries_all, wo_plane, wq_plane, last_slices)
    parts = swap(parts, "z")
    own_grads = lax.dynamic_index_in_dim(
        column_grads.reshape(z_count, local_rows, feature_width),
        lax.axis_index("mp"),
        0,
        keepdims=False,
    )
    item_grad = lax.ppermute(own_grads, ("z", "mp"), turn)
    query_grad = (
        jnp.dot(residual, items_all, preferred_element_type=jnp.float32) * INV_TEMP
    ).astype(jnp.bfloat16)

    query_delta, key_change, value_change, coef_copies, up_part = call(
        attention_kernel,
        (
            jax.ShapeDtypeStruct((sub_count, query_width), f32),
            jax.ShapeDtypeStruct(key_rows.shape, bf16),
            jax.ShapeDtypeStruct(value_rows.shape, bf16),
            jax.ShapeDtypeStruct((mp_count, token_count, 2 * adapter_rank), bf16),
            jax.ShapeDtypeStruct((2 * adapter_rank, key_rows.shape[1]), f32),
        ),
        2**24,
    )(lengths, parts, key_rows, value_rows, key_up_matrix, value_up_matrix, reduced_pair)
    coefficients = swap(coef_copies, "mp")
    query_deltas = spread(query_delta.astype(bf16), "z").reshape(-1, query_width)

    own_rows = hidden_in.reshape(token_count, feature_width)
    up_width = up_part.shape[1]
    share_rows = 2 * adapter_rank // z_count
    loss_end = feature_width + up_width + LANES
    shares = call(
        share_kernel,
        jax.ShapeDtypeStruct((z_count, share_rows, loss_end + feature_width), f32),
        2**26,
    )(coefficients, own_rows, up_part, loss_part, query_deltas, wq_plane)
    shares = swap(shares, "z")
    last_part = (
        shares[:, :sub_count, loss_end:].transpose(1, 0, 2).reshape(sub_count, model_width)
    )

    key_coefficient = coef_copies[0, :, :adapter_rank]
    value_coefficient = coef_copies[0, :, adapter_rank:]
    input_portion = final_product(key_change, key_weight_matrix) + final_product(
        value_change, value_weight_matrix
    )
    input_portion = input_portion + ADAPTER_SCALE * (
        final_product(key_coefficient, key_down_matrix)
        + final_product(value_coefficient, value_down)
    )
    row_ids = jnp.arange(token_count, dtype=jnp.int32)[:, None]
    for sub in range(sub_count):
        input_portion = input_portion + jnp.where(
            row_ids == last_rows[sub], last_part[sub][None, :], 0.0
        )
    input_sum = lax.psum_scatter(
        input_portion.astype(jnp.bfloat16), "mp", scatter_dimension=1, tiled=True
    ).astype(jnp.float32)
    for sub in range(sub_count):
        input_sum = input_sum + jnp.where(
            row_ids == last_rows[sub], item_grad[sub][None, :].astype(jnp.float32), 0.0
        )
    input_grad = input_sum.astype(jnp.bfloat16).reshape(hidden_in.shape)

    share_sum = jnp.sum(shares[:, :, :loss_end], axis=0)
    share_sum = jnp.sum(spread(share_sum, PLANE), axis=0)
    mean_loss = share_sum[0, feature_width + up_width] / batch_size
    summed = spread(share_sum[:, : feature_width + up_width], "z")
    summed = summed.reshape(2 * adapter_rank, feature_width + up_width)
    up_grad = summed[:, feature_width:]
    down_slice = summed[:, :feature_width].astype(jnp.bfloat16)
    down_grad = (
        spread(down_slice, "mp").transpose(1, 0, 2).reshape(-1, model_width).astype(jnp.float32).T
    )
    return (
        mean_loss,
        query_grad,
        item_grad,
        input_grad,
        down_grad[:, :adapter_rank],
        down_grad[:, adapter_rank:],
        up_grad[:adapter_rank],
        up_grad[adapter_rank:],
    )


def solution(mesh):
    fine = Mesh(
        mesh.devices.reshape(8, 4, 2, mesh.devices.shape[1]), ("z", "x", "h", "mp")
    )
    in_specs = (
        P(DP, "mp"),
        P(DP, "mp"),
        P(DP),
        P(DP, None),
        P(None, DP, None, "mp"),
        P(None, DP),
        P(DP, "mp"),
        P(None, "mp"),
        P(None, "mp"),
        P("mp", DP),
        P(),
        P(None, "mp"),
        P(),
        P(None, "mp"),
    )
    out_specs = (
        P(),
        P(DP, "mp"),
        P(DP, "mp"),
        P(None, DP, None, "mp"),
        P(),
        P(),
        P(None, "mp"),
        P(None, "mp"),
    )
    return jax.shard_map(local, mesh=fine, in_specs=in_specs, out_specs=out_specs, check_vma=False)
```

time: 278 us -> 269 us (0.968)
  blocking collectives: 57.5 us -> 15.6 us
  starting transfers between devices: 75.6 us -> 109 us
  waiting for transfers between devices: 45.9 us -> 68.6 us
  other arithmetic: 15.9 us -> 4.88 us
  matrix products: 36.8 us -> 28.7 us
  local copies, waits for them, and re-layouts: 24.2 us -> 16.3 us
  Pallas kernels: 0 us -> 4.22 us
    all_to_all x4 -> x7, waiting for transfers between devices: 6.71 us -> 43.3 us  [spread(): return lax.all_to_all(copies, axes, split_axis=0, concat_axis=0, tiled=True)]
    all_to_all x3 -> x1, blocking collectives: 47.5 us -> 15.6 us  [spread(): return lax.all_to_all(copies, axes, split_axis=0, concat_axis=0, tiled=True)]
    all_to_all x4 -> x7, starting transfers between devices: 30.8 us -> 55 us  [spread(): return lax.all_to_all(copies, axes, split_axis=0, concat_axis=0, tiled=True)]
    all_to_all x3 -> x5, waiting for transfers between devices: 33.6 us -> 20.2 us  [swap(): return lax.all_to_all(blocks, axes, split_axis=0, concat_axis=0, tiled=True)]
    dot_general x11 -> x0, matrix products: 10.7 us -> none  [the longest x1 2.89 us: local(): jnp.dot(last_tokens, wq_full, preferred_element_type=jnp.float32)]
    all_to_all x1 -> x0, blocking collectives: 10.1 us -> none  [swap(): return lax.all_to_all(blocks, axes, split_axis=0, concat_axis=0, tiled=True)]
    all_to_all x3 -> x5, starting transfers between devices: 28.3 us -> 33.7 us  [swap(): return lax.all_to_all(blocks, axes, split_axis=0, concat_axis=0, tiled=True)]
    reduce_sum x7 -> x1, other arithmetic: 5.21 us -> 0.02 us  [local(): share_sum = jnp.sum(shares[:, :, :loss_end], axis=0)]
  transfers between devices with their start and end apart: 12 -> 17, of which waited for: 6 -> 12; matrix products, arithmetic and copies ran while one was open for 19% -> 14% of each run, Pallas kernels for 0% -> 0%
where the time goes in v3:
time: 269 us; the launch traced here: 267 us
  starting transfers between devices  109 us (41%)
  waiting for transfers between devices  68.6 us (26%)
  matrix products  28.7 us (11%)
  between operations  20.1 us (7%)
  local copies, waits for them, and re-layouts  16.3 us (6%)
  blocking collectives  15.6 us (6%)
  other arithmetic  4.88 us (2%)
  Pallas kernels  4.22 us (2%)
    all_to_all x7, starting transfers between devices, spread(): return lax.all_to_all(copies, axes, split_axis=0, concat_axis=0, tiled=True)  55 us
    all_to_all x7, waiting for transfers between devices, spread(): return lax.all_to_all(copies, axes, split_axis=0, concat_axis=0, tiled=True)  43.3 us
    all_to_all x5, starting transfers between devices, swap(): return lax.all_to_all(blocks, axes, split_axis=0, concat_axis=0, tiled=True)  33.7 us
    all_to_all x5, waiting for transfers between devices, swap(): return lax.all_to_all(blocks, axes, split_axis=0, concat_axis=0, tiled=True)  20.2 us
    dot_general x5, matrix products, final_product(): lax.dot_general(left_side, right_side, (((1,), (1,)), ((), ())), preferre...  19.6 us
    all_to_all x1, blocking collectives, spread(): return lax.all_to_all(copies, axes, split_axis=0, concat_axis=0, tiled=True)  15.6 us
    ppermute x1, starting transfers between devices, local(): item_grad = lax.ppermute(own_grads, ('z', 'mp'), turn)  8.44 us
    ppermute x1, starting transfers between devices, local(): other = lax.ppermute(both, 'h', [(0, 1), (1, 0)])  7.21 us
  transfers between devices with their start and end apart: 17, of which 12 were waited for; matrix products, arithmetic and copies ran while one was open for 14% of the time, Pallas kernels for 0%

profile of v3, /device:TPU:1, one launch (start us, length us, event | category | flops | bytes accessed | tf_op | source)
XLA Modules:
  0.0 267.0 jit_solution(8056009434850842331)
XLA Ops:
  7.9 1.5 broadcast_in_dim.128
  9.5 19.7 %all-to-all-start = ((bf16[64,8,512]{2,1,0:T(8,128)(2,1)}), bf16[64,8,512]{2,1,0:T(8,128)(2,1)S(1)}, u32[]{:S(2)}, u32[]{:S(2)}) async-start(bf16[64,8,512]{2,1,0:T(8,128)(2,1)} %broadcast_in_dim.128), calls=%async_computation | async-start | bytes 1048576 | tf_op jit(solution)/shard_map/all_to_all | solution.py:40
  29.2 4.0 %collective-permute-start = (bf16[8,512]{1,0:T(8,128)(2,1)}, bf16[8,512]{1,0:T(8,128)(2,1)S(1)}, u32[]{:S(2)}, u32[]{:S(2)}) collective-permute-start(bf16[8,512]{1,0:T(8,128)(2,1)} %param.14), channel_id=1, source_target_pairs={{0,0},{1,64},{2,128},{3,192},{4,256},{5,320},{6,384},{7,448},{64,1... | collective-permute-start | bytes 24584 | tf_op jit(solution)/shard_map/ppermute | solution.py:242
  33.2 4.4 %collective-permute-done = bf16[8,512]{1,0:T(8,128)(2,1)S(1)} collective-permute-done((bf16[8,512]{1,0:T(8,128)(2,1)}, bf16[8,512]{1,0:T(8,128)(2,1)S(1)}, u32[]{:S(2)}, u32[]{:S(2)}) %collective-permute-start) | collective-permute-done | bytes 8224 | tf_op jit(solution)/shard_map/ppermute | solution.py:242
  37.6 14.0 %all-to-all-done = bf16[64,8,512]{2,1,0:T(8,128)(2,1)S(1)} async-done(((bf16[64,8,512]{2,1,0:T(8,128)(2,1)}), bf16[64,8,512]{2,1,0:T(8,128)(2,1)S(1)}, u32[]{:S(2)}, u32[]{:S(2)}) %all-to-all-start) | async-done | bytes 524320 | tf_op jit(solution)/shard_map/all_to_all | solution.py:40
  52.4 11.1 %all-to-all-start.3 = ((bf16[64,8,512]{2,1,0:T(8,128)(2,1)}), bf16[64,8,512]{2,1,0:T(8,128)(2,1)S(1)}, u32[]{:S(2)}, u32[]{:S(2)}) async-start(bf16[64,8,512]{2,1,0:T(8,128)(2,1)} %broadcast_in_dim.131), calls=%async_computation.3 | async-start | bytes 1048576 | tf_op jit(solution)/shard_map/all_to_all | solution.py:40
  63.6 0.9 pad_maximum_fusion.1
  65.3 0.9 fusion.25
  66.3 7.2 %collective-permute-start.1 = (bf16[2,64,512]{2,1,0:T(8,128)(2,1)S(1)}, bf16[2,64,512]{2,1,0:T(8,128)(2,1)S(1)}, u32[]{:S(2)}, u32[]{:S(2)}) collective-permute-start(bf16[2,64,512]{2,1,0:T(8,128)(2,1)S(1)} %pad_maximum_fusion.1), channel_id=1, source_target_pairs={{0,8},{8,0},{1,9},{9,1},{2,10},{10,2},{3,11},{11,3},{4,12},{12,4},... | collective-permute-start | bytes 393224 | tf_op jit(solution)/shard_map/ppermute | solution.py:261
  73.5 7.6 %all-to-all-done.3 = bf16[64,8,512]{2,1,0:T(8,128)(2,1)S(1)} async-done(((bf16[64,8,512]{2,1,0:T(8,128)(2,1)}), bf16[64,8,512]{2,1,0:T(8,128)(2,1)S(1)}, u32[]{:S(2)}, u32[]{:S(2)}) %all-to-all-start.3) | async-done | bytes 524320 | tf_op jit(solution)/shard_map/all_to_all | solution.py:40
  81.8 5.4 %all-to-all-start.1 = ((f32[8,8,512]{2,1,0:T(8,128)}), f32[8,8,512]{2,1,0:T(8,128)S(1)}, u32[]{:S(2)}, u32[]{:S(2)}) async-start(f32[8,8,512]{2,1,0:T(8,128)} %broadcast_in_dim.129), calls=%async_computation.1 | async-start | bytes 262144 | tf_op jit(solution)/shard_map/all_to_all | solution.py:40
  87.3 5.7 %all-to-all-done.1.parts = f32[8,8,512]{2,1,0:T(8,128)S(1)} async-done(((f32[8,8,512]{2,1,0:T(8,128)}), f32[8,8,512]{2,1,0:T(8,128)S(1)}, u32[]{:S(2)}, u32[]{:S(2)}) %all-to-all-start.1) | async-done | bytes 131104 | tf_op jit(solution)/shard_map/all_to_all | solution.py:40
  93.0 1.1 broadcast_in_dim.132
  94.1 3.5 %all-to-all-start.4 = ((bf16[4,2,2,64,512]{4,3,1,2,0:T(8,128)(2,1)}), bf16[4,2,2,64,512]{4,3,1,2,0:T(8,128)(2,1)S(1)}, u32[]{:S(2)}, u32[]{:S(2)}) async-start(bf16[4,2,2,64,512]{4,3,1,2,0:T(8,128)(2,1)} %broadcast_in_dim.132), calls=%async_computation.4 | async-start | bytes 2097152 | tf_op jit(solution)/shard_map/all_to_all | solution.py:40
  102.3 1.1 copy.91
  103.4 1.0 shard_map.197
  104.4 7.4 %all-to-all-done.4 = bf16[4,2,2,64,512]{4,3,1,2,0:T(8,128)(2,1)S(1)} async-done(((bf16[4,2,2,64,512]{4,3,1,2,0:T(8,128)(2,1)}), bf16[4,2,2,64,512]{4,3,1,2,0:T(8,128)(2,1)S(1)}, u32[]{:S(2)}, u32[]{:S(2)}) %all-to-all-start.4) | async-done | bytes 1048608 | tf_op jit(solution)/shard_map/all_to_all | solution.py:40
  111.7 1.0 copy-done.7
  112.7 13.4 %all-to-all-start.2 = ((bf16[64,8,128]{2,1,0:T(8,128)(2,1)}), bf16[64,8,128]{2,1,0:T(8,128)(2,1)S(1)}, u32[]{:S(2)}, u32[]{:S(2)}) async-start(bf16[64,8,128]{2,1,0:T(8,128)(2,1)} %get-tuple-element.22), calls=%async_computation.2 | async-start | bytes 262144 | tf_op jit(solution)/shard_map/all_to_all | solution.py:44
  126.1 1.3 fusion.20
  127.5 2.6 convolution_convert_fusion
  130.4 0.9 constant_dynamic-slice_fusion.1
  132.0 2.5 fusion.5.keys
  134.7 4.9 %all-to-all-done.2 = bf16[64,8,128]{2,1,0:T(8,128)(2,1)S(1)} async-done(((bf16[64,8,128]{2,1,0:T(8,128)(2,1)}), bf16[64,8,128]{2,1,0:T(8,128)(2,1)S(1)}, u32[]{:S(2)}, u32[]{:S(2)}) %all-to-all-start.2) | async-done | bytes 131104 | tf_op jit(solution)/shard_map/all_to_all | solution.py:44
  139.6 3.3 %all-to-all-start.5 = ((bf16[8,2,512]{2,1,0:T(2,128)(2,1)}), bf16[8,2,512]{2,1,0:T(2,128)(2,1)S(1)}, u32[]{:S(2)}, u32[]{:S(2)}) async-start(bf16[8,2,512]{2,1,0:T(2,128)(2,1)} %bitcast.21), calls=%async_computation.5 | async-start | bytes 32768 | tf_op jit(solution)/shard_map/all_to_all | solution.py:44
  143.0 2.8 %fusion.6.values = bf16[304,128]{1,0:T(8,128)(2,1)S(1)} fusion(f32[304,128]{1,0:T(8,128)S(1)} %convolution_multiply_fusion, bf16[304,4096]{1,0:T(8,128)(2,1)} %bitcast.87, bf16[4096,128]{1,0:T(8,128)(2,1)} %param.22), kind=kOutput, calls=%fused_computation.12 | convolution fusion | flops 318844928 | bytes 3772416 | tf_op jit(solution)/shard_map/dot_general | solution.py:292
  145.8 3.7 %all-to-all-done.5 = bf16[8,2,512]{2,1,0:T(2,128)(2,1)S(1)} async-done(((bf16[8,2,512]{2,1,0:T(2,128)(2,1)}), bf16[8,2,512]{2,1,0:T(2,128)(2,1)S(1)}, u32[]{:S(2)}, u32[]{:S(2)}) %all-to-all-start.5) | async-done | bytes 16416 | tf_op jit(solution)/shard_map/all_to_all | solution.py:44
  149.5 1.2 shard_map.198
  150.8 3.4 %all-to-all-start.6 = ((f32[8,4,512]{2,1,0:T(4,128)}), f32[8,4,512]{2,1,0:T(4,128)S(1)}, u32[]{:S(2)}, u32[]{:S(2)}) async-start(f32[8,4,512]{2,1,0:T(4,128)} %get-tuple-element.25), calls=%async_computation.6 | async-start | bytes 131072 | tf_op jit(solution)/shard_map/all_to_all | solution.py:44
  154.2 1.3 iota_compare_fusion
  155.5 5.7 %all-to-all-done.6.parts = f32[8,4,512]{2,1,0:T(4,128)S(1)} async-done(((f32[8,4,512]{2,1,0:T(4,128)}), f32[8,4,512]{2,1,0:T(4,128)S(1)}, u32[]{:S(2)}, u32[]{:S(2)}) %all-to-all-start.6) | async-done | bytes 65568 | tf_op jit(solution)/shard_map/all_to_all | solution.py:44
  162.8 3.3 %all-to-all-start.8 = ((bf16[8,2,512]{2,1,0:T(2,128)(2,1)}), bf16[8,2,512]{2,1,0:T(2,128)(2,1)S(1)}, u32[]{:S(2)}, u32[]{:S(2)}) async-start(bf16[8,2,512]{2,1,0:T(2,128)(2,1)} %broadcast_in_dim.133), calls=%async_computation.8 | async-start | bytes 32768 | tf_op jit(solution)/shard_map/all_to_all | solution.py:40
  166.1 3.1 %fusion.14 = f32[304,4096]{1,0:T(8,128)} fusion(bf16[4096,16]{0,1:T(8,128)(2,1)S(1)} %copy-done.9, bf16[8,304,32]{2,1,0:T(8,128)(2,1)S(1)} %get-tuple-element.28), kind=kOutput, calls=%fused_computation.29 | convolution fusion | flops 39845888 | bytes 5189632 | tf_op jit(solution)/shard_map/dot_general | solution.py:26
  169.2 0.9 copy.94
  170.1 2.5 all-to-all-done.8
  172.7 10.1 %all-to-all-start.7 = ((bf16[8,304,32]{1,2,0:T(8,128)(2,1)}), bf16[8,304,32]{1,2,0:T(8,128)(2,1)S(1)}, u32[]{:S(2)}, u32[]{:S(2)}) async-start(bf16[8,304,32]{1,2,0:T(8,128)(2,1)} %copy.94), calls=%async_computation.7 | async-start | bytes 393216 | tf_op jit(solution)/shard_map/all_to_all | solution.py:44
  182.7 5.6 %fusion = f32[304,4096]{1,0:T(8,128)} fusion(f32[304,4096]{1,0:T(8,128)} %fusion.14, bf16[4096,16]{0,1:T(8,128)(2,1)S(1)} %copy-done.10, bf16[8,304,32]{2,1,0:T(8,128)(2,1)S(1)} %get-tuple-element.28), kind=kOutput, calls=%fused_computation.1 | convolution fusion | flops 42336256 | bytes 10170368 | tf_op jit(solution)/shard_map/dot_general | solution.py:26
  189.5 1.1 shard_map.200
  190.7 3.5 %all-to-all-start.9 = ((f32[8,4,1280]{2,1,0:T(4,128)}), f32[8,4,1280]{2,1,0:T(4,128)S(1)}, u32[]{:S(2)}, u32[]{:S(2)}) async-start(f32[8,4,1280]{2,1,0:T(4,128)} %shard_map.200), calls=%async_computation.9 | async-start | bytes 327680 | tf_op jit(solution)/shard_map/all_to_all | solution.py:44
  194.4 3.1 %fusion.26 = f32[304,4096]{1,0:T(8,128)} fusion(bf16[304,128]{1,0:T(8,128)(2,1)S(1)} %get-tuple-element.34, bf16[4096,128]{1,0:T(8,128)(2,1)S(1)} %copy-done), kind=kOutput, calls=%fused_computation.52 | convolution fusion | flops 318767104 | bytes 6107136 | tf_op jit(solution)/shard_map/dot_general | solution.py:26
  197.5 4.9 %all-to-all-done.9 = f32[8,4,1280]{2,1,0:T(4,128)S(1)} async-done(((f32[8,4,1280]{2,1,0:T(4,128)}), f32[8,4,1280]{2,1,0:T(4,128)S(1)}, u32[]{:S(2)}, u32[]{:S(2)}) %all-to-all-start.9) | async-done | bytes 163872 | tf_op jit(solution)/shard_map/all_to_all | solution.py:44
  202.5 6.9 %fusion.4 = bf16[304,4096]{1,0:T(8,128)(2,1)} fusion(f32[304,4096]{1,0:T(8,128)} %fusion, f32[304,4096]{1,0:T(8,128)} %fusion.26, bf16[304,128]{1,0:T(8,128)(2,1)S(1)} %get-tuple-element.35, bf16[4096,128]{1,0:T(8,128)(2,1)S(1)} %copy-done.6, f32[4096]{0:T(1024)S(1)} %bitcast.95, f32[4096]{0:T(1024)S(1)} %bitcast.94, ...), kind=kOutput, calls=%fused_computation.6 | convolution fusion | flops 327483392 | bytes 13611616 | tf_op jit(solution)/shard_map/dot_general | solution.py:26
  209.5 15.6 %all_to_all.65 = f32[8,4,768]{2,1,0:T(4,128)S(1)} all-to-all(f32[8,4,768]{2,1,0:T(4,128)S(1)} %broadcast_in_dim.134), channel_id=1, replica_groups=mesh['z'=8,'x'=4,'h'=2,'mp'=8] {'x','h'}, dimensions={0} | all-to-all | bytes 196608 | tf_op jit(solution)/shard_map/all_to_all | solution.py:40
  225.8 3.4 %all-to-all-start.11 = ((f32[8,4,640]{2,1,0:T(4,128)}), f32[8,4,640]{2,1,0:T(4,128)S(1)}, u32[]{:S(2)}, u32[]{:S(2)}) async-start(f32[8,4,640]{2,1,0:T(4,128)} %broadcast_in_dim.151), calls=%async_computation.12 | async-start | bytes 163840 | tf_op jit(solution)/shard_map/all_to_all | solution.py:40
  229.2 8.4 %collective-permute-start.2 = (bf16[8,512]{1,0:T(8,128)(2,1)S(1)}, bf16[8,512]{1,0:T(8,128)(2,1)S(1)}, u32[]{:S(2)}, u32[]{:S(2)}) collective-permute-start(bf16[8,512]{1,0:T(8,128)(2,1)S(1)} %dynamic-slice_bitcast_fusion), channel_id=1, source_target_pairs={{0,0},{1,64},{2,128},{3,192},{4,256},{5,320},{6,384},{7,448},{64,1... | collective-permute-start | bytes 24584 | tf_op jit(solution)/shard_map/ppermute | solution.py:326
  238.4 8.5 %all-to-all-start.12 = ((bf16[8,32,512]{2,1,0:T(8,128)(2,1)}), bf16[8,32,512]{2,1,0:T(8,128)(2,1)S(1)}, u32[]{:S(2)}, u32[]{:S(2)}) async-start(bf16[8,32,512]{2,1,0:T(8,128)(2,1)} %broadcast_in_dim.152), calls=%async_computation.13 | async-start | bytes 524288 | tf_op jit(solution)/shard_map/all_to_all | solution.py:40
  249.5 6.1 %all-to-all-done.12 = bf16[8,32,512]{2,1,0:T(8,128)(2,1)S(1)} async-done(((bf16[8,32,512]{2,1,0:T(8,128)(2,1)}), bf16[8,32,512]{2,1,0:T(8,128)(2,1)S(1)}, u32[]{:S(2)}, u32[]{:S(2)}) %all-to-all-start.12) | async-done | bytes 262176 | tf_op jit(solution)/shard_map/all_to_all | solution.py:40
  256.6 1.9 add_convert_fusion
  (77 shorter events, 13.2 us)
Async XLA Ops:
  7.2 124.8 %copy-start = (bf16[4096,128]{1,0:T(8,128)(2,1)S(1)}, bf16[4096,128]{1,0:T(8,128)(2,1)}, u32[]{:S(2)}) copy-start(bf16[4096,128]{1,0:T(8,128)(2,1)} %param.21) | copy-start | bytes 3145732
  7.2 120.3 %all-gather.2.cloned.1.call-start = ((), (), s32[]{:S(2)}) async-start(), calls=%async_computation.14 | async-start | bytes 2801664 | tf_op jit(solution)/shard_map/all_gather | solution.py:236
  9.5 88.2 %copy-start.13 = (s32[2,1]{0,1:T(1,128)S(1)}, s32[2,1]{0,1:T(1,128)}, u32[]{:S(2)}) copy-start(s32[2,1]{0,1:T(1,128)} %param.19) | copy-start | bytes 28
  9.5 91.4 %copy-start.11 = (s32[8,4]{0,1:T(4,128)S(1)}, s32[8,4]{0,1:T(4,128)}, u32[]{:S(2)}) copy-start(s32[8,4]{0,1:T(4,128)} %param.17) | copy-start | bytes 388
  9.5 91.5 %copy-start.12 = (s32[8]{0:T(128)S(1)}, s32[8]{0:T(128)}, u32[]{:S(2)}) copy-start(s32[8]{0:T(128)} %param.16) | copy-start | bytes 100
  9.5 42.1 %all-to-all-start = ((bf16[64,8,512]{2,1,0:T(8,128)(2,1)}), bf16[64,8,512]{2,1,0:T(8,128)(2,1)S(1)}, u32[]{:S(2)}, u32[]{:S(2)}) async-start(bf16[64,8,512]{2,1,0:T(8,128)(2,1)} %broadcast_in_dim.128), calls=%async_computation | async-start | bytes 1048576 | tf_op jit(solution)/shard_map/all_to_all | solution.py:40
  29.2 8.4 %collective-permute-start = (bf16[8,512]{1,0:T(8,128)(2,1)}, bf16[8,512]{1,0:T(8,128)(2,1)S(1)}, u32[]{:S(2)}, u32[]{:S(2)}) collective-permute-start(bf16[8,512]{1,0:T(8,128)(2,1)} %param.14), channel_id=1, source_target_pairs={{0,0},{1,64},{2,128},{3,192},{4,256},{5,320},{6,384},{7,448},{64,1... | collective-permute-start | bytes 24584 | tf_op jit(solution)/shard_map/ppermute | solution.py:242
  52.4 28.7 %all-to-all-start.3 = ((bf16[64,8,512]{2,1,0:T(8,128)(2,1)}), bf16[64,8,512]{2,1,0:T(8,128)(2,1)S(1)}, u32[]{:S(2)}, u32[]{:S(2)}) async-start(bf16[64,8,512]{2,1,0:T(8,128)(2,1)} %broadcast_in_dim.131), calls=%async_computation.3 | async-start | bytes 1048576 | tf_op jit(solution)/shard_map/all_to_all | solution.py:40
  64.5 0.8 copy-start.4
  64.5 62.9 %copy-start.9 = (bf16[4096,16]{0,1:T(8,128)(2,1)S(1)}, bf16[4096,16]{0,1:T(8,128)(2,1)}, u32[]{:S(2)}) copy-start(bf16[4096,16]{0,1:T(8,128)(2,1)} %param.24) | copy-start | bytes 393220
  66.3 20.9 %collective-permute-start.1 = (bf16[2,64,512]{2,1,0:T(8,128)(2,1)S(1)}, bf16[2,64,512]{2,1,0:T(8,128)(2,1)S(1)}, u32[]{:S(2)}, u32[]{:S(2)}) collective-permute-start(bf16[2,64,512]{2,1,0:T(8,128)(2,1)S(1)} %pad_maximum_fusion.1), channel_id=1, source_target_pairs={{0,8},{8,0},{1,9},{9,1},{2,10},{10,2},{3,11},{11,3},{4,12},{12,4},... | collective-permute-start | bytes 393224 | tf_op jit(solution)/shard_map/ppermute | solution.py:261
  81.1 21.2 %copy-start.8 = (bf16[64,8,512]{2,1,0:T(8,128)(2,1)}, bf16[64,8,512]{2,1,0:T(8,128)(2,1)S(1)}, u32[]{:S(2)}) copy-start(bf16[64,8,512]{2,1,0:T(8,128)(2,1)S(1)} %all-to-all-done.3) | copy-start | bytes 1572868
  81.8 11.2 %all-to-all-start.1 = ((f32[8,8,512]{2,1,0:T(8,128)}), f32[8,8,512]{2,1,0:T(8,128)S(1)}, u32[]{:S(2)}, u32[]{:S(2)}) async-start(f32[8,8,512]{2,1,0:T(8,128)} %broadcast_in_dim.129), calls=%async_computation.1 | async-start | bytes 262144 | tf_op jit(solution)/shard_map/all_to_all | solution.py:40
  87.3 42.9 %copy-start.2 = (bf16[16,128]{1,0:T(8,128)(2,1)S(1)}, bf16[16,128]{1,0:T(8,128)(2,1)}, u32[]{:S(2)}) copy-start(bf16[16,128]{1,0:T(8,128)(2,1)} %key_up.1) | copy-start | bytes 12292
  94.1 17.6 %all-to-all-start.4 = ((bf16[4,2,2,64,512]{4,3,1,2,0:T(8,128)(2,1)}), bf16[4,2,2,64,512]{4,3,1,2,0:T(8,128)(2,1)S(1)}, u32[]{:S(2)}, u32[]{:S(2)}) async-start(bf16[4,2,2,64,512]{4,3,1,2,0:T(8,128)(2,1)} %broadcast_in_dim.132), calls=%async_computation.4 | async-start | bytes 2097152 | tf_op jit(solution)/shard_map/all_to_all | solution.py:40
  111.7 1.0 copy-start.7
  111.7 22.7 %copy-start.3 = (bf16[16,128]{1,0:T(8,128)(2,1)S(1)}, bf16[16,128]{1,0:T(8,128)(2,1)}, u32[]{:S(2)}) copy-start(bf16[16,128]{1,0:T(8,128)(2,1)} %value_up.1) | copy-start | bytes 12292
  112.7 26.9 %all-to-all-start.2 = ((bf16[64,8,128]{2,1,0:T(8,128)(2,1)}), bf16[64,8,128]{2,1,0:T(8,128)(2,1)S(1)}, u32[]{:S(2)}, u32[]{:S(2)}) async-start(bf16[64,8,128]{2,1,0:T(8,128)(2,1)} %get-tuple-element.22), calls=%async_computation.2 | async-start | bytes 262144 | tf_op jit(solution)/shard_map/all_to_all | solution.py:44
  139.6 9.9 %all-to-all-start.5 = ((bf16[8,2,512]{2,1,0:T(2,128)(2,1)}), bf16[8,2,512]{2,1,0:T(2,128)(2,1)S(1)}, u32[]{:S(2)}, u32[]{:S(2)}) async-start(bf16[8,2,512]{2,1,0:T(2,128)(2,1)} %bitcast.21), calls=%async_computation.5 | async-start | bytes 32768 | tf_op jit(solution)/shard_map/all_to_all | solution.py:44
  150.8 10.5 %all-to-all-start.6 = ((f32[8,4,512]{2,1,0:T(4,128)}), f32[8,4,512]{2,1,0:T(4,128)S(1)}, u32[]{:S(2)}, u32[]{:S(2)}) async-start(f32[8,4,512]{2,1,0:T(4,128)} %get-tuple-element.25), calls=%async_computation.6 | async-start | bytes 131072 | tf_op jit(solution)/shard_map/all_to_all | solution.py:44
  162.1 20.6 %copy-start.10 = (bf16[4096,16]{0,1:T(8,128)(2,1)S(1)}, bf16[4096,16]{0,1:T(8,128)(2,1)}, u32[]{:S(2)}) copy-start(bf16[4096,16]{0,1:T(8,128)(2,1)} %param.26) | copy-start | bytes 393220
  162.8 9.9 %all-to-all-start.8 = ((bf16[8,2,512]{2,1,0:T(2,128)(2,1)}), bf16[8,2,512]{2,1,0:T(2,128)(2,1)S(1)}, u32[]{:S(2)}, u32[]{:S(2)}) async-start(bf16[8,2,512]{2,1,0:T(2,128)(2,1)} %broadcast_in_dim.133), calls=%async_computation.8 | async-start | bytes 32768 | tf_op jit(solution)/shard_map/all_to_all | solution.py:40
  172.7 16.5 %all-to-all-start.7 = ((bf16[8,304,32]{1,2,0:T(8,128)(2,1)}), bf16[8,304,32]{1,2,0:T(8,128)(2,1)S(1)}, u32[]{:S(2)}, u32[]{:S(2)}) async-start(bf16[8,304,32]{1,2,0:T(8,128)(2,1)} %copy.94), calls=%async_computation.7 | async-start | bytes 393216 | tf_op jit(solution)/shard_map/all_to_all | solution.py:44
  182.7 6.8 %copy-start.1 = (bf16[2,1,152,512]{3,2,1,0:T(8,128)(2,1)S(1)}, bf16[2,1,152,512]{3,2,1,0:T(8,128)(2,1)}, u32[]{:S(2)}) copy-start(bf16[2,1,152,512]{3,2,1,0:T(8,128)(2,1)} %param.18) | copy-start | bytes 933892
  190.7 11.8 %copy-start.6 = (bf16[4096,128]{1,0:T(8,128)(2,1)S(1)}, bf16[4096,128]{1,0:T(8,128)(2,1)}, u32[]{:S(2)}) copy-start(bf16[4096,128]{1,0:T(8,128)(2,1)} %param.22) | copy-start | bytes 3145732
  190.7 11.8 %all-to-all-start.9 = ((f32[8,4,1280]{2,1,0:T(4,128)}), f32[8,4,1280]{2,1,0:T(4,128)S(1)}, u32[]{:S(2)}, u32[]{:S(2)}) async-start(f32[8,4,1280]{2,1,0:T(4,128)} %shard_map.200), calls=%async_computation.9 | async-start | bytes 327680 | tf_op jit(solution)/shard_map/all_to_all | solution.py:44
  194.2 62.4 %reduce-scatter.2.cloned.1.call-start = ((), (), s32[]{:S(2)}) async-start(), calls=%async_computation.15 | async-start | bytes 2801664 | tf_op jit(solution)/shard_map/reduce_scatter | solution.py:373
  202.5 44.4 %copy-start.5 = (bf16[8,8,8,512]{3,2,1,0:T(8,128)(2,1)S(1)}, bf16[8,8,8,512]{3,2,1,0:T(8,128)(2,1)}, u32[]{:S(2)}) copy-start(bf16[8,8,8,512]{3,2,1,0:T(8,128)(2,1)} %copy-done.4) | copy-start | bytes 1572868
  225.8 11.8 %all-to-all-start.11 = ((f32[8,4,640]{2,1,0:T(4,128)}), f32[8,4,640]{2,1,0:T(4,128)S(1)}, u32[]{:S(2)}, u32[]{:S(2)}) async-start(f32[8,4,640]{2,1,0:T(4,128)} %broadcast_in_dim.151), calls=%async_computation.12 | async-start | bytes 163840 | tf_op jit(solution)/shard_map/all_to_all | solution.py:40
  229.2 18.6 %collective-permute-start.2 = (bf16[8,512]{1,0:T(8,128)(2,1)S(1)}, bf16[8,512]{1,0:T(8,128)(2,1)S(1)}, u32[]{:S(2)}, u32[]{:S(2)}) collective-permute-start(bf16[8,512]{1,0:T(8,128)(2,1)S(1)} %dynamic-slice_bitcast_fusion), channel_id=1, source_target_pairs={{0,0},{1,64},{2,128},{3,192},{4,256},{5,320},{6,384},{7,448},{64,1... | collective-permute-start | bytes 24584 | tf_op jit(solution)/shard_map/ppermute | solution.py:326
  238.4 17.3 %all-to-all-start.12 = ((bf16[8,32,512]{2,1,0:T(8,128)(2,1)}), bf16[8,32,512]{2,1,0:T(8,128)(2,1)S(1)}, u32[]{:S(2)}, u32[]{:S(2)}) async-start(bf16[8,32,512]{2,1,0:T(8,128)(2,1)} %broadcast_in_dim.152), calls=%async_computation.13 | async-start | bytes 524288 | tf_op jit(solution)/shard_map/all_to_all | solution.py:40
Sparse Core Ops, SparseCore 0:
  10.1 55.9 all-gather.1
  209.6 39.1 reduce-scatter.1

commit v4 on v3

v4 whole, which is shorter than its diff:
```python
import functools
import math

import jax
import jax.numpy as jnp
from jax import lax
from jax.experimental import pallas as pl
from jax.experimental.pallas import tpu as pltpu
from jax.sharding import Mesh
from jax.sharding import PartitionSpec as P

HEADS = 32
KV_HEADS = 8
HEAD_DIM = 128
LANES = 128

INV_TEMP = 50.0
HARD_NEGATIVE_ADD = 4.0
ADAPTER_SCALE = 2.0

PLANE = ("x", "h")
DP = ("z", "x", "h")


def final_product(left_side, right_side):
    return lax.dot_general(
        left_side, right_side, (((1,), (1,)), ((), ())), preferred_element_type=jnp.float32
    )


def first_product(left_side, right_side):
    return lax.dot_general(
        left_side, right_side, (((0,), (0,)), ((), ())), preferred_element_type=jnp.float32
    )


def spread(block, axes):
    count = lax.axis_size(axes)
    copies = jnp.broadcast_to(block[None], (count,) + block.shape)
    return lax.all_to_all(copies, axes, split_axis=0, concat_axis=0, tiled=True)


def swap(blocks, axes):
    return lax.all_to_all(blocks, axes, split_axis=0, concat_axis=0, tiled=True)


def call(kernel, out_shape, flops, **layout):
    return pl.pallas_call(
        kernel,
        out_shape=out_shape,
        compiler_params=pltpu.CompilerParams(vmem_limit_bytes=32 * 1024 * 1024),
        cost_estimate=pl.CostEstimate(flops=flops, bytes_accessed=2**20, transcendentals=4096),
        **layout,
    )


def residual_kernel(
    z_count, plane_count, parts, hard, pair, tokens, chunks, residual_out, loss_out
):
    rows = parts.shape[1]
    batch_size = parts.shape[2]
    pair_scores = parts[0]
    for part in range(1, parts.shape[0]):
        pair_scores = pair_scores + parts[part]
    column = lax.broadcasted_iota(jnp.int32, (rows, batch_size), 1)
    inner = column % rows
    outer = column // rows
    item = ((outer % z_count) * plane_count + outer // z_count) * rows + inner
    count = jnp.zeros((rows, batch_size), jnp.float32)
    for choice in range(hard.shape[1]):
        count = count + jnp.where(hard[:, choice : choice + 1] == item, 1.0, 0.0)
    logits = pair_scores * INV_TEMP + HARD_NEGATIVE_ADD * count
    top = jnp.max(logits, axis=1, keepdims=True)
    log_total = top + jnp.log(jnp.sum(jnp.exp(logits - top), axis=1, keepdims=True))
    target = jnp.where(pair[...] == item, 1.0, 0.0)
    picked = jnp.sum(target * logits, axis=1, keepdims=True)
    loss = jnp.sum(log_total - picked, axis=0, keepdims=True)
    loss_out[...] = jnp.broadcast_to(loss, loss_out.shape)
    residual = jnp.exp(logits - log_total) - target
    residual_out[...] = residual.astype(jnp.bfloat16)
    width = z_count * rows
    pad = jnp.zeros((rows, LANES - width), jnp.float32)
    for plane in range(plane_count):
        block = jnp.concatenate([residual[:, plane * width : (plane + 1) * width], pad], axis=1)
        block = block.astype(jnp.bfloat16)
        for z in range(z_count):
            chunks[z * plane_count + plane, :, :LANES] = block
            chunks[z * plane_count + plane, :, LANES:] = tokens[z]


def gradient_kernel(z_count, subs, place, received, queries, loss, *rest):
    pieces, (item_out, parts_out) = rest[:-2], rest[-2:]
    item_rows = item_out.shape[0]
    count = len(pieces)
    width = queries.shape[1] // count
    every = lax.dot_general(
        received[:, :LANES],
        queries[...],
        (((0,), (0,)), ((), ())),
        preferred_element_type=jnp.float32,
    )
    grads = (every[:item_rows] * INV_TEMP).astype(jnp.bfloat16)
    item_out[...] = grads
    picks = subs * z_count
    row = lax.broadcasted_iota(jnp.int32, (picks, item_rows), 0)
    column = lax.broadcasted_iota(jnp.int32, (picks, item_rows), 1)
    per_z = item_rows // z_count
    wanted = jnp.where((row // subs) * per_z + row % subs == column, 1.0, 0.0)
    cotangents = jnp.dot(
        wanted.astype(jnp.bfloat16), grads, preferred_element_type=jnp.float32
    )
    senders = received.shape[0] // per_z
    planes = senders // z_count
    row = lax.broadcasted_iota(jnp.int32, (picks, received.shape[0]), 0)
    column = lax.broadcasted_iota(jnp.int32, (picks, received.shape[0]), 1)
    first = ((row // subs) * planes + place[1:2, 0:1]) * per_z + row % subs
    attn = query = None
    for turn, piece in enumerate(pieces):
        block = lax.rem(place[0:1, 0:1] + (count - turn), count)
        cot = jnp.zeros((picks, width), jnp.float32)
        for choice in range(count):
            cot = cot + jnp.where(
                block == choice, cotangents[:, choice * width : (choice + 1) * width], 0.0
            )
        chosen = jnp.where(first + block * subs == column, 1.0, 0.0).astype(jnp.bfloat16)
        token = jnp.dot(chosen, received[:, LANES:], preferred_element_type=jnp.float32)
        wq_rows = jnp.concatenate([piece[half, 0] for half in range(piece.shape[0])], axis=0)
        wo_rows = jnp.concatenate([piece[half, 1] for half in range(piece.shape[0])], axis=0)
        attn_term = jnp.dot(cot.astype(jnp.bfloat16), wo_rows, preferred_element_type=jnp.float32)
        query_term = jnp.dot(
            token.astype(jnp.bfloat16), wq_rows, preferred_element_type=jnp.float32
        )
        attn = attn_term if attn is None else attn + attn_term
        query = query_term if query is None else query + query_term
    end = attn.shape[1]
    for z in range(z_count):
        parts_out[z, :subs, :end] = attn[z * subs : (z + 1) * subs]
        parts_out[z, subs:, :end] = query[z * subs : (z + 1) * subs]
        parts_out[z, :, end:] = loss[: 2 * subs]


def attention_kernel(
    place,
    lengths,
    parts,
    keys,
    values,
    key_up,
    value_up,
    reduced,
    tokens,
    query_delta_out,
    key_change_out,
    value_change_out,
    coef_out,
    loss_out,
    shares_out,
):
    subs = parts.shape[1] // 2
    token_count = keys.shape[0]
    seq_len = token_count // subs
    group = parts.shape[2] // HEAD_DIM - 1
    total = parts[0]
    for part in range(1, parts.shape[0]):
        total = total + parts[part]
    loss_out[...] = total[:, group * HEAD_DIM :]
    both = total.astype(jnp.bfloat16).astype(jnp.float32)

    def heads(first):
        return jnp.concatenate(
            [
                both[first + sub : first + sub + 1, head * HEAD_DIM : (head + 1) * HEAD_DIM]
                for sub in range(subs)
                for head in range(group)
            ],
            axis=0,
        )

    grad_heads = heads(0)
    q_heads = heads(subs)
    score_scale = 1.0 / math.sqrt(HEAD_DIM)
    raw = final_product(q_heads.astype(jnp.bfloat16), keys[...]) * score_scale
    row_sub = lax.broadcasted_iota(jnp.int32, raw.shape, 0) // group
    token = lax.broadcasted_iota(jnp.int32, raw.shape, 1)
    live = jnp.zeros(raw.shape, jnp.bool_)
    for sub in range(subs):
        first = sub * seq_len
        inside = (token >= first) & (token < first + lengths[sub, 0])
        live = live | (inside & (row_sub == sub))
    raw = jnp.where(live, raw, -jnp.inf)
    weights = jnp.exp(raw - jnp.max(raw, axis=1, keepdims=True))
    probs = weights / jnp.sum(weights, axis=1, keepdims=True)
    prob_half = probs.astype(jnp.bfloat16).astype(jnp.float32)
    prob_grad = final_product(grad_heads.astype(jnp.bfloat16), values[...])
    score_grad = (
        probs * (prob_grad - jnp.sum(probs * prob_grad, axis=1, keepdims=True)) * score_scale
    )
    score_grad = score_grad.astype(jnp.bfloat16)
    delta = jnp.dot(score_grad, keys[...], preferred_element_type=jnp.float32)
    for sub in range(subs):
        for head in range(group):
            row = sub * group + head
            query_delta_out[sub : sub + 1, head * HEAD_DIM : (head + 1) * HEAD_DIM] = delta[
                row : row + 1
            ]
    score_grad = score_grad.astype(jnp.float32)
    key_change = first_product(score_grad, q_heads).astype(jnp.bfloat16)
    value_change = first_product(prob_half, grad_heads).astype(jnp.bfloat16)
    key_change_out[...] = key_change
    value_change_out[...] = value_change
    key_coef = final_product(key_change, key_up[...])
    value_coef = final_product(value_change, value_up[...])
    coef = jnp.concatenate([key_coef, value_coef], axis=1).astype(jnp.bfloat16)
    coef_out[...] = coef
    rank = key_up.shape[0]
    ups = ADAPTER_SCALE * jnp.concatenate(
        [
            first_product(reduced[...], key_change)[:rank],
            first_product(reduced[...], value_change)[rank:],
        ],
        axis=0,
    )
    downs = ADAPTER_SCALE * first_product(coef, tokens[...])
    z_count, mp_count, rows, chunk_width = shares_out.shape
    width = downs.shape[1] // mp_count
    for other in range(mp_count):
        kept = jnp.where(place[2:3, 0:1] == other, ups, 0.0)
        for z in range(z_count):
            mine = slice(z * rows, (z + 1) * rows)
            shares_out[z, other, :, :width] = downs[
                mine, other * width : (other + 1) * width
            ].astype(jnp.bfloat16)
            shares_out[z, other, :, width:] = kept[mine].astype(jnp.bfloat16)


def portion_kernel(
    seq_len, lengths, key_change, value_change, coef, last, key_weight, value_weight, down, out
):
    total = final_product(key_change[...], key_weight[...]) + final_product(
        value_change[...], value_weight[...]
    )
    total = total + ADAPTER_SCALE * jnp.dot(
        coef[...], down[...], preferred_element_type=jnp.float32
    )
    row = lax.broadcasted_iota(jnp.int32, total.shape, 0)
    for sub in range(last.shape[0]):
        chosen = row == sub * seq_len + lengths[sub, 0] - 1
        total = total + jnp.where(chosen, last[sub : sub + 1], 0.0)
    out[...] = total.astype(jnp.bfloat16)


def local(
    query_emb,
    item_emb,
    pair_index,
    hard_index,
    hidden_in,
    lengths,
    w_query,
    key_weight_matrix,
    value_weight_matrix,
    w_out,
    key_down_matrix,
    key_up_matrix,
    value_down,
    value_up_matrix,
):
    bf16, f32 = jnp.bfloat16, jnp.float32
    x_count = lax.axis_size("x")
    z_count = lax.axis_size("z")
    plane_count = lax.axis_size(PLANE)
    dp_count = z_count * plane_count
    mp_count = lax.axis_size("mp")
    local_rows = query_emb.shape[0]
    batch_size = local_rows * dp_count
    feature_width = query_emb.shape[1]
    place = jnp.broadcast_to(
        jnp.stack([lax.axis_index("x"), lax.axis_index(PLANE), lax.axis_index("mp")])[:, None],
        (3, LANES),
    ).astype(jnp.int32)

    sub_count = hidden_in.shape[0]
    seq_len = hidden_in.shape[2]
    token_count = sub_count * seq_len
    full_rows = lax.all_gather(hidden_in, "mp", axis=3, tiled=True)
    model_width = full_rows.shape[3]
    token_inputs = full_rows.reshape(token_count, model_width)
    seq_lengths = lengths[:, 0]
    last_rows = jnp.arange(sub_count, dtype=jnp.int32) * seq_len + seq_lengths - 1

    query_slices = spread(query_emb, "mp")
    chunks = jnp.concatenate(
        [jnp.broadcast_to(item_emb[None], query_slices.shape), query_slices], axis=1
    )
    chunks = jnp.broadcast_to(chunks[:, None], (z_count, plane_count) + chunks.shape[1:])
    received = swap(chunks.reshape((dp_count,) + chunks.shape[2:]), DP)
    queries_all = received[:, local_rows:].reshape(batch_size, feature_width)
    items_all = (
        received[:, :local_rows]
        .reshape(z_count, plane_count, local_rows, feature_width)
        .transpose(1, 0, 2, 3)
        .reshape(batch_size, feature_width)
    )
    partial_scores = final_product(query_emb, items_all)
    score_parts = spread(partial_scores, "mp")

    rows_here, query_width = w_query.shape
    both = jnp.stack([w_query, w_out.T])
    other = lax.ppermute(both, "h", [(0, 1), (1, 0)])
    lower = lax.axis_index("h") == 0
    both = jnp.stack([jnp.where(lower, both, other), jnp.where(lower, other, both)])
    pieces = [both] + [
        lax.ppermute(both, "x", [(a, (a + turn) % x_count) for a in range(x_count)])
        for turn in range(1, x_count)
    ]
    wq_plane = jnp.stack([piece[:, 0] for piece in pieces])
    wq_plane, partial_scores = lax.optimization_barrier((wq_plane, partial_scores))
    wq_full = lax.all_gather(
        wq_plane.reshape(plane_count * rows_here, query_width), "z", axis=0, tiled=True
    )

    last_tokens = jnp.concatenate(
        [
            lax.dynamic_slice_in_dim(token_inputs, last_rows[sub], 1, 0)
            for sub in range(sub_count)
        ],
        axis=0,
    )
    last_slices = (
        last_tokens.reshape(sub_count, z_count, x_count, feature_width // x_count)
        .transpose(1, 2, 0, 3)
        .reshape(z_count, x_count * sub_count, feature_width // x_count)
    )

    adapter_rank = key_down_matrix.shape[1]
    down_both = jnp.concatenate([key_down_matrix, value_down], axis=1)
    reduced_pair = jnp.dot(token_inputs, down_both, preferred_element_type=f32).astype(bf16)
    reduced_key = reduced_pair[:, :adapter_rank]
    reduced_value = reduced_pair[:, adapter_rank:]
    key_rows = (
        jnp.dot(token_inputs, key_weight_matrix, preferred_element_type=f32)
        + ADAPTER_SCALE * jnp.dot(reduced_key, key_up_matrix, preferred_element_type=f32)
    ).astype(bf16)
    value_rows = (
        jnp.dot(token_inputs, value_weight_matrix, preferred_element_type=f32)
        + ADAPTER_SCALE * jnp.dot(reduced_value, value_up_matrix, preferred_element_type=f32)
    ).astype(bf16)

    chunks, residual, loss_part = call(
        functools.partial(residual_kernel, z_count, plane_count),
        (
            jax.ShapeDtypeStruct((dp_count, local_rows, 2 * LANES), bf16),
            jax.ShapeDtypeStruct((local_rows, batch_size), bf16),
            jax.ShapeDtypeStruct((local_rows, LANES), f32),
        ),
        2**24,
    )(score_parts, hard_index, pair_index[:, None], last_slices)
    column_rows = swap(chunks, DP).reshape(batch_size, 2 * LANES)
    column_rows, key_rows, value_rows = lax.optimization_barrier(
        (column_rows, key_rows, value_rows)
    )
    column_grads, parts = call(
        functools.partial(gradient_kernel, z_count, sub_count),
        (
            jax.ShapeDtypeStruct((z_count * local_rows, feature_width), bf16),
            jax.ShapeDtypeStruct((z_count, 2 * sub_count, query_width + LANES), f32),
        ),
        2**26,
    )(place, column_rows, queries_all, loss_part, *pieces)
    parts = swap(parts, "z")
    own_grads = lax.dynamic_index_in_dim(
        column_grads.reshape(z_count, local_rows, feature_width),
        lax.axis_index("mp"),
        0,
        keepdims=False,
    )
    item_grad = lax.ppermute(
        own_grads,
        ("z", "mp"),
        [(a * mp_count + b, b * mp_count + a) for a in range(z_count) for b in range(mp_count)],
    )
    query_grad = (jnp.dot(residual, items_all, preferred_element_type=f32) * INV_TEMP).astype(bf16)

    share_rows = 2 * adapter_rank // z_count
    up_width = key_rows.shape[1]
    query_delta, key_change, value_change, coef, loss_part, shares = call(
        attention_kernel,
        (
            jax.ShapeDtypeStruct((sub_count, query_width), f32),
            jax.ShapeDtypeStruct(key_rows.shape, bf16),
            jax.ShapeDtypeStruct(value_rows.shape, bf16),
            jax.ShapeDtypeStruct((token_count, 2 * adapter_rank), bf16),
            jax.ShapeDtypeStruct((2 * sub_count, LANES), f32),
            jax.ShapeDtypeStruct((z_count, mp_count, share_rows, feature_width + up_width), bf16),
        ),
        2**26,
    )(
        place,
        lengths,
        parts,
        key_rows,
        value_rows,
        key_up_matrix,
        value_up_matrix,
        reduced_pair,
        token_inputs,
    )
    shares = swap(shares.reshape((-1,) + shares.shape[2:]), ("z", "mp"))

    last_part = final_product(query_delta.astype(bf16), wq_full)
    last_part = last_part.reshape(sub_count, z_count, x_count, -1)
    last_part = jnp.roll(last_part[:, :, (0,) + tuple(range(x_count - 1, 0, -1))], lax.axis_index("x"), axis=2)
    last_part = last_part.reshape(sub_count, model_width)
    block = model_width // mp_count
    whole = lambda array: pl.BlockSpec(array.shape, lambda step: (0, 0))
    along = lambda array: pl.BlockSpec((array.shape[0], block), lambda step: (0, step))
    down = lambda array: pl.BlockSpec((block, array.shape[1]), lambda step: (step, 0))
    down_rows = down_both.T
    portion = call(
        functools.partial(portion_kernel, seq_len),
        jax.ShapeDtypeStruct((token_count, model_width), bf16),
        2**29,
        grid=(mp_count,),
        in_specs=[
            whole(lengths),
            whole(key_change),
            whole(value_change),
            whole(coef),
            along(last_part),
            down(key_weight_matrix),
            down(value_weight_matrix),
            along(down_rows),
        ],
        out_specs=pl.BlockSpec((token_count, block), lambda step: (0, step)),
    )(
        lengths,
        key_change,
        value_change,
        coef,
        last_part,
        key_weight_matrix,
        value_weight_matrix,
        down_rows,
    )
    input_sum = lax.psum_scatter(portion, "mp", scatter_dimension=1, tiled=True).astype(f32)
    row_ids = jnp.arange(token_count, dtype=jnp.int32)[:, None]
    for sub in range(sub_count):
        input_sum = input_sum + jnp.where(
            row_ids == last_rows[sub], item_grad[sub][None, :].astype(f32), 0.0
        )
    input_grad = input_sum.astype(bf16).reshape(hidden_in.shape)

    share_sum = jnp.sum(shares.astype(f32), axis=0)
    share_sum = jnp.concatenate([share_sum, loss_part[:share_rows]], axis=1)
    share_sum = jnp.sum(spread(share_sum, PLANE), axis=0)
    mean_loss = share_sum[0, feature_width + up_width] / batch_size
    summed = spread(share_sum[:, : feature_width + up_width].astype(bf16), ("z", "mp"))
    summed, input_grad = lax.optimization_barrier((summed, input_grad))
    summed = summed.reshape(z_count, mp_count, share_rows, feature_width + up_width)
    up_grad = lax.dynamic_index_in_dim(
        summed[:, :, :, feature_width:], lax.axis_index("mp"), 1, keepdims=False
    )
    up_grad = up_grad.reshape(2 * adapter_rank, up_width).astype(f32)
    down_grad = (
        summed[:, :, :, :feature_width]
        .transpose(0, 2, 1, 3)
        .reshape(2 * adapter_rank, model_width)
        .astype(f32)
        .T
    )
    return (
        mean_loss,
        query_grad,
        item_grad,
        input_grad,
        down_grad[:, :adapter_rank],
        down_grad[:, adapter_rank:],
        up_grad[:adapter_rank],
        up_grad[adapter_rank:],
    )


def solution(mesh):
    fine = Mesh(
        mesh.devices.reshape(8, 4, 2, mesh.devices.shape[1]), ("z", "x", "h", "mp")
    )
    in_specs = (
        P(DP, "mp"),
        P(DP, "mp"),
        P(DP),
        P(DP, None),
        P(None, DP, None, "mp"),
        P(None, DP),
        P(DP, "mp"),
        P(None, "mp"),
        P(None, "mp"),
        P("mp", DP),
        P(),
        P(None, "mp"),
        P(),
        P(None, "mp"),
    )
    out_specs = (
        P(),
        P(DP, "mp"),
        P(DP, "mp"),
        P(None, DP, None, "mp"),
        P(),
        P(),
        P(None, "mp"),
        P(None, "mp"),
    )
    return jax.shard_map(local, mesh=fine, in_specs=in_specs, out_specs=out_specs, check_vma=False)
```

time: 269 us -> 273 us (1.015)
  starting transfers between devices: 109 us -> 71.1 us
  waiting for transfers between devices: 68.6 us -> 97.6 us
  local copies, waits for them, and re-layouts: 16.3 us -> 38.2 us
  matrix products: 28.7 us -> 12.1 us
  Pallas kernels: 4.22 us -> 11.6 us
    ppermute x1, waiting for transfers between devices: 0.01 us -> 39.9 us  [local(): other = lax.ppermute(both, 'h', [(0, 1), (1, 0)])]
    all_to_all x7 -> x3, starting transfers between devices: 55 us -> 16.9 us  [spread(): return lax.all_to_all(copies, axes, split_axis=0, concat_axis=0, tiled=True)]
    all_to_all x7 -> x3, waiting for transfers between devices: 43.3 us -> 22 us  [spread(): return lax.all_to_all(copies, axes, split_axis=0, concat_axis=0, tiled=True)]
    unnamed x31 -> x101, local copies, waits for them, and re-layouts: 2.63 us -> 21.1 us
    dot_general x5 -> x2, matrix products: 19.6 us -> 3.7 us  [final_product(): lax.dot_general(left_side, right_side, (((1,), (1,)), ((), ())), preferre...]
    all_to_all x5 -> x4, waiting for transfers between devices: 20.2 us -> 27.6 us  [swap(): return lax.all_to_all(blocks, axes, split_axis=0, concat_axis=0, tiled=True)]
    pallas_call x1, Pallas kernels: 1.14 us -> 5.47 us  [local(): call(functools.partial(portion_kernel, seq_len), jax.ShapeDtypeStruct((to...]
    broadcast_in_dim x8 -> x4, local copies, waits for them, and re-layouts: 6.17 us -> 2.85 us  [spread(): copies = jnp.broadcast_to(block[None], (count,) + block.shape)]
  transfers between devices with their start and end apart: 17 -> 15, of which waited for: 12 -> 8; matrix products, arithmetic and copies ran while one was open for 14% -> 11% of each run, Pallas kernels for 0% -> 2%
where the time goes in v4:
time: 273 us; the launch traced here: 271 us
  waiting for transfers between devices  97.6 us (36%)
  starting transfers between devices  71.1 us (26%)
  local copies, waits for them, and re-layouts  38.2 us (14%)
  between operations  19.7 us (7%)
  blocking collectives  14.3 us (5%)
  matrix products  12.1 us (4%)
  Pallas kernels  11.6 us (4%)
  other arithmetic  6.29 us (2%)
    ppermute x1, waiting for transfers between devices, local(): other = lax.ppermute(both, 'h', [(0, 1), (1, 0)])  39.9 us
    all_to_all x4, starting transfers between devices, swap(): return lax.all_to_all(blocks, axes, split_axis=0, concat_axis=0, tiled=True)  35.4 us
    all_to_all x4, waiting for transfers between devices, swap(): return lax.all_to_all(blocks, axes, split_axis=0, concat_axis=0, tiled=True)  27.6 us
    all_to_all x3, waiting for transfers between devices, spread(): return lax.all_to_all(copies, axes, split_axis=0, concat_axis=0, tiled=True)  22 us
    unnamed x101, local copies, waits for them, and re-layouts  21.1 us
    all_to_all x3, starting transfers between devices, spread(): return lax.all_to_all(copies, axes, split_axis=0, concat_axis=0, tiled=True)  16.9 us
    all_to_all x1, blocking collectives, spread(): return lax.all_to_all(copies, axes, split_axis=0, concat_axis=0, tiled=True)  14.3 us
    ppermute x3, starting transfers between devices, local(): lax.ppermute(both, 'x', [(a, (a + turn) % x_count) for a in range(x_count)])  9.86 us
  transfers between devices with their start and end apart: 15, of which 8 were waited for; matrix products, arithmetic and copies ran while one was open for 11% of the time, Pallas kernels for 2%

profile of v4, /device:TPU:1, one launch (start us, length us, event | category | flops | bytes accessed | tf_op | source)
XLA Modules:
  0.0 270.8 jit_solution(10972162724401511631)
XLA Ops:
  8.6 14.3 %all_to_all.40 = bf16[8,8,512]{2,1,0:T(8,128)(2,1)S(1)} all-to-all(bf16[8,8,512]{2,1,0:T(8,128)(2,1)S(1)} %broadcast_in_dim.92), channel_id=1, replica_groups=mesh['z'=8,'x'=4,'h'=2,'mp'=8] {'mp'}, dimensions={0} | all-to-all | bytes 131072 | tf_op jit(solution)/shard_map/all_to_all | solution.py:40
  23.7 1.1 broadcast_in_dim.93
  24.8 13.4 %all-to-all-start.1 = ((bf16[64,16,512]{2,1,0:T(8,128)(2,1)}), bf16[64,16,512]{2,1,0:T(8,128)(2,1)S(1)}, u32[]{:S(2)}, u32[]{:S(2)}) async-start(bf16[64,16,512]{2,1,0:T(8,128)(2,1)} %bitcast.3), calls=%async_computation.1 | async-start | bytes 2097152 | tf_op jit(solution)/shard_map/all_to_all | solution.py:44
  38.3 6.8 %collective-permute-start = (bf16[2,64,512]{2,1,0:T(8,128)(2,1)S(1)}, bf16[2,64,512]{2,1,0:T(8,128)(2,1)S(1)}, u32[]{:S(2)}, u32[]{:S(2)}) collective-permute-start(bf16[2,64,512]{2,1,0:T(8,128)(2,1)S(1)} %pad_maximum_fusion.3), channel_id=1, source_target_pairs={{0,8},{8,0},{1,9},{9,1},{2,10},{10,2},{3,11},{11,3},{4,12},{12,4},... | collective-permute-start | bytes 393224 | tf_op jit(solution)/shard_map/ppermute | solution.py:309
  45.1 39.9 %collective-permute-done = bf16[2,64,512]{2,1,0:T(8,128)(2,1)S(1)} collective-permute-done((bf16[2,64,512]{2,1,0:T(8,128)(2,1)S(1)}, bf16[2,64,512]{2,1,0:T(8,128)(2,1)S(1)}, u32[]{:S(2)}, u32[]{:S(2)}) %collective-permute-start) | collective-permute-done | bytes 131104 | tf_op jit(solution)/shard_map/ppermute | solution.py:309
  85.1 4.3 %collective-permute-start.3 = (bf16[2,2,64,512]{3,2,1,0:T(8,128)(2,1)S(1)}, bf16[2,2,64,512]{3,2,1,0:T(8,128)(2,1)S(1)}, u32[]{:S(2)}, u32[]{:S(2)}) collective-permute-start(bf16[2,2,64,512]{3,2,1,0:T(8,128)(2,1)S(1)} %copy.133.rest_0_), channel_id=1, source_target_pairs={{0,48},{16,0},{32,16},{48,32},{1,49},{17,1},{33,17},{49,33},{2,50}... | collective-permute-start | bytes 786440 | tf_op jit(solution)/shard_map/ppermute | solution.py:313
  90.1 1.9 collective-permute-start.1
  92.0 3.7 %collective-permute-start.2 = (bf16[2,2,64,512]{3,2,0,1:T(8,128)(2,1)S(1)}, bf16[2,2,64,512]{3,2,0,1:T(8,128)(2,1)S(1)}, u32[]{:S(2)}, u32[]{:S(2)}) collective-permute-start(bf16[2,2,64,512]{3,2,0,1:T(8,128)(2,1)S(1)} %pad_maximum_fusion.1), channel_id=1, source_target_pairs={{0,32},{16,48},{32,0},{48,16},{1,33},{17,49},{33,1},{49,17},{2,34}... | collective-permute-start | bytes 786440 | tf_op jit(solution)/shard_map/ppermute | solution.py:313
  96.4 7.3 %collective-permute-done.2 = bf16[2,2,64,512]{3,2,0,1:T(8,128)(2,1)S(1)} collective-permute-done((bf16[2,2,64,512]{3,2,0,1:T(8,128)(2,1)S(1)}, bf16[2,2,64,512]{3,2,0,1:T(8,128)(2,1)S(1)}, u32[]{:S(2)}, u32[]{:S(2)}) %collective-permute-start.2) | collective-permute-done | bytes 262176 | tf_op jit(solution)/shard_map/ppermute | solution.py:313
  103.8 0.9 pad_maximum_fusion
  104.7 0.9 slice_bitcast_fusion
  105.7 0.8 copy-done.38
  115.8 7.6 %all-to-all-start.2 = ((f32[8,8,512]{2,1,0:T(8,128)}), f32[8,8,512]{2,1,0:T(8,128)}, u32[]{:S(2)}, u32[]{:S(2)}) async-start(f32[8,8,512]{2,1,0:T(8,128)} %broadcast_in_dim.94), calls=%async_computation.2 | async-start | bytes 262144 | tf_op jit(solution)/shard_map/all_to_all | solution.py:40
  123.4 1.1 constant_dynamic-slice_fusion.1
  125.9 3.5 %all-to-all-done.2.parts = f32[8,8,512]{2,1,0:T(8,128)} async-done(((f32[8,8,512]{2,1,0:T(8,128)}), f32[8,8,512]{2,1,0:T(8,128)}, u32[]{:S(2)}, u32[]{:S(2)}) %all-to-all-start.2) | async-done | bytes 131104 | tf_op jit(solution)/shard_map/all_to_all | solution.py:40
  130.8 1.2 shard_map.206
  133.9 8.8 %all-to-all-start.3 = ((bf16[64,8,256]{2,1,0:T(8,128)(2,1)}), bf16[64,8,256]{2,1,0:T(8,128)(2,1)}, u32[]{:S(2)}, u32[]{:S(2)}) async-start(bf16[64,8,256]{2,1,0:T(8,128)(2,1)} %copy-done.17), calls=%async_computation.3 | async-start | bytes 524288 | tf_op jit(solution)/shard_map/all_to_all | solution.py:44
  142.7 3.3 %convolution_convert_fusion = bf16[32,304]{1,0:T(8,128)(2,1)} fusion(bf16[4096,32]{0,1:T(8,128)(2,1)} %copy-done.5, bf16[304,4096]{1,0:T(8,128)(2,1)} %bitcast.80), kind=kOutput, calls=%fused_computation.7 | convolution fusion | flops 79701504 | bytes 2771968 | tf_op jit(solution)/shard_map/dot_general | solution.py:337
  146.0 1.5 copy.130
  147.5 1.1 convolution_multiply_fusion.1
  148.6 1.4 fusion.keys
  150.3 1.5 fusion.1.values
  151.8 4.8 %all-to-all-done.3 = bf16[64,8,256]{2,1,0:T(8,128)(2,1)} async-done(((bf16[64,8,256]{2,1,0:T(8,128)(2,1)}), bf16[64,8,256]{2,1,0:T(8,128)(2,1)}, u32[]{:S(2)}, u32[]{:S(2)}) %all-to-all-start.3) | async-done | bytes 262176 | tf_op jit(solution)/shard_map/all_to_all | solution.py:44
  157.3 1.0 copy-done.4
  158.4 1.0 copy-done.10
  159.3 1.0 copy-done.11
  160.3 0.9 copy-done.12
  161.2 1.0 copy-done.14
  162.2 1.8 shard_map.207
  165.2 4.0 %all-to-all-start.4 = ((f32[8,4,640]{2,1,0:T(4,128)}), f32[8,4,640]{2,1,0:T(4,128)}, u32[]{:S(2)}, u32[]{:S(2)}) async-start(f32[8,4,640]{2,1,0:T(4,128)} %copy-done.18), calls=%async_computation.4 | async-start | bytes 163840 | tf_op jit(solution)/shard_map/all_to_all | solution.py:44
  169.2 1.3 copy.136.lengths
  170.5 1.3 pad_clamp_fusion
  171.8 4.8 %all-to-all-done.4.parts = f32[8,4,640]{2,1,0:T(4,128)} async-done(((f32[8,4,640]{2,1,0:T(4,128)}), f32[8,4,640]{2,1,0:T(4,128)}, u32[]{:S(2)}, u32[]{:S(2)}) %all-to-all-start.4) | async-done | bytes 81952 | tf_op jit(solution)/shard_map/all_to_all | solution.py:44
  176.6 0.9 copy-done.8
  177.5 0.9 copy-done.15
  178.4 0.9 copy-done.16
  180.0 3.1 %shard_map.208 = (f32[2,512]{1,0:T(2,128)S(1)}, bf16[304,128]{1,0:T(8,128)(2,1)S(1)}, bf16[304,128]{1,0:T(8,128)(2,1)S(1)}, bf16[304,32]{1,0:T(8,128)(2,1)S(1)},...) custom-call(s32[3,128]{1,0:T(4,128)S(1)} %broadcast_in_dim.90.place, s32[2,1]{1,0:T(2,128)S(1)} %copy-done.33, ...), custom_call_target="tpu_custom_call" | custom-call | flops 67108864 | bytes 1048576 | tf_op jit(solution)/shard_map/pallas_call | solution.py:386
  185.6 3.5 %fusion.8 = f32[2,4096]{1,0:T(2,128)S(1)} fusion(bf16[4096,512]{1,0:T(8,128)(2,1)} %all-gather.5.cloned.1.call-done, f32[2,512]{1,0:T(2,128)S(1)} %get-tuple-element.38), kind=kOutput, calls=%fused_computation.46 | convolution fusion | flops 8389632 | bytes 4231168 | tf_op jit(solution)/shard_map/dot_general | solution.py:26
  190.0 5.5 %shard_map.209 = bf16[304,4096]{1,0:T(8,128)(2,1)} custom-call(s32[2,1]{1,0:T(2,128)S(1)} %copy-done.34, bf16[304,128]{1,0:T(8,128)(2,1)S(1)} %copy-done.20, bf16[304,128]{1,0:T(8,128)(2,1)S(1)} %copy-done.22, bf16[304,32]{1,0:T(8,128)(2,1)S(1)} %copy-done.24, f32[2,4096]{1,0:T(2,128)S(1)} %reshape.100.last, bf16[4096,128]{1,0:T(8,128)(2,1)S(1)} %copy-done.1, ...), custom_call_target="tpu_custom_call" | custom-call | flops 536870912 | bytes 1048576 | tf_op jit(solution)/shard_map/pallas_call | solution.py:419
  195.5 9.2 %all-to-all-start.5 = ((bf16[64,4,640]{2,1,0:T(4,128)(2,1)}), bf16[64,4,640]{2,1,0:T(4,128)(2,1)S(1)}, u32[]{:S(2)}, u32[]{:S(2)}) async-start(bf16[64,4,640]{2,1,0:T(4,128)(2,1)} %bitcast.24), calls=%async_computation.5 | async-start | bytes 655360 | tf_op jit(solution)/shard_map/all_to_all | solution.py:44
  204.7 17.9 %all-to-all-done.5 = bf16[64,4,640]{2,1,0:T(4,128)(2,1)S(1)} async-done(((bf16[64,4,640]{2,1,0:T(4,128)(2,1)}), bf16[64,4,640]{2,1,0:T(4,128)(2,1)S(1)}, u32[]{:S(2)}, u32[]{:S(2)}) %all-to-all-start.5) | async-done | bytes 327712 | tf_op jit(solution)/shard_map/all_to_all | solution.py:44
  223.5 3.4 %all-to-all-start.6 = ((f32[8,4,768]{2,1,0:T(4,128)}), f32[8,4,768]{2,1,0:T(4,128)S(1)}, u32[]{:S(2)}, u32[]{:S(2)}) async-start(f32[8,4,768]{2,1,0:T(4,128)} %broadcast_in_dim.96), calls=%async_computation.6 | async-start | bytes 196608 | tf_op jit(solution)/shard_map/all_to_all | solution.py:40
  226.9 1.2 iota_compare_fusion
  228.8 2.1 collective-permute-start.4
  230.8 7.6 %all-to-all-done.6 = f32[8,4,768]{2,1,0:T(4,128)S(1)} async-done(((f32[8,4,768]{2,1,0:T(4,128)}), f32[8,4,768]{2,1,0:T(4,128)S(1)}, u32[]{:S(2)}, u32[]{:S(2)}) %all-to-all-start.6) | async-done | bytes 98336 | tf_op jit(solution)/shard_map/all_to_all | solution.py:40
  239.3 5.9 %all-to-all-start.7 = ((bf16[64,4,640]{2,1,0:T(4,128)(2,1)}), bf16[64,4,640]{2,1,0:T(4,128)(2,1)S(1)}, u32[]{:S(2)}, u32[]{:S(2)}) async-start(bf16[64,4,640]{2,1,0:T(4,128)(2,1)} %broadcast_in_dim.97), calls=%async_computation.7 | async-start | bytes 655360 | tf_op jit(solution)/shard_map/all_to_all | solution.py:40
  247.2 1.9 add_convert_fusion
  249.1 10.9 %all-to-all-done.7 = bf16[64,4,640]{2,1,0:T(4,128)(2,1)S(1)} async-done(((bf16[64,4,640]{2,1,0:T(4,128)(2,1)}), bf16[64,4,640]{2,1,0:T(4,128)(2,1)S(1)}, u32[]{:S(2)}, u32[]{:S(2)}) %all-to-all-start.7) | async-done | bytes 327712 | tf_op jit(solution)/shard_map/all_to_all | solution.py:40
  (155 shorter events, 27.2 us)
Async XLA Ops:
  7.2 31.1 %copy-start.41 = (bf16[64,512]{1,0:T(8,128)(2,1)S(1)}, bf16[64,512]{1,0:T(8,128)(2,1)}, u32[]{:S(2)}) copy-start(bf16[64,512]{1,0:T(8,128)(2,1)} %param.21) | copy-start | bytes 196612
  7.2 31.1 %copy-start.40 = (bf16[512,64]{0,1:T(8,128)(2,1)S(1)}, bf16[512,64]{0,1:T(8,128)(2,1)}, u32[]{:S(2)}) copy-start(bf16[512,64]{0,1:T(8,128)(2,1)} %param.24) | copy-start | bytes 196612
  7.2 116.2 %all-gather.3.cloned.1.call-start = ((), (), s32[]{:S(2)}) async-start(), calls=%async_computation.9 | async-start | bytes 2801664 | tf_op jit(solution)/shard_map/all_gather | solution.py:285
  24.8 79.9 %all-to-all-start.1 = ((bf16[64,16,512]{2,1,0:T(8,128)(2,1)}), bf16[64,16,512]{2,1,0:T(8,128)(2,1)S(1)}, u32[]{:S(2)}, u32[]{:S(2)}) async-start(bf16[64,16,512]{2,1,0:T(8,128)(2,1)} %bitcast.3), calls=%async_computation.1 | async-start | bytes 2097152 | tf_op jit(solution)/shard_map/all_to_all | solution.py:44
  38.2 147.4 %all-gather.5.cloned.1.call-start = ((), (), s32[]{:S(2)}) async-start(), calls=%async_computation.10 | async-start | bytes 4718592 | tf_op jit(solution)/shard_map/all_gather | solution.py:318
  38.3 46.7 %collective-permute-start = (bf16[2,64,512]{2,1,0:T(8,128)(2,1)S(1)}, bf16[2,64,512]{2,1,0:T(8,128)(2,1)S(1)}, u32[]{:S(2)}, u32[]{:S(2)}) collective-permute-start(bf16[2,64,512]{2,1,0:T(8,128)(2,1)S(1)} %pad_maximum_fusion.3), channel_id=1, source_target_pairs={{0,8},{8,0},{1,9},{9,1},{2,10},{10,2},{3,11},{11,3},{4,12},{12,4},... | collective-permute-start | bytes 393224 | tf_op jit(solution)/shard_map/ppermute | solution.py:309
  85.1 10.6 %collective-permute-start.3 = (bf16[2,2,64,512]{3,2,1,0:T(8,128)(2,1)S(1)}, bf16[2,2,64,512]{3,2,1,0:T(8,128)(2,1)S(1)}, u32[]{:S(2)}, u32[]{:S(2)}) collective-permute-start(bf16[2,2,64,512]{3,2,1,0:T(8,128)(2,1)S(1)} %copy.133.rest_0_), channel_id=1, source_target_pairs={{0,48},{16,0},{32,16},{48,32},{1,49},{17,1},{33,17},{49,33},{2,50}... | collective-permute-start | bytes 786440 | tf_op jit(solution)/shard_map/ppermute | solution.py:313
  90.1 13.7 %collective-permute-start.1 = (bf16[2,2,64,512]{3,2,0,1:T(8,128)(2,1)S(1)}, bf16[2,2,64,512]{3,2,0,1:T(8,128)(2,1)S(1)}, u32[]{:S(2)}, u32[]{:S(2)}) collective-permute-start(bf16[2,2,64,512]{3,2,0,1:T(8,128)(2,1)S(1)} %pad_maximum_fusion.1), channel_id=1, source_target_pairs={{0,16},{16,32},{32,48},{48,0},{1,17},{17,33},{33,49},{49,1},{2,18}... | collective-permute-start | bytes 786440 | tf_op jit(solution)/shard_map/ppermute | solution.py:313
  92.0 11.7 %collective-permute-start.2 = (bf16[2,2,64,512]{3,2,0,1:T(8,128)(2,1)S(1)}, bf16[2,2,64,512]{3,2,0,1:T(8,128)(2,1)S(1)}, u32[]{:S(2)}, u32[]{:S(2)}) collective-permute-start(bf16[2,2,64,512]{3,2,0,1:T(8,128)(2,1)S(1)} %pad_maximum_fusion.1), channel_id=1, source_target_pairs={{0,32},{16,48},{32,0},{48,16},{1,33},{17,49},{33,1},{49,17},{2,34}... | collective-permute-start | bytes 786440 | tf_op jit(solution)/shard_map/ppermute | solution.py:313
  95.7 10.8 %copy-start.44 = (bf16[8,512]{1,0:T(8,128)(2,1)S(1)}, bf16[8,512]{1,0:T(8,128)(2,1)}, u32[]{:S(2)}) copy-start(bf16[8,512]{1,0:T(8,128)(2,1)} %param.15) | copy-start | bytes 24580
  103.8 3.0 %copy-start.47 = (s32[2,1]{0,1:T(1,128)S(1)}, s32[2,1]{0,1:T(1,128)}, u32[]{:S(2)}) copy-start(s32[2,1]{0,1:T(1,128)} %param.20) | copy-start | bytes 28
  103.8 6.0 %copy-start.45 = (s32[8,4]{0,1:T(4,128)S(1)}, s32[8,4]{0,1:T(4,128)}, u32[]{:S(2)}) copy-start(s32[8,4]{0,1:T(4,128)} %param.18) | copy-start | bytes 388
  103.8 6.7 %copy-start.46 = (s32[8]{0:T(128)S(1)}, s32[8]{0:T(128)}, u32[]{:S(2)}) copy-start(s32[8]{0:T(128)} %param.17) | copy-start | bytes 100
  103.8 9.2 %copy-start.42 = (bf16[4096,16]{0,1:T(8,128)(2,1)S(1)}, bf16[4096,16]{0,1:T(8,128)(2,1)}, u32[]{:S(2)}) copy-start(bf16[4096,16]{0,1:T(8,128)(2,1)} %param.25) | copy-start | bytes 393220
  104.7 8.3 %copy-start.43 = (bf16[4096,16]{0,1:T(8,128)(2,1)S(1)}, bf16[4096,16]{0,1:T(8,128)(2,1)}, u32[]{:S(2)}) copy-start(bf16[4096,16]{0,1:T(8,128)(2,1)} %param.27) | copy-start | bytes 393220
  105.7 0.8 copy-start.38
  114.4 34.2 %copy-start.1 = (bf16[4096,128]{1,0:T(8,128)(2,1)S(1)}, bf16[4096,128]{1,0:T(8,128)(2,1)}, u32[]{:S(2)}) copy-start(bf16[4096,128]{1,0:T(8,128)(2,1)} %key_weight.1) | copy-start | bytes 3145732
  115.8 13.6 %all-to-all-start.2 = ((f32[8,8,512]{2,1,0:T(8,128)}), f32[8,8,512]{2,1,0:T(8,128)}, u32[]{:S(2)}, u32[]{:S(2)}) async-start(f32[8,8,512]{2,1,0:T(8,128)} %broadcast_in_dim.94), calls=%async_computation.2 | async-start | bytes 262144 | tf_op jit(solution)/shard_map/all_to_all | solution.py:40
  123.4 25.2 %copy-start = (bf16[2,1,152,4096]{3,2,1,0:T(8,128)(2,1)S(1)}, bf16[2,1,152,4096]{3,2,1,0:T(8,128)(2,1)}, u32[]{:S(2)}) copy-start(bf16[2,1,152,4096]{3,2,1,0:T(8,128)(2,1)} %all-gather.3.cloned.1.call-done) | copy-start | bytes 7471108
  133.9 13.6 %copy-start.25 = (bf16[16,128]{1,0:T(8,128)(2,1)S(1)}, bf16[16,128]{1,0:T(8,128)(2,1)}, u32[]{:S(2)}) copy-start(bf16[16,128]{1,0:T(8,128)(2,1)} %key_up.1) | copy-start | bytes 12292
  133.9 22.7 %all-to-all-start.3 = ((bf16[64,8,256]{2,1,0:T(8,128)(2,1)}), bf16[64,8,256]{2,1,0:T(8,128)(2,1)}, u32[]{:S(2)}, u32[]{:S(2)}) async-start(bf16[64,8,256]{2,1,0:T(8,128)(2,1)} %copy-done.17), calls=%async_computation.3 | async-start | bytes 524288 | tf_op jit(solution)/shard_map/all_to_all | solution.py:44
  146.0 4.1 %copy-start.26 = (bf16[16,128]{1,0:T(8,128)(2,1)S(1)}, bf16[16,128]{1,0:T(8,128)(2,1)}, u32[]{:S(2)}) copy-start(bf16[16,128]{1,0:T(8,128)(2,1)} %value_up.1) | copy-start | bytes 12292
  147.5 2.6 copy-start.7
  147.5 2.9 %copy-start.2 = (bf16[4096,128]{1,0:T(8,128)(2,1)S(1)}, bf16[4096,128]{1,0:T(8,128)(2,1)}, u32[]{:S(2)}) copy-start(bf16[4096,128]{1,0:T(8,128)(2,1)} %value_weight.1) | copy-start | bytes 3145732
  150.1 7.2 %copy-start.32 = (f32[8,128]{1,0:T(8,128)S(1)}, f32[8,128]{1,0:T(8,128)}, u32[]{:S(2)}) copy-start(f32[8,128]{1,0:T(8,128)} %copy-done.31) | copy-start | bytes 12292
  157.3 1.0 copy-start.4
  158.4 1.0 copy-start.10
  159.3 1.0 copy-start.11
  160.3 0.9 copy-start.12
  161.2 1.0 copy-start.14
  165.2 11.4 %all-to-all-start.4 = ((f32[8,4,640]{2,1,0:T(4,128)}), f32[8,4,640]{2,1,0:T(4,128)}, u32[]{:S(2)}, u32[]{:S(2)}) async-start(f32[8,4,640]{2,1,0:T(4,128)} %copy-done.18), calls=%async_computation.4 | async-start | bytes 163840 | tf_op jit(solution)/shard_map/all_to_all | solution.py:44
  169.2 78.0 %reduce-scatter.2.cloned.1.call-start = ((), (), s32[]{:S(2)}) async-start(), calls=%async_computation.11 | async-start | bytes 2801664 | tf_op jit(solution)/shard_map/reduce_scatter | solution.py:445
  176.6 0.9 copy-start.8
  177.5 0.9 copy-start.15
  178.4 0.9 copy-start.16
  185.6 4.4 %copy-start.3 = (bf16[4096,128]{1,0:T(8,128)(2,1)S(1)}, bf16[4096,128]{1,0:T(8,128)(2,1)}, u32[]{:S(2)}) copy-start(bf16[4096,128]{1,0:T(8,128)(2,1)} %value_weight.1) | copy-start | bytes 3145732
  185.6 4.4 %copy-start.6 = (bf16[4096,32]{0,1:T(8,128)(2,1)S(1)}, bf16[4096,32]{0,1:T(8,128)(2,1)}, u32[]{:S(2)}) copy-start(bf16[4096,32]{0,1:T(8,128)(2,1)} %copy-done.5) | copy-start | bytes 786436
  185.6 4.4 %copy-start.34 = (s32[2,1]{1,0:T(2,128)S(1)}, s32[2,1]{1,0:T(2,128)}, u32[]{:S(2)}) copy-start(s32[2,1]{1,0:T(2,128)} %copy.136.lengths) | copy-start | bytes 28
  185.6 4.4 %copy-start.20 = (bf16[304,128]{1,0:T(8,128)(2,1)S(1)}, bf16[304,128]{1,0:T(8,128)(2,1)}, u32[]{:S(2)}) copy-start(bf16[304,128]{1,0:T(8,128)(2,1)} %copy-done.19) | copy-start | bytes 233476
  185.6 4.4 %copy-start.22 = (bf16[304,128]{1,0:T(8,128)(2,1)S(1)}, bf16[304,128]{1,0:T(8,128)(2,1)}, u32[]{:S(2)}) copy-start(bf16[304,128]{1,0:T(8,128)(2,1)} %copy-done.21) | copy-start | bytes 233476
  185.6 4.4 %copy-start.24 = (bf16[304,32]{1,0:T(8,128)(2,1)S(1)}, bf16[304,32]{1,0:T(8,128)(2,1)}, u32[]{:S(2)}) copy-start(bf16[304,32]{1,0:T(8,128)(2,1)} %copy-done.23) | copy-start | bytes 58372
  195.4 27.4 %copy-start.36 = (f32[4,128]{1,0:T(4,128)S(1)}, f32[4,128]{1,0:T(4,128)}, u32[]{:S(2)}) copy-start(f32[4,128]{1,0:T(4,128)} %copy-done.35) | copy-start | bytes 6148
  195.4 49.8 %copy-start.30 = (bf16[8,512]{1,0:T(8,128)(2,1)S(1)}, bf16[8,512]{1,0:T(8,128)(2,1)}, u32[]{:S(2)}) copy-start(bf16[8,512]{1,0:T(8,128)(2,1)} %copy-done.29) | copy-start | bytes 24580
  195.4 49.8 %copy-start.39 = (bf16[8,8,8,512]{3,2,1,0:T(8,128)(2,1)S(1)}, bf16[8,8,8,512]{3,2,1,0:T(8,128)(2,1)}, u32[]{:S(2)}) copy-start(bf16[8,8,8,512]{3,2,1,0:T(8,128)(2,1)} %copy-done.38) | copy-start | bytes 1572868
  195.5 27.2 %all-to-all-start.5 = ((bf16[64,4,640]{2,1,0:T(4,128)(2,1)}), bf16[64,4,640]{2,1,0:T(4,128)(2,1)S(1)}, u32[]{:S(2)}, u32[]{:S(2)}) async-start(bf16[64,4,640]{2,1,0:T(4,128)(2,1)} %bitcast.24), calls=%async_computation.5 | async-start | bytes 655360 | tf_op jit(solution)/shard_map/all_to_all | solution.py:44
  223.5 15.0 %all-to-all-start.6 = ((f32[8,4,768]{2,1,0:T(4,128)}), f32[8,4,768]{2,1,0:T(4,128)S(1)}, u32[]{:S(2)}, u32[]{:S(2)}) async-start(f32[8,4,768]{2,1,0:T(4,128)} %broadcast_in_dim.96), calls=%async_computation.6 | async-start | bytes 196608 | tf_op jit(solution)/shard_map/all_to_all | solution.py:40
  228.8 17.2 %collective-permute-start.4 = (bf16[8,512]{1,0:T(8,128)(2,1)S(1)}, bf16[8,512]{1,0:T(8,128)(2,1)S(1)}, u32[]{:S(2)}, u32[]{:S(2)}) collective-permute-start(bf16[8,512]{1,0:T(8,128)(2,1)S(1)} %dynamic-slice_bitcast_fusion), channel_id=1, source_target_pairs={{0,0},{1,64},{2,128},{3,192},{4,256},{5,320},{6,384},{7,448},{64,1... | collective-permute-start | bytes 24584 | tf_op jit(solution)/shard_map/ppermute | solution.py:377
  239.3 20.7 %all-to-all-start.7 = ((bf16[64,4,640]{2,1,0:T(4,128)(2,1)}), bf16[64,4,640]{2,1,0:T(4,128)(2,1)S(1)}, u32[]{:S(2)}, u32[]{:S(2)}) async-start(bf16[64,4,640]{2,1,0:T(4,128)(2,1)} %broadcast_in_dim.97), calls=%async_computation.7 | async-start | bytes 655360 | tf_op jit(solution)/shard_map/all_to_all | solution.py:40
  (15 other events, 9.8 us)
Sparse Core Ops, SparseCore 0:
  10.1 73.8 all-gather.2
  106.9 62.3 all-gather.4
  195.6 44.4 reduce-scatter.1

commit v5 on v4

--- a/solution.py
+++ b/solution.py
@@ -48,7 +48,7 @@
     return pl.pallas_call(
         kernel,
         out_shape=out_shape,
-        compiler_params=pltpu.CompilerParams(vmem_limit_bytes=32 * 1024 * 1024),
+        compiler_params=pltpu.CompilerParams(vmem_limit_bytes=56 * 1024 * 1024),
         cost_estimate=pl.CostEstimate(flops=flops, bytes_accessed=2**20, transcendentals=4096),
         **layout,
     )
@@ -88,7 +88,7 @@
             chunks[z * plane_count + plane, :, LANES:] = tokens[z]
 
 
-def gradient_kernel(z_count, subs, place, received, queries, loss, *rest):
+def gradient_kernel(z_count, subs, received, queries, loss, *rest):
     pieces, (item_out, parts_out) = rest[:-2], rest[-2:]
     item_rows = item_out.shape[0]
     count = len(pieces)
@@ -113,10 +113,11 @@
     planes = senders // z_count
     row = lax.broadcasted_iota(jnp.int32, (picks, received.shape[0]), 0)
     column = lax.broadcasted_iota(jnp.int32, (picks, received.shape[0]), 1)
-    first = ((row // subs) * planes + place[1:2, 0:1]) * per_z + row % subs
+    plane = lax.axis_index(PLANE)
+    first = ((row // subs) * planes + plane) * per_z + row % subs
     attn = query = None
     for turn, piece in enumerate(pieces):
-        block = lax.rem(place[0:1, 0:1] + (count - turn), count)
+        block = lax.rem(lax.axis_index("x") + (count - turn), count)
         cot = jnp.zeros((picks, width), jnp.float32)
         for choice in range(count):
             cot = cot + jnp.where(
@@ -140,7 +141,6 @@
 
 
 def attention_kernel(
-    place,
     lengths,
     parts,
     keys,
@@ -149,7 +149,6 @@
     value_up,
     reduced,
     tokens,
-    query_delta_out,
     key_change_out,
     value_change_out,
     coef_out,
@@ -197,12 +196,6 @@
     )
     score_grad = score_grad.astype(jnp.bfloat16)
     delta = jnp.dot(score_grad, keys[...], preferred_element_type=jnp.float32)
-    for sub in range(subs):
-        for head in range(group):
-            row = sub * group + head
-            query_delta_out[sub : sub + 1, head * HEAD_DIM : (head + 1) * HEAD_DIM] = delta[
-                row : row + 1
-            ]
     score_grad = score_grad.astype(jnp.float32)
     key_change = first_product(score_grad, q_heads).astype(jnp.bfloat16)
     value_change = first_product(prob_half, grad_heads).astype(jnp.bfloat16)
@@ -223,29 +216,102 @@
     downs = ADAPTER_SCALE * first_product(coef, tokens[...])
     z_count, mp_count, rows, chunk_width = shares_out.shape
     width = downs.shape[1] // mp_count
+    up_end = width + ups.shape[1]
+    deltas = jnp.concatenate(
+        [
+            jnp.concatenate(
+                [delta[at : at + 1], delta[at + 1 : at + 2]], axis=1
+            )
+            for at in range(0, subs * group, 2)
+        ],
+        axis=0,
+    )
     for other in range(mp_count):
-        kept = jnp.where(place[2:3, 0:1] == other, ups, 0.0)
+        mine = lax.axis_index("mp") == other
+        kept_ups = jnp.where(mine, ups, 0.0)
+        kept_deltas = jnp.where(mine, deltas, 0.0).astype(jnp.bfloat16)
         for z in range(z_count):
-            mine = slice(z * rows, (z + 1) * rows)
+            ranks = slice(z * rows, (z + 1) * rows)
             shares_out[z, other, :, :width] = downs[
-                mine, other * width : (other + 1) * width
+                ranks, other * width : (other + 1) * width
             ].astype(jnp.bfloat16)
-            shares_out[z, other, :, width:] = kept[mine].astype(jnp.bfloat16)
-
-
-def portion_kernel(
-    seq_len, lengths, key_change, value_change, coef, last, key_weight, value_weight, down, out
-):
+            shares_out[z, other, :, width:up_end] = kept_ups[ranks].astype(jnp.bfloat16)
+            shares_out[z, other, :, up_end:] = kept_deltas
+
+
+def home_kernel(subs, received, loss, *rest):
+    pieces, (sums_out, last_out) = rest[:-2], rest[-2:]
+    z_count, mp_count, rows, _ = received.shape
+    copies, _, sum_width = sums_out.shape
+    sum_width = sum_width - loss.shape[1]
+    total = None
+    deltas = []
+    for z in range(z_count):
+        column = None
+        for other in range(mp_count):
+            part = received[z, other].astype(jnp.float32)
+            column = part if column is None else column + part
+        delta = column[:, sum_width:]
+        deltas = deltas + [
+            jnp.concatenate([delta[at : at + 1], delta[at + 1 : at + 2]], axis=1)
+            for at in range(0, rows, 2)
+        ]
+        column = column[:, :sum_width]
+        total = column if total is None else total + column
+    for copy in range(copies):
+        sums_out[copy, :, :sum_width] = total
+        sums_out[copy, :, sum_width:] = loss[:rows]
+    deltas = jnp.concatenate(deltas, axis=0).astype(jnp.bfloat16)
+    count = len(pieces)
+    lasts = []
+    for piece in pieces:
+        wq_rows = jnp.concatenate([piece[half, 0] for half in range(piece.shape[0])], axis=0)
+        lasts.append(final_product(deltas, wq_rows))
+    for choice in range(count):
+        turn = lax.rem(lax.axis_index("x") + (count - choice), count)
+        block = jnp.zeros(lasts[0].shape, jnp.float32)
+        for candidate in range(count):
+            block = block + jnp.where(turn == candidate, lasts[candidate], 0.0)
+        width = block.shape[1]
+        for z in range(z_count):
+            last_out[z, :, choice * width : (choice + 1) * width] = block[
+                z * subs : (z + 1) * subs
+            ]
+
+
+def return_kernel(sums, last, chunks_out, loss_out):
+    z_count, mp_count, rows, chunk_width = chunks_out.shape
+    total = sums[0]
+    for part in range(1, sums.shape[0]):
+        total = total + sums[part]
+    sum_width = total.shape[1] - loss_out.shape[1]
+    loss_out[...] = total[:, sum_width:]
+    total = total[:, :sum_width].astype(jnp.bfloat16)
+    half = chunk_width - sum_width
+    for z in range(z_count):
+        value = last[z]
+        value = jnp.concatenate(
+            [
+                value[sub : sub + 1, side * half : (side + 1) * half]
+                for sub in range(value.shape[0])
+                for side in range(value.shape[1] // half)
+            ],
+            axis=0,
+        )
+        for other in range(mp_count):
+            chunks_out[z, other, :, :sum_width] = total
+            chunks_out[z, other, :, sum_width:] = jnp.where(
+                lax.axis_index("z") == other, value, 0.0
+            ).astype(jnp.bfloat16)
+
+
+def portion_kernel(key_change, value_change, coef, key_weight, value_weight, down, out):
     total = final_product(key_change[...], key_weight[...]) + final_product(
         value_change[...], value_weight[...]
     )
     total = total + ADAPTER_SCALE * jnp.dot(
         coef[...], down[...], preferred_element_type=jnp.float32
     )
-    row = lax.broadcasted_iota(jnp.int32, total.shape, 0)
-    for sub in range(last.shape[0]):
-        chosen = row == sub * seq_len + lengths[sub, 0] - 1
-        total = total + jnp.where(chosen, last[sub : sub + 1], 0.0)
     out[...] = total.astype(jnp.bfloat16)
 
 
@@ -274,11 +340,6 @@
     local_rows = query_emb.shape[0]
     batch_size = local_rows * dp_count
     feature_width = query_emb.shape[1]
-    place = jnp.broadcast_to(
-        jnp.stack([lax.axis_index("x"), lax.axis_index(PLANE), lax.axis_index("mp")])[:, None],
-        (3, LANES),
-    ).astype(jnp.int32)
-
     sub_count = hidden_in.shape[0]
     seq_len = hidden_in.shape[2]
     token_count = sub_count * seq_len
@@ -306,6 +367,7 @@
 
     rows_here, query_width = w_query.shape
     both = jnp.stack([w_query, w_out.T])
+    both, partial_scores = lax.optimization_barrier((both, partial_scores))
     other = lax.ppermute(both, "h", [(0, 1), (1, 0)])
     lower = lax.axis_index("h") == 0
     both = jnp.stack([jnp.where(lower, both, other), jnp.where(lower, other, both)])
@@ -313,11 +375,6 @@
         lax.ppermute(both, "x", [(a, (a + turn) % x_count) for a in range(x_count)])
         for turn in range(1, x_count)
     ]
-    wq_plane = jnp.stack([piece[:, 0] for piece in pieces])
-    wq_plane, partial_scores = lax.optimization_barrier((wq_plane, partial_scores))
-    wq_full = lax.all_gather(
-        wq_plane.reshape(plane_count * rows_here, query_width), "z", axis=0, tiled=True
-    )
 
     last_tokens = jnp.concatenate(
         [
@@ -366,7 +423,7 @@
             jax.ShapeDtypeStruct((z_count, 2 * sub_count, query_width + LANES), f32),
         ),
         2**26,
-    )(place, column_rows, queries_all, loss_part, *pieces)
+    )(column_rows, queries_all, loss_part, *pieces)
     parts = swap(parts, "z")
     own_grads = lax.dynamic_index_in_dim(
         column_grads.reshape(z_count, local_rows, feature_width),
@@ -383,84 +440,78 @@
 
     share_rows = 2 * adapter_rank // z_count
     up_width = key_rows.shape[1]
-    query_delta, key_change, value_change, coef, loss_part, shares = call(
+    sum_width = feature_width + up_width
+    chunk_width = sum_width + sub_count * query_width // share_rows
+    key_change, value_change, coef, loss_part, shares = call(
         attention_kernel,
         (
-            jax.ShapeDtypeStruct((sub_count, query_width), f32),
             jax.ShapeDtypeStruct(key_rows.shape, bf16),
             jax.ShapeDtypeStruct(value_rows.shape, bf16),
             jax.ShapeDtypeStruct((token_count, 2 * adapter_rank), bf16),
             jax.ShapeDtypeStruct((2 * sub_count, LANES), f32),
-            jax.ShapeDtypeStruct((z_count, mp_count, share_rows, feature_width + up_width), bf16),
+            jax.ShapeDtypeStruct((z_count, mp_count, share_rows, chunk_width), bf16),
         ),
         2**26,
-    )(
-        place,
-        lengths,
-        parts,
-        key_rows,
-        value_rows,
-        key_up_matrix,
-        value_up_matrix,
-        reduced_pair,
-        token_inputs,
-    )
-    shares = swap(shares.reshape((-1,) + shares.shape[2:]), ("z", "mp"))
-
-    last_part = final_product(query_delta.astype(bf16), wq_full)
-    last_part = last_part.reshape(sub_count, z_count, x_count, -1)
-    last_part = jnp.roll(last_part[:, :, (0,) + tuple(range(x_count - 1, 0, -1))], lax.axis_index("x"), axis=2)
-    last_part = last_part.reshape(sub_count, model_width)
+    )(lengths, parts, key_rows, value_rows, key_up_matrix, value_up_matrix, reduced_pair, token_inputs)
+    grid_shape = shares.shape
+    shares = swap(shares.reshape((-1,) + grid_shape[2:]), ("z", "mp")).reshape(grid_shape)
+
     block = model_width // mp_count
     whole = lambda array: pl.BlockSpec(array.shape, lambda step: (0, 0))
     along = lambda array: pl.BlockSpec((array.shape[0], block), lambda step: (0, step))
     down = lambda array: pl.BlockSpec((block, array.shape[1]), lambda step: (step, 0))
     down_rows = down_both.T
     portion = call(
-        functools.partial(portion_kernel, seq_len),
+        portion_kernel,
         jax.ShapeDtypeStruct((token_count, model_width), bf16),
         2**29,
         grid=(mp_count,),
         in_specs=[
-            whole(lengths),
             whole(key_change),
             whole(value_change),
             whole(coef),
-            along(last_part),
             down(key_weight_matrix),
             down(value_weight_matrix),
             along(down_rows),
         ],
         out_specs=pl.BlockSpec((token_count, block), lambda step: (0, step)),
-    )(
-        lengths,
-        key_change,
-        value_change,
-        coef,
-        last_part,
-        key_weight_matrix,
-        value_weight_matrix,
-        down_rows,
-    )
+    )(key_change, value_change, coef, key_weight_matrix, value_weight_matrix, down_rows)
     input_sum = lax.psum_scatter(portion, "mp", scatter_dimension=1, tiled=True).astype(f32)
+    sums, last_part = call(
+        functools.partial(home_kernel, sub_count),
+        (
+            jax.ShapeDtypeStruct((plane_count, share_rows, sum_width + LANES), f32),
+            jax.ShapeDtypeStruct((z_count, sub_count, feature_width), f32),
+        ),
+        2**24,
+    )(shares, loss_part, *pieces)
+    chunks, loss_sum = call(
+        return_kernel,
+        (
+            jax.ShapeDtypeStruct(grid_shape, bf16),
+            jax.ShapeDtypeStruct((share_rows, LANES), f32),
+        ),
+        2**24,
+    )(swap(sums, PLANE), last_part)
+    mean_loss = loss_sum[0, 0] / batch_size
+    summed = swap(chunks.reshape((-1,) + grid_shape[2:]), ("z", "mp")).reshape(grid_shape)
+    own = lax.axis_index("mp")
+    up_grad = lax.dynamic_index_in_dim(
+        summed[:, :, :, feature_width:sum_width], own, 1, keepdims=False
+    )
+    up_grad = up_grad.reshape(2 * adapter_rank, up_width).astype(f32)
+    last_rows_grad = jnp.sum(
+        lax.dynamic_index_in_dim(
+            summed[:, :, :, sum_width:], own, 0, keepdims=False
+        ).astype(f32),
+        axis=0,
+    ).reshape(sub_count, feature_width) + item_grad[:sub_count].astype(f32)
     row_ids = jnp.arange(token_count, dtype=jnp.int32)[:, None]
     for sub in range(sub_count):
         input_sum = input_sum + jnp.where(
-            row_ids == last_rows[sub], item_grad[sub][None, :].astype(f32), 0.0
+            row_ids == last_rows[sub], last_rows_grad[sub][None, :], 0.0
         )
     input_grad = input_sum.astype(bf16).reshape(hidden_in.shape)
-
-    share_sum = jnp.sum(shares.astype(f32), axis=0)
-    share_sum = jnp.concatenate([share_sum, loss_part[:share_rows]], axis=1)
-    share_sum = jnp.sum(spread(share_sum, PLANE), axis=0)
-    mean_loss = share_sum[0, feature_width + up_width] / batch_size
-    summed = spread(share_sum[:, : feature_width + up_width].astype(bf16), ("z", "mp"))
-    summed, input_grad = lax.optimization_barrier((summed, input_grad))
-    summed = summed.reshape(z_count, mp_count, share_rows, feature_width + up_width)
-    up_grad = lax.dynamic_index_in_dim(
-        summed[:, :, :, feature_width:], lax.axis_index("mp"), 1, keepdims=False
-    )
-    up_grad = up_grad.reshape(2 * adapter_rank, up_width).astype(f32)
     down_grad = (
         summed[:, :, :, :feature_width]
         .transpose(0, 2, 1, 3)

time: 273 us -> 257 us (0.941)
  blocking collectives: 14.3 us -> 61.2 us
  waiting for transfers between devices: 97.6 us -> 69 us
  local copies, waits for them, and re-layouts: 38.2 us -> 16.7 us
  starting transfers between devices: 71.1 us -> 56.1 us
  Pallas kernels: 11.6 us -> 20.6 us
  matrix products: 12.1 us -> 8.73 us
  other arithmetic: 6.29 us -> 3.4 us
    all_to_all x0 -> x2, blocking collectives: none -> 46.8 us  [swap(): return lax.all_to_all(blocks, axes, split_axis=0, concat_axis=0, tiled=True)]
    ppermute x1, waiting for transfers between devices: 39.9 us -> 0.01 us  [local(): other = lax.ppermute(both, 'h', [(0, 1), (1, 0)])]
    all_to_all x4, waiting for transfers between devices: 27.6 us -> 64.4 us  [swap(): return lax.all_to_all(blocks, axes, split_axis=0, concat_axis=0, tiled=True)]
    all_to_all x3 -> x1, waiting for transfers between devices: 22 us -> 0.01 us  [spread(): return lax.all_to_all(copies, axes, split_axis=0, concat_axis=0, tiled=True)]
    unnamed x101 -> x43, local copies, waits for them, and re-layouts: 21.1 us -> 3.95 us
    all_to_all x3 -> x1, starting transfers between devices: 16.9 us -> 7.03 us  [spread(): return lax.all_to_all(copies, axes, split_axis=0, concat_axis=0, tiled=True)]
    ppermute x3, waiting for transfers between devices: 7.29 us -> 0.01 us  [local(): lax.ppermute(both, 'x', [(a, (a + turn) % x_count) for a in range(x_count)])]
    pallas_call x2 -> x4, Pallas kernels: 8.56 us -> 15.7 us  [the longest x1 7.59 us: local(): call(portion_kernel, jax.ShapeDtypeStruct((token_count, model_width), bf1...]
  transfers between devices with their start and end apart: 15 -> 12, of which waited for: 8 -> 5; matrix products, arithmetic and copies ran while one was open for 11% -> 10% of each run, Pallas kernels for 2% -> 2%
where the time goes in v5:
time: 257 us; the launch traced here: 256 us
  waiting for transfers between devices  69 us (27%)
  blocking collectives  61.2 us (24%)
  starting transfers between devices  56.1 us (22%)
  Pallas kernels  20.6 us (8%)
  between operations  20.2 us (8%)
  local copies, waits for them, and re-layouts  16.7 us (6%)
  matrix products  8.73 us (3%)
  other arithmetic  3.4 us (1%)
    all_to_all x4, waiting for transfers between devices, swap(): return lax.all_to_all(blocks, axes, split_axis=0, concat_axis=0, tiled=True)  64.4 us
    all_to_all x2, blocking collectives, swap(): return lax.all_to_all(blocks, axes, split_axis=0, concat_axis=0, tiled=True)  46.8 us
    all_to_all x4, starting transfers between devices, swap(): return lax.all_to_all(blocks, axes, split_axis=0, concat_axis=0, tiled=True)  35.6 us
    all_to_all x1, blocking collectives, spread(): return lax.all_to_all(copies, axes, split_axis=0, concat_axis=0, tiled=True)  14.3 us
    ppermute x3, starting transfers between devices, local(): lax.ppermute(both, 'x', [(a, (a + turn) % x_count) for a in range(x_count)])  7.91 us
    pallas_call x1, Pallas kernels, local(): call(portion_kernel, jax.ShapeDtypeStruct((token_count, model_width), bf1...  7.59 us
    all_to_all x1, starting transfers between devices, spread(): return lax.all_to_all(copies, axes, split_axis=0, concat_axis=0, tiled=True)  7.03 us
  transfers between devices with their start and end apart: 12, of which 5 were waited for; matrix products, arithmetic and copies ran while one was open for 10% of the time, Pallas kernels for 2%

profile of v5, /device:TPU:1, one launch (start us, length us, event | category | flops | bytes accessed | tf_op | source)
XLA Modules:
  0.0 255.8 jit_solution(6514703289287599702)
XLA Ops:
  7.3 0.7 all-gather.2.cloned.1.call-update
  7.9 0.7 broadcast_in_dim.64
  8.6 14.3 %all_to_all.40 = bf16[8,8,512]{2,1,0:T(8,128)(2,1)S(1)} all-to-all(bf16[8,8,512]{2,1,0:T(8,128)(2,1)S(1)} %broadcast_in_dim.64), channel_id=1, replica_groups=mesh['z'=8,'x'=4,'h'=2,'mp'=8] {'mp'}, dimensions={0} | all-to-all | bytes 131072 | tf_op jit(solution)/shard_map/all_to_all | solution.py:40
  23.0 0.7 broadcast_in_dim.63
  23.7 1.1 broadcast_in_dim.65
  24.8 13.4 %all-to-all-start.1 = ((bf16[64,16,512]{2,1,0:T(8,128)(2,1)}), bf16[64,16,512]{2,1,0:T(8,128)(2,1)S(1)}, u32[]{:S(2)}, u32[]{:S(2)}) async-start(bf16[64,16,512]{2,1,0:T(8,128)(2,1)} %bitcast), calls=%async_computation.1 | async-start | bytes 2097152 | tf_op jit(solution)/shard_map/all_to_all | solution.py:44
  38.4 43.3 %all-to-all-done.1 = bf16[64,16,512]{2,1,0:T(8,128)(2,1)S(1)} async-done(((bf16[64,16,512]{2,1,0:T(8,128)(2,1)}), bf16[64,16,512]{2,1,0:T(8,128)(2,1)S(1)}, u32[]{:S(2)}, u32[]{:S(2)}) %all-to-all-start.1) | async-done | bytes 1048608 | tf_op jit(solution)/shard_map/all_to_all | solution.py:44
  81.6 0.9 slice_bitcast_fusion
  82.8 1.9 collective-permute-start
  87.9 0.7 copy.50.pair
  88.6 0.7 copy.49.hard
  90.6 0.7 broadcast_in_dim.66
  91.2 7.0 %all-to-all-start.2 = ((f32[8,8,512]{2,1,0:T(8,128)}), f32[8,8,512]{2,1,0:T(8,128)}, u32[]{:S(2)}, u32[]{:S(2)}) async-start(f32[8,8,512]{2,1,0:T(8,128)} %broadcast_in_dim.66), calls=%async_computation.2 | async-start | bytes 262144 | tf_op jit(solution)/shard_map/all_to_all | solution.py:40
  98.4 1.9 collective-permute-start.3
  100.3 3.8 %collective-permute-start.2 = (bf16[2,2,64,512]{3,2,1,0:T(8,128)(2,1)S(1)}, bf16[2,2,64,512]{3,2,1,0:T(8,128)(2,1)}, u32[]{:S(2)}, u32[]{:S(2)}) collective-permute-start(bf16[2,2,64,512]{3,2,1,0:T(8,128)(2,1)S(1)} %pad_maximum_fusion.rest_0_), channel_id=1, source_target_pairs={{0,32},{16,48},{32,0},{48,16},{1,33},{17,49},{33,1},{49,17},{2,34}... | collective-permute-start | bytes 786440 | tf_op jit(solution)/shard_map/ppermute | solution.py:375
  104.1 2.2 collective-permute-start.1
  106.3 1.1 constant_dynamic-slice_fusion.1
  107.5 0.6 reshape.90
  108.1 1.3 copy.48
  109.4 3.2 %convolution_convert_fusion = bf16[32,304]{1,0:T(8,128)(2,1)} fusion(bf16[4096,32]{0,1:T(8,128)(2,1)S(1)} %constant_dynamic-update-slice_fusion, bf16[304,4096]{1,0:T(8,128)(2,1)} %bitcast.66), kind=kOutput, calls=%fused_computation.6 | convolution fusion | flops 79701504 | bytes 2771968 | tf_op jit(solution)/shard_map/dot_general | solution.py:394
  112.6 0.9 copy.51
  113.5 2.0 shard_map.197
  115.5 11.5 %all-to-all-start.3 = ((bf16[64,8,256]{2,1,0:T(8,128)(2,1)}), bf16[64,8,256]{2,1,0:T(8,128)(2,1)}, u32[]{:S(2)}, u32[]{:S(2)}) async-start(bf16[64,8,256]{2,1,0:T(8,128)(2,1)} %get-tuple-element.26), calls=%async_computation.3 | async-start | bytes 524288 | tf_op jit(solution)/shard_map/all_to_all | solution.py:44
  127.3 2.7 %fusion.1.values = bf16[304,128]{1,0:T(8,128)(2,1)} fusion(f32[304,128]{1,0:T(8,128)S(1)} %convolution_multiply_fusion, bf16[304,4096]{1,0:T(8,128)(2,1)S(1)} %bitcast.68, bf16[4096,128]{1,0:T(8,128)(2,1)} %value_weight.1), kind=kOutput, calls=%fused_computation.5 | convolution fusion | flops 318844928 | bytes 3772416 | tf_op jit(solution)/shard_map/dot_general | solution.py:402
  130.2 1.5 fusion.keys
  131.6 9.3 %all-to-all-done.3 = bf16[64,8,256]{2,1,0:T(8,128)(2,1)} async-done(((bf16[64,8,256]{2,1,0:T(8,128)(2,1)}), bf16[64,8,256]{2,1,0:T(8,128)(2,1)}, u32[]{:S(2)}, u32[]{:S(2)}) %all-to-all-start.3) | async-done | bytes 262176 | tf_op jit(solution)/shard_map/all_to_all | solution.py:44
  140.9 2.9 %shard_map.198 = (bf16[64,512]{1,0:T(8,128)(2,1)}, f32[8,4,640]{2,1,0:T(4,128)}) custom-call(bf16[512,256]{1,0:T(8,128)(2,1)} %bitcast.12.received, bf16[512,512]{1,0:T(8,128)(2,1)} %get-tuple-element.78.queries, f32[8,128]{1,0:T(8,128)} %get-tuple-element.28.loss, bf16[2,2,64,512]{3,2,1,0:T(8,128)(2,1)} %copy-done.2, ...), custom_call_target="tpu_custom_call" | custom-call | flops 67108864 | bytes 1048576 | tf_op jit(solution)/shard_map/pallas_call | solution.py:419
  143.8 3.4 %all-to-all-start.4 = ((f32[8,4,640]{2,1,0:T(4,128)}), f32[8,4,640]{2,1,0:T(4,128)S(1)}, u32[]{:S(2)}, u32[]{:S(2)}) async-start(f32[8,4,640]{2,1,0:T(4,128)} %get-tuple-element.30), calls=%async_computation.4 | async-start | bytes 163840 | tf_op jit(solution)/shard_map/all_to_all | solution.py:44
  147.2 0.6 copy.52.lengths
  147.9 6.6 %all-to-all-done.4.parts = f32[8,4,640]{2,1,0:T(4,128)S(1)} async-done(((f32[8,4,640]{2,1,0:T(4,128)}), f32[8,4,640]{2,1,0:T(4,128)S(1)}, u32[]{:S(2)}, u32[]{:S(2)}) %all-to-all-start.4) | async-done | bytes 81952 | tf_op jit(solution)/shard_map/all_to_all | solution.py:44
  154.5 0.6 copy-done.6
  155.1 4.1 %shard_map.199 = (bf16[304,128]{1,0:T(8,128)(2,1)}, bf16[304,128]{1,0:T(8,128)(2,1)}, bf16[304,32]{1,0:T(8,128)(2,1)}, f32[4,128]{1,0:T(4,128)}, bf16[8,8,4,896]{3,2,1,0:T(4,128)(2,1)}) custom-call(s32[2,1]{1,0:T(2,128)} %copy.52.lengths, f32[8,4,640]{2,1,0:T(4,128)} %copy-done.6, bf16[304,128]{1,0:T(8,128)(2,1)} %fusion.keys, ...), custom_call_target="tpu_custom_call" | custom-call | flops 67108864 | bytes 1048576 | tf_op jit(solution)/shard_map/pallas_call | solution.py:445
  159.2 7.6 %shard_map.202 = bf16[304,4096]{1,0:T(8,128)(2,1)} custom-call(bf16[304,128]{1,0:T(8,128)(2,1)} %get-tuple-element.40.key_change, bf16[304,128]{1,0:T(8,128)(2,1)} %get-tuple-element.41.value_change, bf16[304,32]{1,0:T(8,128)(2,1)} %get-tuple-element.42.coef, bf16[4096,128]{1,0:T(8,128)(2,1)} %key_weight.1, bf16[4096,128]{1,0:T(8,128)(2,1)} %value_weight.1, ...), custom_call_target="tpu_custom_call" | custom-call | flops 536870912 | bytes 1048576 | tf_op jit(solution)/shard_map/pallas_call | solution.py:464
  166.9 1.0 copy-done.5
  167.9 32.5 %all_to_all.41 = bf16[64,4,896]{2,1,0:T(4,128)(2,1)} all-to-all(bf16[64,4,896]{2,1,0:T(4,128)(2,1)S(1)} %bitcast.84), channel_id=1, replica_groups=mesh['z'=8,'x'=4,'h'=2,'mp'=8] {'z','mp'}, dimensions={0} | all-to-all | bytes 917504 | tf_op jit(solution)/shard_map/all_to_all | solution.py:44
  200.4 2.2 shard_map.200
  202.6 14.3 %all_to_all.42.sums = f32[8,4,768]{2,1,0:T(4,128)} all-to-all(f32[8,4,768]{2,1,0:T(4,128)} %get-tuple-element.35), channel_id=1, replica_groups=mesh['z'=8,'x'=4,'h'=2,'mp'=8] {'x','h'}, dimensions={0} | all-to-all | bytes 196608 | tf_op jit(solution)/shard_map/all_to_all | solution.py:44
  217.0 1.7 shard_map.201
  218.7 7.3 %all-to-all-start.7 = ((bf16[64,4,896]{2,1,0:T(4,128)(2,1)}), bf16[64,4,896]{2,1,0:T(4,128)(2,1)S(1)}, u32[]{:S(2)}, u32[]{:S(2)}) async-start(bf16[64,4,896]{2,1,0:T(4,128)(2,1)} %bitcast.83), calls=%async_computation.8 | async-start | bytes 917504 | tf_op jit(solution)/shard_map/all_to_all | solution.py:44
  226.0 1.3 iota_compare_fusion
  227.3 0.7 dynamic-slice_bitcast_fusion
  228.0 3.5 %collective-permute-start.4 = (bf16[8,512]{1,0:T(8,128)(2,1)S(1)}, bf16[8,512]{1,0:T(8,128)(2,1)S(1)}, u32[]{:S(2)}, u32[]{:S(2)}) collective-permute-start(bf16[8,512]{1,0:T(8,128)(2,1)S(1)} %dynamic-slice_bitcast_fusion), channel_id=1, source_target_pairs={{0,0},{1,64},{2,128},{3,192},{4,256},{5,320},{6,384},{7,448},{64,1... | collective-permute-start | bytes 24584 | tf_op jit(solution)/shard_map/ppermute | solution.py:434
  231.6 0.8 fusion.2
  232.4 3.9 %collective-permute-done.4 = bf16[8,512]{1,0:T(8,128)(2,1)S(1)} collective-permute-done((bf16[8,512]{1,0:T(8,128)(2,1)S(1)}, bf16[8,512]{1,0:T(8,128)(2,1)S(1)}, u32[]{:S(2)}, u32[]{:S(2)}) %collective-permute-start.4) | collective-permute-done | bytes 8224 | tf_op jit(solution)/shard_map/ppermute | solution.py:434
  236.2 1.2 slice.65
  238.1 5.2 %all-to-all-done.7 = bf16[64,4,896]{2,1,0:T(4,128)(2,1)S(1)} async-done(((bf16[64,4,896]{2,1,0:T(4,128)(2,1)}), bf16[64,4,896]{2,1,0:T(4,128)(2,1)S(1)}, u32[]{:S(2)}, u32[]{:S(2)}) %all-to-all-start.7) | async-done | bytes 458784 | tf_op jit(solution)/shard_map/all_to_all | solution.py:44
  244.6 0.8 fusion.6
  245.4 1.9 add_convert_fusion
  (71 shorter events, 3.4 us)
Async XLA Ops:
  7.2 31.1 %copy-start.9 = (bf16[512,64]{0,1:T(8,128)(2,1)S(1)}, bf16[512,64]{0,1:T(8,128)(2,1)}, u32[]{:S(2)}) copy-start(bf16[512,64]{0,1:T(8,128)(2,1)} %param.23) | copy-start | bytes 196612
  7.2 31.1 %copy-start.10 = (bf16[64,512]{1,0:T(8,128)(2,1)S(1)}, bf16[64,512]{1,0:T(8,128)(2,1)}, u32[]{:S(2)}) copy-start(bf16[64,512]{1,0:T(8,128)(2,1)} %param.20) | copy-start | bytes 196612
  7.2 31.1 %copy-start.7 = (bf16[4096,16]{0,1:T(8,128)(2,1)S(1)}, bf16[4096,16]{0,1:T(8,128)(2,1)}, u32[]{:S(2)}) copy-start(bf16[4096,16]{0,1:T(8,128)(2,1)} %param.24) | copy-start | bytes 393220
  7.2 31.1 %copy-start.8 = (bf16[4096,16]{0,1:T(8,128)(2,1)S(1)}, bf16[4096,16]{0,1:T(8,128)(2,1)}, u32[]{:S(2)}) copy-start(bf16[4096,16]{0,1:T(8,128)(2,1)} %param.26) | copy-start | bytes 393220
  7.2 99.1 %all-gather.2.cloned.1.call-start = ((), (), s32[]{:S(2)}) async-start(), calls=%async_computation.9 | async-start | bytes 2801664 | tf_op jit(solution)/shard_map/all_gather | solution.py:346
  24.8 56.8 %all-to-all-start.1 = ((bf16[64,16,512]{2,1,0:T(8,128)(2,1)}), bf16[64,16,512]{2,1,0:T(8,128)(2,1)S(1)}, u32[]{:S(2)}, u32[]{:S(2)}) async-start(bf16[64,16,512]{2,1,0:T(8,128)(2,1)} %bitcast), calls=%async_computation.1 | async-start | bytes 2097152 | tf_op jit(solution)/shard_map/all_to_all | solution.py:44
  38.2 44.4 %copy-start.11 = (bf16[8,512]{1,0:T(8,128)(2,1)S(1)}, bf16[8,512]{1,0:T(8,128)(2,1)}, u32[]{:S(2)}) copy-start(bf16[8,512]{1,0:T(8,128)(2,1)} %param.14) | copy-start | bytes 24580
  38.2 46.5 %copy-start.17 = (s32[2,1]{0,1:T(1,128)S(1)}, s32[2,1]{0,1:T(1,128)}, u32[]{:S(2)}) copy-start(s32[2,1]{0,1:T(1,128)} %param.19) | copy-start | bytes 28
  38.2 49.7 %copy-start.16 = (s32[8]{0:T(128)S(1)}, s32[8]{0:T(128)}, u32[]{:S(2)}) copy-start(s32[8]{0:T(128)} %param.16) | copy-start | bytes 100
  38.2 50.4 %copy-start.15 = (s32[8,4]{0,1:T(4,128)S(1)}, s32[8,4]{0,1:T(4,128)}, u32[]{:S(2)}) copy-start(s32[8,4]{0,1:T(4,128)} %param.17) | copy-start | bytes 388
  38.3 71.1 %copy-start.3 = (bf16[4096,32]{0,1:T(8,128)(2,1)}, bf16[4096,32]{0,1:T(8,128)(2,1)S(1)}, u32[]{:S(2)}) copy-start(bf16[4096,32]{0,1:T(8,128)(2,1)S(1)} %constant_dynamic-update-slice_fusion) | copy-start | bytes 786436
  82.8 15.5 %collective-permute-start = (bf16[2,64,512]{2,1,0:T(8,128)(2,1)S(1)}, bf16[2,64,512]{2,1,0:T(8,128)(2,1)S(1)}, u32[]{:S(2)}, u32[]{:S(2)}) collective-permute-start(bf16[2,64,512]{2,1,0:T(8,128)(2,1)S(1)} %pad_maximum_fusion.2), channel_id=1, source_target_pairs={{0,8},{8,0},{1,9},{9,1},{2,10},{10,2},{3,11},{11,3},{4,12},{12,4},... | collective-permute-start | bytes 393224 | tf_op jit(solution)/shard_map/ppermute | solution.py:371
  91.2 22.2 %all-to-all-start.2 = ((f32[8,8,512]{2,1,0:T(8,128)}), f32[8,8,512]{2,1,0:T(8,128)}, u32[]{:S(2)}, u32[]{:S(2)}) async-start(f32[8,8,512]{2,1,0:T(8,128)} %broadcast_in_dim.66), calls=%async_computation.2 | async-start | bytes 262144 | tf_op jit(solution)/shard_map/all_to_all | solution.py:40
  98.3 31.6 %copy-start.2 = (bf16[2,2,64,512]{3,2,1,0:T(8,128)(2,1)}, bf16[2,2,64,512]{3,2,1,0:T(8,128)(2,1)S(1)}, u32[]{:S(2)}) copy-start(bf16[2,2,64,512]{3,2,1,0:T(8,128)(2,1)S(1)} %pad_maximum_fusion.rest_0_) | copy-start | bytes 786436
  98.4 42.5 %collective-permute-start.3 = (bf16[2,2,64,512]{3,2,1,0:T(8,128)(2,1)S(1)}, bf16[2,2,64,512]{3,2,1,0:T(8,128)(2,1)}, u32[]{:S(2)}, u32[]{:S(2)}) collective-permute-start(bf16[2,2,64,512]{3,2,1,0:T(8,128)(2,1)S(1)} %pad_maximum_fusion.rest_0_), channel_id=1, source_target_pairs={{0,48},{16,0},{32,16},{48,32},{1,49},{17,1},{33,17},{49,33},{2,50}... | collective-permute-start | bytes 786440 | tf_op jit(solution)/shard_map/ppermute | solution.py:375
  100.3 40.6 %collective-permute-start.2 = (bf16[2,2,64,512]{3,2,1,0:T(8,128)(2,1)S(1)}, bf16[2,2,64,512]{3,2,1,0:T(8,128)(2,1)}, u32[]{:S(2)}, u32[]{:S(2)}) collective-permute-start(bf16[2,2,64,512]{3,2,1,0:T(8,128)(2,1)S(1)} %pad_maximum_fusion.rest_0_), channel_id=1, source_target_pairs={{0,32},{16,48},{32,0},{48,16},{1,33},{17,49},{33,1},{49,17},{2,34}... | collective-permute-start | bytes 786440 | tf_op jit(solution)/shard_map/ppermute | solution.py:375
  104.1 36.8 %collective-permute-start.1 = (bf16[2,2,64,512]{3,2,1,0:T(8,128)(2,1)S(1)}, bf16[2,2,64,512]{3,2,1,0:T(8,128)(2,1)}, u32[]{:S(2)}, u32[]{:S(2)}) collective-permute-start(bf16[2,2,64,512]{3,2,1,0:T(8,128)(2,1)S(1)} %pad_maximum_fusion.rest_0_), channel_id=1, source_target_pairs={{0,16},{16,32},{32,48},{48,0},{1,17},{17,33},{33,49},{49,1},{2,18}... | collective-permute-start | bytes 786440 | tf_op jit(solution)/shard_map/ppermute | solution.py:375
  106.3 20.9 %copy-start = (bf16[2,1,152,4096]{3,2,1,0:T(8,128)(2,1)S(1)}, bf16[2,1,152,4096]{3,2,1,0:T(8,128)(2,1)}, u32[]{:S(2)}) copy-start(bf16[2,1,152,4096]{3,2,1,0:T(8,128)(2,1)} %all-gather.2.cloned.1.call-done) | copy-start | bytes 7471108
  108.1 18.9 %copy-start.13 = (bf16[16,128]{1,0:T(8,128)(2,1)S(1)}, bf16[16,128]{1,0:T(8,128)(2,1)}, u32[]{:S(2)}) copy-start(bf16[16,128]{1,0:T(8,128)(2,1)} %value_up.1) | copy-start | bytes 12292
  113.4 16.5 %copy-start.4 = (bf16[32,304]{0,1:T(8,128)(2,1)}, bf16[32,304]{0,1:T(8,128)(2,1)S(1)}, u32[]{:S(2)}) copy-start(bf16[32,304]{0,1:T(8,128)(2,1)S(1)} %copy.51) | copy-start | bytes 58372
  115.5 25.4 %all-to-all-start.3 = ((bf16[64,8,256]{2,1,0:T(8,128)(2,1)}), bf16[64,8,256]{2,1,0:T(8,128)(2,1)}, u32[]{:S(2)}, u32[]{:S(2)}) async-start(bf16[64,8,256]{2,1,0:T(8,128)(2,1)} %get-tuple-element.26), calls=%async_computation.3 | async-start | bytes 524288 | tf_op jit(solution)/shard_map/all_to_all | solution.py:44
  127.0 3.0 %copy-start.12 = (bf16[16,128]{1,0:T(8,128)(2,1)S(1)}, bf16[16,128]{1,0:T(8,128)(2,1)}, u32[]{:S(2)}) copy-start(bf16[16,128]{1,0:T(8,128)(2,1)} %key_up.1) | copy-start | bytes 12292
  127.0 3.2 %copy-start.1 = (bf16[4096,128]{1,0:T(8,128)(2,1)S(1)}, bf16[4096,128]{1,0:T(8,128)(2,1)}, u32[]{:S(2)}) copy-start(bf16[4096,128]{1,0:T(8,128)(2,1)} %key_weight.1) | copy-start | bytes 3145732
  130.2 17.0 %copy-start.18 = (s32[2,1]{0,1:T(1,128)S(1)}, s32[2,1]{0,1:T(1,128)}, u32[]{:S(2)}) copy-start(s32[2,1]{0,1:T(1,128)} %param.19) | copy-start | bytes 28
  143.8 10.7 %all-to-all-start.4 = ((f32[8,4,640]{2,1,0:T(4,128)}), f32[8,4,640]{2,1,0:T(4,128)S(1)}, u32[]{:S(2)}, u32[]{:S(2)}) async-start(f32[8,4,640]{2,1,0:T(4,128)} %get-tuple-element.30), calls=%async_computation.4 | async-start | bytes 163840 | tf_op jit(solution)/shard_map/all_to_all | solution.py:44
  147.1 98.2 %reduce-scatter.2.cloned.1.call-start = ((), (), s32[]{:S(2)}) async-start(), calls=%async_computation.10 | async-start | bytes 2801664 | tf_op jit(solution)/shard_map/reduce_scatter | solution.py:479
  154.5 0.6 copy-start.6
  166.8 1.0 copy-start.5
  166.8 64.7 %copy-start.14 = (bf16[8,512]{1,0:T(8,128)(2,1)S(1)}, bf16[8,512]{1,0:T(8,128)(2,1)}, u32[]{:S(2)}) copy-start(bf16[8,512]{1,0:T(8,128)(2,1)} %get-tuple-element.38) | copy-start | bytes 24580
  218.7 24.6 %all-to-all-start.7 = ((bf16[64,4,896]{2,1,0:T(4,128)(2,1)}), bf16[64,4,896]{2,1,0:T(4,128)(2,1)S(1)}, u32[]{:S(2)}, u32[]{:S(2)}) async-start(bf16[64,4,896]{2,1,0:T(4,128)(2,1)} %bitcast.83), calls=%async_computation.8 | async-start | bytes 917504 | tf_op jit(solution)/shard_map/all_to_all | solution.py:44
  228.0 8.2 %collective-permute-start.4 = (bf16[8,512]{1,0:T(8,128)(2,1)S(1)}, bf16[8,512]{1,0:T(8,128)(2,1)S(1)}, u32[]{:S(2)}, u32[]{:S(2)}) collective-permute-start(bf16[8,512]{1,0:T(8,128)(2,1)S(1)} %dynamic-slice_bitcast_fusion), channel_id=1, source_target_pairs={{0,0},{1,64},{2,128},{3,192},{4,256},{5,320},{6,384},{7,448},{64,1... | collective-permute-start | bytes 24584 | tf_op jit(solution)/shard_map/ppermute | solution.py:434
Sparse Core Ops, SparseCore 0:
  10.1 67.4 all-gather.1
  167.0 49.1 reduce-scatter.1

commit v6 on v5

--- a/solution.py
+++ b/solution.py
@@ -52,6 +52,13 @@
         cost_estimate=pl.CostEstimate(flops=flops, bytes_accessed=2**20, transcendentals=4096),
         **layout,
     )
+
+
+def upright(line):
+    count = line.shape[1]
+    row = lax.broadcasted_iota(jnp.int32, (count, count), 0)
+    column = lax.broadcasted_iota(jnp.int32, (count, count), 1)
+    return jnp.sum(jnp.where(row == column, line, 0), axis=1, keepdims=True)
 
 
 def residual_kernel(
@@ -67,12 +74,12 @@
     outer = column // rows
     item = ((outer % z_count) * plane_count + outer // z_count) * rows + inner
     count = jnp.zeros((rows, batch_size), jnp.float32)
-    for choice in range(hard.shape[1]):
-        count = count + jnp.where(hard[:, choice : choice + 1] == item, 1.0, 0.0)
+    for choice in range(hard.shape[0]):
+        count = count + jnp.where(upright(hard[choice : choice + 1]) == item, 1.0, 0.0)
     logits = pair_scores * INV_TEMP + HARD_NEGATIVE_ADD * count
     top = jnp.max(logits, axis=1, keepdims=True)
     log_total = top + jnp.log(jnp.sum(jnp.exp(logits - top), axis=1, keepdims=True))
-    target = jnp.where(pair[...] == item, 1.0, 0.0)
+    target = jnp.where(upright(pair[...]) == item, 1.0, 0.0)
     picked = jnp.sum(target * logits, axis=1, keepdims=True)
     loss = jnp.sum(log_total - picked, axis=0, keepdims=True)
     loss_out[...] = jnp.broadcast_to(loss, loss_out.shape)
@@ -149,9 +156,10 @@
     value_up,
     reduced,
     tokens,
-    key_change_out,
-    value_change_out,
-    coef_out,
+    key_weight,
+    value_weight,
+    down,
+    portion_out,
     loss_out,
     shares_out,
 ):
@@ -184,7 +192,7 @@
     live = jnp.zeros(raw.shape, jnp.bool_)
     for sub in range(subs):
         first = sub * seq_len
-        inside = (token >= first) & (token < first + lengths[sub, 0])
+        inside = (token >= first) & (token < first + lengths[0, sub])
         live = live | (inside & (row_sub == sub))
     raw = jnp.where(live, raw, -jnp.inf)
     weights = jnp.exp(raw - jnp.max(raw, axis=1, keepdims=True))
@@ -199,12 +207,9 @@
     score_grad = score_grad.astype(jnp.float32)
     key_change = first_product(score_grad, q_heads).astype(jnp.bfloat16)
     value_change = first_product(prob_half, grad_heads).astype(jnp.bfloat16)
-    key_change_out[...] = key_change
-    value_change_out[...] = value_change
     key_coef = final_product(key_change, key_up[...])
     value_coef = final_product(value_change, value_up[...])
     coef = jnp.concatenate([key_coef, value_coef], axis=1).astype(jnp.bfloat16)
-    coef_out[...] = coef
     rank = key_up.shape[0]
     ups = ADAPTER_SCALE * jnp.concatenate(
         [
@@ -237,6 +242,15 @@
             ].astype(jnp.bfloat16)
             shares_out[z, other, :, width:up_end] = kept_ups[ranks].astype(jnp.bfloat16)
             shares_out[z, other, :, up_end:] = kept_deltas
+    for other in range(mp_count):
+        features = slice(other * width, (other + 1) * width)
+        portion = final_product(key_change, key_weight[features]) + final_product(
+            value_change, value_weight[features]
+        )
+        portion = portion + ADAPTER_SCALE * jnp.dot(
+            coef, down[:, features], preferred_element_type=jnp.float32
+        )
+        portion_out[:, features] = portion.astype(jnp.bfloat16)
 
 
 def home_kernel(subs, received, loss, *rest):
@@ -305,16 +319,6 @@
             ).astype(jnp.bfloat16)
 
 
-def portion_kernel(key_change, value_change, coef, key_weight, value_weight, down, out):
-    total = final_product(key_change[...], key_weight[...]) + final_product(
-        value_change[...], value_weight[...]
-    )
-    total = total + ADAPTER_SCALE * jnp.dot(
-        coef[...], down[...], preferred_element_type=jnp.float32
-    )
-    out[...] = total.astype(jnp.bfloat16)
-
-
 def local(
     query_emb,
     item_emb,
@@ -349,15 +353,28 @@
     seq_lengths = lengths[:, 0]
     last_rows = jnp.arange(sub_count, dtype=jnp.int32) * seq_len + seq_lengths - 1
 
-    query_slices = spread(query_emb, "mp")
+    lower = lax.axis_index("h") == 0
+
+    def pair_up(block):
+        other = lax.ppermute(block, "h", [(0, 1), (1, 0)])
+        return jnp.stack([jnp.where(lower, block, other), jnp.where(lower, other, block)])
+
+    emb_pair = pair_up(jnp.stack([item_emb, query_emb]))
+    pair_rows = 2 * local_rows
+    item_pair = emb_pair[:, 0].reshape(pair_rows, feature_width)
+    query_pair = emb_pair[:, 1].reshape(pair_rows, feature_width)
+    both = pair_up(jnp.stack([w_query, w_out.T]))
+
+    query_slices = spread(query_pair, "mp")
+    both, query_slices = lax.optimization_barrier((both, query_slices))
     chunks = jnp.concatenate(
-        [jnp.broadcast_to(item_emb[None], query_slices.shape), query_slices], axis=1
-    )
-    chunks = jnp.broadcast_to(chunks[:, None], (z_count, plane_count) + chunks.shape[1:])
-    received = swap(chunks.reshape((dp_count,) + chunks.shape[2:]), DP)
-    queries_all = received[:, local_rows:].reshape(batch_size, feature_width)
+        [jnp.broadcast_to(item_pair[None], query_slices.shape), query_slices], axis=1
+    )
+    chunks = jnp.broadcast_to(chunks[:, None], (z_count, x_count) + chunks.shape[1:])
+    received = swap(chunks.reshape((z_count * x_count,) + chunks.shape[2:]), ("z", "x"))
+    queries_all = received[:, pair_rows:].reshape(batch_size, feature_width)
     items_all = (
-        received[:, :local_rows]
+        received[:, :pair_rows]
         .reshape(z_count, plane_count, local_rows, feature_width)
         .transpose(1, 0, 2, 3)
         .reshape(batch_size, feature_width)
@@ -365,12 +382,7 @@
     partial_scores = final_product(query_emb, items_all)
     score_parts = spread(partial_scores, "mp")
 
-    rows_here, query_width = w_query.shape
-    both = jnp.stack([w_query, w_out.T])
-    both, partial_scores = lax.optimization_barrier((both, partial_scores))
-    other = lax.ppermute(both, "h", [(0, 1), (1, 0)])
-    lower = lax.axis_index("h") == 0
-    both = jnp.stack([jnp.where(lower, both, other), jnp.where(lower, other, both)])
+    query_width = w_query.shape[1]
     pieces = [both] + [
         lax.ppermute(both, "x", [(a, (a + turn) % x_count) for a in range(x_count)])
         for turn in range(1, x_count)
@@ -411,7 +423,7 @@
             jax.ShapeDtypeStruct((local_rows, LANES), f32),
         ),
         2**24,
-    )(score_parts, hard_index, pair_index[:, None], last_slices)
+    )(score_parts, hard_index.T, pair_index[None], last_slices)
     column_rows = swap(chunks, DP).reshape(batch_size, 2 * LANES)
     column_rows, key_rows, value_rows = lax.optimization_barrier(
         (column_rows, key_rows, value_rows)
@@ -442,40 +454,30 @@
     up_width = key_rows.shape[1]
     sum_width = feature_width + up_width
     chunk_width = sum_width + sub_count * query_width // share_rows
-    key_change, value_change, coef, loss_part, shares = call(
+    portion, loss_part, shares = call(
         attention_kernel,
         (
-            jax.ShapeDtypeStruct(key_rows.shape, bf16),
-            jax.ShapeDtypeStruct(value_rows.shape, bf16),
-            jax.ShapeDtypeStruct((token_count, 2 * adapter_rank), bf16),
+            jax.ShapeDtypeStruct((token_count, model_width), bf16),
             jax.ShapeDtypeStruct((2 * sub_count, LANES), f32),
             jax.ShapeDtypeStruct((z_count, mp_count, share_rows, chunk_width), bf16),
         ),
         2**26,
-    )(lengths, parts, key_rows, value_rows, key_up_matrix, value_up_matrix, reduced_pair, token_inputs)
+    )(
+        lengths.T,
+        parts,
+        key_rows,
+        value_rows,
+        key_up_matrix,
+        value_up_matrix,
+        reduced_pair,
+        token_inputs,
+        key_weight_matrix,
+        value_weight_matrix,
+        down_both.T,
+    )
     grid_shape = shares.shape
     shares = swap(shares.reshape((-1,) + grid_shape[2:]), ("z", "mp")).reshape(grid_shape)
 
-    block = model_width // mp_count
-    whole = lambda array: pl.BlockSpec(array.shape, lambda step: (0, 0))
-    along = lambda array: pl.BlockSpec((array.shape[0], block), lambda step: (0, step))
-    down = lambda array: pl.BlockSpec((block, array.shape[1]), lambda step: (step, 0))
-    down_rows = down_both.T
-    portion = call(
-        portion_kernel,
-        jax.ShapeDtypeStruct((token_count, model_width), bf16),
-        2**29,
-        grid=(mp_count,),
-        in_specs=[
-            whole(key_change),
-            whole(value_change),
-            whole(coef),
-            down(key_weight_matrix),
-            down(value_weight_matrix),
-            along(down_rows),
-        ],
-        out_specs=pl.BlockSpec((token_count, block), lambda step: (0, step)),
-    )(key_change, value_change, coef, key_weight_matrix, value_weight_matrix, down_rows)
     input_sum = lax.psum_scatter(portion, "mp", scatter_dimension=1, tiled=True).astype(f32)
     sums, last_part = call(
         functools.partial(home_kernel, sub_count),

time: 257 us -> 230 us (0.89)
  waiting for transfers between devices: 69 us -> 37.1 us
  starting transfers between devices: 56.1 us -> 66.2 us
  Pallas kernels: 20.6 us -> 16.4 us
  other arithmetic: 3.4 us -> 6.66 us
  blocking collectives: 61.2 us -> 58 us
  local copies, waits for them, and re-layouts: 16.7 us -> 13.9 us
    all_to_all x4 -> x3, waiting for transfers between devices: 64.4 us -> 25.8 us  [swap(): return lax.all_to_all(blocks, axes, split_axis=0, concat_axis=0, tiled=True)]
    all_to_all x1 -> x0, blocking collectives: 14.3 us -> none  [spread(): return lax.all_to_all(copies, axes, split_axis=0, concat_axis=0, tiled=True)]
    all_to_all x2 -> x3, blocking collectives: 46.8 us -> 58 us  [swap(): return lax.all_to_all(blocks, axes, split_axis=0, concat_axis=0, tiled=True)]
    all_to_all x1 -> x2, starting transfers between devices: 7.03 us -> 16.6 us  [spread(): return lax.all_to_all(copies, axes, split_axis=0, concat_axis=0, tiled=True)]
    all_to_all x4 -> x3, starting transfers between devices: 35.6 us -> 26.5 us  [swap(): return lax.all_to_all(blocks, axes, split_axis=0, concat_axis=0, tiled=True)]
    ppermute x1 -> x2, starting transfers between devices: 1.93 us -> 10.2 us  [pair_up(): other = lax.ppermute(block, 'h', [(0, 1), (1, 0)])]
    all_to_all x1 -> x2, waiting for transfers between devices: 0.01 us -> 6.78 us  [spread(): return lax.all_to_all(copies, axes, split_axis=0, concat_axis=0, tiled=True)]
    pallas_call x2 -> x1, Pallas kernels: 11.7 us -> 7.55 us  [local(): call(attention_kernel, (jax.ShapeDtypeStruct((token_count, model_width),...]
  transfers between devices with their start and end apart: 12 -> 13, of which waited for: 5 -> 5; matrix products, arithmetic and copies ran while one was open for 10% -> 12% of each run, Pallas kernels for 2% -> 3%
where the time goes in v6:
time: 230 us; the launch traced here: 228 us
  starting transfers between devices  66.2 us (29%)
  blocking collectives  58 us (25%)
  waiting for transfers between devices  37.1 us (16%)
  between operations  20.1 us (9%)
  Pallas kernels  16.4 us (7%)
  local copies, waits for them, and re-layouts  13.9 us (6%)
  matrix products  9.67 us (4%)
  other arithmetic  6.66 us (3%)
    all_to_all x3, blocking collectives, swap(): return lax.all_to_all(blocks, axes, split_axis=0, concat_axis=0, tiled=True)  58 us
    all_to_all x3, starting transfers between devices, swap(): return lax.all_to_all(blocks, axes, split_axis=0, concat_axis=0, tiled=True)  26.5 us
    all_to_all x3, waiting for transfers between devices, swap(): return lax.all_to_all(blocks, axes, split_axis=0, concat_axis=0, tiled=True)  25.8 us
    all_to_all x2, starting transfers between devices, spread(): return lax.all_to_all(copies, axes, split_axis=0, concat_axis=0, tiled=True)  16.6 us
    ppermute x2, starting transfers between devices, pair_up(): other = lax.ppermute(block, 'h', [(0, 1), (1, 0)])  10.2 us
    ppermute x3, starting transfers between devices, local(): lax.ppermute(both, 'x', [(a, (a + turn) % x_count) for a in range(x_count)])  9.32 us
    pallas_call x1, Pallas kernels, local(): call(attention_kernel, (jax.ShapeDtypeStruct((token_count, model_width),...  7.55 us
    all_to_all x2, waiting for transfers between devices, spread(): return lax.all_to_all(copies, axes, split_axis=0, concat_axis=0, tiled=True)  6.78 us
  transfers between devices with their start and end apart: 13, of which 5 were waited for; matrix products, arithmetic and copies ran while one was open for 12% of the time, Pallas kernels for 3%

profile of v6, /device:TPU:1, one launch (start us, length us, event | category | flops | bytes accessed | tf_op | source)
XLA Modules:
  0.0 228.1 jit_solution(93328728853697319)
XLA Ops:
  7.2 0.7 all-gather.2.cloned.1.call-update
  7.9 0.7 pad_maximum_fusion.4
  8.6 8.3 %collective-permute-start = (bf16[2,8,512]{2,1,0:T(8,128)(2,1)S(1)}, bf16[2,8,512]{2,1,0:T(8,128)(2,1)S(1)}, u32[]{:S(2)}, u32[]{:S(2)}) collective-permute-start(bf16[2,8,512]{2,1,0:T(8,128)(2,1)S(1)} %pad_maximum_fusion.4), channel_id=1, source_target_pairs={{0,8},{8,0},{1,9},{9,1},{2,10},{10,2},{3,11},{11,3},{4,12},{12,4},... | collective-permute-start | bytes 49160 | tf_op jit(solution)/shard_map/ppermute | solution.py:359
  16.9 0.9 pad_maximum_fusion.2
  17.8 1.9 collective-permute-start.1
  19.7 0.7 select_bitcast_fusion.3
  20.5 0.7 broadcast_in_dim.68
  21.1 9.7 %all-to-all-start = ((bf16[8,16,512]{2,1,0:T(8,128)(2,1)}), bf16[8,16,512]{2,1,0:T(8,128)(2,1)S(1)}, u32[]{:S(2)}, u32[]{:S(2)}) async-start(bf16[8,16,512]{2,1,0:T(8,128)(2,1)} %broadcast_in_dim.68), calls=%async_computation | async-start | bytes 262144 | tf_op jit(solution)/shard_map/all_to_all | solution.py:40
  30.8 0.9 select_bitcast_fusion.1
  31.8 6.8 %all-to-all-done = bf16[8,16,512]{2,1,0:T(8,128)(2,1)S(1)} async-done(((bf16[8,16,512]{2,1,0:T(8,128)(2,1)}), bf16[8,16,512]{2,1,0:T(8,128)(2,1)S(1)}, u32[]{:S(2)}, u32[]{:S(2)}) %all-to-all-start) | async-done | bytes 131104 | tf_op jit(solution)/shard_map/all_to_all | solution.py:40
  38.7 1.1 broadcast_in_dim.69
  39.8 10.1 %all-to-all-start.1 = ((bf16[32,32,512]{2,1,0:T(8,128)(2,1)}), bf16[32,32,512]{2,1,0:T(8,128)(2,1)S(1)}, u32[]{:S(2)}, u32[]{:S(2)}) async-start(bf16[32,32,512]{2,1,0:T(8,128)(2,1)} %bitcast.12), calls=%async_computation.1 | async-start | bytes 2097152 | tf_op jit(solution)/shard_map/all_to_all | solution.py:44
  54.5 4.4 %collective-permute-start.4 = (bf16[2,2,64,512]{3,2,1,0:T(8,128)(2,1)S(1)}, bf16[2,2,64,512]{3,2,1,0:T(8,128)(2,1)}, u32[]{:S(2)}, u32[]{:S(2)}) collective-permute-start(bf16[2,2,64,512]{3,2,1,0:T(8,128)(2,1)S(1)} %pad_maximum_fusion.rest_0_), channel_id=1, source_target_pairs={{0,48},{16,0},{32,16},{48,32},{1,49},{17,1},{33,17},{49,33},{2,50}... | collective-permute-start | bytes 786440 | tf_op jit(solution)/shard_map/ppermute | solution.py:387
  58.8 2.5 %collective-permute-start.3 = (bf16[2,2,64,512]{3,2,1,0:T(8,128)(2,1)S(1)}, bf16[2,2,64,512]{3,2,1,0:T(8,128)(2,1)}, u32[]{:S(2)}, u32[]{:S(2)}) collective-permute-start(bf16[2,2,64,512]{3,2,1,0:T(8,128)(2,1)S(1)} %pad_maximum_fusion.rest_0_), channel_id=1, source_target_pairs={{0,32},{16,48},{32,0},{48,16},{1,33},{17,49},{33,1},{49,17},{2,34}... | collective-permute-start | bytes 786440 | tf_op jit(solution)/shard_map/ppermute | solution.py:387
  61.3 2.5 %collective-permute-start.2 = (bf16[2,2,64,512]{3,2,1,0:T(8,128)(2,1)S(1)}, bf16[2,2,64,512]{3,2,1,0:T(8,128)(2,1)}, u32[]{:S(2)}, u32[]{:S(2)}) collective-permute-start(bf16[2,2,64,512]{3,2,1,0:T(8,128)(2,1)S(1)} %pad_maximum_fusion.rest_0_), channel_id=1, source_target_pairs={{0,16},{16,32},{32,48},{48,0},{1,17},{17,33},{33,49},{49,1},{2,18}... | collective-permute-start | bytes 786440 | tf_op jit(solution)/shard_map/ppermute | solution.py:387
  63.8 12.1 %all-to-all-done.1 = bf16[32,32,512]{2,1,0:T(8,128)(2,1)S(1)} async-done(((bf16[32,32,512]{2,1,0:T(8,128)(2,1)}), bf16[32,32,512]{2,1,0:T(8,128)(2,1)S(1)}, u32[]{:S(2)}, u32[]{:S(2)}) %all-to-all-start.1) | async-done | bytes 1048608 | tf_op jit(solution)/shard_map/all_to_all | solution.py:44
  75.9 0.9 fusion.9
  77.0 0.7 broadcast_in_dim.70
  77.7 6.9 %all-to-all-start.2 = ((f32[8,8,512]{2,1,0:T(8,128)}), f32[8,8,512]{2,1,0:T(8,128)}, u32[]{:S(2)}, u32[]{:S(2)}) async-start(f32[8,8,512]{2,1,0:T(8,128)} %broadcast_in_dim.70), calls=%async_computation.2 | async-start | bytes 262144 | tf_op jit(solution)/shard_map/all_to_all | solution.py:40
  84.6 1.1 constant_dynamic-slice_fusion.1
  85.8 0.6 reshape.90
  86.4 1.3 copy.39
  87.7 3.2 %convolution_convert_fusion = bf16[32,304]{1,0:T(8,128)(2,1)} fusion(bf16[4096,32]{0,1:T(8,128)(2,1)S(1)} %constant_dynamic-update-slice_fusion, bf16[304,4096]{1,0:T(8,128)(2,1)} %bitcast.77), kind=kOutput, calls=%fused_computation.6 | convolution fusion | flops 79701504 | bytes 2771968 | tf_op jit(solution)/shard_map/dot_general | solution.py:406
  90.9 1.5 copy.40
  92.3 2.0 shard_map.197
  94.3 9.0 %all-to-all-start.3 = ((bf16[64,8,256]{2,1,0:T(8,128)(2,1)}), bf16[64,8,256]{2,1,0:T(8,128)(2,1)}, u32[]{:S(2)}, u32[]{:S(2)}) async-start(bf16[64,8,256]{2,1,0:T(8,128)(2,1)} %get-tuple-element.26), calls=%async_computation.3 | async-start | bytes 524288 | tf_op jit(solution)/shard_map/all_to_all | solution.py:44
  103.4 1.2 convolution_multiply_fusion
  104.6 2.7 %fusion.1.values = bf16[304,128]{1,0:T(8,128)(2,1)} fusion(f32[304,128]{1,0:T(8,128)S(1)} %convolution_multiply_fusion, bf16[304,4096]{1,0:T(8,128)(2,1)S(1)} %bitcast.79, bf16[4096,128]{1,0:T(8,128)(2,1)} %value_weight.1), kind=kOutput, calls=%fused_computation.5 | convolution fusion | flops 318844928 | bytes 3772416 | tf_op jit(solution)/shard_map/dot_general | solution.py:414
  107.5 1.5 fusion.keys
  108.9 8.5 %all-to-all-done.3 = bf16[64,8,256]{2,1,0:T(8,128)(2,1)} async-done(((bf16[64,8,256]{2,1,0:T(8,128)(2,1)}), bf16[64,8,256]{2,1,0:T(8,128)(2,1)}, u32[]{:S(2)}, u32[]{:S(2)}) %all-to-all-start.3) | async-done | bytes 262176 | tf_op jit(solution)/shard_map/all_to_all | solution.py:44
  117.5 2.9 %shard_map.198 = (bf16[64,512]{1,0:T(8,128)(2,1)}, f32[8,4,640]{2,1,0:T(4,128)}) custom-call(bf16[512,256]{1,0:T(8,128)(2,1)} %bitcast.25.received, bf16[512,512]{1,0:T(8,128)(2,1)} %bitcast.83, f32[8,128]{1,0:T(8,128)} %get-tuple-element.28.loss, bf16[2,2,64,512]{3,2,1,0:T(8,128)(2,1)} %copy-done.2, bf16[2,2,64,512]{3,2,1,0:T(8,128)(2,1)} %collective-permute-done.2.rest_1_, ...), custom_call_target="tpu_custom_call" | custom-call | flops 67108864 | bytes 1048576 | tf_op jit(solution)/shard_map/pallas_call | solution.py:431
  120.4 11.5 %all_to_all.40.parts = f32[8,4,640]{2,1,0:T(4,128)} all-to-all(f32[8,4,640]{2,1,0:T(4,128)} %get-tuple-element.30), channel_id=1, replica_groups=mesh['z'=8,'x'=4,'h'=2,'mp'=8] {'z'}, dimensions={0} | all-to-all | bytes 163840 | tf_op jit(solution)/shard_map/all_to_all | solution.py:44
  131.8 7.5 %shard_map.199 = (bf16[304,4096]{1,0:T(8,128)(2,1)}, f32[4,128]{1,0:T(4,128)}, bf16[8,8,4,896]{3,2,1,0:T(4,128)(2,1)}) custom-call(s32[1,2]{1,0:T(1,128)} %bitcast.115, f32[8,4,640]{2,1,0:T(4,128)} %all_to_all.40.parts, bf16[304,128]{1,0:T(8,128)(2,1)} %fusion.keys, bf16[304,128]{1,0:T(8,128)(2,1)} %fusion.1.values, bf16[16,128]{1,0:T(8,128)(2,1)} %key_up.1, ...), custom_call_target="tpu_custom_call" | custom-call | flops 67108864 | bytes 1048576 | tf_op jit(solution)/shard_map/pallas_call | solution.py:457
  139.4 1.0 copy-done.5
  140.4 32.0 %all_to_all.41 = bf16[64,4,896]{2,1,0:T(4,128)(2,1)} all-to-all(bf16[64,4,896]{2,1,0:T(4,128)(2,1)S(1)} %bitcast.96), channel_id=1, replica_groups=mesh['z'=8,'x'=4,'h'=2,'mp'=8] {'z','mp'}, dimensions={0} | all-to-all | bytes 917504 | tf_op jit(solution)/shard_map/all_to_all | solution.py:44
  172.4 2.2 shard_map.200
  174.6 14.6 %all_to_all.42.sums = f32[8,4,768]{2,1,0:T(4,128)} all-to-all(f32[8,4,768]{2,1,0:T(4,128)} %get-tuple-element.35), channel_id=1, replica_groups=mesh['z'=8,'x'=4,'h'=2,'mp'=8] {'x','h'}, dimensions={0} | all-to-all | bytes 196608 | tf_op jit(solution)/shard_map/all_to_all | solution.py:44
  189.2 1.7 shard_map.201
  190.9 7.3 %all-to-all-start.7 = ((bf16[64,4,896]{2,1,0:T(4,128)(2,1)}), bf16[64,4,896]{2,1,0:T(4,128)(2,1)S(1)}, u32[]{:S(2)}, u32[]{:S(2)}) async-start(bf16[64,4,896]{2,1,0:T(4,128)(2,1)} %bitcast.95), calls=%async_computation.8 | async-start | bytes 917504 | tf_op jit(solution)/shard_map/all_to_all | solution.py:44
  198.3 1.3 iota_compare_fusion
  199.6 0.7 dynamic-slice_bitcast_fusion
  200.3 3.5 %collective-permute-start.5 = (bf16[8,512]{1,0:T(8,128)(2,1)S(1)}, bf16[8,512]{1,0:T(8,128)(2,1)S(1)}, u32[]{:S(2)}, u32[]{:S(2)}) collective-permute-start(bf16[8,512]{1,0:T(8,128)(2,1)S(1)} %dynamic-slice_bitcast_fusion), channel_id=1, source_target_pairs={{0,0},{1,64},{2,128},{3,192},{4,256},{5,320},{6,384},{7,448},{64,1... | collective-permute-start | bytes 24584 | tf_op jit(solution)/shard_map/ppermute | solution.py:446
  203.8 0.8 fusion.2
  204.6 3.9 %collective-permute-done.5 = bf16[8,512]{1,0:T(8,128)(2,1)S(1)} collective-permute-done((bf16[8,512]{1,0:T(8,128)(2,1)S(1)}, bf16[8,512]{1,0:T(8,128)(2,1)S(1)}, u32[]{:S(2)}, u32[]{:S(2)}) %collective-permute-start.5) | collective-permute-done | bytes 8224 | tf_op jit(solution)/shard_map/ppermute | solution.py:446
  208.5 1.2 slice.73
  210.3 5.2 %all-to-all-done.7 = bf16[64,4,896]{2,1,0:T(4,128)(2,1)S(1)} async-done(((bf16[64,4,896]{2,1,0:T(4,128)(2,1)}), bf16[64,4,896]{2,1,0:T(4,128)(2,1)S(1)}, u32[]{:S(2)}, u32[]{:S(2)}) %all-to-all-start.7) | async-done | bytes 458784 | tf_op jit(solution)/shard_map/all_to_all | solution.py:44
  216.8 0.8 fusion.10
  217.6 1.9 add_convert_fusion
  (60 shorter events, 3.1 us)
Async XLA Ops:
  7.2 77.5 %all-gather.2.cloned.1.call-start = ((), (), s32[]{:S(2)}) async-start(), calls=%async_computation.9 | async-start | bytes 2801664 | tf_op jit(solution)/shard_map/all_gather | solution.py:350
  8.6 11.1 %collective-permute-start = (bf16[2,8,512]{2,1,0:T(8,128)(2,1)S(1)}, bf16[2,8,512]{2,1,0:T(8,128)(2,1)S(1)}, u32[]{:S(2)}, u32[]{:S(2)}) collective-permute-start(bf16[2,8,512]{2,1,0:T(8,128)(2,1)S(1)} %pad_maximum_fusion.4), channel_id=1, source_target_pairs={{0,8},{8,0},{1,9},{9,1},{2,10},{10,2},{3,11},{11,3},{4,12},{12,4},... | collective-permute-start | bytes 49160 | tf_op jit(solution)/shard_map/ppermute | solution.py:359
  17.8 13.1 %collective-permute-start.1 = (bf16[2,64,512]{2,1,0:T(8,128)(2,1)S(1)}, bf16[2,64,512]{2,1,0:T(8,128)(2,1)S(1)}, u32[]{:S(2)}, u32[]{:S(2)}) collective-permute-start(bf16[2,64,512]{2,1,0:T(8,128)(2,1)S(1)} %pad_maximum_fusion.2), channel_id=1, source_target_pairs={{0,8},{8,0},{1,9},{9,1},{2,10},{10,2},{3,11},{11,3},{4,12},{12,4},... | collective-permute-start | bytes 393224 | tf_op jit(solution)/shard_map/ppermute | solution.py:359
  21.1 17.5 %all-to-all-start = ((bf16[8,16,512]{2,1,0:T(8,128)(2,1)}), bf16[8,16,512]{2,1,0:T(8,128)(2,1)S(1)}, u32[]{:S(2)}, u32[]{:S(2)}) async-start(bf16[8,16,512]{2,1,0:T(8,128)(2,1)} %broadcast_in_dim.68), calls=%async_computation | async-start | bytes 262144 | tf_op jit(solution)/shard_map/all_to_all | solution.py:40
  30.8 19.1 %copy-start.12 = (s32[2,1]{0,1:T(1,128)S(1)}, s32[2,1]{0,1:T(1,128)}, u32[]{:S(2)}) copy-start(s32[2,1]{0,1:T(1,128)} %param.19) | copy-start | bytes 28
  30.8 23.6 %copy-start.6 = (bf16[4096,16]{0,1:T(8,128)(2,1)S(1)}, bf16[4096,16]{0,1:T(8,128)(2,1)}, u32[]{:S(2)}) copy-start(bf16[4096,16]{0,1:T(8,128)(2,1)} %param.24) | copy-start | bytes 393220
  31.8 22.7 %copy-start.7 = (bf16[4096,16]{0,1:T(8,128)(2,1)S(1)}, bf16[4096,16]{0,1:T(8,128)(2,1)}, u32[]{:S(2)}) copy-start(bf16[4096,16]{0,1:T(8,128)(2,1)} %param.26) | copy-start | bytes 393220
  31.8 44.9 %copy-start.2 = (bf16[2,2,64,512]{3,2,1,0:T(8,128)(2,1)}, bf16[2,2,64,512]{3,2,1,0:T(8,128)(2,1)S(1)}, u32[]{:S(2)}) copy-start(bf16[2,2,64,512]{3,2,1,0:T(8,128)(2,1)S(1)} %pad_maximum_fusion.rest_0_) | copy-start | bytes 786436
  39.8 37.0 %copy-start.8 = (bf16[8,512]{1,0:T(8,128)(2,1)S(1)}, bf16[8,512]{1,0:T(8,128)(2,1)}, u32[]{:S(2)}) copy-start(bf16[8,512]{1,0:T(8,128)(2,1)} %param.14) | copy-start | bytes 24580
  39.8 36.1 %all-to-all-start.1 = ((bf16[32,32,512]{2,1,0:T(8,128)(2,1)}), bf16[32,32,512]{2,1,0:T(8,128)(2,1)S(1)}, u32[]{:S(2)}, u32[]{:S(2)}) async-start(bf16[32,32,512]{2,1,0:T(8,128)(2,1)} %bitcast.12), calls=%async_computation.1 | async-start | bytes 2097152 | tf_op jit(solution)/shard_map/all_to_all | solution.py:44
  54.5 36.4 %copy-start.3 = (bf16[4096,32]{0,1:T(8,128)(2,1)}, bf16[4096,32]{0,1:T(8,128)(2,1)S(1)}, u32[]{:S(2)}) copy-start(bf16[4096,32]{0,1:T(8,128)(2,1)S(1)} %constant_dynamic-update-slice_fusion) | copy-start | bytes 786436
  54.5 63.0 %collective-permute-start.4 = (bf16[2,2,64,512]{3,2,1,0:T(8,128)(2,1)S(1)}, bf16[2,2,64,512]{3,2,1,0:T(8,128)(2,1)}, u32[]{:S(2)}, u32[]{:S(2)}) collective-permute-start(bf16[2,2,64,512]{3,2,1,0:T(8,128)(2,1)S(1)} %pad_maximum_fusion.rest_0_), channel_id=1, source_target_pairs={{0,48},{16,0},{32,16},{48,32},{1,49},{17,1},{33,17},{49,33},{2,50}... | collective-permute-start | bytes 786440 | tf_op jit(solution)/shard_map/ppermute | solution.py:387
  58.8 58.6 %collective-permute-start.3 = (bf16[2,2,64,512]{3,2,1,0:T(8,128)(2,1)S(1)}, bf16[2,2,64,512]{3,2,1,0:T(8,128)(2,1)}, u32[]{:S(2)}, u32[]{:S(2)}) collective-permute-start(bf16[2,2,64,512]{3,2,1,0:T(8,128)(2,1)S(1)} %pad_maximum_fusion.rest_0_), channel_id=1, source_target_pairs={{0,32},{16,48},{32,0},{48,16},{1,33},{17,49},{33,1},{49,17},{2,34}... | collective-permute-start | bytes 786440 | tf_op jit(solution)/shard_map/ppermute | solution.py:387
  61.3 56.1 %collective-permute-start.2 = (bf16[2,2,64,512]{3,2,1,0:T(8,128)(2,1)S(1)}, bf16[2,2,64,512]{3,2,1,0:T(8,128)(2,1)}, u32[]{:S(2)}, u32[]{:S(2)}) collective-permute-start(bf16[2,2,64,512]{3,2,1,0:T(8,128)(2,1)S(1)} %pad_maximum_fusion.rest_0_), channel_id=1, source_target_pairs={{0,16},{16,32},{32,48},{48,0},{1,17},{17,33},{33,49},{49,1},{2,18}... | collective-permute-start | bytes 786440 | tf_op jit(solution)/shard_map/ppermute | solution.py:387
  77.7 14.6 %all-to-all-start.2 = ((f32[8,8,512]{2,1,0:T(8,128)}), f32[8,8,512]{2,1,0:T(8,128)}, u32[]{:S(2)}, u32[]{:S(2)}) async-start(f32[8,8,512]{2,1,0:T(8,128)} %broadcast_in_dim.70), calls=%async_computation.2 | async-start | bytes 262144 | tf_op jit(solution)/shard_map/all_to_all | solution.py:40
  84.6 20.0 %copy-start = (bf16[2,1,152,4096]{3,2,1,0:T(8,128)(2,1)S(1)}, bf16[2,1,152,4096]{3,2,1,0:T(8,128)(2,1)}, u32[]{:S(2)}) copy-start(bf16[2,1,152,4096]{3,2,1,0:T(8,128)(2,1)} %all-gather.2.cloned.1.call-done) | copy-start | bytes 7471108
  86.4 17.0 %copy-start.10 = (bf16[16,128]{1,0:T(8,128)(2,1)S(1)}, bf16[16,128]{1,0:T(8,128)(2,1)}, u32[]{:S(2)}) copy-start(bf16[16,128]{1,0:T(8,128)(2,1)} %value_up.1) | copy-start | bytes 12292
  94.3 23.1 %all-to-all-start.3 = ((bf16[64,8,256]{2,1,0:T(8,128)(2,1)}), bf16[64,8,256]{2,1,0:T(8,128)(2,1)}, u32[]{:S(2)}, u32[]{:S(2)}) async-start(bf16[64,8,256]{2,1,0:T(8,128)(2,1)} %get-tuple-element.26), calls=%async_computation.3 | async-start | bytes 524288 | tf_op jit(solution)/shard_map/all_to_all | solution.py:44
  103.3 4.0 %copy-start.4 = (bf16[32,304]{0,1:T(8,128)(2,1)S(1)}, bf16[32,304]{0,1:T(8,128)(2,1)}, u32[]{:S(2)}) copy-start(bf16[32,304]{0,1:T(8,128)(2,1)} %copy.40) | copy-start | bytes 58372
  103.3 4.0 %copy-start.9 = (bf16[16,128]{1,0:T(8,128)(2,1)S(1)}, bf16[16,128]{1,0:T(8,128)(2,1)}, u32[]{:S(2)}) copy-start(bf16[16,128]{1,0:T(8,128)(2,1)} %key_up.1) | copy-start | bytes 12292
  103.3 114.3 %reduce-scatter.2.cloned.1.call-start = ((), (), s32[]{:S(2)}) async-start(), calls=%async_computation.10 | async-start | bytes 2801664 | tf_op jit(solution)/shard_map/reduce_scatter | solution.py:481
  103.4 4.1 %copy-start.1 = (bf16[4096,128]{1,0:T(8,128)(2,1)S(1)}, bf16[4096,128]{1,0:T(8,128)(2,1)}, u32[]{:S(2)}) copy-start(bf16[4096,128]{1,0:T(8,128)(2,1)} %key_weight.1) | copy-start | bytes 3145732
  139.4 1.0 copy-start.5
  139.4 64.5 %copy-start.11 = (bf16[8,512]{1,0:T(8,128)(2,1)S(1)}, bf16[8,512]{1,0:T(8,128)(2,1)}, u32[]{:S(2)}) copy-start(bf16[8,512]{1,0:T(8,128)(2,1)} %get-tuple-element.38) | copy-start | bytes 24580
  190.9 24.6 %all-to-all-start.7 = ((bf16[64,4,896]{2,1,0:T(4,128)(2,1)}), bf16[64,4,896]{2,1,0:T(4,128)(2,1)S(1)}, u32[]{:S(2)}, u32[]{:S(2)}) async-start(bf16[64,4,896]{2,1,0:T(4,128)(2,1)} %bitcast.95), calls=%async_computation.8 | async-start | bytes 917504 | tf_op jit(solution)/shard_map/all_to_all | solution.py:44
  200.3 8.2 %collective-permute-start.5 = (bf16[8,512]{1,0:T(8,128)(2,1)S(1)}, bf16[8,512]{1,0:T(8,128)(2,1)S(1)}, u32[]{:S(2)}, u32[]{:S(2)}) collective-permute-start(bf16[8,512]{1,0:T(8,128)(2,1)S(1)} %dynamic-slice_bitcast_fusion), channel_id=1, source_target_pairs={{0,0},{1,64},{2,128},{3,192},{4,256},{5,320},{6,384},{7,448},{64,1... | collective-permute-start | bytes 24584 | tf_op jit(solution)/shard_map/ppermute | solution.py:446
Sparse Core Ops, SparseCore 0:
  10.1 48.4 all-gather.1
  139.5 48.7 reduce-scatter.1

commit v7 on v6

--- a/solution.py
+++ b/solution.py
@@ -19,6 +19,7 @@
 ADAPTER_SCALE = 2.0
 
 PLANE = ("x", "h")
+MP = ("y", "c")
 DP = ("z", "x", "h")
 
 
@@ -42,6 +43,12 @@
 
 def swap(blocks, axes):
     return lax.all_to_all(blocks, axes, split_axis=0, concat_axis=0, tiled=True)
+
+
+def feature_block(side, turn):
+    y_count = lax.axis_size("y")
+    core = lax.rem(lax.axis_index("c") + side, 2)
+    return lax.rem(lax.axis_index("y") + (y_count - turn), y_count) * 2 + core
 
 
 def call(kernel, out_shape, flops, **layout):
@@ -87,12 +94,45 @@
     residual_out[...] = residual.astype(jnp.bfloat16)
     width = z_count * rows
     pad = jnp.zeros((rows, LANES - width), jnp.float32)
+    y_count = lax.axis_size("y")
+    slices = []
+    for z in range(z_count):
+        side = lax.rem(lax.axis_index("c") + z, 2)
+        turn = lax.rem(lax.axis_index("y") + (y_count - z // 2), y_count)
+        slices.append(tokens[side * y_count + turn])
     for plane in range(plane_count):
         block = jnp.concatenate([residual[:, plane * width : (plane + 1) * width], pad], axis=1)
         block = block.astype(jnp.bfloat16)
         for z in range(z_count):
             chunks[z * plane_count + plane, :, :LANES] = block
-            chunks[z * plane_count + plane, :, LANES:] = tokens[z]
+            chunks[z * plane_count + plane, :, LANES:] = slices[z]
+
+
+def token_kernel(
+    mine, theirs, key_weight, value_weight, key_down, value_down, key_up, value_up, *outs
+):
+    low_key_out, low_value_out, keys_out, values_out = outs
+    width = mine.shape[2]
+    sums = [None] * 4
+    for side, pieces in enumerate((mine, theirs)):
+        for turn in range(pieces.shape[0]):
+            start = pl.multiple_of(feature_block(side, turn) * width, width)
+            rows = pl.ds(start, width)
+            piece = pieces[turn]
+            terms = [
+                final_product(piece, key_down[:, rows]),
+                final_product(piece, value_down[:, rows]),
+                jnp.dot(piece, key_weight[rows], preferred_element_type=jnp.float32),
+                jnp.dot(piece, value_weight[rows], preferred_element_type=jnp.float32),
+            ]
+            sums = [b if a is None else a + b for a, b in zip(sums, terms)]
+    low_key, low_value = sums[0].astype(jnp.bfloat16), sums[1].astype(jnp.bfloat16)
+    low_key_out[...] = low_key
+    low_value_out[...] = low_value
+    key_rise = jnp.dot(low_key, key_up[...], preferred_element_type=jnp.float32)
+    value_rise = jnp.dot(low_value, value_up[...], preferred_element_type=jnp.float32)
+    keys_out[...] = (sums[2] + ADAPTER_SCALE * key_rise).astype(jnp.bfloat16)
+    values_out[...] = (sums[3] + ADAPTER_SCALE * value_rise).astype(jnp.bfloat16)
 
 
 def gradient_kernel(z_count, subs, received, queries, loss, *rest):
@@ -154,12 +194,13 @@
     values,
     key_up,
     value_up,
-    reduced,
-    tokens,
-    key_weight,
-    value_weight,
-    down,
-    portion_out,
+    low_key,
+    low_value,
+    mine,
+    theirs,
+    key_change_out,
+    value_change_out,
+    coef_out,
     loss_out,
     shares_out,
 ):
@@ -210,17 +251,15 @@
     key_coef = final_product(key_change, key_up[...])
     value_coef = final_product(value_change, value_up[...])
     coef = jnp.concatenate([key_coef, value_coef], axis=1).astype(jnp.bfloat16)
-    rank = key_up.shape[0]
+    key_change_out[...] = key_change
+    value_change_out[...] = value_change
+    coef_out[...] = coef
     ups = ADAPTER_SCALE * jnp.concatenate(
-        [
-            first_product(reduced[...], key_change)[:rank],
-            first_product(reduced[...], value_change)[rank:],
-        ],
+        [first_product(low_key[...], key_change), first_product(low_value[...], value_change)],
         axis=0,
     )
-    downs = ADAPTER_SCALE * first_product(coef, tokens[...])
     z_count, mp_count, rows, chunk_width = shares_out.shape
-    width = downs.shape[1] // mp_count
+    width = mine.shape[2]
     up_end = width + ups.shape[1]
     deltas = jnp.concatenate(
         [
@@ -232,25 +271,39 @@
         axis=0,
     )
     for other in range(mp_count):
-        mine = lax.axis_index("mp") == other
-        kept_ups = jnp.where(mine, ups, 0.0)
-        kept_deltas = jnp.where(mine, deltas, 0.0).astype(jnp.bfloat16)
+        own = lax.axis_index(MP) == other
+        kept_ups = jnp.where(own, ups, 0.0)
+        kept_deltas = jnp.where(own, deltas, 0.0).astype(jnp.bfloat16)
         for z in range(z_count):
             ranks = slice(z * rows, (z + 1) * rows)
-            shares_out[z, other, :, :width] = downs[
-                ranks, other * width : (other + 1) * width
-            ].astype(jnp.bfloat16)
             shares_out[z, other, :, width:up_end] = kept_ups[ranks].astype(jnp.bfloat16)
             shares_out[z, other, :, up_end:] = kept_deltas
-    for other in range(mp_count):
-        features = slice(other * width, (other + 1) * width)
-        portion = final_product(key_change, key_weight[features]) + final_product(
-            value_change, value_weight[features]
-        )
-        portion = portion + ADAPTER_SCALE * jnp.dot(
-            coef, down[:, features], preferred_element_type=jnp.float32
-        )
-        portion_out[:, features] = portion.astype(jnp.bfloat16)
+    for side, pieces in enumerate((mine, theirs)):
+        for turn in range(pieces.shape[0]):
+            block = feature_block(side, turn)
+            downs = ADAPTER_SCALE * first_product(coef, pieces[turn])
+            for z in range(z_count):
+                ranks = slice(z * rows, (z + 1) * rows)
+                shares_out[z, block, :, :width] = downs[ranks].astype(jnp.bfloat16)
+
+
+def portion_kernel(
+    key_change, value_change, coef, key_weight, value_weight, key_down, value_down, keep, give
+):
+    rank = key_down.shape[0]
+    y_count, _, width = keep.shape
+    for side, out in enumerate((keep, give)):
+        for turn in range(y_count):
+            block = feature_block(side, (y_count - turn) % y_count)
+            start = pl.multiple_of(block * width, width)
+            rows = pl.ds(start, width)
+            portion = final_product(key_change[...], key_weight[rows]) + final_product(
+                value_change[...], value_weight[rows]
+            )
+            lows = jnp.dot(
+                coef[:, :rank], key_down[:, rows], preferred_element_type=jnp.float32
+            ) + jnp.dot(coef[:, rank:], value_down[:, rows], preferred_element_type=jnp.float32)
+            out[turn] = (portion + ADAPTER_SCALE * lows).astype(jnp.bfloat16)
 
 
 def home_kernel(subs, received, loss, *rest):
@@ -340,16 +393,15 @@
     z_count = lax.axis_size("z")
     plane_count = lax.axis_size(PLANE)
     dp_count = z_count * plane_count
-    mp_count = lax.axis_size("mp")
+    y_count = lax.axis_size("y")
+    mp_count = lax.axis_size(MP)
     local_rows = query_emb.shape[0]
     batch_size = local_rows * dp_count
     feature_width = query_emb.shape[1]
     sub_count = hidden_in.shape[0]
     seq_len = hidden_in.shape[2]
     token_count = sub_count * seq_len
-    full_rows = lax.all_gather(hidden_in, "mp", axis=3, tiled=True)
-    model_width = full_rows.shape[3]
-    token_inputs = full_rows.reshape(token_count, model_width)
+    model_width = feature_width * mp_count
     seq_lengths = lengths[:, 0]
     last_rows = jnp.arange(sub_count, dtype=jnp.int32) * seq_len + seq_lengths - 1
 
@@ -359,14 +411,19 @@
         other = lax.ppermute(block, "h", [(0, 1), (1, 0)])
         return jnp.stack([jnp.where(lower, block, other), jnp.where(lower, other, block)])
 
-    emb_pair = pair_up(jnp.stack([item_emb, query_emb]))
+    both = pair_up(jnp.stack([w_query, w_out.T]))
     pair_rows = 2 * local_rows
-    item_pair = emb_pair[:, 0].reshape(pair_rows, feature_width)
-    query_pair = emb_pair[:, 1].reshape(pair_rows, feature_width)
-    both = pair_up(jnp.stack([w_query, w_out.T]))
-
-    query_slices = spread(query_pair, "mp")
-    both, query_slices = lax.optimization_barrier((both, query_slices))
+    emb_pair = spread(jnp.concatenate([item_emb, query_emb], axis=0), ("h",) + MP)
+    emb_pair = emb_pair.reshape(2, mp_count, pair_rows, feature_width)
+    item_pair = lax.dynamic_index_in_dim(
+        emb_pair[:, :, :local_rows], lax.axis_index(MP), 1, keepdims=False
+    ).reshape(pair_rows, feature_width)
+
+    query_slices = (
+        emb_pair[:, :, local_rows:].transpose(1, 0, 2, 3).reshape(mp_count, pair_rows, -1)
+    )
+    own_tokens = hidden_in.reshape(token_count, feature_width)
+    both, own_tokens, query_slices = lax.optimization_barrier((both, own_tokens, query_slices))
     chunks = jnp.concatenate(
         [jnp.broadcast_to(item_pair[None], query_slices.shape), query_slices], axis=1
     )
@@ -380,40 +437,33 @@
         .reshape(batch_size, feature_width)
     )
     partial_scores = final_product(query_emb, items_all)
-    score_parts = spread(partial_scores, "mp")
+    score_parts = spread(partial_scores, MP)
 
     query_width = w_query.shape[1]
-    pieces = [both] + [
-        lax.ppermute(both, "x", [(a, (a + turn) % x_count) for a in range(x_count)])
-        for turn in range(1, x_count)
-    ]
+    def around(block, axis, turn):
+        count = lax.axis_size(axis)
+        return lax.ppermute(block, axis, [(a, (a + turn) % count) for a in range(count)])
+
+    pieces = [both] + [around(both, "x", turn) for turn in range(1, x_count)]
+
+    mine = jnp.stack(
+        [own_tokens] + [around(own_tokens, "y", turn) for turn in range(1, y_count)]
+    )
+    theirs = around(mine, "c", 1)
 
     last_tokens = jnp.concatenate(
         [
-            lax.dynamic_slice_in_dim(token_inputs, last_rows[sub], 1, 0)
+            lax.dynamic_slice_in_dim(side, last_rows[sub], 1, 1)
+            for side in (mine, theirs)
             for sub in range(sub_count)
         ],
-        axis=0,
+        axis=1,
     )
     last_slices = (
-        last_tokens.reshape(sub_count, z_count, x_count, feature_width // x_count)
-        .transpose(1, 2, 0, 3)
-        .reshape(z_count, x_count * sub_count, feature_width // x_count)
-    )
-
-    adapter_rank = key_down_matrix.shape[1]
-    down_both = jnp.concatenate([key_down_matrix, value_down], axis=1)
-    reduced_pair = jnp.dot(token_inputs, down_both, preferred_element_type=f32).astype(bf16)
-    reduced_key = reduced_pair[:, :adapter_rank]
-    reduced_value = reduced_pair[:, adapter_rank:]
-    key_rows = (
-        jnp.dot(token_inputs, key_weight_matrix, preferred_element_type=f32)
-        + ADAPTER_SCALE * jnp.dot(reduced_key, key_up_matrix, preferred_element_type=f32)
-    ).astype(bf16)
-    value_rows = (
-        jnp.dot(token_inputs, value_weight_matrix, preferred_element_type=f32)
-        + ADAPTER_SCALE * jnp.dot(reduced_value, value_up_matrix, preferred_element_type=f32)
-    ).astype(bf16)
+        last_tokens.reshape(y_count, 2, sub_count, x_count, feature_width // x_count)
+        .transpose(1, 0, 3, 2, 4)
+        .reshape(mp_count, x_count * sub_count, feature_width // x_count)
+    )
 
     chunks, residual, loss_part = call(
         functools.partial(residual_kernel, z_count, plane_count),
@@ -425,6 +475,23 @@
         2**24,
     )(score_parts, hard_index.T, pair_index[None], last_slices)
     column_rows = swap(chunks, DP).reshape(batch_size, 2 * LANES)
+    adapter_rank = key_down_matrix.shape[1]
+    up_width = key_up_matrix.shape[1]
+    mine, theirs, residual = lax.optimization_barrier((mine, theirs, residual))
+    low_shape = jax.ShapeDtypeStruct((token_count, adapter_rank), bf16)
+    head_shape = jax.ShapeDtypeStruct((token_count, up_width), bf16)
+    low_key, low_value, key_rows, value_rows = call(
+        token_kernel, (low_shape, low_shape, head_shape, head_shape), 2**30
+    )(
+        mine,
+        theirs,
+        key_weight_matrix,
+        value_weight_matrix,
+        key_down_matrix.T,
+        value_down.T,
+        key_up_matrix,
+        value_up_matrix,
+    )
     column_rows, key_rows, value_rows = lax.optimization_barrier(
         (column_rows, key_rows, value_rows)
     )
@@ -439,25 +506,26 @@
     parts = swap(parts, "z")
     own_grads = lax.dynamic_index_in_dim(
         column_grads.reshape(z_count, local_rows, feature_width),
-        lax.axis_index("mp"),
+        lax.axis_index(MP),
         0,
         keepdims=False,
     )
     item_grad = lax.ppermute(
         own_grads,
-        ("z", "mp"),
+        ("z",) + MP,
         [(a * mp_count + b, b * mp_count + a) for a in range(z_count) for b in range(mp_count)],
     )
     query_grad = (jnp.dot(residual, items_all, preferred_element_type=f32) * INV_TEMP).astype(bf16)
 
     share_rows = 2 * adapter_rank // z_count
-    up_width = key_rows.shape[1]
     sum_width = feature_width + up_width
     chunk_width = sum_width + sub_count * query_width // share_rows
-    portion, loss_part, shares = call(
+    key_change, value_change, coef, loss_part, shares = call(
         attention_kernel,
         (
-            jax.ShapeDtypeStruct((token_count, model_width), bf16),
+            head_shape,
+            head_shape,
+            jax.ShapeDtypeStruct((token_count, 2 * adapter_rank), bf16),
             jax.ShapeDtypeStruct((2 * sub_count, LANES), f32),
             jax.ShapeDtypeStruct((z_count, mp_count, share_rows, chunk_width), bf16),
         ),
@@ -469,16 +537,29 @@
         value_rows,
         key_up_matrix,
         value_up_matrix,
-        reduced_pair,
-        token_inputs,
+        low_key,
+        low_value,
+        mine,
+        theirs,
+    )
+    grid_shape = shares.shape
+    shares = swap(shares.reshape((-1,) + grid_shape[2:]), ("z",) + MP).reshape(grid_shape)
+
+    block_shape = jax.ShapeDtypeStruct((y_count, token_count, feature_width), bf16)
+    keep, give = call(portion_kernel, (block_shape, block_shape), 2**30)(
+        key_change,
+        value_change,
+        coef,
         key_weight_matrix,
         value_weight_matrix,
-        down_both.T,
-    )
-    grid_shape = shares.shape
-    shares = swap(shares.reshape((-1,) + grid_shape[2:]), ("z", "mp")).reshape(grid_shape)
-
-    input_sum = lax.psum_scatter(portion, "mp", scatter_dimension=1, tiled=True).astype(f32)
+        key_down_matrix.T,
+        value_down.T,
+    )
+    shares, got = lax.optimization_barrier((shares, around(give, "c", 1)))
+    pair_sum = keep.astype(f32) + got.astype(f32)
+    input_sum = pair_sum[0]
+    pair_sum = pair_sum.astype(bf16)
+
     sums, last_part = call(
         functools.partial(home_kernel, sub_count),
         (
@@ -487,6 +568,10 @@
         ),
         2**24,
     )(shares, loss_part, *pieces)
+    arrived = [around(pair_sum[turn], "y", turn) for turn in range(1, y_count)]
+    sums, arrived[1] = lax.optimization_barrier((swap(sums, PLANE), arrived[1]))
+    for block in arrived:
+        input_sum = input_sum + block.astype(f32)
     chunks, loss_sum = call(
         return_kernel,
         (
@@ -494,10 +579,10 @@
             jax.ShapeDtypeStruct((share_rows, LANES), f32),
         ),
         2**24,
-    )(swap(sums, PLANE), last_part)
+    )(sums, last_part)
     mean_loss = loss_sum[0, 0] / batch_size
-    summed = swap(chunks.reshape((-1,) + grid_shape[2:]), ("z", "mp")).reshape(grid_shape)
-    own = lax.axis_index("mp")
+    summed = swap(chunks.reshape((-1,) + grid_shape[2:]), ("z",) + MP).reshape(grid_shape)
+    own = lax.axis_index(MP)
     up_grad = lax.dynamic_index_in_dim(
         summed[:, :, :, feature_width:sum_width], own, 1, keepdims=False
     )
@@ -534,33 +619,31 @@
 
 
 def solution(mesh):
-    fine = Mesh(
-        mesh.devices.reshape(8, 4, 2, mesh.devices.shape[1]), ("z", "x", "h", "mp")
-    )
+    fine = Mesh(mesh.devices.reshape(8, 4, 2, 4, 2), DP + MP)
     in_specs = (
-        P(DP, "mp"),
-        P(DP, "mp"),
+        P(DP, MP),
+        P(DP, MP),
         P(DP),
         P(DP, None),
-        P(None, DP, None, "mp"),
+        P(None, DP, None, MP),
         P(None, DP),
-        P(DP, "mp"),
-        P(None, "mp"),
-        P(None, "mp"),
-        P("mp", DP),
+        P(DP, MP),
+        P(None, MP),
+        P(None, MP),
+        P(MP, DP),
         P(),
-        P(None, "mp"),
+        P(None, MP),
         P(),
-        P(None, "mp"),
+        P(None, MP),
     )
     out_specs = (
         P(),
-        P(DP, "mp"),
-        P(DP, "mp"),
-        P(None, DP, None, "mp"),
+        P(DP, MP),
+        P(DP, MP),
+        P(None, DP, None, MP),
         P(),
         P(),
-        P(None, "mp"),
-        P(None, "mp"),
+        P(None, MP),
+        P(None, MP),
     )
     return jax.shard_map(local, mesh=fine, in_specs=in_specs, out_specs=out_specs, check_vma=False)

time: 230 us -> 252 us (1.096)
  starting transfers between devices: 66.2 us -> 90.3 us
  waiting for transfers between devices: 37.1 us -> 57.7 us
  between operations: 20.1 us -> 6.77 us
  matrix products: 9.67 us -> 1.01 us
  Pallas kernels: 16.4 us -> 24.4 us
  blocking collectives: 58 us -> 50 us
    ppermute x4 -> x12, waiting for transfers between devices: 3.87 us -> 43.3 us  [the longest x11 39.4 us: around(): lax.ppermute(block, axis, [(a, (a + turn) % count) for a in range(count)])]
    all_to_all x3, waiting for transfers between devices: 25.8 us -> 0.01 us  [swap(): return lax.all_to_all(blocks, axes, split_axis=0, concat_axis=0, tiled=True)]
    ppermute x4 -> x12, starting transfers between devices: 12.9 us -> 37.4 us  [the longest x11 33.9 us: around(): lax.ppermute(block, axis, [(a, (a + turn) % count) for a in range(count)])]
    ppermute x2 -> x1, waiting for transfers between devices: 0.01 us -> 9.53 us  [pair_up(): other = lax.ppermute(block, 'h', [(0, 1), (1, 0)])]
    dot_general x5 -> x0, matrix products: 8.66 us -> none  [the longest x1 3.16 us: local(): jnp.dot(token_inputs, down_both, preferred_element_type=f32).astype(bf16)]
    all_to_all x3, blocking collectives: 58 us -> 50 us  [swap(): return lax.all_to_all(blocks, axes, split_axis=0, concat_axis=0, tiled=True)]
    pallas_call x1 -> x3, Pallas kernels: 7.55 us -> 15.5 us  [the longest x1 5.83 us: local(): call(token_kernel, (low_shape, low_shape, head_shape, head_shape), 2 ** 30)]
    all_to_all x3, starting transfers between devices: 26.5 us -> 32.2 us  [swap(): return lax.all_to_all(blocks, axes, split_axis=0, concat_axis=0, tiled=True)]
  transfers between devices with their start and end apart: 13 -> 18, of which waited for: 5 -> 9; matrix products, arithmetic and copies ran while one was open for 12% -> 5% of each run, Pallas kernels for 3% -> 3%
where the time goes in v7:
time: 252 us; the launch traced here: 251 us
  starting transfers between devices  90.3 us (36%)
  waiting for transfers between devices  57.7 us (23%)
  blocking collectives  50 us (20%)
  Pallas kernels  24.4 us (10%)
  local copies, waits for them, and re-layouts  11.7 us (5%)
  other arithmetic  8.72 us (3%)
  between operations  6.77 us (3%)
    all_to_all x3, blocking collectives, swap(): return lax.all_to_all(blocks, axes, split_axis=0, concat_axis=0, tiled=True)  50 us
    ppermute x11, waiting for transfers between devices, around(): lax.ppermute(block, axis, [(a, (a + turn) % count) for a in range(count)])  39.4 us
    ppermute x11, starting transfers between devices, around(): lax.ppermute(block, axis, [(a, (a + turn) % count) for a in range(count)])  33.9 us
    all_to_all x3, starting transfers between devices, swap(): return lax.all_to_all(blocks, axes, split_axis=0, concat_axis=0, tiled=True)  32.2 us
    all_to_all x2, starting transfers between devices, spread(): return lax.all_to_all(copies, axes, split_axis=0, concat_axis=0, tiled=True)  13.5 us
    ppermute x1, waiting for transfers between devices, pair_up(): other = lax.ppermute(block, 'h', [(0, 1), (1, 0)])  9.53 us
    ppermute x1, starting transfers between devices, pair_up(): other = lax.ppermute(block, 'h', [(0, 1), (1, 0)])  7.25 us
    pallas_call x1, Pallas kernels, local(): call(token_kernel, (low_shape, low_shape, head_shape, head_shape), 2 ** 30)  5.83 us
  transfers between devices with their start and end apart: 18, of which 9 were waited for; matrix products, arithmetic and copies ran while one was open for 5% of the time, Pallas kernels for 3%

profile of v7, /device:TPU:1, one launch (start us, length us, event | category | flops | bytes accessed | tf_op | source)
XLA Modules:
  0.0 250.6 jit_solution(9759079658186575907)
XLA Ops:
  1.4 0.7 broadcast_in_dim.64
  2.1 10.2 %all-to-all-start = ((bf16[16,16,512]{2,1,0:T(8,128)(2,1)}), bf16[16,16,512]{2,1,0:T(8,128)(2,1)S(1)}, u32[]{:S(2)}, u32[]{:S(2)}) async-start(bf16[16,16,512]{2,1,0:T(8,128)(2,1)} %broadcast_in_dim.64), calls=%async_computation | async-start | bytes 524288 | tf_op jit(solution)/shard_map/all_to_all | solution.py:41
  12.3 0.9 pad_maximum_fusion.3
  13.2 7.2 %collective-permute-start = (bf16[2,64,512]{2,1,0:T(8,128)(2,1)S(1)}, bf16[2,64,512]{2,1,0:T(8,128)(2,1)S(1)}, u32[]{:S(2)}, u32[]{:S(2)}) collective-permute-start(bf16[2,64,512]{2,1,0:T(8,128)(2,1)S(1)} %pad_maximum_fusion.3), channel_id=1, source_target_pairs={{0,8},{8,0},{1,9},{9,1},{2,10},{10,2},{3,11},{11,3},{4,12},{12,4},... | collective-permute-start | bytes 393224 | tf_op jit(solution)/shard_map/ppermute | solution.py:411
  20.4 9.5 %collective-permute-done = bf16[2,64,512]{2,1,0:T(8,128)(2,1)S(1)} collective-permute-done((bf16[2,64,512]{2,1,0:T(8,128)(2,1)S(1)}, bf16[2,64,512]{2,1,0:T(8,128)(2,1)S(1)}, u32[]{:S(2)}, u32[]{:S(2)}) %collective-permute-start) | collective-permute-done | bytes 131104 | tf_op jit(solution)/shard_map/ppermute | solution.py:411
  30.0 0.9 select_bitcast_fusion.1
  31.7 1.1 broadcast_in_dim.67
  32.8 11.5 %all-to-all-start.1 = ((bf16[32,32,512]{2,1,0:T(8,128)(2,1)}), bf16[32,32,512]{2,1,0:T(8,128)(2,1)S(1)}, u32[]{:S(2)}, u32[]{:S(2)}) async-start(bf16[32,32,512]{2,1,0:T(8,128)(2,1)} %bitcast.11), calls=%async_computation.1 | async-start | bytes 2097152 | tf_op jit(solution)/shard_map/all_to_all | solution.py:45
  44.3 1.9 collective-permute-start.3
  46.2 3.5 %collective-permute-start.2 = (bf16[304,512]{1,0:T(8,128)(2,1)S(1)}, bf16[304,512]{1,0:T(8,128)(2,1)S(1)}, u32[]{:S(2)}, u32[]{:S(2)}) collective-permute-start(bf16[304,512]{1,0:T(8,128)(2,1)S(1)} %bitcast.107), channel_id=1, source_target_pairs={{0,4},{2,6},{4,0},{6,2},{1,5},{3,7},{5,1},{7,3},{8,12},{10,14},{12... | collective-permute-start | bytes 933896 | tf_op jit(solution)/shard_map/ppermute | solution.py:445
  49.7 1.9 collective-permute-start.1
  51.6 2.5 collective-permute-done.3
  54.1 20.2 %collective-permute-done.2 = bf16[304,512]{1,0:T(8,128)(2,1)S(1)} collective-permute-done((bf16[304,512]{1,0:T(8,128)(2,1)S(1)}, bf16[304,512]{1,0:T(8,128)(2,1)S(1)}, u32[]{:S(2)}, u32[]{:S(2)}) %collective-permute-start.2) | collective-permute-done | bytes 311328 | tf_op jit(solution)/shard_map/ppermute | solution.py:445
  74.5 3.6 %collective-permute-start.4 = (bf16[4,304,512]{2,1,0:T(8,128)(2,1)S(1)}, bf16[4,304,512]{2,1,0:T(8,128)(2,1)S(1)}, u32[]{:S(2)}, u32[]{:S(2)}) collective-permute-start(bf16[4,304,512]{2,1,0:T(8,128)(2,1)S(1)} %pad_maximum_fusion.mine), channel_id=1, source_target_pairs={{0,1},{1,0},{2,3},{3,2},{4,5},{5,4},{6,7},{7,6},{8,9},{9,8},{10,11... | collective-permute-start | bytes 3735560 | tf_op jit(solution)/shard_map/ppermute | solution.py:445
  82.7 0.9 fusion.9
  84.6 3.3 %all-to-all-start.2 = ((f32[8,8,512]{2,1,0:T(8,128)}), f32[8,8,512]{2,1,0:T(8,128)S(1)}, u32[]{:S(2)}, u32[]{:S(2)}) async-start(f32[8,8,512]{2,1,0:T(8,128)} %broadcast_in_dim.68), calls=%async_computation.2 | async-start | bytes 262144 | tf_op jit(solution)/shard_map/all_to_all | solution.py:41
  88.1 0.8 copy.32
  88.8 4.9 %all-to-all-done.2.parts = f32[8,8,512]{2,1,0:T(8,128)S(1)} async-done(((f32[8,8,512]{2,1,0:T(8,128)}), f32[8,8,512]{2,1,0:T(8,128)S(1)}, u32[]{:S(2)}, u32[]{:S(2)}) %all-to-all-start.2) | async-done | bytes 131104 | tf_op jit(solution)/shard_map/all_to_all | solution.py:41
  94.3 2.0 shard_map.197
  96.3 11.7 %all-to-all-start.3 = ((bf16[64,8,256]{2,1,0:T(8,128)(2,1)}), bf16[64,8,256]{2,1,0:T(8,128)(2,1)S(1)}, u32[]{:S(2)}, u32[]{:S(2)}) async-start(bf16[64,8,256]{2,1,0:T(8,128)(2,1)} %get-tuple-element.43), calls=%async_computation.3 | async-start | bytes 524288 | tf_op jit(solution)/shard_map/all_to_all | solution.py:45
  108.1 4.1 %collective-permute-start.7 = (bf16[2,2,64,512]{3,2,1,0:T(8,128)(2,1)S(1)}, bf16[2,2,64,512]{3,2,1,0:T(8,128)(2,1)S(1)}, u32[]{:S(2)}, u32[]{:S(2)}) collective-permute-start(bf16[2,2,64,512]{3,2,1,0:T(8,128)(2,1)S(1)} %copy-done.2), channel_id=1, source_target_pairs={{0,48},{16,0},{32,16},{48,32},{1,49},{17,1},{33,17},{49,33},{2,50}... | collective-permute-start | bytes 786440 | tf_op jit(solution)/shard_map/ppermute | solution.py:445
  112.2 2.5 collective-permute-start.6
  114.7 2.5 collective-permute-start.5
  117.2 5.8 %shard_map.198 = (bf16[304,16]{1,0:T(8,128)(2,1)}, bf16[304,16]{1,0:T(8,128)(2,1)}, bf16[304,128]{1,0:T(8,128)(2,1)}, bf16[304,128]{1,0:T(8,128)(2,1)}) custom-call(bf16[4,304,512]{2,1,0:T(8,128)(2,1)} %copy-done, bf16[4,304,512]{2,1,0:T(8,128)(2,1)} %copy-done.1, bf16[4096,128]{1,0:T(8,128)(2,1)} %key_weight.3, bf16[4096,128]{1,0:T(8,128)(2,1)} %value_weight.3, ...), custom_call_target="tpu_custom_call" | custom-call | flops 1073741824 | bytes 1048576 | tf_op jit(solution)/shard_map/pallas_call | solution.py:483
  123.6 7.2 %collective-permute-done.5.rest_1_ = bf16[2,2,64,512]{3,2,1,0:T(8,128)(2,1)S(1)} collective-permute-done((bf16[2,2,64,512]{3,2,1,0:T(8,128)(2,1)S(1)}, bf16[2,2,64,512]{3,2,1,0:T(8,128)(2,1)S(1)}, u32[]{:S(2)}, u32[]{:S(2)}) %collective-permute-start.5) | collective-permute-done | bytes 262176 | tf_op jit(solution)/shard_map/ppermute | solution.py:445
  131.6 2.9 %shard_map.199 = (bf16[64,512]{1,0:T(8,128)(2,1)}, f32[8,4,640]{2,1,0:T(4,128)}) custom-call(bf16[512,256]{1,0:T(8,128)(2,1)} %bitcast.100, bf16[512,512]{1,0:T(8,128)(2,1)} %bitcast.92, f32[8,128]{1,0:T(8,128)} %get-tuple-element.50.loss, bf16[2,2,64,512]{3,2,1,0:T(8,128)(2,1)} %pad_maximum_fusion.1.rest_0_, bf16[2,2,64,512]{3,2,1,0:T(8,128)(2,1)} %copy-done.6, ...), custom_call_target="tpu_custom_call" | custom-call | flops 67108864 | bytes 1048576 | tf_op jit(solution)/shard_map/pallas_call | solution.py:498
  134.5 13.2 %all_to_all.40.parts = f32[8,4,640]{2,1,0:T(4,128)} all-to-all(f32[8,4,640]{2,1,0:T(4,128)} %get-tuple-element.52), channel_id=1, replica_groups=mesh['z'=8,'x'=4,'h'=2,'y'=4,'c'=2] {'z'}, dimensions={0} | all-to-all | bytes 163840 | tf_op jit(solution)/shard_map/all_to_all | solution.py:45
  147.6 4.1 %shard_map.200 = (bf16[304,128]{1,0:T(8,128)(2,1)}, bf16[304,128]{1,0:T(8,128)(2,1)}, bf16[304,32]{1,0:T(8,128)(2,1)}, f32[4,128]{1,0:T(4,128)}, bf16[8,8,4,896]{3,2,1,0:T(4,128)(2,1)}) custom-call(s32[1,2]{1,0:T(1,128)} %bitcast.130, f32[8,4,640]{2,1,0:T(4,128)} %all_to_all.40.parts, bf16[304,128]{1,0:T(8,128)(2,1)} %get-tuple-element.53.keys, ...), custom_call_target="tpu_custom_call" | custom-call | flops 67108864 | bytes 1048576 | tf_op jit(solution)/shard_map/pallas_call | solution.py:523
  151.8 5.6 %shard_map.201 = (bf16[4,304,512]{2,1,0:T(8,128)(2,1)}, bf16[4,304,512]{2,1,0:T(8,128)(2,1)}) custom-call(bf16[304,128]{1,0:T(8,128)(2,1)} %get-tuple-element.58.key_change, bf16[304,128]{1,0:T(8,128)(2,1)} %get-tuple-element.59.value_change, bf16[304,32]{1,0:T(8,128)(2,1)} %get-tuple-element.60.coef, bf16[4096,128]{1,0:T(8,128)(2,1)} %key_weight.3, ...), custom_call_target="tpu_custom_call" | custom-call | flops 1073741824 | bytes 1048576 | tf_op jit(solution)/shard_map/pallas_call | solution.py:549
  157.3 3.9 %collective-permute-start.8 = (bf16[4,304,512]{2,1,0:T(8,128)(2,1)}, bf16[4,304,512]{2,1,0:T(8,128)(2,1)S(1)}, u32[]{:S(2)}, u32[]{:S(2)}) collective-permute-start(bf16[4,304,512]{2,1,0:T(8,128)(2,1)} %get-tuple-element.61), channel_id=1, source_target_pairs={{0,1},{1,0},{2,3},{3,2},{4,5},{5,4},{6,7},{7,6},{8,9},{9,8},{10,11... | collective-permute-start | bytes 3735560 | tf_op jit(solution)/shard_map/ppermute | solution.py:445
  161.3 21.3 %all_to_all.41 = bf16[64,4,896]{2,1,0:T(4,128)(2,1)} all-to-all(bf16[64,4,896]{2,1,0:T(4,128)(2,1)S(1)} %bitcast.104), channel_id=1, replica_groups=mesh['z'=8,'x'=4,'h'=2,'y'=4,'c'=2] {'z','y','c'}, dimensions={0} | all-to-all | bytes 917504 | tf_op jit(solution)/shard_map/all_to_all | solution.py:45
  182.6 1.8 convert_add_fusion
  184.4 0.9 slice_bitcast_fusion.2
  185.3 1.9 collective-permute-start.9
  187.2 2.3 shard_map.202
  189.5 15.5 %all_to_all.42.sums = f32[8,4,768]{2,1,0:T(4,128)} all-to-all(f32[8,4,768]{2,1,0:T(4,128)} %get-tuple-element.64), channel_id=1, replica_groups=mesh['z'=8,'x'=4,'h'=2,'y'=4,'c'=2] {'x','h'}, dimensions={0} | all-to-all | bytes 196608 | tf_op jit(solution)/shard_map/all_to_all | solution.py:45
  205.0 1.8 shard_map.203
  206.7 9.0 %all-to-all-start.7 = ((bf16[64,4,896]{2,1,0:T(4,128)(2,1)}), bf16[64,4,896]{2,1,0:T(4,128)(2,1)S(1)}, u32[]{:S(2)}, u32[]{:S(2)}) async-start(bf16[64,4,896]{2,1,0:T(4,128)(2,1)} %bitcast.103), calls=%async_computation.7 | async-start | bytes 917504 | tf_op jit(solution)/shard_map/all_to_all | solution.py:45
  215.7 1.3 iota_compare_fusion
  217.7 3.5 %collective-permute-start.10 = (bf16[8,512]{1,0:T(8,128)(2,1)S(1)}, bf16[8,512]{1,0:T(8,128)(2,1)S(1)}, u32[]{:S(2)}, u32[]{:S(2)}) collective-permute-start(bf16[8,512]{1,0:T(8,128)(2,1)S(1)} %dynamic-slice_bitcast_fusion.1), channel_id=1, source_target_pairs={{0,0},{1,64},{2,128},{3,192},{4,256},{5,320},{6,384},{7,448},{64,1... | collective-permute-start | bytes 24584 | tf_op jit(solution)/shard_map/ppermute | solution.py:513
  221.3 0.8 fusion
  222.1 3.9 %collective-permute-done.10 = bf16[8,512]{1,0:T(8,128)(2,1)S(1)} collective-permute-done((bf16[8,512]{1,0:T(8,128)(2,1)S(1)}, bf16[8,512]{1,0:T(8,128)(2,1)S(1)}, u32[]{:S(2)}, u32[]{:S(2)}) %collective-permute-start.10) | collective-permute-done | bytes 8224 | tf_op jit(solution)/shard_map/ppermute | solution.py:513
  225.9 4.8 %collective-permute-start.11 = (bf16[304,512]{1,0:T(8,128)(2,1)}, bf16[304,512]{1,0:T(8,128)(2,1)}, u32[]{:S(2)}, u32[]{:S(2)}) collective-permute-start(bf16[304,512]{1,0:T(8,128)(2,1)} %get-tuple-element.100), channel_id=1, source_target_pairs={{0,2},{2,4},{4,6},{6,0},{1,3},{3,5},{5,7},{7,1},{8,10},{10,12},{12... | collective-permute-start | bytes 933896 | tf_op jit(solution)/shard_map/ppermute | solution.py:445
  230.8 3.2 %collective-permute-start.12 = (bf16[304,512]{1,0:T(8,128)(2,1)}, bf16[304,512]{1,0:T(8,128)(2,1)}, u32[]{:S(2)}, u32[]{:S(2)}) collective-permute-start(bf16[304,512]{1,0:T(8,128)(2,1)} %get-tuple-element.101), channel_id=1, source_target_pairs={{0,6},{2,0},{4,2},{6,4},{1,7},{3,1},{5,3},{7,5},{8,14},{10,8},{12,... | collective-permute-start | bytes 933896 | tf_op jit(solution)/shard_map/ppermute | solution.py:445
  234.0 1.2 slice.80
  236.5 0.8 fusion.10
  238.4 8.3 %collective-permute-done.12 = bf16[304,512]{1,0:T(8,128)(2,1)} collective-permute-done((bf16[304,512]{1,0:T(8,128)(2,1)}, bf16[304,512]{1,0:T(8,128)(2,1)}, u32[]{:S(2)}, u32[]{:S(2)}) %collective-permute-start.12) | collective-permute-done | bytes 311328 | tf_op jit(solution)/shard_map/ppermute | solution.py:445
  246.8 2.1 fusion.6
  (67 shorter events, 8.4 us)
Async XLA Ops:
  2.1 29.5 %all-to-all-start = ((bf16[16,16,512]{2,1,0:T(8,128)(2,1)}), bf16[16,16,512]{2,1,0:T(8,128)(2,1)S(1)}, u32[]{:S(2)}, u32[]{:S(2)}) async-start(bf16[16,16,512]{2,1,0:T(8,128)(2,1)} %broadcast_in_dim.64), calls=%async_computation | async-start | bytes 524288 | tf_op jit(solution)/shard_map/all_to_all | solution.py:41
  13.2 16.8 %collective-permute-start = (bf16[2,64,512]{2,1,0:T(8,128)(2,1)S(1)}, bf16[2,64,512]{2,1,0:T(8,128)(2,1)S(1)}, u32[]{:S(2)}, u32[]{:S(2)}) collective-permute-start(bf16[2,64,512]{2,1,0:T(8,128)(2,1)S(1)} %pad_maximum_fusion.3), channel_id=1, source_target_pairs={{0,8},{8,0},{1,9},{9,1},{2,10},{10,2},{3,11},{11,3},{4,12},{12,4},... | collective-permute-start | bytes 393224 | tf_op jit(solution)/shard_map/ppermute | solution.py:411
  32.8 11.5 %copy-start.9 = (bf16[2,1,152,512]{3,2,1,0:T(8,128)(2,1)S(1)}, bf16[2,1,152,512]{3,2,1,0:T(8,128)(2,1)}, u32[]{:S(2)}) copy-start(bf16[2,1,152,512]{3,2,1,0:T(8,128)(2,1)} %param.18) | copy-start | bytes 933892
  32.8 49.9 %all-to-all-start.1 = ((bf16[32,32,512]{2,1,0:T(8,128)(2,1)}), bf16[32,32,512]{2,1,0:T(8,128)(2,1)S(1)}, u32[]{:S(2)}, u32[]{:S(2)}) async-start(bf16[32,32,512]{2,1,0:T(8,128)(2,1)} %bitcast.11), calls=%async_computation.1 | async-start | bytes 2097152 | tf_op jit(solution)/shard_map/all_to_all | solution.py:45
  44.3 9.8 %collective-permute-start.3 = (bf16[304,512]{1,0:T(8,128)(2,1)S(1)}, bf16[304,512]{1,0:T(8,128)(2,1)S(1)}, u32[]{:S(2)}, u32[]{:S(2)}) collective-permute-start(bf16[304,512]{1,0:T(8,128)(2,1)S(1)} %bitcast.106), channel_id=1, source_target_pairs={{0,6},{2,0},{4,2},{6,4},{1,7},{3,1},{5,3},{7,5},{8,14},{10,8},{12,... | collective-permute-start | bytes 933896 | tf_op jit(solution)/shard_map/ppermute | solution.py:445
  46.2 28.1 %collective-permute-start.2 = (bf16[304,512]{1,0:T(8,128)(2,1)S(1)}, bf16[304,512]{1,0:T(8,128)(2,1)S(1)}, u32[]{:S(2)}, u32[]{:S(2)}) collective-permute-start(bf16[304,512]{1,0:T(8,128)(2,1)S(1)} %bitcast.107), channel_id=1, source_target_pairs={{0,4},{2,6},{4,0},{6,2},{1,5},{3,7},{5,1},{7,3},{8,12},{10,14},{12... | collective-permute-start | bytes 933896 | tf_op jit(solution)/shard_map/ppermute | solution.py:445
  49.7 24.6 %collective-permute-start.1 = (bf16[304,512]{1,0:T(8,128)(2,1)S(1)}, bf16[304,512]{1,0:T(8,128)(2,1)S(1)}, u32[]{:S(2)}, u32[]{:S(2)}) collective-permute-start(bf16[304,512]{1,0:T(8,128)(2,1)S(1)} %bitcast.108), channel_id=1, source_target_pairs={{0,2},{2,4},{4,6},{6,0},{1,3},{3,5},{5,7},{7,1},{8,10},{10,12},{12... | collective-permute-start | bytes 933896 | tf_op jit(solution)/shard_map/ppermute | solution.py:445
  74.3 3.8 %copy-start.12 = (s32[2,1]{0,1:T(1,128)S(1)}, s32[2,1]{0,1:T(1,128)}, u32[]{:S(2)}) copy-start(s32[2,1]{0,1:T(1,128)} %param.19) | copy-start | bytes 28
  74.5 13.4 %copy-start = (bf16[4,304,512]{2,1,0:T(8,128)(2,1)}, bf16[4,304,512]{2,1,0:T(8,128)(2,1)S(1)}, u32[]{:S(2)}) copy-start(bf16[4,304,512]{2,1,0:T(8,128)(2,1)S(1)} %pad_maximum_fusion.mine) | copy-start | bytes 3735556
  74.5 13.4 %collective-permute-start.4 = (bf16[4,304,512]{2,1,0:T(8,128)(2,1)S(1)}, bf16[4,304,512]{2,1,0:T(8,128)(2,1)S(1)}, u32[]{:S(2)}, u32[]{:S(2)}) collective-permute-start(bf16[4,304,512]{2,1,0:T(8,128)(2,1)S(1)} %pad_maximum_fusion.mine), channel_id=1, source_target_pairs={{0,1},{1,0},{2,3},{3,2},{4,5},{5,4},{6,7},{7,6},{8,9},{9,8},{10,11... | collective-permute-start | bytes 3735560 | tf_op jit(solution)/shard_map/ppermute | solution.py:445
  82.7 1.0 copy-start.10
  83.6 24.5 %copy-start.2 = (bf16[2,2,64,512]{3,2,1,0:T(8,128)(2,1)S(1)}, bf16[2,2,64,512]{3,2,1,0:T(8,128)(2,1)}, u32[]{:S(2)}) copy-start(bf16[2,2,64,512]{3,2,1,0:T(8,128)(2,1)} %pad_maximum_fusion.1.rest_0_) | copy-start | bytes 786436
  84.6 9.1 %all-to-all-start.2 = ((f32[8,8,512]{2,1,0:T(8,128)}), f32[8,8,512]{2,1,0:T(8,128)S(1)}, u32[]{:S(2)}, u32[]{:S(2)}) async-start(f32[8,8,512]{2,1,0:T(8,128)} %broadcast_in_dim.68), calls=%async_computation.2 | async-start | bytes 262144 | tf_op jit(solution)/shard_map/all_to_all | solution.py:41
  88.0 29.2 %copy-start.1 = (bf16[4,304,512]{2,1,0:T(8,128)(2,1)}, bf16[4,304,512]{2,1,0:T(8,128)(2,1)S(1)}, u32[]{:S(2)}) copy-start(bf16[4,304,512]{2,1,0:T(8,128)(2,1)S(1)} %collective-permute-done.4.theirs) | copy-start | bytes 3735556
  93.7 0.7 copy-start.7
  96.3 26.7 %all-to-all-start.3 = ((bf16[64,8,256]{2,1,0:T(8,128)(2,1)}), bf16[64,8,256]{2,1,0:T(8,128)(2,1)S(1)}, u32[]{:S(2)}, u32[]{:S(2)}) async-start(bf16[64,8,256]{2,1,0:T(8,128)(2,1)} %get-tuple-element.43), calls=%async_computation.3 | async-start | bytes 524288 | tf_op jit(solution)/shard_map/all_to_all | solution.py:45
  108.1 15.0 %collective-permute-start.7 = (bf16[2,2,64,512]{3,2,1,0:T(8,128)(2,1)S(1)}, bf16[2,2,64,512]{3,2,1,0:T(8,128)(2,1)S(1)}, u32[]{:S(2)}, u32[]{:S(2)}) collective-permute-start(bf16[2,2,64,512]{3,2,1,0:T(8,128)(2,1)S(1)} %copy-done.2), channel_id=1, source_target_pairs={{0,48},{16,0},{32,16},{48,32},{1,49},{17,1},{33,17},{49,33},{2,50}... | collective-permute-start | bytes 786440 | tf_op jit(solution)/shard_map/ppermute | solution.py:445
  112.2 11.4 %collective-permute-start.6 = (bf16[2,2,64,512]{3,2,1,0:T(8,128)(2,1)S(1)}, bf16[2,2,64,512]{3,2,1,0:T(8,128)(2,1)S(1)}, u32[]{:S(2)}, u32[]{:S(2)}) collective-permute-start(bf16[2,2,64,512]{3,2,1,0:T(8,128)(2,1)S(1)} %copy-done.2), channel_id=1, source_target_pairs={{0,32},{16,48},{32,0},{48,16},{1,33},{17,49},{33,1},{49,17},{2,34}... | collective-permute-start | bytes 786440 | tf_op jit(solution)/shard_map/ppermute | solution.py:445
  114.7 16.2 %collective-permute-start.5 = (bf16[2,2,64,512]{3,2,1,0:T(8,128)(2,1)S(1)}, bf16[2,2,64,512]{3,2,1,0:T(8,128)(2,1)S(1)}, u32[]{:S(2)}, u32[]{:S(2)}) collective-permute-start(bf16[2,2,64,512]{3,2,1,0:T(8,128)(2,1)S(1)} %copy-done.2), channel_id=1, source_target_pairs={{0,16},{16,32},{32,48},{48,0},{1,17},{17,33},{33,49},{49,1},{2,18}... | collective-permute-start | bytes 786440 | tf_op jit(solution)/shard_map/ppermute | solution.py:445
  123.0 7.9 %copy-start.3 = (bf16[64,8,256]{2,1,0:T(8,128)(2,1)}, bf16[64,8,256]{2,1,0:T(8,128)(2,1)S(1)}, u32[]{:S(2)}) copy-start(bf16[64,8,256]{2,1,0:T(8,128)(2,1)S(1)} %all-to-all-done.3) | copy-start | bytes 786436
  123.0 7.9 %copy-start.4 = (bf16[2,2,64,512]{3,2,1,0:T(8,128)(2,1)}, bf16[2,2,64,512]{3,2,1,0:T(8,128)(2,1)S(1)}, u32[]{:S(2)}) copy-start(bf16[2,2,64,512]{3,2,1,0:T(8,128)(2,1)S(1)} %collective-permute-done.7.rest_3_) | copy-start | bytes 786436
  123.6 7.3 %copy-start.5 = (bf16[2,2,64,512]{3,2,1,0:T(8,128)(2,1)}, bf16[2,2,64,512]{3,2,1,0:T(8,128)(2,1)S(1)}, u32[]{:S(2)}) copy-start(bf16[2,2,64,512]{3,2,1,0:T(8,128)(2,1)S(1)} %collective-permute-done.6.rest_2_) | copy-start | bytes 786436
  130.9 0.7 copy-start.6
  151.8 9.5 %copy-start.8 = (bf16[8,8,4,896]{3,2,1,0:T(4,128)(2,1)S(1)}, bf16[8,8,4,896]{3,2,1,0:T(4,128)(2,1)}, u32[]{:S(2)}) copy-start(bf16[8,8,4,896]{3,2,1,0:T(4,128)(2,1)} %get-tuple-element.57) | copy-start | bytes 1376260
  157.3 25.2 %collective-permute-start.8 = (bf16[4,304,512]{2,1,0:T(8,128)(2,1)}, bf16[4,304,512]{2,1,0:T(8,128)(2,1)S(1)}, u32[]{:S(2)}, u32[]{:S(2)}) collective-permute-start(bf16[4,304,512]{2,1,0:T(8,128)(2,1)} %get-tuple-element.61), channel_id=1, source_target_pairs={{0,1},{1,0},{2,3},{3,2},{4,5},{5,4},{6,7},{7,6},{8,9},{9,8},{10,11... | collective-permute-start | bytes 3735560 | tf_op jit(solution)/shard_map/ppermute | solution.py:445
  185.3 19.7 %collective-permute-start.9 = (bf16[304,512]{1,0:T(8,128)(2,1)S(1)}, bf16[304,512]{1,0:T(8,128)(2,1)}, u32[]{:S(2)}, u32[]{:S(2)}) collective-permute-start(bf16[304,512]{1,0:T(8,128)(2,1)S(1)} %get-tuple-element.102), channel_id=1, source_target_pairs={{0,4},{2,6},{4,0},{6,2},{1,5},{3,7},{5,1},{7,3},{8,12},{10,14},{12... | collective-permute-start | bytes 933896 | tf_op jit(solution)/shard_map/ppermute | solution.py:445
  187.2 34.1 %copy-start.11 = (bf16[8,512]{1,0:T(8,128)(2,1)S(1)}, bf16[8,512]{1,0:T(8,128)(2,1)}, u32[]{:S(2)}) copy-start(bf16[8,512]{1,0:T(8,128)(2,1)} %get-tuple-element.70) | copy-start | bytes 24580
  206.7 29.1 %all-to-all-start.7 = ((bf16[64,4,896]{2,1,0:T(4,128)(2,1)}), bf16[64,4,896]{2,1,0:T(4,128)(2,1)S(1)}, u32[]{:S(2)}, u32[]{:S(2)}) async-start(bf16[64,4,896]{2,1,0:T(4,128)(2,1)} %bitcast.103), calls=%async_computation.7 | async-start | bytes 917504 | tf_op jit(solution)/shard_map/all_to_all | solution.py:45
  217.7 8.2 %collective-permute-start.10 = (bf16[8,512]{1,0:T(8,128)(2,1)S(1)}, bf16[8,512]{1,0:T(8,128)(2,1)S(1)}, u32[]{:S(2)}, u32[]{:S(2)}) collective-permute-start(bf16[8,512]{1,0:T(8,128)(2,1)S(1)} %dynamic-slice_bitcast_fusion.1), channel_id=1, source_target_pairs={{0,0},{1,64},{2,128},{3,192},{4,256},{5,320},{6,384},{7,448},{64,1... | collective-permute-start | bytes 24584 | tf_op jit(solution)/shard_map/ppermute | solution.py:513
  225.9 12.5 %collective-permute-start.11 = (bf16[304,512]{1,0:T(8,128)(2,1)}, bf16[304,512]{1,0:T(8,128)(2,1)}, u32[]{:S(2)}, u32[]{:S(2)}) collective-permute-start(bf16[304,512]{1,0:T(8,128)(2,1)} %get-tuple-element.100), channel_id=1, source_target_pairs={{0,2},{2,4},{4,6},{6,0},{1,3},{3,5},{5,7},{7,1},{8,10},{10,12},{12... | collective-permute-start | bytes 933896 | tf_op jit(solution)/shard_map/ppermute | solution.py:445
  230.8 16.0 %collective-permute-start.12 = (bf16[304,512]{1,0:T(8,128)(2,1)}, bf16[304,512]{1,0:T(8,128)(2,1)}, u32[]{:S(2)}, u32[]{:S(2)}) collective-permute-start(bf16[304,512]{1,0:T(8,128)(2,1)} %get-tuple-element.101), channel_id=1, source_target_pairs={{0,6},{2,0},{4,2},{6,4},{1,7},{3,1},{5,3},{7,5},{8,14},{10,8},{12,... | collective-permute-start | bytes 933896 | tf_op jit(solution)/shard_map/ppermute | solution.py:445

commit v8 on v6

--- a/solution.py
+++ b/solution.py
@@ -95,11 +95,26 @@
             chunks[z * plane_count + plane, :, LANES:] = tokens[z]
 
 
-def gradient_kernel(z_count, subs, received, queries, loss, *rest):
-    pieces, (item_out, parts_out) = rest[:-2], rest[-2:]
+def token_kernel(tokens, key_weight, value_weight, down, key_up, value_up, low, keys, values):
+    rank = key_up.shape[0]
+    lows = jnp.dot(tokens[...], down[...], preferred_element_type=jnp.float32)
+    lows = lows.astype(jnp.bfloat16)
+    low[...] = lows
+    for side, (weight, up, out) in enumerate(
+        ((key_weight, key_up, keys), (value_weight, value_up, values))
+    ):
+        base = jnp.dot(tokens[...], weight[...], preferred_element_type=jnp.float32)
+        mine = lows[:, side * rank : (side + 1) * rank]
+        rise = jnp.dot(mine, up[...], preferred_element_type=jnp.float32)
+        out[...] = (base + ADAPTER_SCALE * rise).astype(jnp.bfloat16)
+
+
+def gradient_kernel(
+    z_count, subs, received, queries, loss, wq_plane, wo_plane, item_out, parts_out
+):
     item_rows = item_out.shape[0]
-    count = len(pieces)
-    width = queries.shape[1] // count
+    width = received.shape[1] - LANES
+    count = queries.shape[1] // width
     every = lax.dot_general(
         received[:, :LANES],
         queries[...],
@@ -123,17 +138,12 @@
     plane = lax.axis_index(PLANE)
     first = ((row // subs) * planes + plane) * per_z + row % subs
     attn = query = None
-    for turn, piece in enumerate(pieces):
-        block = lax.rem(lax.axis_index("x") + (count - turn), count)
-        cot = jnp.zeros((picks, width), jnp.float32)
-        for choice in range(count):
-            cot = cot + jnp.where(
-                block == choice, cotangents[:, choice * width : (choice + 1) * width], 0.0
-            )
+    for block in range(count):
+        cot = cotangents[:, block * width : (block + 1) * width]
         chosen = jnp.where(first + block * subs == column, 1.0, 0.0).astype(jnp.bfloat16)
         token = jnp.dot(chosen, received[:, LANES:], preferred_element_type=jnp.float32)
-        wq_rows = jnp.concatenate([piece[half, 0] for half in range(piece.shape[0])], axis=0)
-        wo_rows = jnp.concatenate([piece[half, 1] for half in range(piece.shape[0])], axis=0)
+        rows = slice(block * width, (block + 1) * width)
+        wq_rows, wo_rows = wq_plane[rows], wo_plane[rows]
         attn_term = jnp.dot(cot.astype(jnp.bfloat16), wo_rows, preferred_element_type=jnp.float32)
         query_term = jnp.dot(
             token.astype(jnp.bfloat16), wq_rows, preferred_element_type=jnp.float32
@@ -156,10 +166,9 @@
     value_up,
     reduced,
     tokens,
-    key_weight,
-    value_weight,
-    down,
-    portion_out,
+    key_change_out,
+    value_change_out,
+    coef_out,
     loss_out,
     shares_out,
 ):
@@ -210,6 +219,9 @@
     key_coef = final_product(key_change, key_up[...])
     value_coef = final_product(value_change, value_up[...])
     coef = jnp.concatenate([key_coef, value_coef], axis=1).astype(jnp.bfloat16)
+    key_change_out[...] = key_change
+    value_change_out[...] = value_change
+    coef_out[...] = coef
     rank = key_up.shape[0]
     ups = ADAPTER_SCALE * jnp.concatenate(
         [
@@ -242,19 +254,21 @@
             ].astype(jnp.bfloat16)
             shares_out[z, other, :, width:up_end] = kept_ups[ranks].astype(jnp.bfloat16)
             shares_out[z, other, :, up_end:] = kept_deltas
-    for other in range(mp_count):
-        features = slice(other * width, (other + 1) * width)
-        portion = final_product(key_change, key_weight[features]) + final_product(
-            value_change, value_weight[features]
+
+def portion_kernel(key_change, value_change, coef, key_weight, value_weight, down, out):
+    width = 4 * LANES
+    for start in range(0, out.shape[1], width):
+        features = slice(start, start + width)
+        portion = final_product(key_change[...], key_weight[features]) + final_product(
+            value_change[...], value_weight[features]
         )
         portion = portion + ADAPTER_SCALE * jnp.dot(
-            coef, down[:, features], preferred_element_type=jnp.float32
+            coef[...], down[:, features], preferred_element_type=jnp.float32
         )
-        portion_out[:, features] = portion.astype(jnp.bfloat16)
-
-
-def home_kernel(subs, received, loss, *rest):
-    pieces, (sums_out, last_out) = rest[:-2], rest[-2:]
+        out[:, features] = portion.astype(jnp.bfloat16)
+
+
+def home_kernel(subs, received, loss, wq_plane, sums_out, last_out):
     z_count, mp_count, rows, _ = received.shape
     copies, _, sum_width = sums_out.shape
     sum_width = sum_width - loss.shape[1]
@@ -276,21 +290,9 @@
         sums_out[copy, :, :sum_width] = total
         sums_out[copy, :, sum_width:] = loss[:rows]
     deltas = jnp.concatenate(deltas, axis=0).astype(jnp.bfloat16)
-    count = len(pieces)
-    lasts = []
-    for piece in pieces:
-        wq_rows = jnp.concatenate([piece[half, 0] for half in range(piece.shape[0])], axis=0)
-        lasts.append(final_product(deltas, wq_rows))
-    for choice in range(count):
-        turn = lax.rem(lax.axis_index("x") + (count - choice), count)
-        block = jnp.zeros(lasts[0].shape, jnp.float32)
-        for candidate in range(count):
-            block = block + jnp.where(turn == candidate, lasts[candidate], 0.0)
-        width = block.shape[1]
-        for z in range(z_count):
-            last_out[z, :, choice * width : (choice + 1) * width] = block[
-                z * subs : (z + 1) * subs
-            ]
+    last = final_product(deltas, wq_plane[...])
+    for z in range(z_count):
+        last_out[z] = last[z * subs : (z + 1) * subs]
 
 
 def return_kernel(sums, last, chunks_out, loss_out):
@@ -359,13 +361,18 @@
         other = lax.ppermute(block, "h", [(0, 1), (1, 0)])
         return jnp.stack([jnp.where(lower, block, other), jnp.where(lower, other, block)])
 
-    emb_pair = pair_up(jnp.stack([item_emb, query_emb]))
+    both = pair_up(jnp.stack([w_query, w_out.T]))
+
     pair_rows = 2 * local_rows
-    item_pair = emb_pair[:, 0].reshape(pair_rows, feature_width)
-    query_pair = emb_pair[:, 1].reshape(pair_rows, feature_width)
-    both = pair_up(jnp.stack([w_query, w_out.T]))
-
-    query_slices = spread(query_pair, "mp")
+    emb_pair = spread(jnp.concatenate([item_emb, query_emb], axis=0), ("h", "mp"))
+    emb_pair = emb_pair.reshape(2, mp_count, pair_rows, feature_width)
+    item_pair = lax.dynamic_index_in_dim(
+        emb_pair[:, :, :local_rows], lax.axis_index("mp"), 1, keepdims=False
+    ).reshape(pair_rows, feature_width)
+
+    query_slices = (
+        emb_pair[:, :, local_rows:].transpose(1, 0, 2, 3).reshape(mp_count, pair_rows, -1)
+    )
     both, query_slices = lax.optimization_barrier((both, query_slices))
     chunks = jnp.concatenate(
         [jnp.broadcast_to(item_pair[None], query_slices.shape), query_slices], axis=1
@@ -383,10 +390,10 @@
     score_parts = spread(partial_scores, "mp")
 
     query_width = w_query.shape[1]
-    pieces = [both] + [
-        lax.ppermute(both, "x", [(a, (a + turn) % x_count) for a in range(x_count)])
-        for turn in range(1, x_count)
-    ]
+    both = lax.all_gather(both, "x", axis=0, tiled=False)
+    plane_shape = (feature_width, query_width)
+    wq_plane = both[:, :, 0].reshape(plane_shape)
+    wo_plane = both[:, :, 1].reshape(plane_shape)
 
     last_tokens = jnp.concatenate(
         [
@@ -400,20 +407,6 @@
         .transpose(1, 2, 0, 3)
         .reshape(z_count, x_count * sub_count, feature_width // x_count)
     )
-
-    adapter_rank = key_down_matrix.shape[1]
-    down_both = jnp.concatenate([key_down_matrix, value_down], axis=1)
-    reduced_pair = jnp.dot(token_inputs, down_both, preferred_element_type=f32).astype(bf16)
-    reduced_key = reduced_pair[:, :adapter_rank]
-    reduced_value = reduced_pair[:, adapter_rank:]
-    key_rows = (
-        jnp.dot(token_inputs, key_weight_matrix, preferred_element_type=f32)
-        + ADAPTER_SCALE * jnp.dot(reduced_key, key_up_matrix, preferred_element_type=f32)
-    ).astype(bf16)
-    value_rows = (
-        jnp.dot(token_inputs, value_weight_matrix, preferred_element_type=f32)
-        + ADAPTER_SCALE * jnp.dot(reduced_value, value_up_matrix, preferred_element_type=f32)
-    ).astype(bf16)
 
     chunks, residual, loss_part = call(
         functools.partial(residual_kernel, z_count, plane_count),
@@ -425,6 +418,22 @@
         2**24,
     )(score_parts, hard_index.T, pair_index[None], last_slices)
     column_rows = swap(chunks, DP).reshape(batch_size, 2 * LANES)
+    adapter_rank = key_down_matrix.shape[1]
+    up_width = key_up_matrix.shape[1]
+    down_both = jnp.concatenate([key_down_matrix, value_down], axis=1)
+    late_tokens, residual = lax.optimization_barrier((token_inputs, residual))
+    head_shape = jax.ShapeDtypeStruct((token_count, up_width), bf16)
+    low_shape = jax.ShapeDtypeStruct((token_count, 2 * adapter_rank), bf16)
+    reduced_pair, key_rows, value_rows = call(
+        token_kernel, (low_shape, head_shape, head_shape), 2**30
+    )(
+        late_tokens,
+        key_weight_matrix,
+        value_weight_matrix,
+        down_both,
+        key_up_matrix,
+        value_up_matrix,
+    )
     column_rows, key_rows, value_rows = lax.optimization_barrier(
         (column_rows, key_rows, value_rows)
     )
@@ -435,7 +444,7 @@
             jax.ShapeDtypeStruct((z_count, 2 * sub_count, query_width + LANES), f32),
         ),
         2**26,
-    )(column_rows, queries_all, loss_part, *pieces)
+    )(column_rows, queries_all, loss_part, wq_plane, wo_plane)
     parts = swap(parts, "z")
     own_grads = lax.dynamic_index_in_dim(
         column_grads.reshape(z_count, local_rows, feature_width),
@@ -451,13 +460,14 @@
     query_grad = (jnp.dot(residual, items_all, preferred_element_type=f32) * INV_TEMP).astype(bf16)
 
     share_rows = 2 * adapter_rank // z_count
-    up_width = key_rows.shape[1]
     sum_width = feature_width + up_width
     chunk_width = sum_width + sub_count * query_width // share_rows
-    portion, loss_part, shares = call(
+    key_change, value_change, coef, loss_part, shares = call(
         attention_kernel,
         (
-            jax.ShapeDtypeStruct((token_count, model_width), bf16),
+            head_shape,
+            head_shape,
+            low_shape,
             jax.ShapeDtypeStruct((2 * sub_count, LANES), f32),
             jax.ShapeDtypeStruct((z_count, mp_count, share_rows, chunk_width), bf16),
         ),
@@ -471,13 +481,14 @@
         value_up_matrix,
         reduced_pair,
         token_inputs,
-        key_weight_matrix,
-        value_weight_matrix,
-        down_both.T,
     )
     grid_shape = shares.shape
     shares = swap(shares.reshape((-1,) + grid_shape[2:]), ("z", "mp")).reshape(grid_shape)
 
+    portion = call(portion_kernel, jax.ShapeDtypeStruct((token_count, model_width), bf16), 2**30)(
+        key_change, value_change, coef, key_weight_matrix, value_weight_matrix, down_both.T
+    )
+    shares, portion = lax.optimization_barrier((shares, portion))
     input_sum = lax.psum_scatter(portion, "mp", scatter_dimension=1, tiled=True).astype(f32)
     sums, last_part = call(
         functools.partial(home_kernel, sub_count),
@@ -486,7 +497,7 @@
             jax.ShapeDtypeStruct((z_count, sub_count, feature_width), f32),
         ),
         2**24,
-    )(shares, loss_part, *pieces)
+    )(shares, loss_part, wq_plane)
     chunks, loss_sum = call(
         return_kernel,
         (

time: 230 us -> 228 us (level)
  waiting for transfers between devices: 37.1 us -> 67.4 us
  blocking collectives: 58 us -> 28.2 us
  matrix products: 9.67 us -> 1.01 us
  Pallas kernels: 16.4 us -> 24.8 us
  starting transfers between devices: 66.2 us -> 63.3 us
    all_to_all x3 -> x2, blocking collectives: 58 us -> 28.2 us  [swap(): return lax.all_to_all(blocks, axes, split_axis=0, concat_axis=0, tiled=True)]
    all_to_all x3 -> x4, waiting for transfers between devices: 25.8 us -> 50.4 us  [swap(): return lax.all_to_all(blocks, axes, split_axis=0, concat_axis=0, tiled=True)]
    ppermute x2 -> x1, waiting for transfers between devices: 0.01 us -> 10.9 us  [pair_up(): other = lax.ppermute(block, 'h', [(0, 1), (1, 0)])]
    ppermute x3 -> x0, starting transfers between devices: 9.32 us -> none  [local(): lax.ppermute(both, 'x', [(a, (a + turn) % x_count) for a in range(x_count)])]
    all_to_all x3 -> x4, starting transfers between devices: 26.5 us -> 35.6 us  [swap(): return lax.all_to_all(blocks, axes, split_axis=0, concat_axis=0, tiled=True)]
    dot_general x5 -> x0, matrix products: 8.66 us -> none  [the longest x1 3.16 us: local(): jnp.dot(token_inputs, down_both, preferred_element_type=f32).astype(bf16)]
    pallas_call x1 -> x3, Pallas kernels: 7.55 us -> 16.1 us  [the longest x1 6.74 us: local(): call(token_kernel, (low_shape, head_shape, head_shape), 2 ** 30)]
    ppermute x2 -> x1, starting transfers between devices: 10.2 us -> 7.25 us  [pair_up(): other = lax.ppermute(block, 'h', [(0, 1), (1, 0)])]
  transfers between devices with their start and end apart: 13 -> 11, of which waited for: 5 -> 7; matrix products, arithmetic and copies ran while one was open for 12% -> 8% of each run, Pallas kernels for 3% -> 8%
where the time goes in v8:
time: 228 us; the launch traced here: 227 us
  waiting for transfers between devices  67.4 us (30%)
  starting transfers between devices  63.3 us (28%)
  blocking collectives  28.2 us (12%)
  Pallas kernels  24.8 us (11%)
  between operations  19.7 us (9%)
  local copies, waits for them, and re-layouts  15.8 us (7%)
  other arithmetic  6.58 us (3%)
    all_to_all x4, waiting for transfers between devices, swap(): return lax.all_to_all(blocks, axes, split_axis=0, concat_axis=0, tiled=True)  50.4 us
    all_to_all x4, starting transfers between devices, swap(): return lax.all_to_all(blocks, axes, split_axis=0, concat_axis=0, tiled=True)  35.6 us
    all_to_all x2, blocking collectives, swap(): return lax.all_to_all(blocks, axes, split_axis=0, concat_axis=0, tiled=True)  28.2 us
    all_to_all x2, starting transfers between devices, spread(): return lax.all_to_all(copies, axes, split_axis=0, concat_axis=0, tiled=True)  16.8 us
    ppermute x1, waiting for transfers between devices, pair_up(): other = lax.ppermute(block, 'h', [(0, 1), (1, 0)])  10.9 us
    ppermute x1, starting transfers between devices, pair_up(): other = lax.ppermute(block, 'h', [(0, 1), (1, 0)])  7.25 us
    pallas_call x1, Pallas kernels, local(): call(token_kernel, (low_shape, head_shape, head_shape), 2 ** 30)  6.74 us
    pallas_call x1, Pallas kernels, local(): call(portion_kernel, jax.ShapeDtypeStruct((token_count, model_width), bf1...  5.24 us
  transfers between devices with their start and end apart: 11, of which 7 were waited for; matrix products, arithmetic and copies ran while one was open for 8% of the time, Pallas kernels for 8%

profile of v8, /device:TPU:1, one launch (start us, length us, event | category | flops | bytes accessed | tf_op | source)
XLA Modules:
  0.0 226.8 jit_solution(7573918061520528383)
XLA Ops:
  7.2 0.7 all-gather.4.cloned.1.call-update
  7.9 0.7 pad_maximum_fusion.3
  8.6 0.7 broadcast_in_dim.64
  9.3 10.2 %all-to-all-start = ((bf16[16,16,512]{2,1,0:T(8,128)(2,1)}), bf16[16,16,512]{2,1,0:T(8,128)(2,1)S(1)}, u32[]{:S(2)}, u32[]{:S(2)}) async-start(bf16[16,16,512]{2,1,0:T(8,128)(2,1)} %broadcast_in_dim.64), calls=%async_computation | async-start | bytes 524288 | tf_op jit(solution)/shard_map/all_to_all | solution.py:40
  19.5 0.9 pad_maximum_fusion.2
  20.4 7.2 %collective-permute-start = (bf16[2,64,512]{2,1,0:T(8,128)(2,1)S(1)}, bf16[2,64,512]{2,1,0:T(8,128)(2,1)S(1)}, u32[]{:S(2)}, u32[]{:S(2)}) collective-permute-start(bf16[2,64,512]{2,1,0:T(8,128)(2,1)S(1)} %pad_maximum_fusion.2), channel_id=1, source_target_pairs={{0,8},{8,0},{1,9},{9,1},{2,10},{10,2},{3,11},{11,3},{4,12},{12,4},... | collective-permute-start | bytes 393224 | tf_op jit(solution)/shard_map/ppermute | solution.py:361
  27.7 10.9 %collective-permute-done = bf16[2,64,512]{2,1,0:T(8,128)(2,1)S(1)} collective-permute-done((bf16[2,64,512]{2,1,0:T(8,128)(2,1)S(1)}, bf16[2,64,512]{2,1,0:T(8,128)(2,1)S(1)}, u32[]{:S(2)}, u32[]{:S(2)}) %collective-permute-start) | collective-permute-done | bytes 131104 | tf_op jit(solution)/shard_map/ppermute | solution.py:361
  38.6 0.9 select_bitcast_fusion.1
  39.5 0.7 pad_maximum_fusion
  40.4 1.1 broadcast_in_dim.67
  41.5 12.2 %all-to-all-start.1 = ((bf16[32,32,512]{2,1,0:T(8,128)(2,1)}), bf16[32,32,512]{2,1,0:T(8,128)(2,1)S(1)}, u32[]{:S(2)}, u32[]{:S(2)}) async-start(bf16[32,32,512]{2,1,0:T(8,128)(2,1)} %bitcast.10), calls=%async_computation.1 | async-start | bytes 2097152 | tf_op jit(solution)/shard_map/all_to_all | solution.py:44
  58.3 21.1 %all-to-all-done.1 = bf16[32,32,512]{2,1,0:T(8,128)(2,1)S(1)} async-done(((bf16[32,32,512]{2,1,0:T(8,128)(2,1)}), bf16[32,32,512]{2,1,0:T(8,128)(2,1)S(1)}, u32[]{:S(2)}, u32[]{:S(2)}) %all-to-all-start.1) | async-done | bytes 1048608 | tf_op jit(solution)/shard_map/all_to_all | solution.py:44
  79.4 0.9 fusion.3
  80.6 0.7 broadcast_in_dim.68
  81.3 6.6 %all-to-all-start.2 = ((f32[8,8,512]{2,1,0:T(8,128)}), f32[8,8,512]{2,1,0:T(8,128)S(1)}, u32[]{:S(2)}, u32[]{:S(2)}) async-start(f32[8,8,512]{2,1,0:T(8,128)} %broadcast_in_dim.68), calls=%async_computation.2 | async-start | bytes 262144 | tf_op jit(solution)/shard_map/all_to_all | solution.py:40
  87.9 0.9 constant_dynamic-slice_fusion.1
  88.8 0.6 copy.47
  89.5 4.2 %all-to-all-done.2.parts = f32[8,8,512]{2,1,0:T(8,128)S(1)} async-done(((f32[8,8,512]{2,1,0:T(8,128)}), f32[8,8,512]{2,1,0:T(8,128)S(1)}, u32[]{:S(2)}, u32[]{:S(2)}) %all-to-all-start.2) | async-done | bytes 131104 | tf_op jit(solution)/shard_map/all_to_all | solution.py:40
  93.7 0.7 copy-done.3
  94.3 2.0 shard_map.197
  96.3 8.9 %all-to-all-start.3 = ((bf16[64,8,256]{2,1,0:T(8,128)(2,1)}), bf16[64,8,256]{2,1,0:T(8,128)(2,1)S(1)}, u32[]{:S(2)}, u32[]{:S(2)}) async-start(bf16[64,8,256]{2,1,0:T(8,128)(2,1)} %get-tuple-element.35), calls=%async_computation.3 | async-start | bytes 524288 | tf_op jit(solution)/shard_map/all_to_all | solution.py:44
  105.3 1.3 copy.48.down
  106.6 2.3 %fusion.2 = (bf16[4,2,1,64,512]{4,3,2,1,0:T(8,128)(2,1)}, bf16[4,2,1,64,512]{4,3,2,1,0:T(8,128)(2,1)}) fusion(bf16[4,2,2,64,512]{4,3,2,1,0:T(8,128)(2,1)} %bitcast.90), kind=kLoop, calls=%fused_computation.27 | loop fusion | bytes 2097152 | tf_op jit(solution)/shard_map/slice | solution.py:396
  108.9 6.7 %shard_map.198 = (bf16[304,32]{1,0:T(8,128)(2,1)}, bf16[304,128]{1,0:T(8,128)(2,1)}, bf16[304,128]{1,0:T(8,128)(2,1)}) custom-call(bf16[304,4096]{1,0:T(8,128)(2,1)} %bitcast.73, bf16[4096,128]{1,0:T(8,128)(2,1)} %key_weight.3, bf16[4096,128]{1,0:T(8,128)(2,1)} %value_weight.3, bf16[4096,32]{1,0:T(8,128)(2,1)} %copy.48.down, bf16[16,128]{1,0:T(8,128)(2,1)} %key_up.3, ...), custom_call_target="tpu_custom_call" | custom-call | flops 1073741824 | bytes 1048576 | tf_op jit(solution)/shard_map/pallas_call | solution.py:427
  115.6 3.7 %all-to-all-done.3 = bf16[64,8,256]{2,1,0:T(8,128)(2,1)S(1)} async-done(((bf16[64,8,256]{2,1,0:T(8,128)(2,1)}), bf16[64,8,256]{2,1,0:T(8,128)(2,1)S(1)}, u32[]{:S(2)}, u32[]{:S(2)}) %all-to-all-start.3) | async-done | bytes 262176 | tf_op jit(solution)/shard_map/all_to_all | solution.py:44
  119.3 0.7 copy-done.2
  120.0 2.9 %shard_map.199 = (bf16[64,512]{1,0:T(8,128)(2,1)}, f32[8,4,640]{2,1,0:T(4,128)}) custom-call(bf16[512,256]{1,0:T(8,128)(2,1)} %bitcast.89, bf16[512,512]{1,0:T(8,128)(2,1)} %bitcast.79, f32[8,128]{1,0:T(8,128)} %get-tuple-element.41.loss, bf16[512,512]{1,0:T(8,128)(2,1)} %bitcast.77, bf16[512,512]{1,0:T(8,128)(2,1)} %bitcast.80), custom_call_target="tpu_custom_call" | custom-call | flops 67108864 | bytes 1048576 | tf_op jit(solution)/shard_map/pallas_call | solution.py:440
  122.9 11.4 %all_to_all.40.parts = f32[8,4,640]{2,1,0:T(4,128)} all-to-all(f32[8,4,640]{2,1,0:T(4,128)} %get-tuple-element.43), channel_id=1, replica_groups=mesh['z'=8,'x'=4,'h'=2,'mp'=8] {'z'}, dimensions={0} | all-to-all | bytes 163840 | tf_op jit(solution)/shard_map/all_to_all | solution.py:44
  134.3 4.1 %shard_map.200 = (bf16[304,128]{1,0:T(8,128)(2,1)}, bf16[304,128]{1,0:T(8,128)(2,1)}, bf16[304,32]{1,0:T(8,128)(2,1)}, f32[4,128]{1,0:T(4,128)}, bf16[8,8,4,896]{3,2,1,0:T(4,128)(2,1)}) custom-call(s32[1,2]{1,0:T(1,128)} %bitcast.109, f32[8,4,640]{2,1,0:T(4,128)} %all_to_all.40.parts, bf16[304,128]{1,0:T(8,128)(2,1)} %get-tuple-element.44.keys, ...), custom_call_target="tpu_custom_call" | custom-call | flops 67108864 | bytes 1048576 | tf_op jit(solution)/shard_map/pallas_call | solution.py:465
  138.4 8.8 %all-to-all-start.5 = ((bf16[64,4,896]{2,1,0:T(4,128)(2,1)}), bf16[64,4,896]{2,1,0:T(4,128)(2,1)S(1)}, u32[]{:S(2)}, u32[]{:S(2)}) async-start(bf16[64,4,896]{2,1,0:T(4,128)(2,1)} %bitcast.94), calls=%async_computation.5 | async-start | bytes 917504 | tf_op jit(solution)/shard_map/all_to_all | solution.py:44
  147.3 5.2 %shard_map.201 = bf16[304,4096]{1,0:T(8,128)(2,1)} custom-call(bf16[304,128]{1,0:T(8,128)(2,1)} %get-tuple-element.48.key_change, bf16[304,128]{1,0:T(8,128)(2,1)} %get-tuple-element.49.value_change, bf16[304,32]{1,0:T(8,128)(2,1)} %get-tuple-element.50.coef, bf16[4096,128]{1,0:T(8,128)(2,1)} %key_weight.3, bf16[4096,128]{1,0:T(8,128)(2,1)} %value_weight.3, ...), custom_call_target="tpu_custom_call" | custom-call | flops 1073741824 | bytes 1048576 | tf_op jit(solution)/shard_map/pallas_call | solution.py:488
  152.5 12.0 %all-to-all-done.5 = bf16[64,4,896]{2,1,0:T(4,128)(2,1)S(1)} async-done(((bf16[64,4,896]{2,1,0:T(4,128)(2,1)}), bf16[64,4,896]{2,1,0:T(4,128)(2,1)S(1)}, u32[]{:S(2)}, u32[]{:S(2)}) %all-to-all-start.5) | async-done | bytes 458784 | tf_op jit(solution)/shard_map/all_to_all | solution.py:44
  164.5 0.7 copy-done
  165.3 2.1 shard_map.202
  167.3 16.9 %all_to_all.41.sums = f32[8,4,768]{2,1,0:T(4,128)} all-to-all(f32[8,4,768]{2,1,0:T(4,128)} %get-tuple-element.53), channel_id=1, replica_groups=mesh['z'=8,'x'=4,'h'=2,'mp'=8] {'x','h'}, dimensions={0} | all-to-all | bytes 196608 | tf_op jit(solution)/shard_map/all_to_all | solution.py:44
  184.2 1.7 shard_map.203
  185.9 5.7 %all-to-all-start.7 = ((bf16[64,4,896]{2,1,0:T(4,128)(2,1)}), bf16[64,4,896]{2,1,0:T(4,128)(2,1)S(1)}, u32[]{:S(2)}, u32[]{:S(2)}) async-start(bf16[64,4,896]{2,1,0:T(4,128)(2,1)} %bitcast.93), calls=%async_computation.8 | async-start | bytes 917504 | tf_op jit(solution)/shard_map/all_to_all | solution.py:44
  191.6 1.3 iota_compare_fusion
  192.9 0.7 dynamic-slice_bitcast_fusion.1
  193.6 3.6 %collective-permute-start.1 = (bf16[8,512]{1,0:T(8,128)(2,1)S(1)}, bf16[8,512]{1,0:T(8,128)(2,1)S(1)}, u32[]{:S(2)}, u32[]{:S(2)}) collective-permute-start(bf16[8,512]{1,0:T(8,128)(2,1)S(1)} %dynamic-slice_bitcast_fusion.1), channel_id=1, source_target_pairs={{0,0},{1,64},{2,128},{3,192},{4,256},{5,320},{6,384},{7,448},{64,1... | collective-permute-start | bytes 24584 | tf_op jit(solution)/shard_map/ppermute | solution.py:455
  197.2 0.8 fusion
  198.0 1.1 collective-permute-done.1
  199.1 1.2 slice.73
  201.0 13.6 %all-to-all-done.7 = bf16[64,4,896]{2,1,0:T(4,128)(2,1)S(1)} async-done(((bf16[64,4,896]{2,1,0:T(4,128)(2,1)}), bf16[64,4,896]{2,1,0:T(4,128)(2,1)S(1)}, u32[]{:S(2)}, u32[]{:S(2)}) %all-to-all-start.7) | async-done | bytes 458784 | tf_op jit(solution)/shard_map/all_to_all | solution.py:44
  215.3 0.6 fusion.6
  215.9 0.8 fusion.4
  216.7 1.9 add_convert_fusion
  218.6 0.6 copy.65
  (47 shorter events, 1.8 us)
Async XLA Ops:
  7.2 80.7 %all-gather.4.cloned.1.call-start = ((), (), s32[]{:S(2)}) async-start(), calls=%async_computation.9 | async-start | bytes 2801664 | tf_op jit(solution)/shard_map/all_gather | solution.py:352
  9.3 30.9 %all-to-all-start = ((bf16[16,16,512]{2,1,0:T(8,128)(2,1)}), bf16[16,16,512]{2,1,0:T(8,128)(2,1)S(1)}, u32[]{:S(2)}, u32[]{:S(2)}) async-start(bf16[16,16,512]{2,1,0:T(8,128)(2,1)} %broadcast_in_dim.64), calls=%async_computation | async-start | bytes 524288 | tf_op jit(solution)/shard_map/all_to_all | solution.py:40
  20.4 18.2 %collective-permute-start = (bf16[2,64,512]{2,1,0:T(8,128)(2,1)S(1)}, bf16[2,64,512]{2,1,0:T(8,128)(2,1)S(1)}, u32[]{:S(2)}, u32[]{:S(2)}) collective-permute-start(bf16[2,64,512]{2,1,0:T(8,128)(2,1)S(1)} %pad_maximum_fusion.2), channel_id=1, source_target_pairs={{0,8},{8,0},{1,9},{9,1},{2,10},{10,2},{3,11},{11,3},{4,12},{12,4},... | collective-permute-start | bytes 393224 | tf_op jit(solution)/shard_map/ppermute | solution.py:361
  40.3 13.5 %copy-start.8 = (s32[2,1]{0,1:T(1,128)S(1)}, s32[2,1]{0,1:T(1,128)}, u32[]{:S(2)}) copy-start(s32[2,1]{0,1:T(1,128)} %param.19) | copy-start | bytes 28
  40.3 18.0 %copy-start.4 = (bf16[4096,16]{0,1:T(8,128)(2,1)S(1)}, bf16[4096,16]{0,1:T(8,128)(2,1)}, u32[]{:S(2)}) copy-start(bf16[4096,16]{0,1:T(8,128)(2,1)} %param.24) | copy-start | bytes 393220
  41.5 38.9 %copy-start.6 = (bf16[8,512]{1,0:T(8,128)(2,1)S(1)}, bf16[8,512]{1,0:T(8,128)(2,1)}, u32[]{:S(2)}) copy-start(bf16[8,512]{1,0:T(8,128)(2,1)} %param.14) | copy-start | bytes 24580
  41.5 37.9 %all-to-all-start.1 = ((bf16[32,32,512]{2,1,0:T(8,128)(2,1)}), bf16[32,32,512]{2,1,0:T(8,128)(2,1)S(1)}, u32[]{:S(2)}, u32[]{:S(2)}) async-start(bf16[32,32,512]{2,1,0:T(8,128)(2,1)} %bitcast.10), calls=%async_computation.1 | async-start | bytes 2097152 | tf_op jit(solution)/shard_map/all_to_all | solution.py:44
  53.7 52.9 %all-gather.6.cloned.1.call-start = ((), (), s32[]{:S(2)}) async-start(), calls=%async_computation.11 | async-start | bytes 1310720 | tf_op jit(solution)/shard_map/all_gather | solution.py:393
  58.3 46.9 %copy-start.5 = (bf16[4096,16]{0,1:T(8,128)(2,1)S(1)}, bf16[4096,16]{0,1:T(8,128)(2,1)}, u32[]{:S(2)}) copy-start(bf16[4096,16]{0,1:T(8,128)(2,1)} %param.26) | copy-start | bytes 393220
  81.3 12.4 %all-to-all-start.2 = ((f32[8,8,512]{2,1,0:T(8,128)}), f32[8,8,512]{2,1,0:T(8,128)S(1)}, u32[]{:S(2)}, u32[]{:S(2)}) async-start(f32[8,8,512]{2,1,0:T(8,128)} %broadcast_in_dim.68), calls=%async_computation.2 | async-start | bytes 262144 | tf_op jit(solution)/shard_map/all_to_all | solution.py:40
  93.7 0.7 copy-start.3
  96.3 23.0 %all-to-all-start.3 = ((bf16[64,8,256]{2,1,0:T(8,128)(2,1)}), bf16[64,8,256]{2,1,0:T(8,128)(2,1)S(1)}, u32[]{:S(2)}, u32[]{:S(2)}) async-start(bf16[64,8,256]{2,1,0:T(8,128)(2,1)} %get-tuple-element.35), calls=%async_computation.3 | async-start | bytes 524288 | tf_op jit(solution)/shard_map/all_to_all | solution.py:44
  105.2 10.4 %copy-start.1 = (bf16[4096,32]{0,1:T(8,128)(2,1)}, bf16[4096,32]{0,1:T(8,128)(2,1)S(1)}, u32[]{:S(2)}) copy-start(bf16[4096,32]{0,1:T(8,128)(2,1)S(1)} %constant_dynamic-update-slice_fusion) | copy-start | bytes 786436
  119.3 0.7 copy-start.2
  138.4 26.1 %all-to-all-start.5 = ((bf16[64,4,896]{2,1,0:T(4,128)(2,1)}), bf16[64,4,896]{2,1,0:T(4,128)(2,1)S(1)}, u32[]{:S(2)}, u32[]{:S(2)}) async-start(bf16[64,4,896]{2,1,0:T(4,128)(2,1)} %bitcast.94), calls=%async_computation.5 | async-start | bytes 917504 | tf_op jit(solution)/shard_map/all_to_all | solution.py:44
  147.2 69.5 %reduce-scatter.2.cloned.1.call-start = ((), (), s32[]{:S(2)}) async-start(), calls=%async_computation.10 | async-start | bytes 2801664 | tf_op jit(solution)/shard_map/reduce_scatter | solution.py:492
  152.5 44.7 %copy-start.7 = (bf16[8,512]{1,0:T(8,128)(2,1)S(1)}, bf16[8,512]{1,0:T(8,128)(2,1)}, u32[]{:S(2)}) copy-start(bf16[8,512]{1,0:T(8,128)(2,1)} %get-tuple-element.56) | copy-start | bytes 24580
  164.5 0.8 copy-start
  185.9 28.7 %all-to-all-start.7 = ((bf16[64,4,896]{2,1,0:T(4,128)(2,1)}), bf16[64,4,896]{2,1,0:T(4,128)(2,1)S(1)}, u32[]{:S(2)}, u32[]{:S(2)}) async-start(bf16[64,4,896]{2,1,0:T(4,128)(2,1)} %bitcast.93), calls=%async_computation.8 | async-start | bytes 917504 | tf_op jit(solution)/shard_map/all_to_all | solution.py:44
  193.6 5.5 %collective-permute-start.1 = (bf16[8,512]{1,0:T(8,128)(2,1)S(1)}, bf16[8,512]{1,0:T(8,128)(2,1)S(1)}, u32[]{:S(2)}, u32[]{:S(2)}) collective-permute-start(bf16[8,512]{1,0:T(8,128)(2,1)S(1)} %dynamic-slice_bitcast_fusion.1), channel_id=1, source_target_pairs={{0,0},{1,64},{2,128},{3,192},{4,256},{5,320},{6,384},{7,448},{64,1... | collective-permute-start | bytes 24584 | tf_op jit(solution)/shard_map/ppermute | solution.py:455
Sparse Core Ops, SparseCore 0:
  10.1 49.1 all-gather.3
  62.0 30.3 all-gather.5
  164.7 41.7 reduce-scatter.1

commit v9 on v8

--- a/solution.py
+++ b/solution.py
@@ -355,31 +355,31 @@
     seq_lengths = lengths[:, 0]
     last_rows = jnp.arange(sub_count, dtype=jnp.int32) * seq_len + seq_lengths - 1
 
-    lower = lax.axis_index("h") == 0
-
-    def pair_up(block):
-        other = lax.ppermute(block, "h", [(0, 1), (1, 0)])
-        return jnp.stack([jnp.where(lower, block, other), jnp.where(lower, other, block)])
-
-    both = pair_up(jnp.stack([w_query, w_out.T]))
-
+    core = lax.rem(lax.axis_index("mp"), 2)
     pair_rows = 2 * local_rows
     emb_pair = spread(jnp.concatenate([item_emb, query_emb], axis=0), ("h", "mp"))
     emb_pair = emb_pair.reshape(2, mp_count, pair_rows, feature_width)
     item_pair = lax.dynamic_index_in_dim(
         emb_pair[:, :, :local_rows], lax.axis_index("mp"), 1, keepdims=False
     ).reshape(pair_rows, feature_width)
-
-    query_slices = (
-        emb_pair[:, :, local_rows:].transpose(1, 0, 2, 3).reshape(mp_count, pair_rows, -1)
-    )
+    query_slices = lax.dynamic_index_in_dim(
+        emb_pair[:, :, local_rows:], core, 0, keepdims=False
+    )
+    both = jnp.stack([w_query, w_out.T])
     both, query_slices = lax.optimization_barrier((both, query_slices))
-    chunks = jnp.concatenate(
-        [jnp.broadcast_to(item_pair[None], query_slices.shape), query_slices], axis=1
-    )
+    item_copies = jnp.broadcast_to(item_pair[None], (mp_count,) + item_pair.shape)
+    chunks = jnp.concatenate([item_copies, query_slices], axis=1)
     chunks = jnp.broadcast_to(chunks[:, None], (z_count, x_count) + chunks.shape[1:])
     received = swap(chunks.reshape((z_count * x_count,) + chunks.shape[2:]), ("z", "x"))
-    queries_all = received[:, pair_rows:].reshape(batch_size, feature_width)
+    query_half = received[:, pair_rows:]
+    other_half = lax.ppermute(query_half, "mp", [(a, a ^ 1) for a in range(mp_count)])
+    queries_all = jnp.stack(
+        [
+            jnp.where(core == 0, query_half, other_half),
+            jnp.where(core == 0, other_half, query_half),
+        ],
+        axis=1,
+    ).reshape(batch_size, feature_width)
     items_all = (
         received[:, :pair_rows]
         .reshape(z_count, plane_count, local_rows, feature_width)
@@ -390,6 +390,9 @@
     score_parts = spread(partial_scores, "mp")
 
     query_width = w_query.shape[1]
+    other = lax.ppermute(both, "h", [(0, 1), (1, 0)])
+    lower = lax.axis_index("h") == 0
+    both = jnp.stack([jnp.where(lower, both, other), jnp.where(lower, other, both)])
     both = lax.all_gather(both, "x", axis=0, tiled=False)
     plane_shape = (feature_width, query_width)
     wq_plane = both[:, :, 0].reshape(plane_shape)

time: 228 us -> 219 us (0.961)
  waiting for transfers between devices: 67.4 us -> 59.1 us
  starting transfers between devices: 63.3 us -> 57.9 us
  blocking collectives: 28.2 us -> 33.1 us
    all_to_all x4, waiting for transfers between devices: 50.4 us -> 28.8 us  [swap(): return lax.all_to_all(blocks, axes, split_axis=0, concat_axis=0, tiled=True)]
    all_to_all x2, waiting for transfers between devices: 4.24 us -> 15.1 us  [spread(): return lax.all_to_all(copies, axes, split_axis=0, concat_axis=0, tiled=True)]
    all_to_all x2, blocking collectives: 28.2 us -> 33.1 us  [swap(): return lax.all_to_all(blocks, axes, split_axis=0, concat_axis=0, tiled=True)]
    all_gather x1, waiting for transfers between devices: 0.01 us -> 3.37 us  [local(): both = lax.all_gather(both, 'x', axis=0, tiled=False)]
    all_to_all x2, starting transfers between devices: 16.8 us -> 13.7 us  [spread(): return lax.all_to_all(copies, axes, split_axis=0, concat_axis=0, tiled=True)]
    ppermute x1 -> x2, waiting for transfers between devices: 10.9 us -> 9.91 us  [the longest x1 9.9 us: local(): other = lax.ppermute(both, 'h', [(0, 1), (1, 0)])]
    ppermute x1 -> x2, starting transfers between devices: 7.25 us -> 6.22 us  [the longest x1 3.28 us: local(): lax.ppermute(query_half, 'mp', [(a, a ^ 1) for a in range(mp_count)])]
  transfers between devices with their start and end apart: 11 -> 12, of which waited for: 7 -> 9; matrix products, arithmetic and copies ran while one was open for 8% -> 8% of each run, Pallas kernels for 8% -> 8%
where the time goes in v9:
time: 219 us; the launch traced here: 217 us
  waiting for transfers between devices  59.1 us (27%)
  starting transfers between devices  57.9 us (26%)
  blocking collectives  33.1 us (15%)
  Pallas kernels  24.8 us (11%)
  between operations  19.8 us (9%)
  local copies, waits for them, and re-layouts  15.7 us (7%)
  other arithmetic  5.83 us (3%)
    all_to_all x4, starting transfers between devices, swap(): return lax.all_to_all(blocks, axes, split_axis=0, concat_axis=0, tiled=True)  34.3 us
    all_to_all x2, blocking collectives, swap(): return lax.all_to_all(blocks, axes, split_axis=0, concat_axis=0, tiled=True)  33.1 us
    all_to_all x4, waiting for transfers between devices, swap(): return lax.all_to_all(blocks, axes, split_axis=0, concat_axis=0, tiled=True)  28.8 us
    all_to_all x2, waiting for transfers between devices, spread(): return lax.all_to_all(copies, axes, split_axis=0, concat_axis=0, tiled=True)  15.1 us
    all_to_all x2, starting transfers between devices, spread(): return lax.all_to_all(copies, axes, split_axis=0, concat_axis=0, tiled=True)  13.7 us
    ppermute x1, waiting for transfers between devices, local(): other = lax.ppermute(both, 'h', [(0, 1), (1, 0)])  9.9 us
    pallas_call x1, Pallas kernels, local(): call(token_kernel, (low_shape, head_shape, head_shape), 2 ** 30)  6.74 us
    pallas_call x1, Pallas kernels, local(): call(portion_kernel, jax.ShapeDtypeStruct((token_count, model_width), bf1...  5.24 us
  transfers between devices with their start and end apart: 12, of which 9 were waited for; matrix products, arithmetic and copies ran while one was open for 8% of the time, Pallas kernels for 8%

profile of v9, /device:TPU:1, one launch (start us, length us, event | category | flops | bytes accessed | tf_op | source)
XLA Modules:
  0.0 217.2 jit_solution(406647600192628657)
XLA Ops:
  7.2 0.7 all-gather.4.cloned.1.call-update
  7.9 0.8 pad_maximum_fusion.4
  8.7 0.7 broadcast_in_dim.64
  9.4 10.3 %all-to-all-start = ((bf16[16,16,512]{2,1,0:T(8,128)(2,1)}), bf16[16,16,512]{2,1,0:T(8,128)(2,1)S(1)}, u32[]{:S(2)}, u32[]{:S(2)}) async-start(bf16[16,16,512]{2,1,0:T(8,128)(2,1)} %broadcast_in_dim.64), calls=%async_computation | async-start | bytes 524288 | tf_op jit(solution)/shard_map/all_to_all | solution.py:40
  19.7 0.9 pad_maximum_fusion.3
  20.6 11.0 %all-to-all-done = bf16[16,16,512]{2,1,0:T(8,128)(2,1)S(1)} async-done(((bf16[16,16,512]{2,1,0:T(8,128)(2,1)}), bf16[16,16,512]{2,1,0:T(8,128)(2,1)S(1)}, u32[]{:S(2)}, u32[]{:S(2)}) %all-to-all-start) | async-done | bytes 262176 | tf_op jit(solution)/shard_map/all_to_all | solution.py:40
  31.7 1.0 broadcast_in_dim.67
  32.7 11.2 %all-to-all-start.1 = ((bf16[32,24,512]{2,1,0:T(8,128)(2,1)}), bf16[32,24,512]{2,1,0:T(8,128)(2,1)S(1)}, u32[]{:S(2)}, u32[]{:S(2)}) async-start(bf16[32,24,512]{2,1,0:T(8,128)(2,1)} %bitcast.7), calls=%async_computation.1 | async-start | bytes 1572864 | tf_op jit(solution)/shard_map/all_to_all | solution.py:44
  43.9 2.9 %collective-permute-start.1 = (bf16[2,64,512]{2,1,0:T(8,128)(2,1)S(1)}, bf16[2,64,512]{2,1,0:T(8,128)(2,1)S(1)}, u32[]{:S(2)}, u32[]{:S(2)}) collective-permute-start(bf16[2,64,512]{2,1,0:T(8,128)(2,1)S(1)} %pad_maximum_fusion.3), channel_id=1, source_target_pairs={{0,8},{8,0},{1,9},{9,1},{2,10},{10,2},{3,11},{11,3},{4,12},{12,4},... | collective-permute-start | bytes 393224 | tf_op jit(solution)/shard_map/ppermute | solution.py:393
  50.1 9.9 %collective-permute-done.1 = bf16[2,64,512]{2,1,0:T(8,128)(2,1)S(1)} collective-permute-done((bf16[2,64,512]{2,1,0:T(8,128)(2,1)S(1)}, bf16[2,64,512]{2,1,0:T(8,128)(2,1)S(1)}, u32[]{:S(2)}, u32[]{:S(2)}) %collective-permute-start.1) | collective-permute-done | bytes 131104 | tf_op jit(solution)/shard_map/ppermute | solution.py:393
  60.0 0.7 pad_maximum_fusion.1
  60.8 1.3 copy.49.down
  63.5 2.5 %all-to-all-done.1 = bf16[32,24,512]{2,1,0:T(8,128)(2,1)S(1)} async-done(((bf16[32,24,512]{2,1,0:T(8,128)(2,1)}), bf16[32,24,512]{2,1,0:T(8,128)(2,1)S(1)}, u32[]{:S(2)}, u32[]{:S(2)}) %all-to-all-start.1) | async-done | bytes 786464 | tf_op jit(solution)/shard_map/all_to_all | solution.py:44
  66.0 3.3 %collective-permute-start = (bf16[32,8,512]{2,1,0:T(8,128)(2,1)S(1)}, bf16[32,8,512]{2,1,0:T(8,128)(2,1)S(1)}, u32[]{:S(2)}, u32[]{:S(2)}) collective-permute-start(bf16[32,8,512]{2,1,0:T(8,128)(2,1)S(1)} %slice.89), channel_id=1, source_target_pairs={{0,1},{1,0},{2,3},{3,2},{4,5},{5,4},{6,7},{7,6},{8,9},{9,8},{10,11... | collective-permute-start | bytes 786440 | tf_op jit(solution)/shard_map/ppermute | solution.py:375
  69.6 0.7 broadcast_in_dim.68
  70.3 3.3 %all-to-all-start.2 = ((f32[8,8,512]{2,1,0:T(8,128)}), f32[8,8,512]{2,1,0:T(8,128)S(1)}, u32[]{:S(2)}, u32[]{:S(2)}) async-start(f32[8,8,512]{2,1,0:T(8,128)} %broadcast_in_dim.68), calls=%async_computation.2 | async-start | bytes 262144 | tf_op jit(solution)/shard_map/all_to_all | solution.py:40
  73.7 0.9 constant_dynamic-slice_fusion.1
  74.7 0.6 copy.48
  75.3 4.2 %all-to-all-done.2.parts = f32[8,8,512]{2,1,0:T(8,128)S(1)} async-done(((f32[8,8,512]{2,1,0:T(8,128)}), f32[8,8,512]{2,1,0:T(8,128)S(1)}, u32[]{:S(2)}, u32[]{:S(2)}) %all-to-all-start.2) | async-done | bytes 131104 | tf_op jit(solution)/shard_map/all_to_all | solution.py:40
  79.4 0.6 copy-done.3
  80.1 2.0 shard_map.197
  82.1 8.9 %all-to-all-start.3 = ((bf16[64,8,256]{2,1,0:T(8,128)(2,1)}), bf16[64,8,256]{2,1,0:T(8,128)(2,1)S(1)}, u32[]{:S(2)}, u32[]{:S(2)}) async-start(bf16[64,8,256]{2,1,0:T(8,128)(2,1)} %get-tuple-element.35), calls=%async_computation.3 | async-start | bytes 524288 | tf_op jit(solution)/shard_map/all_to_all | solution.py:44
  91.0 3.4 %all-gather.6.cloned.1.call-done = bf16[8,2,64,512]{3,2,1,0:T(8,128)(2,1)} async-done(((bf16[2,2,64,512]{3,2,1,0:T(8,128)(2,1)}), bf16[8,2,64,512]{3,2,1,0:T(8,128)(2,1)}) %all-gather.6.cloned.1.call-update) | async-done | bytes 1048592 | tf_op jit(solution)/shard_map/all_gather | solution.py:396
  94.4 2.3 %fusion.2 = (bf16[4,2,1,64,512]{4,3,2,1,0:T(8,128)(2,1)}, bf16[4,2,1,64,512]{4,3,2,1,0:T(8,128)(2,1)}) fusion(bf16[4,2,2,64,512]{4,3,2,1,0:T(8,128)(2,1)} %bitcast.91), kind=kLoop, calls=%fused_computation.29 | loop fusion | bytes 2097152 | tf_op jit(solution)/shard_map/slice | solution.py:399
  96.7 0.9 copy.50
  97.6 6.7 %shard_map.198 = (bf16[304,32]{1,0:T(8,128)(2,1)}, bf16[304,128]{1,0:T(8,128)(2,1)}, bf16[304,128]{1,0:T(8,128)(2,1)}) custom-call(bf16[304,4096]{1,0:T(8,128)(2,1)} %bitcast.74, bf16[4096,128]{1,0:T(8,128)(2,1)} %key_weight.3, bf16[4096,128]{1,0:T(8,128)(2,1)} %value_weight.3, bf16[4096,32]{1,0:T(8,128)(2,1)} %copy.49.down, bf16[16,128]{1,0:T(8,128)(2,1)} %key_up.3, ...), custom_call_target="tpu_custom_call" | custom-call | flops 1073741824 | bytes 1048576 | tf_op jit(solution)/shard_map/pallas_call | solution.py:430
  104.3 0.7 all-to-all-done.3
  105.1 0.7 copy-done.2
  105.8 2.9 %shard_map.199 = (bf16[64,512]{1,0:T(8,128)(2,1)}, f32[8,4,640]{2,1,0:T(4,128)}) custom-call(bf16[512,256]{1,0:T(8,128)(2,1)} %bitcast.90, bf16[512,512]{1,0:T(8,128)(2,1)} %bitcast.80, f32[8,128]{1,0:T(8,128)} %get-tuple-element.41.loss, bf16[512,512]{1,0:T(8,128)(2,1)} %bitcast.78, bf16[512,512]{1,0:T(8,128)(2,1)} %bitcast.81), custom_call_target="tpu_custom_call" | custom-call | flops 67108864 | bytes 1048576 | tf_op jit(solution)/shard_map/pallas_call | solution.py:443
  108.7 14.3 %all_to_all.40.parts = f32[8,4,640]{2,1,0:T(4,128)} all-to-all(f32[8,4,640]{2,1,0:T(4,128)} %get-tuple-element.43), channel_id=1, replica_groups=mesh['z'=8,'x'=4,'h'=2,'mp'=8] {'z'}, dimensions={0} | all-to-all | bytes 163840 | tf_op jit(solution)/shard_map/all_to_all | solution.py:44
  123.0 4.1 %shard_map.200 = (bf16[304,128]{1,0:T(8,128)(2,1)}, bf16[304,128]{1,0:T(8,128)(2,1)}, bf16[304,32]{1,0:T(8,128)(2,1)}, f32[4,128]{1,0:T(4,128)}, bf16[8,8,4,896]{3,2,1,0:T(4,128)(2,1)}) custom-call(s32[1,2]{1,0:T(1,128)} %bitcast.107, f32[8,4,640]{2,1,0:T(4,128)} %all_to_all.40.parts, bf16[304,128]{1,0:T(8,128)(2,1)} %get-tuple-element.44.keys, ...), custom_call_target="tpu_custom_call" | custom-call | flops 67108864 | bytes 1048576 | tf_op jit(solution)/shard_map/pallas_call | solution.py:468
  127.1 8.5 %all-to-all-start.5 = ((bf16[64,4,896]{2,1,0:T(4,128)(2,1)}), bf16[64,4,896]{2,1,0:T(4,128)(2,1)S(1)}, u32[]{:S(2)}, u32[]{:S(2)}) async-start(bf16[64,4,896]{2,1,0:T(4,128)(2,1)} %bitcast.94), calls=%async_computation.5 | async-start | bytes 917504 | tf_op jit(solution)/shard_map/all_to_all | solution.py:44
  135.7 5.2 %shard_map.201 = bf16[304,4096]{1,0:T(8,128)(2,1)} custom-call(bf16[304,128]{1,0:T(8,128)(2,1)} %get-tuple-element.48.key_change, bf16[304,128]{1,0:T(8,128)(2,1)} %get-tuple-element.49.value_change, bf16[304,32]{1,0:T(8,128)(2,1)} %get-tuple-element.50.coef, bf16[4096,128]{1,0:T(8,128)(2,1)} %key_weight.3, bf16[4096,128]{1,0:T(8,128)(2,1)} %value_weight.3, ...), custom_call_target="tpu_custom_call" | custom-call | flops 1073741824 | bytes 1048576 | tf_op jit(solution)/shard_map/pallas_call | solution.py:491
  141.0 12.0 %all-to-all-done.5 = bf16[64,4,896]{2,1,0:T(4,128)(2,1)S(1)} async-done(((bf16[64,4,896]{2,1,0:T(4,128)(2,1)}), bf16[64,4,896]{2,1,0:T(4,128)(2,1)S(1)}, u32[]{:S(2)}, u32[]{:S(2)}) %all-to-all-start.5) | async-done | bytes 458784 | tf_op jit(solution)/shard_map/all_to_all | solution.py:44
  153.0 0.7 copy-done
  153.7 2.1 shard_map.202
  155.8 18.8 %all_to_all.41.sums = f32[8,4,768]{2,1,0:T(4,128)} all-to-all(f32[8,4,768]{2,1,0:T(4,128)} %get-tuple-element.53), channel_id=1, replica_groups=mesh['z'=8,'x'=4,'h'=2,'mp'=8] {'x','h'}, dimensions={0} | all-to-all | bytes 196608 | tf_op jit(solution)/shard_map/all_to_all | solution.py:44
  174.6 1.8 shard_map.203
  176.3 5.7 %all-to-all-start.7 = ((bf16[64,4,896]{2,1,0:T(4,128)(2,1)}), bf16[64,4,896]{2,1,0:T(4,128)(2,1)S(1)}, u32[]{:S(2)}, u32[]{:S(2)}) async-start(bf16[64,4,896]{2,1,0:T(4,128)(2,1)} %bitcast.93), calls=%async_computation.8 | async-start | bytes 917504 | tf_op jit(solution)/shard_map/all_to_all | solution.py:44
  182.0 1.3 iota_compare_fusion
  183.3 0.7 dynamic-slice_bitcast_fusion.2
  184.0 3.6 %collective-permute-start.2 = (bf16[8,512]{1,0:T(8,128)(2,1)S(1)}, bf16[8,512]{1,0:T(8,128)(2,1)S(1)}, u32[]{:S(2)}, u32[]{:S(2)}) collective-permute-start(bf16[8,512]{1,0:T(8,128)(2,1)S(1)} %dynamic-slice_bitcast_fusion.2), channel_id=1, source_target_pairs={{0,0},{1,64},{2,128},{3,192},{4,256},{5,320},{6,384},{7,448},{64,1... | collective-permute-start | bytes 24584 | tf_op jit(solution)/shard_map/ppermute | solution.py:458
  187.6 0.8 fusion
  188.4 1.2 collective-permute-done.2
  189.6 1.2 slice.73
  191.4 13.6 %all-to-all-done.7 = bf16[64,4,896]{2,1,0:T(4,128)(2,1)S(1)} async-done(((bf16[64,4,896]{2,1,0:T(4,128)(2,1)}), bf16[64,4,896]{2,1,0:T(4,128)(2,1)S(1)}, u32[]{:S(2)}, u32[]{:S(2)}) %all-to-all-start.7) | async-done | bytes 458784 | tf_op jit(solution)/shard_map/all_to_all | solution.py:44
  206.3 0.8 fusion.3
  207.1 1.9 add_convert_fusion
  (53 shorter events, 3.2 us)
Async XLA Ops:
  7.2 66.5 %all-gather.4.cloned.1.call-start = ((), (), s32[]{:S(2)}) async-start(), calls=%async_computation.9 | async-start | bytes 2801664 | tf_op jit(solution)/shard_map/all_gather | solution.py:352
  7.9 36.0 %copy-start.4 = (bf16[4096,16]{0,1:T(8,128)(2,1)S(1)}, bf16[4096,16]{0,1:T(8,128)(2,1)}, u32[]{:S(2)}) copy-start(bf16[4096,16]{0,1:T(8,128)(2,1)} %param.24) | copy-start | bytes 393220
  9.4 37.5 %copy-start.8 = (s32[2,1]{0,1:T(1,128)S(1)}, s32[2,1]{0,1:T(1,128)}, u32[]{:S(2)}) copy-start(s32[2,1]{0,1:T(1,128)} %param.19) | copy-start | bytes 28
  9.4 22.2 %all-to-all-start = ((bf16[16,16,512]{2,1,0:T(8,128)(2,1)}), bf16[16,16,512]{2,1,0:T(8,128)(2,1)S(1)}, u32[]{:S(2)}, u32[]{:S(2)}) async-start(bf16[16,16,512]{2,1,0:T(8,128)(2,1)} %broadcast_in_dim.64), calls=%async_computation | async-start | bytes 524288 | tf_op jit(solution)/shard_map/all_to_all | solution.py:40
  31.6 29.2 %copy-start.5 = (bf16[4096,16]{0,1:T(8,128)(2,1)S(1)}, bf16[4096,16]{0,1:T(8,128)(2,1)}, u32[]{:S(2)}) copy-start(bf16[4096,16]{0,1:T(8,128)(2,1)} %param.26) | copy-start | bytes 393220
  32.7 33.3 %all-to-all-start.1 = ((bf16[32,24,512]{2,1,0:T(8,128)(2,1)}), bf16[32,24,512]{2,1,0:T(8,128)(2,1)S(1)}, u32[]{:S(2)}, u32[]{:S(2)}) async-start(bf16[32,24,512]{2,1,0:T(8,128)(2,1)} %bitcast.7), calls=%async_computation.1 | async-start | bytes 1572864 | tf_op jit(solution)/shard_map/all_to_all | solution.py:44
  43.9 50.5 %all-gather.6.cloned.1.call-start = ((), (), s32[]{:S(2)}) async-start(), calls=%async_computation.11 | async-start | bytes 1310720 | tf_op jit(solution)/shard_map/all_gather | solution.py:396
  43.9 16.1 %collective-permute-start.1 = (bf16[2,64,512]{2,1,0:T(8,128)(2,1)S(1)}, bf16[2,64,512]{2,1,0:T(8,128)(2,1)S(1)}, u32[]{:S(2)}, u32[]{:S(2)}) collective-permute-start(bf16[2,64,512]{2,1,0:T(8,128)(2,1)S(1)} %pad_maximum_fusion.3), channel_id=1, source_target_pairs={{0,8},{8,0},{1,9},{9,1},{2,10},{10,2},{3,11},{11,3},{4,12},{12,4},... | collective-permute-start | bytes 393224 | tf_op jit(solution)/shard_map/ppermute | solution.py:393
  60.0 9.4 %copy-start.6 = (bf16[8,512]{1,0:T(8,128)(2,1)S(1)}, bf16[8,512]{1,0:T(8,128)(2,1)}, u32[]{:S(2)}) copy-start(bf16[8,512]{1,0:T(8,128)(2,1)} %param.14) | copy-start | bytes 24580
  60.8 13.8 %copy-start.1 = (bf16[4096,32]{0,1:T(8,128)(2,1)}, bf16[4096,32]{0,1:T(8,128)(2,1)S(1)}, u32[]{:S(2)}) copy-start(bf16[4096,32]{0,1:T(8,128)(2,1)S(1)} %constant_dynamic-update-slice_fusion) | copy-start | bytes 786436
  66.0 30.6 %collective-permute-start = (bf16[32,8,512]{2,1,0:T(8,128)(2,1)S(1)}, bf16[32,8,512]{2,1,0:T(8,128)(2,1)S(1)}, u32[]{:S(2)}, u32[]{:S(2)}) collective-permute-start(bf16[32,8,512]{2,1,0:T(8,128)(2,1)S(1)} %slice.89), channel_id=1, source_target_pairs={{0,1},{1,0},{2,3},{3,2},{4,5},{5,4},{6,7},{7,6},{8,9},{9,8},{10,11... | collective-permute-start | bytes 786440 | tf_op jit(solution)/shard_map/ppermute | solution.py:375
  70.3 9.1 %all-to-all-start.2 = ((f32[8,8,512]{2,1,0:T(8,128)}), f32[8,8,512]{2,1,0:T(8,128)S(1)}, u32[]{:S(2)}, u32[]{:S(2)}) async-start(f32[8,8,512]{2,1,0:T(8,128)} %broadcast_in_dim.68), calls=%async_computation.2 | async-start | bytes 262144 | tf_op jit(solution)/shard_map/all_to_all | solution.py:40
  79.4 0.6 copy-start.3
  82.1 23.0 %all-to-all-start.3 = ((bf16[64,8,256]{2,1,0:T(8,128)(2,1)}), bf16[64,8,256]{2,1,0:T(8,128)(2,1)S(1)}, u32[]{:S(2)}, u32[]{:S(2)}) async-start(bf16[64,8,256]{2,1,0:T(8,128)(2,1)} %get-tuple-element.35), calls=%async_computation.3 | async-start | bytes 524288 | tf_op jit(solution)/shard_map/all_to_all | solution.py:44
  105.1 0.7 copy-start.2
  127.1 25.8 %all-to-all-start.5 = ((bf16[64,4,896]{2,1,0:T(4,128)(2,1)}), bf16[64,4,896]{2,1,0:T(4,128)(2,1)S(1)}, u32[]{:S(2)}, u32[]{:S(2)}) async-start(bf16[64,4,896]{2,1,0:T(4,128)(2,1)} %bitcast.94), calls=%async_computation.5 | async-start | bytes 917504 | tf_op jit(solution)/shard_map/all_to_all | solution.py:44
  135.7 71.4 %reduce-scatter.2.cloned.1.call-start = ((), (), s32[]{:S(2)}) async-start(), calls=%async_computation.10 | async-start | bytes 2801664 | tf_op jit(solution)/shard_map/reduce_scatter | solution.py:495
  141.0 46.6 %copy-start.7 = (bf16[8,512]{1,0:T(8,128)(2,1)S(1)}, bf16[8,512]{1,0:T(8,128)(2,1)}, u32[]{:S(2)}) copy-start(bf16[8,512]{1,0:T(8,128)(2,1)} %get-tuple-element.56) | copy-start | bytes 24580
  153.0 0.8 copy-start
  176.3 28.7 %all-to-all-start.7 = ((bf16[64,4,896]{2,1,0:T(4,128)(2,1)}), bf16[64,4,896]{2,1,0:T(4,128)(2,1)S(1)}, u32[]{:S(2)}, u32[]{:S(2)}) async-start(bf16[64,4,896]{2,1,0:T(4,128)(2,1)} %bitcast.93), calls=%async_computation.8 | async-start | bytes 917504 | tf_op jit(solution)/shard_map/all_to_all | solution.py:44
  184.0 5.5 %collective-permute-start.2 = (bf16[8,512]{1,0:T(8,128)(2,1)S(1)}, bf16[8,512]{1,0:T(8,128)(2,1)S(1)}, u32[]{:S(2)}, u32[]{:S(2)}) collective-permute-start(bf16[8,512]{1,0:T(8,128)(2,1)S(1)} %dynamic-slice_bitcast_fusion.2), channel_id=1, source_target_pairs={{0,0},{1,64},{2,128},{3,192},{4,256},{5,320},{6,384},{7,448},{64,1... | collective-permute-start | bytes 24584 | tf_op jit(solution)/shard_map/ppermute | solution.py:458
Sparse Core Ops, SparseCore 0:
  10.1 51.0 all-gather.3
  63.9 30.4 all-gather.5
  153.1 43.7 reduce-scatter.1

commit v10 on v9

--- a/solution.py
+++ b/solution.py
@@ -231,29 +231,13 @@
         axis=0,
     )
     downs = ADAPTER_SCALE * first_product(coef, tokens[...])
-    z_count, mp_count, rows, chunk_width = shares_out.shape
-    width = downs.shape[1] // mp_count
-    up_end = width + ups.shape[1]
-    deltas = jnp.concatenate(
-        [
-            jnp.concatenate(
-                [delta[at : at + 1], delta[at + 1 : at + 2]], axis=1
-            )
-            for at in range(0, subs * group, 2)
-        ],
-        axis=0,
-    )
-    for other in range(mp_count):
-        mine = lax.axis_index("mp") == other
-        kept_ups = jnp.where(mine, ups, 0.0)
-        kept_deltas = jnp.where(mine, deltas, 0.0).astype(jnp.bfloat16)
-        for z in range(z_count):
-            ranks = slice(z * rows, (z + 1) * rows)
-            shares_out[z, other, :, :width] = downs[
-                ranks, other * width : (other + 1) * width
-            ].astype(jnp.bfloat16)
-            shares_out[z, other, :, width:up_end] = kept_ups[ranks].astype(jnp.bfloat16)
-            shares_out[z, other, :, up_end:] = kept_deltas
+    ranks = downs.shape[0]
+    for chunk in range(shares_out.shape[0]):
+        features = slice(chunk * LANES, (chunk + 1) * LANES)
+        shares_out[chunk, :ranks] = downs[:, features].astype(jnp.bfloat16)
+        own_up = jnp.broadcast_to(ups[chunk : chunk + 1], delta.shape)
+        shares_out[chunk, ranks:] = jnp.concatenate([delta, own_up], axis=0).astype(jnp.bfloat16)
+
 
 def portion_kernel(key_change, value_change, coef, key_weight, value_weight, down, out):
     width = 4 * LANES
@@ -268,57 +252,81 @@
         out[:, features] = portion.astype(jnp.bfloat16)
 
 
-def home_kernel(subs, received, loss, wq_plane, sums_out, last_out):
-    z_count, mp_count, rows, _ = received.shape
-    copies, _, sum_width = sums_out.shape
-    sum_width = sum_width - loss.shape[1]
-    total = None
-    deltas = []
+def home_kernel(z_count, subs, received, loss, wq_plane, out):
+    senders, rows, _ = received.shape
+    x_count = senders // z_count
+    sides = 2 * subs * (wq_plane.shape[1] // LANES)
+    ranks = rows - sides
+    half = sides // 2
+    total = received[0].astype(jnp.float32)
+    for sender in range(1, senders):
+        total = total + received[sender].astype(jnp.float32)
+    deltas = jnp.concatenate(
+        [
+            received[z * x_count + lax.axis_index("x"), ranks:].astype(jnp.float32)[:half]
+            for z in range(z_count)
+        ],
+        axis=0,
+    ).astype(jnp.bfloat16)
+    heads = half // subs
+    picks = subs * z_count
+    row = lax.broadcasted_iota(jnp.int32, (picks, deltas.shape[0]), 0)
+    column = lax.broadcasted_iota(jnp.int32, (picks, deltas.shape[0]), 1)
+    last = None
+    for head in range(heads):
+        wanted = jnp.where(row * heads + head == column, 1.0, 0.0).astype(jnp.bfloat16)
+        delta = jnp.dot(wanted, deltas, preferred_element_type=jnp.float32).astype(jnp.bfloat16)
+        term = final_product(delta, wq_plane[:, head * LANES : (head + 1) * LANES])
+        last = term if last is None else last + term
+    lines = [total[ranks + half : ranks + half + 1]]
+    left = loss[:1]
+    for _ in range(3):
+        term = left.astype(jnp.bfloat16).astype(jnp.float32)
+        lines.append(term)
+        left = left - term
+    lines.append(jnp.zeros((half - len(lines), LANES), jnp.float32))
+    downs = total[:ranks].astype(jnp.bfloat16)
+    copies = out.shape[0] // z_count
     for z in range(z_count):
-        column = None
-        for other in range(mp_count):
-            part = received[z, other].astype(jnp.float32)
-            column = part if column is None else column + part
-        delta = column[:, sum_width:]
-        deltas = deltas + [
-            jnp.concatenate([delta[at : at + 1], delta[at + 1 : at + 2]], axis=1)
-            for at in range(0, rows, 2)
+        blocks = [
+            last[z * subs + sub : z * subs + sub + 1, side * LANES : (side + 1) * LANES]
+            for sub in range(subs)
+            for side in range(heads)
         ]
-        column = column[:, :sum_width]
-        total = column if total is None else total + column
-    for copy in range(copies):
-        sums_out[copy, :, :sum_width] = total
-        sums_out[copy, :, sum_width:] = loss[:rows]
-    deltas = jnp.concatenate(deltas, axis=0).astype(jnp.bfloat16)
-    last = final_product(deltas, wq_plane[...])
-    for z in range(z_count):
-        last_out[z] = last[z * subs : (z + 1) * subs]
-
-
-def return_kernel(sums, last, chunks_out, loss_out):
-    z_count, mp_count, rows, chunk_width = chunks_out.shape
-    total = sums[0]
-    for part in range(1, sums.shape[0]):
-        total = total + sums[part]
-    sum_width = total.shape[1] - loss_out.shape[1]
-    loss_out[...] = total[:, sum_width:]
-    total = total[:, :sum_width].astype(jnp.bfloat16)
-    half = chunk_width - sum_width
-    for z in range(z_count):
-        value = last[z]
-        value = jnp.concatenate(
-            [
-                value[sub : sub + 1, side * half : (side + 1) * half]
-                for sub in range(value.shape[0])
-                for side in range(value.shape[1] // half)
-            ],
-            axis=0,
-        )
-        for other in range(mp_count):
-            chunks_out[z, other, :, :sum_width] = total
-            chunks_out[z, other, :, sum_width:] = jnp.where(
-                lax.axis_index("z") == other, value, 0.0
-            ).astype(jnp.bfloat16)
+        extra = jnp.concatenate(blocks + lines, axis=0).astype(jnp.bfloat16)
+        for copy in range(copies):
+            out[copy * z_count + z, :ranks] = downs
+            out[copy * z_count + z, ranks:] = extra
+
+
+def return_kernel(mp_count, received, out, last_out):
+    senders, rows, _ = received.shape
+    half = last_out.shape[0]
+    ranks = rows - 2 * half
+    total = received[0, :ranks].astype(jnp.float32)
+    for sender in range(1, senders):
+        total = total + received[sender, :ranks].astype(jnp.float32)
+    lasts = None
+    for other in range(mp_count):
+        term = received[lax.axis_index("h") * mp_count + other, ranks:].astype(jnp.float32)[:half]
+        lasts = term if lasts is None else lasts + term
+    last_out[...] = lasts
+    lines = None
+    for side in range(senders // mp_count):
+        term = received[side * mp_count + lax.axis_index("mp"), ranks:].astype(jnp.float32)[half:]
+        lines = term if lines is None else lines + term
+    left = lines[1:2] + lines[2:3] + lines[3:4]
+    parts = [lines[:1]]
+    for _ in range(3):
+        term = left.astype(jnp.bfloat16).astype(jnp.float32)
+        parts.append(term)
+        left = left - term
+    parts.append(jnp.zeros((2 * half - len(parts), LANES), jnp.float32))
+    extra = jnp.concatenate(parts, axis=0).astype(jnp.bfloat16)
+    downs = total.astype(jnp.bfloat16)
+    for copy in range(out.shape[0]):
+        out[copy, :ranks] = downs
+        out[copy, ranks:] = extra
 
 
 def local(
@@ -449,22 +457,10 @@
         2**26,
     )(column_rows, queries_all, loss_part, wq_plane, wo_plane)
     parts = swap(parts, "z")
-    own_grads = lax.dynamic_index_in_dim(
-        column_grads.reshape(z_count, local_rows, feature_width),
-        lax.axis_index("mp"),
-        0,
-        keepdims=False,
-    )
-    item_grad = lax.ppermute(
-        own_grads,
-        ("z", "mp"),
-        [(a * mp_count + b, b * mp_count + a) for a in range(z_count) for b in range(mp_count)],
-    )
     query_grad = (jnp.dot(residual, items_all, preferred_element_type=f32) * INV_TEMP).astype(bf16)
 
-    share_rows = 2 * adapter_rank // z_count
-    sum_width = feature_width + up_width
-    chunk_width = sum_width + sub_count * query_width // share_rows
+    ranks = 2 * adapter_rank
+    share_shape = (z_count * x_count, ranks + 2 * sub_count * query_width // LANES, LANES)
     key_change, value_change, coef, loss_part, shares = call(
         attention_kernel,
         (
@@ -472,7 +468,7 @@
             head_shape,
             low_shape,
             jax.ShapeDtypeStruct((2 * sub_count, LANES), f32),
-            jax.ShapeDtypeStruct((z_count, mp_count, share_rows, chunk_width), bf16),
+            jax.ShapeDtypeStruct(share_shape, bf16),
         ),
         2**26,
     )(
@@ -485,56 +481,49 @@
         reduced_pair,
         token_inputs,
     )
-    grid_shape = shares.shape
-    shares = swap(shares.reshape((-1,) + grid_shape[2:]), ("z", "mp")).reshape(grid_shape)
+    shares = swap(shares, ("z", "x"))
 
     portion = call(portion_kernel, jax.ShapeDtypeStruct((token_count, model_width), bf16), 2**30)(
         key_change, value_change, coef, key_weight_matrix, value_weight_matrix, down_both.T
     )
-    shares, portion = lax.optimization_barrier((shares, portion))
     input_sum = lax.psum_scatter(portion, "mp", scatter_dimension=1, tiled=True).astype(f32)
-    sums, last_part = call(
-        functools.partial(home_kernel, sub_count),
+    middle = call(
+        functools.partial(home_kernel, z_count, sub_count),
+        jax.ShapeDtypeStruct((2 * mp_count,) + share_shape[1:], bf16),
+        2**26,
+    )(shares, loss_part, wq_plane)
+    chunks, last_part = call(
+        functools.partial(return_kernel, mp_count),
         (
-            jax.ShapeDtypeStruct((plane_count, share_rows, sum_width + LANES), f32),
-            jax.ShapeDtypeStruct((z_count, sub_count, feature_width), f32),
+            jax.ShapeDtypeStruct(share_shape, bf16),
+            jax.ShapeDtypeStruct((sub_count * query_width // LANES, LANES), f32),
         ),
         2**24,
-    )(shares, loss_part, wq_plane)
-    chunks, loss_sum = call(
-        return_kernel,
-        (
-            jax.ShapeDtypeStruct(grid_shape, bf16),
-            jax.ShapeDtypeStruct((share_rows, LANES), f32),
-        ),
-        2**24,
-    )(swap(sums, PLANE), last_part)
-    mean_loss = loss_sum[0, 0] / batch_size
-    summed = swap(chunks.reshape((-1,) + grid_shape[2:]), ("z", "mp")).reshape(grid_shape)
-    own = lax.axis_index("mp")
-    up_grad = lax.dynamic_index_in_dim(
-        summed[:, :, :, feature_width:sum_width], own, 1, keepdims=False
-    )
-    up_grad = up_grad.reshape(2 * adapter_rank, up_width).astype(f32)
-    last_rows_grad = jnp.sum(
-        lax.dynamic_index_in_dim(
-            summed[:, :, :, sum_width:], own, 0, keepdims=False
-        ).astype(f32),
-        axis=0,
-    ).reshape(sub_count, feature_width) + item_grad[:sub_count].astype(f32)
+    )(swap(middle, ("h", "mp")))
+    summed = swap(chunks, ("z", "x"))
+    up_grad = summed[:, ranks].astype(f32)
+    mean_loss = jnp.sum(summed[:x_count, ranks + 1 : ranks + 4, 0].astype(f32)) / batch_size
+    own_grads = lax.dynamic_index_in_dim(
+        column_grads.reshape(z_count, local_rows, feature_width),
+        lax.axis_index("mp"),
+        0,
+        keepdims=False,
+    )
+    own_last = last_part.reshape(sub_count, feature_width).astype(bf16)
+    at_home = lax.ppermute(
+        jnp.concatenate([own_grads, own_last], axis=0),
+        ("z", "mp"),
+        [(a * mp_count + b, b * mp_count + a) for a in range(z_count) for b in range(mp_count)],
+    )
+    item_grad = at_home[:local_rows]
+    last_rows_grad = at_home[local_rows:].astype(f32) + item_grad[:sub_count].astype(f32)
     row_ids = jnp.arange(token_count, dtype=jnp.int32)[:, None]
     for sub in range(sub_count):
         input_sum = input_sum + jnp.where(
             row_ids == last_rows[sub], last_rows_grad[sub][None, :], 0.0
         )
     input_grad = input_sum.astype(bf16).reshape(hidden_in.shape)
-    down_grad = (
-        summed[:, :, :, :feature_width]
-        .transpose(0, 2, 1, 3)
-        .reshape(2 * adapter_rank, model_width)
-        .astype(f32)
-        .T
-    )
+    down_grad = summed[:, :ranks].transpose(1, 0, 2).reshape(ranks, model_width).astype(f32).T
     return (
         mean_loss,
         query_grad,

time: 219 us -> 211 us (0.963)
  waiting for transfers between devices: 59.1 us -> 52.3 us
  blocking collectives: 33.1 us -> 29.6 us
  starting transfers between devices: 57.9 us -> 60.2 us
    all_to_all x4, waiting for transfers between devices: 28.8 us -> 15.9 us  [swap(): return lax.all_to_all(blocks, axes, split_axis=0, concat_axis=0, tiled=True)]
    ppermute x1, waiting for transfers between devices: 1.15 us -> 7.31 us  [local(): lax.ppermute(jnp.concatenate([own_grads, own_last], axis=0), ('z', 'mp'),...]
    all_to_all x2, blocking collectives: 33.1 us -> 29.6 us  [swap(): return lax.all_to_all(blocks, axes, split_axis=0, concat_axis=0, tiled=True)]
    all_to_all x4, starting transfers between devices: 34.3 us -> 36.7 us  [swap(): return lax.all_to_all(blocks, axes, split_axis=0, concat_axis=0, tiled=True)]
  transfers between devices with their start and end apart: 12 -> 12, of which waited for: 9 -> 9; matrix products, arithmetic and copies ran while one was open for 8% -> 9% of each run, Pallas kernels for 8% -> 6%
where the time goes in v10:
time: 211 us; the launch traced here: 210 us
  starting transfers between devices  60.2 us (29%)
  waiting for transfers between devices  52.3 us (25%)
  blocking collectives  29.6 us (14%)
  Pallas kernels  25.1 us (12%)
  between operations  19.7 us (9%)
  local copies, waits for them, and re-layouts  15 us (7%)
  other arithmetic  7.07 us (3%)
    all_to_all x4, starting transfers between devices, swap(): return lax.all_to_all(blocks, axes, split_axis=0, concat_axis=0, tiled=True)  36.7 us
    all_to_all x2, blocking collectives, swap(): return lax.all_to_all(blocks, axes, split_axis=0, concat_axis=0, tiled=True)  29.6 us
    all_to_all x4, waiting for transfers between devices, swap(): return lax.all_to_all(blocks, axes, split_axis=0, concat_axis=0, tiled=True)  15.9 us
    all_to_all x2, waiting for transfers between devices, spread(): return lax.all_to_all(copies, axes, split_axis=0, concat_axis=0, tiled=True)  15.1 us
    all_to_all x2, starting transfers between devices, spread(): return lax.all_to_all(copies, axes, split_axis=0, concat_axis=0, tiled=True)  13.7 us
    ppermute x1, waiting for transfers between devices, local(): other = lax.ppermute(both, 'h', [(0, 1), (1, 0)])  9.9 us
    ppermute x1, waiting for transfers between devices, local(): lax.ppermute(jnp.concatenate([own_grads, own_last], axis=0), ('z', 'mp'),...  7.31 us
    pallas_call x1, Pallas kernels, local(): call(token_kernel, (low_shape, head_shape, head_shape), 2 ** 30)  6.74 us
  transfers between devices with their start and end apart: 12, of which 9 were waited for; matrix products, arithmetic and copies ran while one was open for 9% of the time, Pallas kernels for 6%

profile of v10, /device:TPU:1, one launch (start us, length us, event | category | flops | bytes accessed | tf_op | source)
XLA Modules:
  0.0 210.0 jit_solution(10811977111195782335)
XLA Ops:
  7.2 0.7 all-gather.4.cloned.1.call-update
  7.9 0.8 pad_maximum_fusion.4
  8.7 0.7 broadcast_in_dim.64
  9.4 10.3 %all-to-all-start = ((bf16[16,16,512]{2,1,0:T(8,128)(2,1)}), bf16[16,16,512]{2,1,0:T(8,128)(2,1)S(1)}, u32[]{:S(2)}, u32[]{:S(2)}) async-start(bf16[16,16,512]{2,1,0:T(8,128)(2,1)} %broadcast_in_dim.64), calls=%async_computation | async-start | bytes 524288 | tf_op jit(solution)/shard_map/all_to_all | solution.py:40
  19.7 0.9 pad_maximum_fusion.3
  20.6 11.0 %all-to-all-done = bf16[16,16,512]{2,1,0:T(8,128)(2,1)S(1)} async-done(((bf16[16,16,512]{2,1,0:T(8,128)(2,1)}), bf16[16,16,512]{2,1,0:T(8,128)(2,1)S(1)}, u32[]{:S(2)}, u32[]{:S(2)}) %all-to-all-start) | async-done | bytes 262176 | tf_op jit(solution)/shard_map/all_to_all | solution.py:40
  31.7 1.0 broadcast_in_dim.67
  32.7 11.2 %all-to-all-start.1 = ((bf16[32,24,512]{2,1,0:T(8,128)(2,1)}), bf16[32,24,512]{2,1,0:T(8,128)(2,1)S(1)}, u32[]{:S(2)}, u32[]{:S(2)}) async-start(bf16[32,24,512]{2,1,0:T(8,128)(2,1)} %bitcast.7), calls=%async_computation.1 | async-start | bytes 1572864 | tf_op jit(solution)/shard_map/all_to_all | solution.py:44
  43.9 2.9 %collective-permute-start.1 = (bf16[2,64,512]{2,1,0:T(8,128)(2,1)S(1)}, bf16[2,64,512]{2,1,0:T(8,128)(2,1)S(1)}, u32[]{:S(2)}, u32[]{:S(2)}) collective-permute-start(bf16[2,64,512]{2,1,0:T(8,128)(2,1)S(1)} %pad_maximum_fusion.3), channel_id=1, source_target_pairs={{0,8},{8,0},{1,9},{9,1},{2,10},{10,2},{3,11},{11,3},{4,12},{12,4},... | collective-permute-start | bytes 393224 | tf_op jit(solution)/shard_map/ppermute | solution.py:401
  50.1 9.9 %collective-permute-done.1 = bf16[2,64,512]{2,1,0:T(8,128)(2,1)S(1)} collective-permute-done((bf16[2,64,512]{2,1,0:T(8,128)(2,1)S(1)}, bf16[2,64,512]{2,1,0:T(8,128)(2,1)S(1)}, u32[]{:S(2)}, u32[]{:S(2)}) %collective-permute-start.1) | collective-permute-done | bytes 131104 | tf_op jit(solution)/shard_map/ppermute | solution.py:401
  60.0 0.7 pad_maximum_fusion.1
  60.8 1.3 copy.45.down
  63.5 2.5 %all-to-all-done.1 = bf16[32,24,512]{2,1,0:T(8,128)(2,1)S(1)} async-done(((bf16[32,24,512]{2,1,0:T(8,128)(2,1)}), bf16[32,24,512]{2,1,0:T(8,128)(2,1)S(1)}, u32[]{:S(2)}, u32[]{:S(2)}) %all-to-all-start.1) | async-done | bytes 786464 | tf_op jit(solution)/shard_map/all_to_all | solution.py:44
  66.0 3.3 %collective-permute-start = (bf16[32,8,512]{2,1,0:T(8,128)(2,1)S(1)}, bf16[32,8,512]{2,1,0:T(8,128)(2,1)S(1)}, u32[]{:S(2)}, u32[]{:S(2)}) collective-permute-start(bf16[32,8,512]{2,1,0:T(8,128)(2,1)S(1)} %slice.94), channel_id=1, source_target_pairs={{0,1},{1,0},{2,3},{3,2},{4,5},{5,4},{6,7},{7,6},{8,9},{9,8},{10,11... | collective-permute-start | bytes 786440 | tf_op jit(solution)/shard_map/ppermute | solution.py:383
  69.6 0.7 broadcast_in_dim.68
  70.3 3.3 %all-to-all-start.2 = ((f32[8,8,512]{2,1,0:T(8,128)}), f32[8,8,512]{2,1,0:T(8,128)S(1)}, u32[]{:S(2)}, u32[]{:S(2)}) async-start(f32[8,8,512]{2,1,0:T(8,128)} %broadcast_in_dim.68), calls=%async_computation.2 | async-start | bytes 262144 | tf_op jit(solution)/shard_map/all_to_all | solution.py:40
  73.7 0.9 constant_dynamic-slice_fusion.1
  75.3 4.2 %all-to-all-done.2.parts = f32[8,8,512]{2,1,0:T(8,128)S(1)} async-done(((f32[8,8,512]{2,1,0:T(8,128)}), f32[8,8,512]{2,1,0:T(8,128)S(1)}, u32[]{:S(2)}, u32[]{:S(2)}) %all-to-all-start.2) | async-done | bytes 131104 | tf_op jit(solution)/shard_map/all_to_all | solution.py:40
  79.4 0.6 copy-done.3
  80.1 2.0 shard_map.197
  82.1 8.9 %all-to-all-start.3 = ((bf16[64,8,256]{2,1,0:T(8,128)(2,1)}), bf16[64,8,256]{2,1,0:T(8,128)(2,1)S(1)}, u32[]{:S(2)}, u32[]{:S(2)}) async-start(bf16[64,8,256]{2,1,0:T(8,128)(2,1)} %get-tuple-element.31), calls=%async_computation.3 | async-start | bytes 524288 | tf_op jit(solution)/shard_map/all_to_all | solution.py:44
  91.0 3.3 %all-gather.6.cloned.1.call-done = bf16[8,2,64,512]{3,2,1,0:T(8,128)(2,1)} async-done(((bf16[2,2,64,512]{3,2,1,0:T(8,128)(2,1)}), bf16[8,2,64,512]{3,2,1,0:T(8,128)(2,1)}) %all-gather.6.cloned.1.call-update) | async-done | bytes 1048592 | tf_op jit(solution)/shard_map/all_gather | solution.py:404
  94.4 2.3 %fusion.2 = (bf16[4,2,1,64,512]{4,3,2,1,0:T(8,128)(2,1)}, bf16[4,2,1,64,512]{4,3,2,1,0:T(8,128)(2,1)}) fusion(bf16[4,2,2,64,512]{4,3,2,1,0:T(8,128)(2,1)} %bitcast.80), kind=kLoop, calls=%fused_computation.31 | loop fusion | bytes 2097152 | tf_op jit(solution)/shard_map/slice | solution.py:407
  96.7 0.9 copy.46
  97.6 6.7 %shard_map.198 = (bf16[304,32]{1,0:T(8,128)(2,1)}, bf16[304,128]{1,0:T(8,128)(2,1)}, bf16[304,128]{1,0:T(8,128)(2,1)}) custom-call(bf16[304,4096]{1,0:T(8,128)(2,1)} %bitcast.69, bf16[4096,128]{1,0:T(8,128)(2,1)} %key_weight.3, bf16[4096,128]{1,0:T(8,128)(2,1)} %value_weight.3, bf16[4096,32]{1,0:T(8,128)(2,1)} %copy.45.down, bf16[16,128]{1,0:T(8,128)(2,1)} %key_up.3, ...), custom_call_target="tpu_custom_call" | custom-call | flops 1073741824 | bytes 1048576 | tf_op jit(solution)/shard_map/pallas_call | solution.py:438
  104.3 0.7 all-to-all-done.3
  105.1 0.7 copy-done.1
  105.8 2.9 %shard_map.199 = (bf16[64,512]{1,0:T(8,128)(2,1)}, f32[8,4,640]{2,1,0:T(4,128)}) custom-call(bf16[512,256]{1,0:T(8,128)(2,1)} %bitcast.79, bf16[512,512]{1,0:T(8,128)(2,1)} %bitcast.75, f32[8,128]{1,0:T(8,128)} %get-tuple-element.37.loss, bf16[512,512]{1,0:T(8,128)(2,1)} %bitcast.73, bf16[512,512]{1,0:T(8,128)(2,1)} %bitcast.76), custom_call_target="tpu_custom_call" | custom-call | flops 67108864 | bytes 1048576 | tf_op jit(solution)/shard_map/pallas_call | solution.py:451
  108.7 14.3 %all_to_all.40.parts = f32[8,4,640]{2,1,0:T(4,128)} all-to-all(f32[8,4,640]{2,1,0:T(4,128)} %get-tuple-element.39), channel_id=1, replica_groups=mesh['z'=8,'x'=4,'h'=2,'mp'=8] {'z'}, dimensions={0} | all-to-all | bytes 163840 | tf_op jit(solution)/shard_map/all_to_all | solution.py:44
  123.0 4.1 %shard_map.200 = (bf16[304,128]{1,0:T(8,128)(2,1)}, bf16[304,128]{1,0:T(8,128)(2,1)}, bf16[304,32]{1,0:T(8,128)(2,1)}, f32[4,128]{1,0:T(4,128)}, bf16[32,48,128]{2,1,0:T(8,128)(2,1)}) custom-call(s32[1,2]{1,0:T(1,128)} %bitcast.94, f32[8,4,640]{2,1,0:T(4,128)} %all_to_all.40.parts, bf16[304,128]{1,0:T(8,128)(2,1)} %get-tuple-element.40.keys, ...), custom_call_target="tpu_custom_call" | custom-call | flops 67108864 | bytes 1048576 | tf_op jit(solution)/shard_map/pallas_call | solution.py:464
  127.1 5.2 %shard_map.203 = bf16[304,4096]{1,0:T(8,128)(2,1)} custom-call(bf16[304,128]{1,0:T(8,128)(2,1)} %get-tuple-element.49.key_change, bf16[304,128]{1,0:T(8,128)(2,1)} %get-tuple-element.50.value_change, bf16[304,32]{1,0:T(8,128)(2,1)} %get-tuple-element.51.coef, bf16[4096,128]{1,0:T(8,128)(2,1)} %key_weight.3, bf16[4096,128]{1,0:T(8,128)(2,1)} %value_weight.3, ...), custom_call_target="tpu_custom_call" | custom-call | flops 1073741824 | bytes 1048576 | tf_op jit(solution)/shard_map/pallas_call | solution.py:486
  132.4 1.0 copy-done.4
  133.3 15.3 %all_to_all.41.received = bf16[32,48,128]{2,1,0:T(8,128)(2,1)} all-to-all(bf16[32,48,128]{2,1,0:T(8,128)(2,1)S(1)} %copy-done.4), channel_id=1, replica_groups=mesh['z'=8,'x'=4,'h'=2,'mp'=8] {'z','x'}, dimensions={0} | all-to-all | bytes 786432 | tf_op jit(solution)/shard_map/all_to_all | solution.py:44
  148.6 2.4 %shard_map.201 = bf16[16,48,128]{2,1,0:T(8,128)(2,1)} custom-call(bf16[32,48,128]{2,1,0:T(8,128)(2,1)} %all_to_all.41.received, f32[4,128]{1,0:T(4,128)} %get-tuple-element.44.loss, bf16[512,512]{1,0:T(8,128)(2,1)} %bitcast.74), custom_call_target="tpu_custom_call" | custom-call | flops 67108864 | bytes 1048576 | tf_op jit(solution)/shard_map/pallas_call | solution.py:490
  151.1 12.7 %all-to-all-start.6 = ((bf16[16,48,128]{2,1,0:T(8,128)(2,1)}), bf16[16,48,128]{2,1,0:T(8,128)(2,1)S(1)}, u32[]{:S(2)}, u32[]{:S(2)}) async-start(bf16[16,48,128]{2,1,0:T(8,128)(2,1)} %shard_map.201), calls=%async_computation.6 | async-start | bytes 393216 | tf_op jit(solution)/shard_map/all_to_all | solution.py:44
  163.8 1.3 iota_compare_fusion
  165.1 0.7 dynamic-slice_bitcast_fusion.2
  165.8 10.1 %all-to-all-done.6.received = bf16[16,48,128]{2,1,0:T(8,128)(2,1)S(1)} async-done(((bf16[16,48,128]{2,1,0:T(8,128)(2,1)}), bf16[16,48,128]{2,1,0:T(8,128)(2,1)S(1)}, u32[]{:S(2)}, u32[]{:S(2)}) %all-to-all-start.6) | async-done | bytes 196640 | tf_op jit(solution)/shard_map/all_to_all | solution.py:44
  175.9 0.7 copy-done.2
  176.5 1.7 shard_map.202
  178.3 0.7 convert_element_type.38
  179.0 3.9 %all-to-all-start.7 = ((bf16[32,48,128]{2,1,0:T(8,128)(2,1)}), bf16[32,48,128]{2,1,0:T(8,128)(2,1)S(1)}, u32[]{:S(2)}, u32[]{:S(2)}) async-start(bf16[32,48,128]{2,1,0:T(8,128)(2,1)} %get-tuple-element.45), calls=%async_computation.7 | async-start | bytes 786432 | tf_op jit(solution)/shard_map/all_to_all | solution.py:44
  182.9 3.5 %collective-permute-start.2 = (bf16[10,512]{1,0:T(8,128)(2,1)S(1)}, bf16[10,512]{1,0:T(8,128)(2,1)S(1)}, u32[]{:S(2)}, u32[]{:S(2)}) collective-permute-start(bf16[10,512]{1,0:T(8,128)(2,1)S(1)} %pad_maximum_fusion.6), channel_id=1, source_target_pairs={{0,0},{1,64},{2,128},{3,192},{4,256},{5,320},{6,384},{7,448},{64,1... | collective-permute-start | bytes 30728 | tf_op jit(solution)/shard_map/ppermute | solution.py:513
  186.4 0.8 fusion
  187.2 7.3 %collective-permute-done.2 = bf16[10,512]{1,0:T(8,128)(2,1)S(1)} collective-permute-done((bf16[10,512]{1,0:T(8,128)(2,1)S(1)}, bf16[10,512]{1,0:T(8,128)(2,1)S(1)}, u32[]{:S(2)}, u32[]{:S(2)}) %collective-permute-start.2) | collective-permute-done | bytes 10272 | tf_op jit(solution)/shard_map/ppermute | solution.py:513
  195.1 2.6 %all-to-all-done.7 = bf16[32,48,128]{2,1,0:T(8,128)(2,1)S(1)} async-done(((bf16[32,48,128]{2,1,0:T(8,128)(2,1)}), bf16[32,48,128]{2,1,0:T(8,128)(2,1)S(1)}, u32[]{:S(2)}, u32[]{:S(2)}) %all-to-all-start.7) | async-done | bytes 393248 | tf_op jit(solution)/shard_map/all_to_all | solution.py:44
  199.6 0.8 fusion.3
  200.4 1.9 add_convert_fusion
  (52 shorter events, 3.9 us)
Async XLA Ops:
  7.2 66.5 %all-gather.4.cloned.1.call-start = ((), (), s32[]{:S(2)}) async-start(), calls=%async_computation.9 | async-start | bytes 2801664 | tf_op jit(solution)/shard_map/all_gather | solution.py:360
  7.9 36.0 %copy-start.5 = (bf16[4096,16]{0,1:T(8,128)(2,1)S(1)}, bf16[4096,16]{0,1:T(8,128)(2,1)}, u32[]{:S(2)}) copy-start(bf16[4096,16]{0,1:T(8,128)(2,1)} %param.24) | copy-start | bytes 393220
  9.4 37.5 %copy-start.9 = (s32[2,1]{0,1:T(1,128)S(1)}, s32[2,1]{0,1:T(1,128)}, u32[]{:S(2)}) copy-start(s32[2,1]{0,1:T(1,128)} %param.19) | copy-start | bytes 28
  9.4 22.2 %all-to-all-start = ((bf16[16,16,512]{2,1,0:T(8,128)(2,1)}), bf16[16,16,512]{2,1,0:T(8,128)(2,1)S(1)}, u32[]{:S(2)}, u32[]{:S(2)}) async-start(bf16[16,16,512]{2,1,0:T(8,128)(2,1)} %broadcast_in_dim.64), calls=%async_computation | async-start | bytes 524288 | tf_op jit(solution)/shard_map/all_to_all | solution.py:40
  31.6 29.2 %copy-start.6 = (bf16[4096,16]{0,1:T(8,128)(2,1)S(1)}, bf16[4096,16]{0,1:T(8,128)(2,1)}, u32[]{:S(2)}) copy-start(bf16[4096,16]{0,1:T(8,128)(2,1)} %param.26) | copy-start | bytes 393220
  32.7 33.3 %all-to-all-start.1 = ((bf16[32,24,512]{2,1,0:T(8,128)(2,1)}), bf16[32,24,512]{2,1,0:T(8,128)(2,1)S(1)}, u32[]{:S(2)}, u32[]{:S(2)}) async-start(bf16[32,24,512]{2,1,0:T(8,128)(2,1)} %bitcast.7), calls=%async_computation.1 | async-start | bytes 1572864 | tf_op jit(solution)/shard_map/all_to_all | solution.py:44
  43.9 50.5 %all-gather.6.cloned.1.call-start = ((), (), s32[]{:S(2)}) async-start(), calls=%async_computation.11 | async-start | bytes 1310720 | tf_op jit(solution)/shard_map/all_gather | solution.py:404
  43.9 16.1 %collective-permute-start.1 = (bf16[2,64,512]{2,1,0:T(8,128)(2,1)S(1)}, bf16[2,64,512]{2,1,0:T(8,128)(2,1)S(1)}, u32[]{:S(2)}, u32[]{:S(2)}) collective-permute-start(bf16[2,64,512]{2,1,0:T(8,128)(2,1)S(1)} %pad_maximum_fusion.3), channel_id=1, source_target_pairs={{0,8},{8,0},{1,9},{9,1},{2,10},{10,2},{3,11},{11,3},{4,12},{12,4},... | collective-permute-start | bytes 393224 | tf_op jit(solution)/shard_map/ppermute | solution.py:401
  60.0 9.4 %copy-start.7 = (bf16[8,512]{1,0:T(8,128)(2,1)S(1)}, bf16[8,512]{1,0:T(8,128)(2,1)}, u32[]{:S(2)}) copy-start(bf16[8,512]{1,0:T(8,128)(2,1)} %param.14) | copy-start | bytes 24580
  60.8 13.8 %copy-start = (bf16[4096,32]{0,1:T(8,128)(2,1)}, bf16[4096,32]{0,1:T(8,128)(2,1)S(1)}, u32[]{:S(2)}) copy-start(bf16[4096,32]{0,1:T(8,128)(2,1)S(1)} %constant_dynamic-update-slice_fusion) | copy-start | bytes 786436
  66.0 30.6 %collective-permute-start = (bf16[32,8,512]{2,1,0:T(8,128)(2,1)S(1)}, bf16[32,8,512]{2,1,0:T(8,128)(2,1)S(1)}, u32[]{:S(2)}, u32[]{:S(2)}) collective-permute-start(bf16[32,8,512]{2,1,0:T(8,128)(2,1)S(1)} %slice.94), channel_id=1, source_target_pairs={{0,1},{1,0},{2,3},{3,2},{4,5},{5,4},{6,7},{7,6},{8,9},{9,8},{10,11... | collective-permute-start | bytes 786440 | tf_op jit(solution)/shard_map/ppermute | solution.py:383
  70.3 9.1 %all-to-all-start.2 = ((f32[8,8,512]{2,1,0:T(8,128)}), f32[8,8,512]{2,1,0:T(8,128)S(1)}, u32[]{:S(2)}, u32[]{:S(2)}) async-start(f32[8,8,512]{2,1,0:T(8,128)} %broadcast_in_dim.68), calls=%async_computation.2 | async-start | bytes 262144 | tf_op jit(solution)/shard_map/all_to_all | solution.py:40
  79.4 0.6 copy-start.3
  82.1 23.0 %all-to-all-start.3 = ((bf16[64,8,256]{2,1,0:T(8,128)(2,1)}), bf16[64,8,256]{2,1,0:T(8,128)(2,1)S(1)}, u32[]{:S(2)}, u32[]{:S(2)}) async-start(bf16[64,8,256]{2,1,0:T(8,128)(2,1)} %get-tuple-element.31), calls=%async_computation.3 | async-start | bytes 524288 | tf_op jit(solution)/shard_map/all_to_all | solution.py:44
  91.0 109.5 %reduce-scatter.2.cloned.1.call-start = ((), (), s32[]{:S(2)}) async-start(), calls=%async_computation.10 | async-start | bytes 2801664 | tf_op jit(solution)/shard_map/reduce_scatter | solution.py:489
  105.1 0.7 copy-start.1
  132.4 1.0 copy-start.4
  132.4 54.0 %copy-start.8 = (bf16[8,512]{1,0:T(8,128)(2,1)S(1)}, bf16[8,512]{1,0:T(8,128)(2,1)}, u32[]{:S(2)}) copy-start(bf16[8,512]{1,0:T(8,128)(2,1)} %get-tuple-element.46) | copy-start | bytes 24580
  151.1 24.8 %all-to-all-start.6 = ((bf16[16,48,128]{2,1,0:T(8,128)(2,1)}), bf16[16,48,128]{2,1,0:T(8,128)(2,1)S(1)}, u32[]{:S(2)}, u32[]{:S(2)}) async-start(bf16[16,48,128]{2,1,0:T(8,128)(2,1)} %shard_map.201), calls=%async_computation.6 | async-start | bytes 393216 | tf_op jit(solution)/shard_map/all_to_all | solution.py:44
  175.9 0.7 copy-start.2
  179.0 18.7 %all-to-all-start.7 = ((bf16[32,48,128]{2,1,0:T(8,128)(2,1)}), bf16[32,48,128]{2,1,0:T(8,128)(2,1)S(1)}, u32[]{:S(2)}, u32[]{:S(2)}) async-start(bf16[32,48,128]{2,1,0:T(8,128)(2,1)} %get-tuple-element.45), calls=%async_computation.7 | async-start | bytes 786432 | tf_op jit(solution)/shard_map/all_to_all | solution.py:44
  182.9 11.6 %collective-permute-start.2 = (bf16[10,512]{1,0:T(8,128)(2,1)S(1)}, bf16[10,512]{1,0:T(8,128)(2,1)S(1)}, u32[]{:S(2)}, u32[]{:S(2)}) collective-permute-start(bf16[10,512]{1,0:T(8,128)(2,1)S(1)} %pad_maximum_fusion.6), channel_id=1, source_target_pairs={{0,0},{1,64},{2,128},{3,192},{4,256},{5,320},{6,384},{7,448},{64,1... | collective-permute-start | bytes 30728 | tf_op jit(solution)/shard_map/ppermute | solution.py:513
Sparse Core Ops, SparseCore 0:
  10.1 51.0 all-gather.3
  63.9 30.4 all-gather.5
  132.5 44.7 reduce-scatter.1

commit v11 on v10

--- a/solution.py
+++ b/solution.py
@@ -44,13 +44,12 @@
     return lax.all_to_all(blocks, axes, split_axis=0, concat_axis=0, tiled=True)
 
 
-def call(kernel, out_shape, flops, **layout):
+def call(kernel, out_shape, flops, mebibytes=56):
     return pl.pallas_call(
         kernel,
         out_shape=out_shape,
-        compiler_params=pltpu.CompilerParams(vmem_limit_bytes=56 * 1024 * 1024),
+        compiler_params=pltpu.CompilerParams(vmem_limit_bytes=mebibytes * 1024 * 1024),
         cost_estimate=pl.CostEstimate(flops=flops, bytes_accessed=2**20, transcendentals=4096),
-        **layout,
     )
 
 
@@ -427,12 +426,13 @@
             jax.ShapeDtypeStruct((local_rows, LANES), f32),
         ),
         2**24,
+        8,
     )(score_parts, hard_index.T, pair_index[None], last_slices)
     column_rows = swap(chunks, DP).reshape(batch_size, 2 * LANES)
     adapter_rank = key_down_matrix.shape[1]
     up_width = key_up_matrix.shape[1]
     down_both = jnp.concatenate([key_down_matrix, value_down], axis=1)
-    late_tokens, residual = lax.optimization_barrier((token_inputs, residual))
+    late_tokens, column_rows = lax.optimization_barrier((token_inputs, column_rows))
     head_shape = jax.ShapeDtypeStruct((token_count, up_width), bf16)
     low_shape = jax.ShapeDtypeStruct((token_count, 2 * adapter_rank), bf16)
     reduced_pair, key_rows, value_rows = call(
@@ -445,9 +445,6 @@
         key_up_matrix,
         value_up_matrix,
     )
-    column_rows, key_rows, value_rows = lax.optimization_barrier(
-        (column_rows, key_rows, value_rows)
-    )
     column_grads, parts = call(
         functools.partial(gradient_kernel, z_count, sub_count),
         (
@@ -455,6 +452,7 @@
             jax.ShapeDtypeStruct((z_count, 2 * sub_count, query_width + LANES), f32),
         ),
         2**26,
+        8,
     )(column_rows, queries_all, loss_part, wq_plane, wo_plane)
     parts = swap(parts, "z")
     query_grad = (jnp.dot(residual, items_all, preferred_element_type=f32) * INV_TEMP).astype(bf16)
@@ -491,6 +489,7 @@
         functools.partial(home_kernel, z_count, sub_count),
         jax.ShapeDtypeStruct((2 * mp_count,) + share_shape[1:], bf16),
         2**26,
+        8,
     )(shares, loss_part, wq_plane)
     chunks, last_part = call(
         functools.partial(return_kernel, mp_count),
@@ -499,10 +498,9 @@
             jax.ShapeDtypeStruct((sub_count * query_width // LANES, LANES), f32),
         ),
         2**24,
+        8,
     )(swap(middle, ("h", "mp")))
     summed = swap(chunks, ("z", "x"))
-    up_grad = summed[:, ranks].astype(f32)
-    mean_loss = jnp.sum(summed[:x_count, ranks + 1 : ranks + 4, 0].astype(f32)) / batch_size
     own_grads = lax.dynamic_index_in_dim(
         column_grads.reshape(z_count, local_rows, feature_width),
         lax.axis_index("mp"),
@@ -523,6 +521,9 @@
             row_ids == last_rows[sub], last_rows_grad[sub][None, :], 0.0
         )
     input_grad = input_sum.astype(bf16).reshape(hidden_in.shape)
+    summed, input_grad = lax.optimization_barrier((summed, input_grad))
+    up_grad = summed[:, ranks].astype(f32)
+    mean_loss = jnp.sum(summed[:x_count, ranks + 1 : ranks + 4, 0].astype(f32)) / batch_size
     down_grad = summed[:, :ranks].transpose(1, 0, 2).reshape(ranks, model_width).astype(f32).T
     return (
         mean_loss,

time: 211 us -> 206 us (0.976)
  waiting for transfers between devices: 52.3 us -> 63.8 us
  blocking collectives: 29.6 us -> 20 us
  local copies, waits for them, and re-layouts: 15 us -> 10.4 us
  Pallas kernels: 25.1 us -> 20.6 us
  starting transfers between devices: 60.2 us -> 62.5 us
    all_to_all x4 -> x5, waiting for transfers between devices: 15.9 us -> 31.1 us  [swap(): return lax.all_to_all(blocks, axes, split_axis=0, concat_axis=0, tiled=True)]
    all_to_all x2 -> x1, blocking collectives: 29.6 us -> 20 us  [swap(): return lax.all_to_all(blocks, axes, split_axis=0, concat_axis=0, tiled=True)]
    ppermute x1, waiting for transfers between devices: 7.31 us -> 0.01 us  [local(): lax.ppermute(jnp.concatenate([own_grads, own_last], axis=0), ('z', 'mp'),...]
    all_gather x1, waiting for transfers between devices: 3.32 us -> 7.68 us  [local(): both = lax.all_gather(both, 'x', axis=0, tiled=False)]
    all_to_all x4 -> x5, starting transfers between devices: 36.7 us -> 40.3 us  [swap(): return lax.all_to_all(blocks, axes, split_axis=0, concat_axis=0, tiled=True)]
  transfers between devices with their start and end apart: 12 -> 13, of which waited for: 9 -> 8; matrix products, arithmetic and copies ran while one was open for 9% -> 7% of each run, Pallas kernels for 6% -> 5%
where the time goes in v11:
time: 206 us; the launch traced here: 204 us
  waiting for transfers between devices  63.8 us (31%)
  starting transfers between devices  62.5 us (30%)
  Pallas kernels  20.6 us (10%)
  blocking collectives  20 us (10%)
  between operations  19.8 us (10%)
  local copies, waits for them, and re-layouts  10.4 us (5%)
  other arithmetic  6.39 us (3%)
    all_to_all x5, starting transfers between devices, swap(): return lax.all_to_all(blocks, axes, split_axis=0, concat_axis=0, tiled=True)  40.3 us
    all_to_all x5, waiting for transfers between devices, swap(): return lax.all_to_all(blocks, axes, split_axis=0, concat_axis=0, tiled=True)  31.1 us
    all_to_all x1, blocking collectives, swap(): return lax.all_to_all(blocks, axes, split_axis=0, concat_axis=0, tiled=True)  20 us
    all_to_all x2, waiting for transfers between devices, spread(): return lax.all_to_all(copies, axes, split_axis=0, concat_axis=0, tiled=True)  15.7 us
    all_to_all x2, starting transfers between devices, spread(): return lax.all_to_all(copies, axes, split_axis=0, concat_axis=0, tiled=True)  13.5 us
    ppermute x1, waiting for transfers between devices, local(): other = lax.ppermute(both, 'h', [(0, 1), (1, 0)])  8.53 us
    all_gather x1, waiting for transfers between devices, local(): both = lax.all_gather(both, 'x', axis=0, tiled=False)  7.68 us
    pallas_call x1, Pallas kernels, local(): call(token_kernel, (low_shape, head_shape, head_shape), 2 ** 30)  6.73 us
  transfers between devices with their start and end apart: 13, of which 8 were waited for; matrix products, arithmetic and copies ran while one was open for 7% of the time, Pallas kernels for 5%

profile of v11, /device:TPU:1, one launch (start us, length us, event | category | flops | bytes accessed | tf_op | source)
XLA Modules:
  0.0 204.5 jit_solution(18186707472669609728)
XLA Ops:
  7.2 0.7 all-gather.4.cloned.1.call-update
  7.9 0.7 pad_maximum_fusion.4
  8.6 0.7 broadcast_in_dim.64
  9.4 10.2 %all-to-all-start = ((bf16[16,16,512]{2,1,0:T(8,128)(2,1)}), bf16[16,16,512]{2,1,0:T(8,128)(2,1)S(1)}, u32[]{:S(2)}, u32[]{:S(2)}) async-start(bf16[16,16,512]{2,1,0:T(8,128)(2,1)} %broadcast_in_dim.64), calls=%async_computation | async-start | bytes 524288 | tf_op jit(solution)/shard_map/all_to_all | solution.py:40
  19.6 0.9 pad_maximum_fusion.3
  20.5 11.0 %all-to-all-done = bf16[16,16,512]{2,1,0:T(8,128)(2,1)S(1)} async-done(((bf16[16,16,512]{2,1,0:T(8,128)(2,1)}), bf16[16,16,512]{2,1,0:T(8,128)(2,1)S(1)}, u32[]{:S(2)}, u32[]{:S(2)}) %all-to-all-start) | async-done | bytes 262176 | tf_op jit(solution)/shard_map/all_to_all | solution.py:40
  31.5 0.9 broadcast_in_dim.67
  32.5 11.2 %all-to-all-start.1 = ((bf16[32,24,512]{2,1,0:T(8,128)(2,1)}), bf16[32,24,512]{2,1,0:T(8,128)(2,1)S(1)}, u32[]{:S(2)}, u32[]{:S(2)}) async-start(bf16[32,24,512]{2,1,0:T(8,128)(2,1)} %bitcast.8), calls=%async_computation.1 | async-start | bytes 1572864 | tf_op jit(solution)/shard_map/all_to_all | solution.py:44
  43.7 2.9 %collective-permute-start.1 = (bf16[2,64,512]{2,1,0:T(8,128)(2,1)S(1)}, bf16[2,64,512]{2,1,0:T(8,128)(2,1)S(1)}, u32[]{:S(2)}, u32[]{:S(2)}) collective-permute-start(bf16[2,64,512]{2,1,0:T(8,128)(2,1)S(1)} %pad_maximum_fusion.3), channel_id=1, source_target_pairs={{0,8},{8,0},{1,9},{9,1},{2,10},{10,2},{3,11},{11,3},{4,12},{12,4},... | collective-permute-start | bytes 393224 | tf_op jit(solution)/shard_map/ppermute | solution.py:400
  46.7 0.6 fusion.7
  51.2 8.5 %collective-permute-done.1 = bf16[2,64,512]{2,1,0:T(8,128)(2,1)S(1)} collective-permute-done((bf16[2,64,512]{2,1,0:T(8,128)(2,1)S(1)}, bf16[2,64,512]{2,1,0:T(8,128)(2,1)S(1)}, u32[]{:S(2)}, u32[]{:S(2)}) %collective-permute-start.1) | collective-permute-done | bytes 131104 | tf_op jit(solution)/shard_map/ppermute | solution.py:400
  59.7 0.7 pad_maximum_fusion.1
  60.5 5.2 %all-to-all-done.1 = bf16[32,24,512]{2,1,0:T(8,128)(2,1)S(1)} async-done(((bf16[32,24,512]{2,1,0:T(8,128)(2,1)}), bf16[32,24,512]{2,1,0:T(8,128)(2,1)S(1)}, u32[]{:S(2)}, u32[]{:S(2)}) %all-to-all-start.1) | async-done | bytes 786464 | tf_op jit(solution)/shard_map/all_to_all | solution.py:44
  65.8 3.3 %collective-permute-start = (bf16[32,8,512]{2,1,0:T(8,128)(2,1)S(1)}, bf16[32,8,512]{2,1,0:T(8,128)(2,1)S(1)}, u32[]{:S(2)}, u32[]{:S(2)}) collective-permute-start(bf16[32,8,512]{2,1,0:T(8,128)(2,1)S(1)} %slice.94), channel_id=1, source_target_pairs={{0,1},{1,0},{2,3},{3,2},{4,5},{5,4},{6,7},{7,6},{8,9},{9,8},{10,11... | collective-permute-start | bytes 786440 | tf_op jit(solution)/shard_map/ppermute | solution.py:382
  69.2 0.2 convolution_bitcast_fusion
  69.4 0.7 broadcast_in_dim.68
  70.1 3.3 %all-to-all-start.2 = ((f32[8,8,512]{2,1,0:T(8,128)}), f32[8,8,512]{2,1,0:T(8,128)S(1)}, u32[]{:S(2)}, u32[]{:S(2)}) async-start(f32[8,8,512]{2,1,0:T(8,128)} %broadcast_in_dim.68), calls=%async_computation.2 | async-start | bytes 262144 | tf_op jit(solution)/shard_map/all_to_all | solution.py:40
  73.5 0.9 constant_dynamic-slice_fusion.1
  74.5 4.7 %all-to-all-done.2.parts = f32[8,8,512]{2,1,0:T(8,128)S(1)} async-done(((f32[8,8,512]{2,1,0:T(8,128)}), f32[8,8,512]{2,1,0:T(8,128)S(1)}, u32[]{:S(2)}, u32[]{:S(2)}) %all-to-all-start.2) | async-done | bytes 131104 | tf_op jit(solution)/shard_map/all_to_all | solution.py:40
  79.2 1.1 shard_map.197
  80.3 6.6 %all-to-all-start.3 = ((bf16[64,8,256]{2,1,0:T(8,128)(2,1)}), bf16[64,8,256]{2,1,0:T(8,128)(2,1)S(1)}, u32[]{:S(2)}, u32[]{:S(2)}) async-start(bf16[64,8,256]{2,1,0:T(8,128)(2,1)} %get-tuple-element.30), calls=%async_computation.3 | async-start | bytes 524288 | tf_op jit(solution)/shard_map/all_to_all | solution.py:44
  86.9 7.7 %all-gather.6.cloned.1.call-done = bf16[8,2,64,512]{3,2,1,0:T(8,128)(2,1)} async-done(((bf16[2,2,64,512]{3,2,1,0:T(8,128)(2,1)}), bf16[8,2,64,512]{3,2,1,0:T(8,128)(2,1)}) %all-gather.6.cloned.1.call-update) | async-done | bytes 1048592 | tf_op jit(solution)/shard_map/all_gather | solution.py:403
  94.6 1.3 fusion.2
  95.9 0.1 select_bitcast_fusion.1
  96.1 4.9 %all-to-all-done.3 = bf16[64,8,256]{2,1,0:T(8,128)(2,1)S(1)} async-done(((bf16[64,8,256]{2,1,0:T(8,128)(2,1)}), bf16[64,8,256]{2,1,0:T(8,128)(2,1)S(1)}, u32[]{:S(2)}, u32[]{:S(2)}) %all-to-all-start.3) | async-done | bytes 262176 | tf_op jit(solution)/shard_map/all_to_all | solution.py:44
  101.0 1.4 shard_map.198
  102.4 3.4 %all-to-all-start.4 = ((f32[8,4,640]{2,1,0:T(4,128)}), f32[8,4,640]{2,1,0:T(4,128)S(1)}, u32[]{:S(2)}, u32[]{:S(2)}) async-start(f32[8,4,640]{2,1,0:T(4,128)} %get-tuple-element.34), calls=%async_computation.4 | async-start | bytes 163840 | tf_op jit(solution)/shard_map/all_to_all | solution.py:44
  105.9 1.3 copy.48.down
  107.2 6.7 %shard_map.199 = (bf16[304,32]{1,0:T(8,128)(2,1)}, bf16[304,128]{1,0:T(8,128)(2,1)}, bf16[304,128]{1,0:T(8,128)(2,1)}) custom-call(bf16[304,4096]{1,0:T(8,128)(2,1)} %bitcast.77, bf16[4096,128]{1,0:T(8,128)(2,1)} %key_weight.3, bf16[4096,128]{1,0:T(8,128)(2,1)} %value_weight.3, bf16[4096,32]{1,0:T(8,128)(2,1)} %copy.48.down, bf16[16,128]{1,0:T(8,128)(2,1)} %key_up.3, ...), custom_call_target="tpu_custom_call" | custom-call | flops 1073741824 | bytes 1048576 | tf_op jit(solution)/shard_map/pallas_call | solution.py:438
  113.9 0.6 copy-done.5
  114.6 4.1 %shard_map.200 = (bf16[304,128]{1,0:T(8,128)(2,1)}, bf16[304,128]{1,0:T(8,128)(2,1)}, bf16[304,32]{1,0:T(8,128)(2,1)}, f32[4,128]{1,0:T(4,128)}, bf16[32,48,128]{2,1,0:T(8,128)(2,1)}) custom-call(s32[1,2]{1,0:T(1,128)} %bitcast.93, f32[8,4,640]{2,1,0:T(4,128)} %copy-done.5, bf16[304,128]{1,0:T(8,128)(2,1)} %get-tuple-element.36.keys, ...), custom_call_target="tpu_custom_call" | custom-call | flops 67108864 | bytes 1048576 | tf_op jit(solution)/shard_map/pallas_call | solution.py:462
  118.7 5.2 %shard_map.203 = bf16[304,4096]{1,0:T(8,128)(2,1)} custom-call(bf16[304,128]{1,0:T(8,128)(2,1)} %get-tuple-element.42.key_change, bf16[304,128]{1,0:T(8,128)(2,1)} %get-tuple-element.43.value_change, bf16[304,32]{1,0:T(8,128)(2,1)} %get-tuple-element.44.coef, bf16[4096,128]{1,0:T(8,128)(2,1)} %key_weight.3, bf16[4096,128]{1,0:T(8,128)(2,1)} %value_weight.3, ...), custom_call_target="tpu_custom_call" | custom-call | flops 1073741824 | bytes 1048576 | tf_op jit(solution)/shard_map/pallas_call | solution.py:484
  123.9 1.0 copy-done.4
  124.9 20.0 %all_to_all.40.received = bf16[32,48,128]{2,1,0:T(8,128)(2,1)S(1)} all-to-all(bf16[32,48,128]{2,1,0:T(8,128)(2,1)S(1)} %copy-done.4), channel_id=1, replica_groups=mesh['z'=8,'x'=4,'h'=2,'mp'=8] {'z','x'}, dimensions={0} | all-to-all | bytes 786432 | tf_op jit(solution)/shard_map/all_to_all | solution.py:44
  144.9 1.2 shard_map.201
  146.1 12.5 %all-to-all-start.6 = ((bf16[16,48,128]{2,1,0:T(8,128)(2,1)}), bf16[16,48,128]{2,1,0:T(8,128)(2,1)S(1)}, u32[]{:S(2)}, u32[]{:S(2)}) async-start(bf16[16,48,128]{2,1,0:T(8,128)(2,1)} %shard_map.201), calls=%async_computation.6 | async-start | bytes 393216 | tf_op jit(solution)/shard_map/all_to_all | solution.py:44
  158.6 1.3 iota_compare_fusion
  159.9 10.9 %all-to-all-done.6.received = bf16[16,48,128]{2,1,0:T(8,128)(2,1)S(1)} async-done(((bf16[16,48,128]{2,1,0:T(8,128)(2,1)}), bf16[16,48,128]{2,1,0:T(8,128)(2,1)S(1)}, u32[]{:S(2)}, u32[]{:S(2)}) %all-to-all-start.6) | async-done | bytes 196640 | tf_op jit(solution)/shard_map/all_to_all | solution.py:44
  170.8 0.8 shard_map.202
  171.7 2.3 %collective-permute-start.2 = (bf16[10,512]{1,0:T(8,128)(2,1)S(1)}, bf16[10,512]{1,0:T(8,128)(2,1)S(1)}, u32[]{:S(2)}, u32[]{:S(2)}) collective-permute-start(bf16[10,512]{1,0:T(8,128)(2,1)S(1)} %pad_maximum_fusion.6), channel_id=1, source_target_pairs={{0,0},{1,64},{2,128},{3,192},{4,256},{5,320},{6,384},{7,448},{64,1... | collective-permute-start | bytes 30728 | tf_op jit(solution)/shard_map/ppermute | solution.py:511
  174.0 6.7 %all-to-all-start.7 = ((bf16[32,48,128]{2,1,0:T(8,128)(2,1)}), bf16[32,48,128]{2,1,0:T(8,128)(2,1)S(1)}, u32[]{:S(2)}, u32[]{:S(2)}) async-start(bf16[32,48,128]{2,1,0:T(8,128)(2,1)} %get-tuple-element.41), calls=%async_computation.7 | async-start | bytes 786432 | tf_op jit(solution)/shard_map/all_to_all | solution.py:44
  180.7 0.8 fusion
  181.5 0.6 slice.101
  182.1 1.9 add_convert_fusion
  184.0 10.1 %all-to-all-done.7 = bf16[32,48,128]{2,1,0:T(8,128)(2,1)S(1)} async-done(((bf16[32,48,128]{2,1,0:T(8,128)(2,1)}), bf16[32,48,128]{2,1,0:T(8,128)(2,1)S(1)}, u32[]{:S(2)}, u32[]{:S(2)}) %all-to-all-start.7) | async-done | bytes 393248 | tf_op jit(solution)/shard_map/all_to_all | solution.py:44
  194.1 0.6 convert_reduce_fusion
  194.7 0.8 fusion.3
  195.6 0.6 fusion.5
  (53 shorter events, 0.8 us)
Async XLA Ops:
  7.2 66.3 %all-gather.4.cloned.1.call-start = ((), (), s32[]{:S(2)}) async-start(), calls=%async_computation.9 | async-start | bytes 2801664 | tf_op jit(solution)/shard_map/all_gather | solution.py:359
  7.9 38.8 %copy-start.9 = (s32[2,1]{0,1:T(1,128)S(1)}, s32[2,1]{0,1:T(1,128)}, u32[]{:S(2)}) copy-start(s32[2,1]{0,1:T(1,128)} %param.19) | copy-start | bytes 28
  9.4 22.1 %all-to-all-start = ((bf16[16,16,512]{2,1,0:T(8,128)(2,1)}), bf16[16,16,512]{2,1,0:T(8,128)(2,1)S(1)}, u32[]{:S(2)}, u32[]{:S(2)}) async-start(bf16[16,16,512]{2,1,0:T(8,128)(2,1)} %broadcast_in_dim.64), calls=%async_computation | async-start | bytes 524288 | tf_op jit(solution)/shard_map/all_to_all | solution.py:40
  31.4 29.1 %copy-start.6 = (bf16[4096,16]{0,1:T(8,128)(2,1)S(1)}, bf16[4096,16]{0,1:T(8,128)(2,1)}, u32[]{:S(2)}) copy-start(bf16[4096,16]{0,1:T(8,128)(2,1)} %param.24) | copy-start | bytes 393220
  32.5 33.3 %all-to-all-start.1 = ((bf16[32,24,512]{2,1,0:T(8,128)(2,1)}), bf16[32,24,512]{2,1,0:T(8,128)(2,1)S(1)}, u32[]{:S(2)}, u32[]{:S(2)}) async-start(bf16[32,24,512]{2,1,0:T(8,128)(2,1)} %bitcast.8), calls=%async_computation.1 | async-start | bytes 1572864 | tf_op jit(solution)/shard_map/all_to_all | solution.py:44
  43.7 25.5 %copy-start.8 = (bf16[8,512]{1,0:T(8,128)(2,1)S(1)}, bf16[8,512]{1,0:T(8,128)(2,1)}, u32[]{:S(2)}) copy-start(bf16[8,512]{1,0:T(8,128)(2,1)} %param.14) | copy-start | bytes 24580
  43.7 50.9 %all-gather.6.cloned.1.call-start = ((), (), s32[]{:S(2)}) async-start(), calls=%async_computation.11 | async-start | bytes 1310720 | tf_op jit(solution)/shard_map/all_gather | solution.py:403
  43.7 16.0 %collective-permute-start.1 = (bf16[2,64,512]{2,1,0:T(8,128)(2,1)S(1)}, bf16[2,64,512]{2,1,0:T(8,128)(2,1)S(1)}, u32[]{:S(2)}, u32[]{:S(2)}) collective-permute-start(bf16[2,64,512]{2,1,0:T(8,128)(2,1)S(1)} %pad_maximum_fusion.3), channel_id=1, source_target_pairs={{0,8},{8,0},{1,9},{9,1},{2,10},{10,2},{3,11},{11,3},{4,12},{12,4},... | collective-permute-start | bytes 393224 | tf_op jit(solution)/shard_map/ppermute | solution.py:400
  59.7 19.5 %copy-start = (s32[8,4]{0,1:T(4,128)S(1)}, s32[8,4]{0,1:T(4,128)}, u32[]{:S(2)}) copy-start(s32[8,4]{0,1:T(4,128)} %param.17) | copy-start | bytes 388
  59.7 19.5 %copy-start.2 = (s32[8]{0:T(128)S(1)}, s32[8]{0:T(128)}, u32[]{:S(2)}) copy-start(s32[8]{0:T(128)} %param.16) | copy-start | bytes 100
  65.8 30.1 %collective-permute-start = (bf16[32,8,512]{2,1,0:T(8,128)(2,1)S(1)}, bf16[32,8,512]{2,1,0:T(8,128)(2,1)S(1)}, u32[]{:S(2)}, u32[]{:S(2)}) collective-permute-start(bf16[32,8,512]{2,1,0:T(8,128)(2,1)S(1)} %slice.94), channel_id=1, source_target_pairs={{0,1},{1,0},{2,3},{3,2},{4,5},{5,4},{6,7},{7,6},{8,9},{9,8},{10,11... | collective-permute-start | bytes 786440 | tf_op jit(solution)/shard_map/ppermute | solution.py:382
  70.1 9.1 %all-to-all-start.2 = ((f32[8,8,512]{2,1,0:T(8,128)}), f32[8,8,512]{2,1,0:T(8,128)S(1)}, u32[]{:S(2)}, u32[]{:S(2)}) async-start(f32[8,8,512]{2,1,0:T(8,128)} %broadcast_in_dim.68), calls=%async_computation.2 | async-start | bytes 262144 | tf_op jit(solution)/shard_map/all_to_all | solution.py:40
  80.3 20.7 %all-to-all-start.3 = ((bf16[64,8,256]{2,1,0:T(8,128)(2,1)}), bf16[64,8,256]{2,1,0:T(8,128)(2,1)S(1)}, u32[]{:S(2)}, u32[]{:S(2)}) async-start(bf16[64,8,256]{2,1,0:T(8,128)(2,1)} %get-tuple-element.30), calls=%async_computation.3 | async-start | bytes 524288 | tf_op jit(solution)/shard_map/all_to_all | solution.py:44
  95.9 10.0 %copy-start.7 = (bf16[4096,16]{0,1:T(8,128)(2,1)S(1)}, bf16[4096,16]{0,1:T(8,128)(2,1)}, u32[]{:S(2)}) copy-start(bf16[4096,16]{0,1:T(8,128)(2,1)} %param.26) | copy-start | bytes 393220
  102.4 11.5 %all-to-all-start.4 = ((f32[8,4,640]{2,1,0:T(4,128)}), f32[8,4,640]{2,1,0:T(4,128)S(1)}, u32[]{:S(2)}, u32[]{:S(2)}) async-start(f32[8,4,640]{2,1,0:T(4,128)} %get-tuple-element.34), calls=%async_computation.4 | async-start | bytes 163840 | tf_op jit(solution)/shard_map/all_to_all | solution.py:44
  105.8 76.3 %reduce-scatter.2.cloned.1.call-start = ((), (), s32[]{:S(2)}) async-start(), calls=%async_computation.10 | async-start | bytes 2801664 | tf_op jit(solution)/shard_map/reduce_scatter | solution.py:487
  105.9 8.1 %copy-start.3 = (bf16[4096,32]{0,1:T(8,128)(2,1)}, bf16[4096,32]{0,1:T(8,128)(2,1)S(1)}, u32[]{:S(2)}) copy-start(bf16[4096,32]{0,1:T(8,128)(2,1)S(1)} %constant_dynamic-update-slice_fusion) | copy-start | bytes 786436
  113.9 0.6 copy-start.5
  123.9 1.0 copy-start.4
  123.9 21.0 %copy-start.1 = (f32[4,128]{1,0:T(4,128)S(1)}, f32[4,128]{1,0:T(4,128)}, u32[]{:S(2)}) copy-start(f32[4,128]{1,0:T(4,128)} %get-tuple-element.40.loss) | copy-start | bytes 6148
  146.1 24.7 %all-to-all-start.6 = ((bf16[16,48,128]{2,1,0:T(8,128)(2,1)}), bf16[16,48,128]{2,1,0:T(8,128)(2,1)S(1)}, u32[]{:S(2)}, u32[]{:S(2)}) async-start(bf16[16,48,128]{2,1,0:T(8,128)(2,1)} %shard_map.201), calls=%async_computation.6 | async-start | bytes 393216 | tf_op jit(solution)/shard_map/all_to_all | solution.py:44
  171.7 9.8 %collective-permute-start.2 = (bf16[10,512]{1,0:T(8,128)(2,1)S(1)}, bf16[10,512]{1,0:T(8,128)(2,1)S(1)}, u32[]{:S(2)}, u32[]{:S(2)}) collective-permute-start(bf16[10,512]{1,0:T(8,128)(2,1)S(1)} %pad_maximum_fusion.6), channel_id=1, source_target_pairs={{0,0},{1,64},{2,128},{3,192},{4,256},{5,320},{6,384},{7,448},{64,1... | collective-permute-start | bytes 30728 | tf_op jit(solution)/shard_map/ppermute | solution.py:511
  174.0 20.1 %all-to-all-start.7 = ((bf16[32,48,128]{2,1,0:T(8,128)(2,1)}), bf16[32,48,128]{2,1,0:T(8,128)(2,1)S(1)}, u32[]{:S(2)}, u32[]{:S(2)}) async-start(bf16[32,48,128]{2,1,0:T(8,128)(2,1)} %get-tuple-element.41), calls=%async_computation.7 | async-start | bytes 786432 | tf_op jit(solution)/shard_map/all_to_all | solution.py:44
Sparse Core Ops, SparseCore 0:
  10.1 51.2 all-gather.3
  64.0 30.4 all-gather.5
  124.1 48.8 reduce-scatter.1

commit v12 on v11

--- a/solution.py
+++ b/solution.py
@@ -484,6 +484,7 @@
     portion = call(portion_kernel, jax.ShapeDtypeStruct((token_count, model_width), bf16), 2**30)(
         key_change, value_change, coef, key_weight_matrix, value_weight_matrix, down_both.T
     )
+    shares, portion = lax.optimization_barrier((shares, portion))
     input_sum = lax.psum_scatter(portion, "mp", scatter_dimension=1, tiled=True).astype(f32)
     middle = call(
         functools.partial(home_kernel, z_count, sub_count),

time: 206 us -> 201 us (0.976)
  blocking collectives: 20 us -> 0 us
  starting transfers between devices: 62.5 us -> 70 us
  waiting for transfers between devices: 63.8 us -> 70.8 us
    all_to_all x1 -> x0, blocking collectives: 20 us -> none  [swap(): return lax.all_to_all(blocks, axes, split_axis=0, concat_axis=0, tiled=True)]
    reduce_scatter x1, waiting for transfers between devices: 0.02 us -> 10.9 us  [local(): lax.psum_scatter(portion, 'mp', scatter_dimension=1, tiled=True).astype(f32)]
    all_to_all x5 -> x6, starting transfers between devices: 40.3 us -> 48.2 us  [swap(): return lax.all_to_all(blocks, axes, split_axis=0, concat_axis=0, tiled=True)]
    all_to_all x5 -> x6, waiting for transfers between devices: 31.1 us -> 27.3 us  [swap(): return lax.all_to_all(blocks, axes, split_axis=0, concat_axis=0, tiled=True)]
  transfers between devices with their start and end apart: 13 -> 14, of which waited for: 8 -> 9; matrix products, arithmetic and copies ran while one was open for 7% -> 7% of each run, Pallas kernels for 5% -> 8%
where the time goes in v12:
time: 201 us; the launch traced here: 198 us
  waiting for transfers between devices  70.8 us (35%)
  starting transfers between devices  70 us (35%)
  Pallas kernels  20.6 us (10%)
  between operations  19.8 us (10%)
  local copies, waits for them, and re-layouts  9.48 us (5%)
  other arithmetic  6.4 us (3%)
    all_to_all x6, starting transfers between devices, swap(): return lax.all_to_all(blocks, axes, split_axis=0, concat_axis=0, tiled=True)  48.2 us
    all_to_all x6, waiting for transfers between devices, swap(): return lax.all_to_all(blocks, axes, split_axis=0, concat_axis=0, tiled=True)  27.3 us
    all_to_all x2, waiting for transfers between devices, spread(): return lax.all_to_all(copies, axes, split_axis=0, concat_axis=0, tiled=True)  15.7 us
    all_to_all x2, starting transfers between devices, spread(): return lax.all_to_all(copies, axes, split_axis=0, concat_axis=0, tiled=True)  13.5 us
    reduce_scatter x1, waiting for transfers between devices, local(): lax.psum_scatter(portion, 'mp', scatter_dimension=1, tiled=True).astype(f32)  10.9 us
    ppermute x1, waiting for transfers between devices, local(): other = lax.ppermute(both, 'h', [(0, 1), (1, 0)])  8.53 us
    all_gather x1, waiting for transfers between devices, local(): both = lax.all_gather(both, 'x', axis=0, tiled=False)  7.68 us
    pallas_call x1, Pallas kernels, local(): call(token_kernel, (low_shape, head_shape, head_shape), 2 ** 30)  6.73 us
  transfers between devices with their start and end apart: 14, of which 9 were waited for; matrix products, arithmetic and copies ran while one was open for 7% of the time, Pallas kernels for 8%

profile of v12, /device:TPU:1, one launch (start us, length us, event | category | flops | bytes accessed | tf_op | source)
XLA Modules:
  0.0 198.1 jit_solution(10912731275577816446)
XLA Ops:
  7.2 0.7 all-gather.4.cloned.1.call-update
  7.9 0.7 pad_maximum_fusion.4
  8.6 0.7 broadcast_in_dim.64
  9.4 10.2 %all-to-all-start = ((bf16[16,16,512]{2,1,0:T(8,128)(2,1)}), bf16[16,16,512]{2,1,0:T(8,128)(2,1)S(1)}, u32[]{:S(2)}, u32[]{:S(2)}) async-start(bf16[16,16,512]{2,1,0:T(8,128)(2,1)} %broadcast_in_dim.64), calls=%async_computation | async-start | bytes 524288 | tf_op jit(solution)/shard_map/all_to_all | solution.py:40
  19.6 0.9 pad_maximum_fusion.3
  20.5 11.0 %all-to-all-done = bf16[16,16,512]{2,1,0:T(8,128)(2,1)S(1)} async-done(((bf16[16,16,512]{2,1,0:T(8,128)(2,1)}), bf16[16,16,512]{2,1,0:T(8,128)(2,1)S(1)}, u32[]{:S(2)}, u32[]{:S(2)}) %all-to-all-start) | async-done | bytes 262176 | tf_op jit(solution)/shard_map/all_to_all | solution.py:40
  31.5 0.9 broadcast_in_dim.67
  32.5 11.2 %all-to-all-start.1 = ((bf16[32,24,512]{2,1,0:T(8,128)(2,1)}), bf16[32,24,512]{2,1,0:T(8,128)(2,1)S(1)}, u32[]{:S(2)}, u32[]{:S(2)}) async-start(bf16[32,24,512]{2,1,0:T(8,128)(2,1)} %bitcast.8), calls=%async_computation.1 | async-start | bytes 1572864 | tf_op jit(solution)/shard_map/all_to_all | solution.py:44
  43.7 2.9 %collective-permute-start.1 = (bf16[2,64,512]{2,1,0:T(8,128)(2,1)S(1)}, bf16[2,64,512]{2,1,0:T(8,128)(2,1)S(1)}, u32[]{:S(2)}, u32[]{:S(2)}) collective-permute-start(bf16[2,64,512]{2,1,0:T(8,128)(2,1)S(1)} %pad_maximum_fusion.3), channel_id=1, source_target_pairs={{0,8},{8,0},{1,9},{9,1},{2,10},{10,2},{3,11},{11,3},{4,12},{12,4},... | collective-permute-start | bytes 393224 | tf_op jit(solution)/shard_map/ppermute | solution.py:400
  46.7 0.6 fusion.7
  51.2 8.5 %collective-permute-done.1 = bf16[2,64,512]{2,1,0:T(8,128)(2,1)S(1)} collective-permute-done((bf16[2,64,512]{2,1,0:T(8,128)(2,1)S(1)}, bf16[2,64,512]{2,1,0:T(8,128)(2,1)S(1)}, u32[]{:S(2)}, u32[]{:S(2)}) %collective-permute-start.1) | collective-permute-done | bytes 131104 | tf_op jit(solution)/shard_map/ppermute | solution.py:400
  59.7 0.7 pad_maximum_fusion.1
  60.5 5.2 %all-to-all-done.1 = bf16[32,24,512]{2,1,0:T(8,128)(2,1)S(1)} async-done(((bf16[32,24,512]{2,1,0:T(8,128)(2,1)}), bf16[32,24,512]{2,1,0:T(8,128)(2,1)S(1)}, u32[]{:S(2)}, u32[]{:S(2)}) %all-to-all-start.1) | async-done | bytes 786464 | tf_op jit(solution)/shard_map/all_to_all | solution.py:44
  65.8 3.3 %collective-permute-start = (bf16[32,8,512]{2,1,0:T(8,128)(2,1)S(1)}, bf16[32,8,512]{2,1,0:T(8,128)(2,1)S(1)}, u32[]{:S(2)}, u32[]{:S(2)}) collective-permute-start(bf16[32,8,512]{2,1,0:T(8,128)(2,1)S(1)} %slice.94), channel_id=1, source_target_pairs={{0,1},{1,0},{2,3},{3,2},{4,5},{5,4},{6,7},{7,6},{8,9},{9,8},{10,11... | collective-permute-start | bytes 786440 | tf_op jit(solution)/shard_map/ppermute | solution.py:382
  69.2 0.2 convolution_bitcast_fusion
  69.4 0.7 broadcast_in_dim.68
  70.1 3.3 %all-to-all-start.2 = ((f32[8,8,512]{2,1,0:T(8,128)}), f32[8,8,512]{2,1,0:T(8,128)S(1)}, u32[]{:S(2)}, u32[]{:S(2)}) async-start(f32[8,8,512]{2,1,0:T(8,128)} %broadcast_in_dim.68), calls=%async_computation.2 | async-start | bytes 262144 | tf_op jit(solution)/shard_map/all_to_all | solution.py:40
  73.5 0.9 constant_dynamic-slice_fusion.1
  74.5 4.7 %all-to-all-done.2.parts = f32[8,8,512]{2,1,0:T(8,128)S(1)} async-done(((f32[8,8,512]{2,1,0:T(8,128)}), f32[8,8,512]{2,1,0:T(8,128)S(1)}, u32[]{:S(2)}, u32[]{:S(2)}) %all-to-all-start.2) | async-done | bytes 131104 | tf_op jit(solution)/shard_map/all_to_all | solution.py:40
  79.2 1.1 shard_map.197
  80.3 6.6 %all-to-all-start.3 = ((bf16[64,8,256]{2,1,0:T(8,128)(2,1)}), bf16[64,8,256]{2,1,0:T(8,128)(2,1)S(1)}, u32[]{:S(2)}, u32[]{:S(2)}) async-start(bf16[64,8,256]{2,1,0:T(8,128)(2,1)} %get-tuple-element.32), calls=%async_computation.3 | async-start | bytes 524288 | tf_op jit(solution)/shard_map/all_to_all | solution.py:44
  86.9 7.7 %all-gather.6.cloned.1.call-done = bf16[8,2,64,512]{3,2,1,0:T(8,128)(2,1)} async-done(((bf16[2,2,64,512]{3,2,1,0:T(8,128)(2,1)}), bf16[8,2,64,512]{3,2,1,0:T(8,128)(2,1)}) %all-gather.6.cloned.1.call-update) | async-done | bytes 1048592 | tf_op jit(solution)/shard_map/all_gather | solution.py:403
  94.6 1.3 fusion.2
  95.9 0.1 select_bitcast_fusion.1
  96.1 4.9 %all-to-all-done.3 = bf16[64,8,256]{2,1,0:T(8,128)(2,1)S(1)} async-done(((bf16[64,8,256]{2,1,0:T(8,128)(2,1)}), bf16[64,8,256]{2,1,0:T(8,128)(2,1)S(1)}, u32[]{:S(2)}, u32[]{:S(2)}) %all-to-all-start.3) | async-done | bytes 262176 | tf_op jit(solution)/shard_map/all_to_all | solution.py:44
  101.0 1.5 shard_map.198
  102.4 3.4 %all-to-all-start.4 = ((f32[8,4,640]{2,1,0:T(4,128)}), f32[8,4,640]{2,1,0:T(4,128)S(1)}, u32[]{:S(2)}, u32[]{:S(2)}) async-start(f32[8,4,640]{2,1,0:T(4,128)} %get-tuple-element.36), calls=%async_computation.4 | async-start | bytes 163840 | tf_op jit(solution)/shard_map/all_to_all | solution.py:44
  105.8 1.3 copy.48.down
  107.2 6.7 %shard_map.199 = (bf16[304,32]{1,0:T(8,128)(2,1)}, bf16[304,128]{1,0:T(8,128)(2,1)}, bf16[304,128]{1,0:T(8,128)(2,1)}) custom-call(bf16[304,4096]{1,0:T(8,128)(2,1)} %bitcast.77, bf16[4096,128]{1,0:T(8,128)(2,1)} %key_weight.3, bf16[4096,128]{1,0:T(8,128)(2,1)} %value_weight.3, bf16[4096,32]{1,0:T(8,128)(2,1)} %copy.48.down, bf16[16,128]{1,0:T(8,128)(2,1)} %key_up.3, ...), custom_call_target="tpu_custom_call" | custom-call | flops 1073741824 | bytes 1048576 | tf_op jit(solution)/shard_map/pallas_call | solution.py:438
  113.9 0.6 copy-done.4
  114.5 4.1 %shard_map.200 = (bf16[304,128]{1,0:T(8,128)(2,1)}, bf16[304,128]{1,0:T(8,128)(2,1)}, bf16[304,32]{1,0:T(8,128)(2,1)}, f32[4,128]{1,0:T(4,128)}, bf16[32,48,128]{2,1,0:T(8,128)(2,1)}) custom-call(s32[1,2]{1,0:T(1,128)} %bitcast.93, f32[8,4,640]{2,1,0:T(4,128)} %copy-done.4, bf16[304,128]{1,0:T(8,128)(2,1)} %get-tuple-element.38.keys, ...), custom_call_target="tpu_custom_call" | custom-call | flops 67108864 | bytes 1048576 | tf_op jit(solution)/shard_map/pallas_call | solution.py:462
  118.6 8.7 %all-to-all-start.5 = ((bf16[32,48,128]{2,1,0:T(8,128)(2,1)}), bf16[32,48,128]{2,1,0:T(8,128)(2,1)S(1)}, u32[]{:S(2)}, u32[]{:S(2)}) async-start(bf16[32,48,128]{2,1,0:T(8,128)(2,1)} %get-tuple-element.41), calls=%async_computation.5 | async-start | bytes 786432 | tf_op jit(solution)/shard_map/all_to_all | solution.py:44
  127.4 5.2 %shard_map.201 = bf16[304,4096]{1,0:T(8,128)(2,1)} custom-call(bf16[304,128]{1,0:T(8,128)(2,1)} %get-tuple-element.42.key_change, bf16[304,128]{1,0:T(8,128)(2,1)} %get-tuple-element.43.value_change, bf16[304,32]{1,0:T(8,128)(2,1)} %get-tuple-element.44.coef, bf16[4096,128]{1,0:T(8,128)(2,1)} %key_weight.3, bf16[4096,128]{1,0:T(8,128)(2,1)} %value_weight.3, ...), custom_call_target="tpu_custom_call" | custom-call | flops 1073741824 | bytes 1048576 | tf_op jit(solution)/shard_map/pallas_call | solution.py:484
  132.6 6.3 %all-to-all-done.5.received = bf16[32,48,128]{2,1,0:T(8,128)(2,1)S(1)} async-done(((bf16[32,48,128]{2,1,0:T(8,128)(2,1)}), bf16[32,48,128]{2,1,0:T(8,128)(2,1)S(1)}, u32[]{:S(2)}, u32[]{:S(2)}) %all-to-all-start.5) | async-done | bytes 393248 | tf_op jit(solution)/shard_map/all_to_all | solution.py:44
  138.9 1.2 shard_map.202
  140.1 12.5 %all-to-all-start.6 = ((bf16[16,48,128]{2,1,0:T(8,128)(2,1)}), bf16[16,48,128]{2,1,0:T(8,128)(2,1)S(1)}, u32[]{:S(2)}, u32[]{:S(2)}) async-start(bf16[16,48,128]{2,1,0:T(8,128)(2,1)} %shard_map.202), calls=%async_computation.6 | async-start | bytes 393216 | tf_op jit(solution)/shard_map/all_to_all | solution.py:44
  152.6 1.3 iota_compare_fusion
  154.0 10.9 %all-to-all-done.6.received = bf16[16,48,128]{2,1,0:T(8,128)(2,1)S(1)} async-done(((bf16[16,48,128]{2,1,0:T(8,128)(2,1)}), bf16[16,48,128]{2,1,0:T(8,128)(2,1)S(1)}, u32[]{:S(2)}, u32[]{:S(2)}) %all-to-all-start.6) | async-done | bytes 196640 | tf_op jit(solution)/shard_map/all_to_all | solution.py:44
  164.8 0.8 shard_map.203
  165.6 1.9 collective-permute-start.2
  167.6 5.9 %all-to-all-start.7 = ((bf16[32,48,128]{2,1,0:T(8,128)(2,1)}), bf16[32,48,128]{2,1,0:T(8,128)(2,1)S(1)}, u32[]{:S(2)}, u32[]{:S(2)}) async-start(bf16[32,48,128]{2,1,0:T(8,128)(2,1)} %get-tuple-element.47), calls=%async_computation.7 | async-start | bytes 786432 | tf_op jit(solution)/shard_map/all_to_all | solution.py:44
  173.5 0.8 fusion
  174.3 0.6 slice.101
  174.9 10.9 %reduce-scatter.2.cloned.1.call-done = bf16[304,512]{1,0:T(8,128)(2,1)} async-done(((bf16[304,4096]{1,0:T(8,128)(2,1)}), bf16[304,512]{1,0:T(8,128)(2,1)}) %reduce-scatter.2.cloned.1.call-update) | async-done | bytes 311312 | tf_op jit(solution)/shard_map/reduce_scatter | solution.py:488
  185.8 1.9 add_convert_fusion
  187.7 0.6 convert_reduce_fusion
  188.3 0.8 fusion.3
  189.1 0.6 fusion.5
  (52 shorter events, 0.7 us)
Async XLA Ops:
  7.2 66.3 %all-gather.4.cloned.1.call-start = ((), (), s32[]{:S(2)}) async-start(), calls=%async_computation.9 | async-start | bytes 2801664 | tf_op jit(solution)/shard_map/all_gather | solution.py:359
  7.9 38.8 %copy-start.8 = (s32[2,1]{0,1:T(1,128)S(1)}, s32[2,1]{0,1:T(1,128)}, u32[]{:S(2)}) copy-start(s32[2,1]{0,1:T(1,128)} %param.19) | copy-start | bytes 28
  9.4 22.1 %all-to-all-start = ((bf16[16,16,512]{2,1,0:T(8,128)(2,1)}), bf16[16,16,512]{2,1,0:T(8,128)(2,1)S(1)}, u32[]{:S(2)}, u32[]{:S(2)}) async-start(bf16[16,16,512]{2,1,0:T(8,128)(2,1)} %broadcast_in_dim.64), calls=%async_computation | async-start | bytes 524288 | tf_op jit(solution)/shard_map/all_to_all | solution.py:40
  31.4 29.1 %copy-start.5 = (bf16[4096,16]{0,1:T(8,128)(2,1)S(1)}, bf16[4096,16]{0,1:T(8,128)(2,1)}, u32[]{:S(2)}) copy-start(bf16[4096,16]{0,1:T(8,128)(2,1)} %param.24) | copy-start | bytes 393220
  32.5 33.3 %all-to-all-start.1 = ((bf16[32,24,512]{2,1,0:T(8,128)(2,1)}), bf16[32,24,512]{2,1,0:T(8,128)(2,1)S(1)}, u32[]{:S(2)}, u32[]{:S(2)}) async-start(bf16[32,24,512]{2,1,0:T(8,128)(2,1)} %bitcast.8), calls=%async_computation.1 | async-start | bytes 1572864 | tf_op jit(solution)/shard_map/all_to_all | solution.py:44
  43.7 25.5 %copy-start.7 = (bf16[8,512]{1,0:T(8,128)(2,1)S(1)}, bf16[8,512]{1,0:T(8,128)(2,1)}, u32[]{:S(2)}) copy-start(bf16[8,512]{1,0:T(8,128)(2,1)} %param.14) | copy-start | bytes 24580
  43.7 50.9 %all-gather.6.cloned.1.call-start = ((), (), s32[]{:S(2)}) async-start(), calls=%async_computation.11 | async-start | bytes 1310720 | tf_op jit(solution)/shard_map/all_gather | solution.py:403
  43.7 16.0 %collective-permute-start.1 = (bf16[2,64,512]{2,1,0:T(8,128)(2,1)S(1)}, bf16[2,64,512]{2,1,0:T(8,128)(2,1)S(1)}, u32[]{:S(2)}, u32[]{:S(2)}) collective-permute-start(bf16[2,64,512]{2,1,0:T(8,128)(2,1)S(1)} %pad_maximum_fusion.3), channel_id=1, source_target_pairs={{0,8},{8,0},{1,9},{9,1},{2,10},{10,2},{3,11},{11,3},{4,12},{12,4},... | collective-permute-start | bytes 393224 | tf_op jit(solution)/shard_map/ppermute | solution.py:400
  59.7 19.5 %copy-start = (s32[8,4]{0,1:T(4,128)S(1)}, s32[8,4]{0,1:T(4,128)}, u32[]{:S(2)}) copy-start(s32[8,4]{0,1:T(4,128)} %param.17) | copy-start | bytes 388
  59.7 19.5 %copy-start.2 = (s32[8]{0:T(128)S(1)}, s32[8]{0:T(128)}, u32[]{:S(2)}) copy-start(s32[8]{0:T(128)} %param.16) | copy-start | bytes 100
  65.8 30.1 %collective-permute-start = (bf16[32,8,512]{2,1,0:T(8,128)(2,1)S(1)}, bf16[32,8,512]{2,1,0:T(8,128)(2,1)S(1)}, u32[]{:S(2)}, u32[]{:S(2)}) collective-permute-start(bf16[32,8,512]{2,1,0:T(8,128)(2,1)S(1)} %slice.94), channel_id=1, source_target_pairs={{0,1},{1,0},{2,3},{3,2},{4,5},{5,4},{6,7},{7,6},{8,9},{9,8},{10,11... | collective-permute-start | bytes 786440 | tf_op jit(solution)/shard_map/ppermute | solution.py:382
  70.1 9.1 %all-to-all-start.2 = ((f32[8,8,512]{2,1,0:T(8,128)}), f32[8,8,512]{2,1,0:T(8,128)S(1)}, u32[]{:S(2)}, u32[]{:S(2)}) async-start(f32[8,8,512]{2,1,0:T(8,128)} %broadcast_in_dim.68), calls=%async_computation.2 | async-start | bytes 262144 | tf_op jit(solution)/shard_map/all_to_all | solution.py:40
  80.3 20.7 %all-to-all-start.3 = ((bf16[64,8,256]{2,1,0:T(8,128)(2,1)}), bf16[64,8,256]{2,1,0:T(8,128)(2,1)S(1)}, u32[]{:S(2)}, u32[]{:S(2)}) async-start(bf16[64,8,256]{2,1,0:T(8,128)(2,1)} %get-tuple-element.32), calls=%async_computation.3 | async-start | bytes 524288 | tf_op jit(solution)/shard_map/all_to_all | solution.py:44
  95.8 9.9 %copy-start.6 = (bf16[4096,16]{0,1:T(8,128)(2,1)S(1)}, bf16[4096,16]{0,1:T(8,128)(2,1)}, u32[]{:S(2)}) copy-start(bf16[4096,16]{0,1:T(8,128)(2,1)} %param.26) | copy-start | bytes 393220
  102.4 11.5 %all-to-all-start.4 = ((f32[8,4,640]{2,1,0:T(4,128)}), f32[8,4,640]{2,1,0:T(4,128)S(1)}, u32[]{:S(2)}, u32[]{:S(2)}) async-start(f32[8,4,640]{2,1,0:T(4,128)} %get-tuple-element.36), calls=%async_computation.4 | async-start | bytes 163840 | tf_op jit(solution)/shard_map/all_to_all | solution.py:44
  105.8 8.1 %copy-start.3 = (bf16[4096,32]{0,1:T(8,128)(2,1)}, bf16[4096,32]{0,1:T(8,128)(2,1)S(1)}, u32[]{:S(2)}) copy-start(bf16[4096,32]{0,1:T(8,128)(2,1)S(1)} %constant_dynamic-update-slice_fusion) | copy-start | bytes 786436
  113.9 0.6 copy-start.4
  118.6 20.3 %all-to-all-start.5 = ((bf16[32,48,128]{2,1,0:T(8,128)(2,1)}), bf16[32,48,128]{2,1,0:T(8,128)(2,1)S(1)}, u32[]{:S(2)}, u32[]{:S(2)}) async-start(bf16[32,48,128]{2,1,0:T(8,128)(2,1)} %get-tuple-element.41), calls=%async_computation.5 | async-start | bytes 786432 | tf_op jit(solution)/shard_map/all_to_all | solution.py:44
  127.3 58.4 %reduce-scatter.2.cloned.1.call-start = ((), (), s32[]{:S(2)}) async-start(), calls=%async_computation.10 | async-start | bytes 2801664 | tf_op jit(solution)/shard_map/reduce_scatter | solution.py:488
  132.6 6.3 %copy-start.1 = (f32[4,128]{1,0:T(4,128)S(1)}, f32[4,128]{1,0:T(4,128)}, u32[]{:S(2)}) copy-start(f32[4,128]{1,0:T(4,128)} %get-tuple-element.46.loss) | copy-start | bytes 6148
  140.1 24.7 %all-to-all-start.6 = ((bf16[16,48,128]{2,1,0:T(8,128)(2,1)}), bf16[16,48,128]{2,1,0:T(8,128)(2,1)S(1)}, u32[]{:S(2)}, u32[]{:S(2)}) async-start(bf16[16,48,128]{2,1,0:T(8,128)(2,1)} %shard_map.202), calls=%async_computation.6 | async-start | bytes 393216 | tf_op jit(solution)/shard_map/all_to_all | solution.py:44
  165.6 8.6 %collective-permute-start.2 = (bf16[10,512]{1,0:T(8,128)(2,1)S(1)}, bf16[10,512]{1,0:T(8,128)(2,1)S(1)}, u32[]{:S(2)}, u32[]{:S(2)}) collective-permute-start(bf16[10,512]{1,0:T(8,128)(2,1)S(1)} %pad_maximum_fusion.6), channel_id=1, source_target_pairs={{0,0},{1,64},{2,128},{3,192},{4,256},{5,320},{6,384},{7,448},{64,1... | collective-permute-start | bytes 30728 | tf_op jit(solution)/shard_map/ppermute | solution.py:512
  167.6 20.1 %all-to-all-start.7 = ((bf16[32,48,128]{2,1,0:T(8,128)(2,1)}), bf16[32,48,128]{2,1,0:T(8,128)(2,1)S(1)}, u32[]{:S(2)}, u32[]{:S(2)}) async-start(bf16[32,48,128]{2,1,0:T(8,128)(2,1)} %get-tuple-element.47), calls=%async_computation.7 | async-start | bytes 786432 | tf_op jit(solution)/shard_map/all_to_all | solution.py:44
Sparse Core Ops, SparseCore 0:
  10.1 51.2 all-gather.3
  64.0 30.4 all-gather.5
  139.0 46.7 reduce-scatter.1

commit v13 on v12

--- a/solution.py
+++ b/solution.py
@@ -522,7 +522,6 @@
             row_ids == last_rows[sub], last_rows_grad[sub][None, :], 0.0
         )
     input_grad = input_sum.astype(bf16).reshape(hidden_in.shape)
-    summed, input_grad = lax.optimization_barrier((summed, input_grad))
     up_grad = summed[:, ranks].astype(f32)
     mean_loss = jnp.sum(summed[:x_count, ranks + 1 : ranks + 4, 0].astype(f32)) / batch_size
     down_grad = summed[:, :ranks].transpose(1, 0, 2).reshape(ranks, model_width).astype(f32).T

time: 201 us -> 198 us (0.985)
    reduce_scatter x1, waiting for transfers between devices: 10.9 us -> 0.01 us  [local(): lax.psum_scatter(portion, 'mp', scatter_dimension=1, tiled=True).astype(f32)]
    ppermute x1, waiting for transfers between devices: 0.01 us -> 7.27 us  [local(): lax.ppermute(jnp.concatenate([own_grads, own_last], axis=0), ('z', 'mp'),...]
    all_to_all x6, waiting for transfers between devices: 27.3 us -> 29.6 us  [swap(): return lax.all_to_all(blocks, axes, split_axis=0, concat_axis=0, tiled=True)]
    all_to_all x6, starting transfers between devices: 48.2 us -> 46.2 us  [swap(): return lax.all_to_all(blocks, axes, split_axis=0, concat_axis=0, tiled=True)]
  transfers between devices with their start and end apart: 14 -> 14, of which waited for: 9 -> 10; matrix products, arithmetic and copies ran while one was open for 7% -> 7% of each run, Pallas kernels for 8% -> 8%
where the time goes in v13:
time: 198 us; the launch traced here: 196 us
  starting transfers between devices  69.6 us (35%)
  waiting for transfers between devices  69.5 us (35%)
  Pallas kernels  20.6 us (10%)
  between operations  19.8 us (10%)
  local copies, waits for them, and re-layouts  9.47 us (5%)
  other arithmetic  6.39 us (3%)
    all_to_all x6, starting transfers between devices, swap(): return lax.all_to_all(blocks, axes, split_axis=0, concat_axis=0, tiled=True)  46.2 us
    all_to_all x6, waiting for transfers between devices, swap(): return lax.all_to_all(blocks, axes, split_axis=0, concat_axis=0, tiled=True)  29.6 us
    all_to_all x2, waiting for transfers between devices, spread(): return lax.all_to_all(copies, axes, split_axis=0, concat_axis=0, tiled=True)  15.7 us
    all_to_all x2, starting transfers between devices, spread(): return lax.all_to_all(copies, axes, split_axis=0, concat_axis=0, tiled=True)  13.5 us
    ppermute x1, waiting for transfers between devices, local(): other = lax.ppermute(both, 'h', [(0, 1), (1, 0)])  8.53 us
    all_gather x1, waiting for transfers between devices, local(): both = lax.all_gather(both, 'x', axis=0, tiled=False)  7.68 us
    ppermute x1, waiting for transfers between devices, local(): lax.ppermute(jnp.concatenate([own_grads, own_last], axis=0), ('z', 'mp'),...  7.27 us
    pallas_call x1, Pallas kernels, local(): call(token_kernel, (low_shape, head_shape, head_shape), 2 ** 30)  6.73 us
  transfers between devices with their start and end apart: 14, of which 10 were waited for; matrix products, arithmetic and copies ran while one was open for 7% of the time, Pallas kernels for 8%

profile of v13, /device:TPU:1, one launch (start us, length us, event | category | flops | bytes accessed | tf_op | source)
XLA Modules:
  0.0 196.4 jit_solution(4438405915004121391)
XLA Ops:
  7.2 0.7 all-gather.4.cloned.1.call-update
  7.9 0.7 pad_maximum_fusion.4
  8.6 0.7 broadcast_in_dim.64
  9.4 10.2 %all-to-all-start = ((bf16[16,16,512]{2,1,0:T(8,128)(2,1)}), bf16[16,16,512]{2,1,0:T(8,128)(2,1)S(1)}, u32[]{:S(2)}, u32[]{:S(2)}) async-start(bf16[16,16,512]{2,1,0:T(8,128)(2,1)} %broadcast_in_dim.64), calls=%async_computation | async-start | bytes 524288 | tf_op jit(solution)/shard_map/all_to_all | solution.py:40
  19.6 0.9 pad_maximum_fusion.3
  20.5 11.0 %all-to-all-done = bf16[16,16,512]{2,1,0:T(8,128)(2,1)S(1)} async-done(((bf16[16,16,512]{2,1,0:T(8,128)(2,1)}), bf16[16,16,512]{2,1,0:T(8,128)(2,1)S(1)}, u32[]{:S(2)}, u32[]{:S(2)}) %all-to-all-start) | async-done | bytes 262176 | tf_op jit(solution)/shard_map/all_to_all | solution.py:40
  31.5 0.9 broadcast_in_dim.67
  32.5 11.2 %all-to-all-start.1 = ((bf16[32,24,512]{2,1,0:T(8,128)(2,1)}), bf16[32,24,512]{2,1,0:T(8,128)(2,1)S(1)}, u32[]{:S(2)}, u32[]{:S(2)}) async-start(bf16[32,24,512]{2,1,0:T(8,128)(2,1)} %bitcast.8), calls=%async_computation.1 | async-start | bytes 1572864 | tf_op jit(solution)/shard_map/all_to_all | solution.py:44
  43.7 2.9 %collective-permute-start.1 = (bf16[2,64,512]{2,1,0:T(8,128)(2,1)S(1)}, bf16[2,64,512]{2,1,0:T(8,128)(2,1)S(1)}, u32[]{:S(2)}, u32[]{:S(2)}) collective-permute-start(bf16[2,64,512]{2,1,0:T(8,128)(2,1)S(1)} %pad_maximum_fusion.3), channel_id=1, source_target_pairs={{0,8},{8,0},{1,9},{9,1},{2,10},{10,2},{3,11},{11,3},{4,12},{12,4},... | collective-permute-start | bytes 393224 | tf_op jit(solution)/shard_map/ppermute | solution.py:400
  46.7 0.6 fusion.7
  51.2 8.5 %collective-permute-done.1 = bf16[2,64,512]{2,1,0:T(8,128)(2,1)S(1)} collective-permute-done((bf16[2,64,512]{2,1,0:T(8,128)(2,1)S(1)}, bf16[2,64,512]{2,1,0:T(8,128)(2,1)S(1)}, u32[]{:S(2)}, u32[]{:S(2)}) %collective-permute-start.1) | collective-permute-done | bytes 131104 | tf_op jit(solution)/shard_map/ppermute | solution.py:400
  59.7 0.7 pad_maximum_fusion.1
  60.5 5.2 %all-to-all-done.1 = bf16[32,24,512]{2,1,0:T(8,128)(2,1)S(1)} async-done(((bf16[32,24,512]{2,1,0:T(8,128)(2,1)}), bf16[32,24,512]{2,1,0:T(8,128)(2,1)S(1)}, u32[]{:S(2)}, u32[]{:S(2)}) %all-to-all-start.1) | async-done | bytes 786464 | tf_op jit(solution)/shard_map/all_to_all | solution.py:44
  65.8 3.3 %collective-permute-start = (bf16[32,8,512]{2,1,0:T(8,128)(2,1)S(1)}, bf16[32,8,512]{2,1,0:T(8,128)(2,1)S(1)}, u32[]{:S(2)}, u32[]{:S(2)}) collective-permute-start(bf16[32,8,512]{2,1,0:T(8,128)(2,1)S(1)} %slice.94), channel_id=1, source_target_pairs={{0,1},{1,0},{2,3},{3,2},{4,5},{5,4},{6,7},{7,6},{8,9},{9,8},{10,11... | collective-permute-start | bytes 786440 | tf_op jit(solution)/shard_map/ppermute | solution.py:382
  69.2 0.2 convolution_bitcast_fusion
  69.4 0.7 broadcast_in_dim.68
  70.1 3.3 %all-to-all-start.2 = ((f32[8,8,512]{2,1,0:T(8,128)}), f32[8,8,512]{2,1,0:T(8,128)S(1)}, u32[]{:S(2)}, u32[]{:S(2)}) async-start(f32[8,8,512]{2,1,0:T(8,128)} %broadcast_in_dim.68), calls=%async_computation.2 | async-start | bytes 262144 | tf_op jit(solution)/shard_map/all_to_all | solution.py:40
  73.5 0.9 constant_dynamic-slice_fusion.1
  74.5 4.7 %all-to-all-done.2.parts = f32[8,8,512]{2,1,0:T(8,128)S(1)} async-done(((f32[8,8,512]{2,1,0:T(8,128)}), f32[8,8,512]{2,1,0:T(8,128)S(1)}, u32[]{:S(2)}, u32[]{:S(2)}) %all-to-all-start.2) | async-done | bytes 131104 | tf_op jit(solution)/shard_map/all_to_all | solution.py:40
  79.2 1.1 shard_map.197
  80.3 6.6 %all-to-all-start.3 = ((bf16[64,8,256]{2,1,0:T(8,128)(2,1)}), bf16[64,8,256]{2,1,0:T(8,128)(2,1)S(1)}, u32[]{:S(2)}, u32[]{:S(2)}) async-start(bf16[64,8,256]{2,1,0:T(8,128)(2,1)} %get-tuple-element.30), calls=%async_computation.3 | async-start | bytes 524288 | tf_op jit(solution)/shard_map/all_to_all | solution.py:44
  86.9 7.7 %all-gather.6.cloned.1.call-done = bf16[8,2,64,512]{3,2,1,0:T(8,128)(2,1)} async-done(((bf16[2,2,64,512]{3,2,1,0:T(8,128)(2,1)}), bf16[8,2,64,512]{3,2,1,0:T(8,128)(2,1)}) %all-gather.6.cloned.1.call-update) | async-done | bytes 1048592 | tf_op jit(solution)/shard_map/all_gather | solution.py:403
  94.6 1.3 fusion.2
  96.0 4.9 %all-to-all-done.3 = bf16[64,8,256]{2,1,0:T(8,128)(2,1)S(1)} async-done(((bf16[64,8,256]{2,1,0:T(8,128)(2,1)}), bf16[64,8,256]{2,1,0:T(8,128)(2,1)S(1)}, u32[]{:S(2)}, u32[]{:S(2)}) %all-to-all-start.3) | async-done | bytes 262176 | tf_op jit(solution)/shard_map/all_to_all | solution.py:44
  101.0 1.5 shard_map.198
  102.4 3.4 %all-to-all-start.4 = ((f32[8,4,640]{2,1,0:T(4,128)}), f32[8,4,640]{2,1,0:T(4,128)S(1)}, u32[]{:S(2)}, u32[]{:S(2)}) async-start(f32[8,4,640]{2,1,0:T(4,128)} %get-tuple-element.34), calls=%async_computation.4 | async-start | bytes 163840 | tf_op jit(solution)/shard_map/all_to_all | solution.py:44
  105.8 1.3 copy.48.down
  107.2 6.7 %shard_map.199 = (bf16[304,32]{1,0:T(8,128)(2,1)}, bf16[304,128]{1,0:T(8,128)(2,1)}, bf16[304,128]{1,0:T(8,128)(2,1)}) custom-call(bf16[304,4096]{1,0:T(8,128)(2,1)} %bitcast.78, bf16[4096,128]{1,0:T(8,128)(2,1)} %key_weight.3, bf16[4096,128]{1,0:T(8,128)(2,1)} %value_weight.3, bf16[4096,32]{1,0:T(8,128)(2,1)} %copy.48.down, bf16[16,128]{1,0:T(8,128)(2,1)} %key_up.3, ...), custom_call_target="tpu_custom_call" | custom-call | flops 1073741824 | bytes 1048576 | tf_op jit(solution)/shard_map/pallas_call | solution.py:438
  113.9 0.6 copy-done.4
  114.5 4.1 %shard_map.200 = (bf16[304,128]{1,0:T(8,128)(2,1)}, bf16[304,128]{1,0:T(8,128)(2,1)}, bf16[304,32]{1,0:T(8,128)(2,1)}, f32[4,128]{1,0:T(4,128)}, bf16[32,48,128]{2,1,0:T(8,128)(2,1)}) custom-call(s32[1,2]{1,0:T(1,128)} %bitcast.94, f32[8,4,640]{2,1,0:T(4,128)} %copy-done.4, bf16[304,128]{1,0:T(8,128)(2,1)} %get-tuple-element.36.keys, ...), custom_call_target="tpu_custom_call" | custom-call | flops 67108864 | bytes 1048576 | tf_op jit(solution)/shard_map/pallas_call | solution.py:462
  118.6 8.7 %all-to-all-start.5 = ((bf16[32,48,128]{2,1,0:T(8,128)(2,1)}), bf16[32,48,128]{2,1,0:T(8,128)(2,1)S(1)}, u32[]{:S(2)}, u32[]{:S(2)}) async-start(bf16[32,48,128]{2,1,0:T(8,128)(2,1)} %get-tuple-element.39), calls=%async_computation.5 | async-start | bytes 786432 | tf_op jit(solution)/shard_map/all_to_all | solution.py:44
  127.4 5.2 %shard_map.201 = bf16[304,4096]{1,0:T(8,128)(2,1)} custom-call(bf16[304,128]{1,0:T(8,128)(2,1)} %get-tuple-element.40.key_change, bf16[304,128]{1,0:T(8,128)(2,1)} %get-tuple-element.41.value_change, bf16[304,32]{1,0:T(8,128)(2,1)} %get-tuple-element.42.coef, bf16[4096,128]{1,0:T(8,128)(2,1)} %key_weight.3, bf16[4096,128]{1,0:T(8,128)(2,1)} %value_weight.3, ...), custom_call_target="tpu_custom_call" | custom-call | flops 1073741824 | bytes 1048576 | tf_op jit(solution)/shard_map/pallas_call | solution.py:484
  132.6 6.3 %all-to-all-done.5.received = bf16[32,48,128]{2,1,0:T(8,128)(2,1)S(1)} async-done(((bf16[32,48,128]{2,1,0:T(8,128)(2,1)}), bf16[32,48,128]{2,1,0:T(8,128)(2,1)S(1)}, u32[]{:S(2)}, u32[]{:S(2)}) %all-to-all-start.5) | async-done | bytes 393248 | tf_op jit(solution)/shard_map/all_to_all | solution.py:44
  138.9 1.2 shard_map.202
  140.1 12.5 %all-to-all-start.6 = ((bf16[16,48,128]{2,1,0:T(8,128)(2,1)}), bf16[16,48,128]{2,1,0:T(8,128)(2,1)S(1)}, u32[]{:S(2)}, u32[]{:S(2)}) async-start(bf16[16,48,128]{2,1,0:T(8,128)(2,1)} %shard_map.202), calls=%async_computation.6 | async-start | bytes 393216 | tf_op jit(solution)/shard_map/all_to_all | solution.py:44
  152.6 1.3 iota_compare_fusion
  154.0 10.9 %all-to-all-done.6.received = bf16[16,48,128]{2,1,0:T(8,128)(2,1)S(1)} async-done(((bf16[16,48,128]{2,1,0:T(8,128)(2,1)}), bf16[16,48,128]{2,1,0:T(8,128)(2,1)S(1)}, u32[]{:S(2)}, u32[]{:S(2)}) %all-to-all-start.6) | async-done | bytes 196640 | tf_op jit(solution)/shard_map/all_to_all | solution.py:44
  164.8 0.8 shard_map.203
  165.6 3.9 %all-to-all-start.7 = ((bf16[32,48,128]{2,1,0:T(8,128)(2,1)}), bf16[32,48,128]{2,1,0:T(8,128)(2,1)S(1)}, u32[]{:S(2)}, u32[]{:S(2)}) async-start(bf16[32,48,128]{2,1,0:T(8,128)(2,1)} %get-tuple-element.45), calls=%async_computation.7 | async-start | bytes 786432 | tf_op jit(solution)/shard_map/all_to_all | solution.py:44
  169.5 3.6 %collective-permute-start.2 = (bf16[10,512]{1,0:T(8,128)(2,1)S(1)}, bf16[10,512]{1,0:T(8,128)(2,1)S(1)}, u32[]{:S(2)}, u32[]{:S(2)}) collective-permute-start(bf16[10,512]{1,0:T(8,128)(2,1)S(1)} %pad_maximum_fusion.6), channel_id=1, source_target_pairs={{0,0},{1,64},{2,128},{3,192},{4,256},{5,320},{6,384},{7,448},{64,1... | collective-permute-start | bytes 30728 | tf_op jit(solution)/shard_map/ppermute | solution.py:512
  173.2 0.8 fusion
  173.9 7.3 %collective-permute-done.2 = bf16[10,512]{1,0:T(8,128)(2,1)S(1)} collective-permute-done((bf16[10,512]{1,0:T(8,128)(2,1)S(1)}, bf16[10,512]{1,0:T(8,128)(2,1)S(1)}, u32[]{:S(2)}, u32[]{:S(2)}) %collective-permute-start.2) | collective-permute-done | bytes 10272 | tf_op jit(solution)/shard_map/ppermute | solution.py:512
  181.2 0.6 slice.98
  181.8 2.3 %all-to-all-done.7 = bf16[32,48,128]{2,1,0:T(8,128)(2,1)S(1)} async-done(((bf16[32,48,128]{2,1,0:T(8,128)(2,1)}), bf16[32,48,128]{2,1,0:T(8,128)(2,1)S(1)}, u32[]{:S(2)}, u32[]{:S(2)}) %all-to-all-start.7) | async-done | bytes 393248 | tf_op jit(solution)/shard_map/all_to_all | solution.py:44
  184.1 0.6 convert_reduce_fusion
  185.4 0.6 fusion.5
  186.0 0.8 fusion.3
  186.9 1.9 add_convert_fusion
  (52 shorter events, 0.8 us)
Async XLA Ops:
  7.2 66.3 %all-gather.4.cloned.1.call-start = ((), (), s32[]{:S(2)}) async-start(), calls=%async_computation.9 | async-start | bytes 2801664 | tf_op jit(solution)/shard_map/all_gather | solution.py:359
  7.9 38.8 %copy-start.8 = (s32[2,1]{0,1:T(1,128)S(1)}, s32[2,1]{0,1:T(1,128)}, u32[]{:S(2)}) copy-start(s32[2,1]{0,1:T(1,128)} %param.19) | copy-start | bytes 28
  9.4 22.1 %all-to-all-start = ((bf16[16,16,512]{2,1,0:T(8,128)(2,1)}), bf16[16,16,512]{2,1,0:T(8,128)(2,1)S(1)}, u32[]{:S(2)}, u32[]{:S(2)}) async-start(bf16[16,16,512]{2,1,0:T(8,128)(2,1)} %broadcast_in_dim.64), calls=%async_computation | async-start | bytes 524288 | tf_op jit(solution)/shard_map/all_to_all | solution.py:40
  31.4 29.1 %copy-start.5 = (bf16[4096,16]{0,1:T(8,128)(2,1)S(1)}, bf16[4096,16]{0,1:T(8,128)(2,1)}, u32[]{:S(2)}) copy-start(bf16[4096,16]{0,1:T(8,128)(2,1)} %param.24) | copy-start | bytes 393220
  32.5 33.3 %all-to-all-start.1 = ((bf16[32,24,512]{2,1,0:T(8,128)(2,1)}), bf16[32,24,512]{2,1,0:T(8,128)(2,1)S(1)}, u32[]{:S(2)}, u32[]{:S(2)}) async-start(bf16[32,24,512]{2,1,0:T(8,128)(2,1)} %bitcast.8), calls=%async_computation.1 | async-start | bytes 1572864 | tf_op jit(solution)/shard_map/all_to_all | solution.py:44
  43.7 25.5 %copy-start.7 = (bf16[8,512]{1,0:T(8,128)(2,1)S(1)}, bf16[8,512]{1,0:T(8,128)(2,1)}, u32[]{:S(2)}) copy-start(bf16[8,512]{1,0:T(8,128)(2,1)} %param.14) | copy-start | bytes 24580
  43.7 50.9 %all-gather.6.cloned.1.call-start = ((), (), s32[]{:S(2)}) async-start(), calls=%async_computation.11 | async-start | bytes 1310720 | tf_op jit(solution)/shard_map/all_gather | solution.py:403
  43.7 16.0 %collective-permute-start.1 = (bf16[2,64,512]{2,1,0:T(8,128)(2,1)S(1)}, bf16[2,64,512]{2,1,0:T(8,128)(2,1)S(1)}, u32[]{:S(2)}, u32[]{:S(2)}) collective-permute-start(bf16[2,64,512]{2,1,0:T(8,128)(2,1)S(1)} %pad_maximum_fusion.3), channel_id=1, source_target_pairs={{0,8},{8,0},{1,9},{9,1},{2,10},{10,2},{3,11},{11,3},{4,12},{12,4},... | collective-permute-start | bytes 393224 | tf_op jit(solution)/shard_map/ppermute | solution.py:400
  59.7 19.5 %copy-start = (s32[8,4]{0,1:T(4,128)S(1)}, s32[8,4]{0,1:T(4,128)}, u32[]{:S(2)}) copy-start(s32[8,4]{0,1:T(4,128)} %param.17) | copy-start | bytes 388
  59.7 19.5 %copy-start.2 = (s32[8]{0:T(128)S(1)}, s32[8]{0:T(128)}, u32[]{:S(2)}) copy-start(s32[8]{0:T(128)} %param.16) | copy-start | bytes 100
  65.8 30.1 %collective-permute-start = (bf16[32,8,512]{2,1,0:T(8,128)(2,1)S(1)}, bf16[32,8,512]{2,1,0:T(8,128)(2,1)S(1)}, u32[]{:S(2)}, u32[]{:S(2)}) collective-permute-start(bf16[32,8,512]{2,1,0:T(8,128)(2,1)S(1)} %slice.94), channel_id=1, source_target_pairs={{0,1},{1,0},{2,3},{3,2},{4,5},{5,4},{6,7},{7,6},{8,9},{9,8},{10,11... | collective-permute-start | bytes 786440 | tf_op jit(solution)/shard_map/ppermute | solution.py:382
  70.1 9.1 %all-to-all-start.2 = ((f32[8,8,512]{2,1,0:T(8,128)}), f32[8,8,512]{2,1,0:T(8,128)S(1)}, u32[]{:S(2)}, u32[]{:S(2)}) async-start(f32[8,8,512]{2,1,0:T(8,128)} %broadcast_in_dim.68), calls=%async_computation.2 | async-start | bytes 262144 | tf_op jit(solution)/shard_map/all_to_all | solution.py:40
  80.3 20.7 %all-to-all-start.3 = ((bf16[64,8,256]{2,1,0:T(8,128)(2,1)}), bf16[64,8,256]{2,1,0:T(8,128)(2,1)S(1)}, u32[]{:S(2)}, u32[]{:S(2)}) async-start(bf16[64,8,256]{2,1,0:T(8,128)(2,1)} %get-tuple-element.30), calls=%async_computation.3 | async-start | bytes 524288 | tf_op jit(solution)/shard_map/all_to_all | solution.py:44
  95.8 9.9 %copy-start.6 = (bf16[4096,16]{0,1:T(8,128)(2,1)S(1)}, bf16[4096,16]{0,1:T(8,128)(2,1)}, u32[]{:S(2)}) copy-start(bf16[4096,16]{0,1:T(8,128)(2,1)} %param.26) | copy-start | bytes 393220
  102.4 11.5 %all-to-all-start.4 = ((f32[8,4,640]{2,1,0:T(4,128)}), f32[8,4,640]{2,1,0:T(4,128)S(1)}, u32[]{:S(2)}, u32[]{:S(2)}) async-start(f32[8,4,640]{2,1,0:T(4,128)} %get-tuple-element.34), calls=%async_computation.4 | async-start | bytes 163840 | tf_op jit(solution)/shard_map/all_to_all | solution.py:44
  105.8 8.1 %copy-start.3 = (bf16[4096,32]{0,1:T(8,128)(2,1)}, bf16[4096,32]{0,1:T(8,128)(2,1)S(1)}, u32[]{:S(2)}) copy-start(bf16[4096,32]{0,1:T(8,128)(2,1)S(1)} %constant_dynamic-update-slice_fusion) | copy-start | bytes 786436
  113.9 0.6 copy-start.4
  118.6 20.2 %all-to-all-start.5 = ((bf16[32,48,128]{2,1,0:T(8,128)(2,1)}), bf16[32,48,128]{2,1,0:T(8,128)(2,1)S(1)}, u32[]{:S(2)}, u32[]{:S(2)}) async-start(bf16[32,48,128]{2,1,0:T(8,128)(2,1)} %get-tuple-element.39), calls=%async_computation.5 | async-start | bytes 786432 | tf_op jit(solution)/shard_map/all_to_all | solution.py:44
  127.3 59.5 %reduce-scatter.2.cloned.1.call-start = ((), (), s32[]{:S(2)}) async-start(), calls=%async_computation.10 | async-start | bytes 2801664 | tf_op jit(solution)/shard_map/reduce_scatter | solution.py:488
  132.6 6.3 %copy-start.1 = (f32[4,128]{1,0:T(4,128)S(1)}, f32[4,128]{1,0:T(4,128)}, u32[]{:S(2)}) copy-start(f32[4,128]{1,0:T(4,128)} %get-tuple-element.44.loss) | copy-start | bytes 6148
  140.1 24.7 %all-to-all-start.6 = ((bf16[16,48,128]{2,1,0:T(8,128)(2,1)}), bf16[16,48,128]{2,1,0:T(8,128)(2,1)S(1)}, u32[]{:S(2)}, u32[]{:S(2)}) async-start(bf16[16,48,128]{2,1,0:T(8,128)(2,1)} %shard_map.202), calls=%async_computation.6 | async-start | bytes 393216 | tf_op jit(solution)/shard_map/all_to_all | solution.py:44
  165.6 18.5 %all-to-all-start.7 = ((bf16[32,48,128]{2,1,0:T(8,128)(2,1)}), bf16[32,48,128]{2,1,0:T(8,128)(2,1)S(1)}, u32[]{:S(2)}, u32[]{:S(2)}) async-start(bf16[32,48,128]{2,1,0:T(8,128)(2,1)} %get-tuple-element.45), calls=%async_computation.7 | async-start | bytes 786432 | tf_op jit(solution)/shard_map/all_to_all | solution.py:44
  169.5 11.7 %collective-permute-start.2 = (bf16[10,512]{1,0:T(8,128)(2,1)S(1)}, bf16[10,512]{1,0:T(8,128)(2,1)S(1)}, u32[]{:S(2)}, u32[]{:S(2)}) collective-permute-start(bf16[10,512]{1,0:T(8,128)(2,1)S(1)} %pad_maximum_fusion.6), channel_id=1, source_target_pairs={{0,0},{1,64},{2,128},{3,192},{4,256},{5,320},{6,384},{7,448},{64,1... | collective-permute-start | bytes 30728 | tf_op jit(solution)/shard_map/ppermute | solution.py:512
Sparse Core Ops, SparseCore 0:
  10.1 51.2 all-gather.3
  64.0 30.4 all-gather.5
  139.0 46.7 reduce-scatter.1
